TPU v7x, 128 devices: a whole 4x4x4 slice. The times are simulated.
128 devices in a mesh: row: 8 (over x, y_hi), col: 16 (over y_lo, z, core).
Axes of the slice: x: 4, y: 4 (y_hi: 2, y_lo: 2; y = y_hi * 2 + y_lo), z: 4, core: 2. Of those that a mesh axis runs over, the one named last changes fastest.
Arguments:
- coupling: bfloat16 [32768, 32768], P('row', 'col'), may hold values from -0.03125 to 0.03125
- amplitude: float32 [64, 32768], P(None, 'col'), may hold values from -0.95 to 0.95
- target: float32 [64, 32768], P(None, 'col'), may hold values from -6 to 6
- shadow_target: float32 [64, 32768], P(None, 'col'), may hold values from -10.2 to 10.2
Outputs:
- solution: float32 [64, 32768], P(None, 'col')
- shadow_solution: float32 [64, 32768], P(None, 'col')
- residual: float32 [64, 32768], P(None, 'col')
- shadow_residual: float32 [64, 32768], P(None, 'col')
All inputs are finite; a program needn't handle non-finite values.
Results may differ from a plain program's by a relative error of at most 0.0036.
Values may be sent and summed in bfloat16 or wider, within the bound.
No kernel may reach another device: no remote copies, remote signals or barrier semaphores. Data moves between devices by JAX's collectives and lax.ppermute only.
A program may use at most 128 MiB of HBM per device.

v0:
```python
import jax
import jax.numpy as jnp
from jax import lax
from jax.sharding import PartitionSpec as P

ITERS = 2


SELF_GAIN = 0.5
COUPLE_GAIN = 0.3


def on_device(coupling, amplitude, target, shadow_target):
    row_rows = coupling.shape[0]
    col_rows = coupling.shape[1]
    row_index = lax.axis_index("row")
    col_index = lax.axis_index("col")
    slope = 1.0 - amplitude * amplitude
    solution = jnp.zeros_like(target)
    shadow_solution = jnp.zeros_like(target)
    residual = target
    shadow_residual = shadow_target
    direction = target
    shadow_direction = shadow_target
    align = lax.psum(jnp.sum(shadow_residual * residual, axis=1), "col")
    for iteration in range(ITERS):
        scaled = (slope * direction).astype(jnp.bfloat16)
        primary_gathered = lax.all_gather(scaled, "col", axis=1, tiled=True)
        row_block = lax.dynamic_slice_in_dim(primary_gathered, row_index * row_rows, row_rows, 1)
        primary_partial_value = jnp.dot(row_block, coupling, preferred_element_type=jnp.float32)
        product = lax.psum(primary_partial_value, "row")
        image = direction - SELF_GAIN * slope * direction - COUPLE_GAIN * product
        shadow_scaled = shadow_direction.astype(jnp.bfloat16)
        partial_value = lax.dot_general(
            shadow_scaled, coupling, (((1,), (1,)), ((), ())), preferred_element_type=jnp.float32
        )
        summed = lax.psum(partial_value, "col")
        gathered = lax.all_gather(summed, "row", axis=1, tiled=True)
        own_block = lax.dynamic_slice_in_dim(gathered, col_index * col_rows, col_rows, 1)
        shadow_image = (
            shadow_direction
            - SELF_GAIN * slope * shadow_direction
            - COUPLE_GAIN * slope * own_block
        )
        curve = lax.psum(jnp.sum(shadow_direction * image, axis=1), "col")
        step_size = align / curve
        column_step = step_size[:, None]
        solution = solution + column_step * direction
        shadow_solution = shadow_solution + column_step * shadow_direction
        residual = residual - column_step * image
        shadow_residual = shadow_residual - column_step * shadow_image
        if iteration + 1 < ITERS:
            align_next = lax.psum(jnp.sum(shadow_residual * residual, axis=1), "col")
        if iteration + 1 < ITERS:
            blend = (align_next / align)[:, None]
            direction = residual + blend * direction
            shadow_direction = shadow_residual + blend * shadow_direction
            align = align_next
    return (solution, shadow_solution, residual, shadow_residual)


def solution(mesh):
    return jax.shard_map(
        on_device,
        mesh=mesh,
        in_specs=(P("row", "col"), P(None, "col"), P(None, "col"), P(None, "col")),
        out_specs=(P(None, "col"), P(None, "col"), P(None, "col"), P(None, "col")),
        check_vma=False,
    )
```

profile of v0, /device:TPU:0, one launch (start us, length us, event | category | flops | bytes accessed | tf_op | source)
XLA Modules:
  0.0 766.2 jit_solution(14258358741011477803)
XLA Ops:
  7.2 0.0 all-gather.5.cloned.1.call-start
  7.2 2.1 multiply_convert_fusion.1
  9.3 0.0 all-gather.5.cloned.1.call-update
  9.3 0.0 all-reduce.8.cloned.1.call-start
  9.4 12.1 %fusion.14 = f32[64,4096]{1,0:T(8,128)} fusion(bf16[4096,2048]{1,0:T(8,128)(2,1)} %param.4, f32[64,2048]{1,0:T(8,128)} %param.7), kind=kOutput, calls=%fused_computation.31 | convolution fusion | flops 1073872896 | bytes 18350080 | tf_op jit(solution)/shard_map/dot_general | solution.py:34
  21.5 0.0 copy-start
  21.5 0.0 copy-start.1
  21.5 0.0 copy-start.2
  21.5 0.0 all-reduce.8.cloned.1.call-update
  21.5 0.0 all-reduce.6.cloned.1.call-start
  21.6 28.6 %all-gather.5.cloned.1.call-done = bf16[64,32768]{1,0:T(8,128)(2,1)} async-done(((bf16[64,2048]{1,0:T(8,128)(2,1)}), bf16[64,32768]{1,0:T(8,128)(2,1)}) %all-gather.5.cloned.1.call-update) | async-done | bytes 4194320 | tf_op jit(solution)/shard_map/all_gather | solution.py:28
  50.2 9.8 %fusion.10 = f32[64,2048]{1,0:T(8,128)} fusion(bf16[4096,2048]{1,0:T(8,128)(2,1)} %param.4, bf16[64,32768]{1,0:T(8,128)(2,1)} %all-gather.5.cloned.1.call-done, s32[]{:T(128)S(6)} %select_n.8), kind=kOutput, calls=%fused_computation.24 | convolution fusion | flops 1073741824 | bytes 17825796 | tf_op jit(solution)/shard_map/dot_general | solution.py:30
  60.0 0.0 all-reduce.6.cloned.1.call-update
  60.0 0.0 all-gather.7.cloned.1.call-start
  60.0 112.2 %all-reduce.8.cloned.1.call-done = f32[64,4096]{1,0:T(8,128)} async-done(((f32[64,4096]{1,0:T(8,128)}), f32[64,4096]{1,0:T(8,128)}) %all-reduce.8.cloned.1.call-update) | async-done | bytes 1048592 | tf_op jit(solution)/shard_map/psum | solution.py:37
  172.2 0.0 all-gather.7.cloned.1.call-update
  172.2 0.0 all-gather.9.cloned.1.call-start
  172.3 89.5 %all-reduce.6.cloned.1.call-done = f32[64,2048]{1,0:T(8,128)} async-done(((f32[64,2048]{1,0:T(8,128)}), f32[64,2048]{1,0:T(8,128)}) %all-reduce.6.cloned.1.call-update) | async-done | bytes 524304 | tf_op jit(solution)/shard_map/psum | solution.py:31
  261.8 0.0 copy-done
  261.8 0.0 copy-done.1
  261.8 0.0 copy-done.2
  261.8 1.3 multiply_reduce_fusion.2
  263.1 27.3 %all-reduce = (f32[64]{0:T(128)S(1)}, f32[64]{0:T(128)S(1)}) all-reduce(f32[64]{0:T(128)S(1)} %get-tuple-element.5, f32[64]{0:T(128)S(1)} %get-tuple-element.4), channel_id=1, replica_groups=mesh['row'=8,'col'=16] {'col'}, use_global_device_ids=true, to_apply=%region_1.0 | all-reduce | flops 128 | bytes 1024 | tf_op jit(solution)/shard_map/psum | solution.py:25
  290.5 80.2 %all-gather.7.cloned.1.call-done = f32[64,32768]{1,0:T(8,128)} async-done(((f32[64,4096]{1,0:T(8,128)}), f32[64,32768]{1,0:T(8,128)}) %all-gather.7.cloned.1.call-update) | async-done | bytes 8388624 | tf_op jit(solution)/shard_map/all_gather | solution.py:38
  370.7 1.6 multiply_reduce_fusion.1
  372.3 29.1 %psum.60 = f32[64]{0:T(128)S(1)} all-reduce(f32[64]{0:T(128)S(1)} %get-tuple-element.10), channel_id=1, replica_groups=mesh['row'=8,'col'=16] {'col'}, use_global_device_ids=true, to_apply=%region_7.0 | all-reduce | flops 64 | bytes 512 | tf_op jit(solution)/shard_map/psum | solution.py:53
  401.5 0.9 multiply_convert_fusion
  402.3 0.0 all-gather.9.cloned.1.call-update
  402.3 0.0 all-reduce.12.cloned.1.call-start
  402.4 12.0 %fusion.12 = f32[64,4096]{1,0:T(8,128)} fusion(bf16[4096,2048]{1,0:T(8,128)(2,1)} %param.4, f32[64,2048]{1,0:T(8,128)S(1)} %get-tuple-element.12, f32[64,2048]{1,0:T(8,128)S(1)} %copy-done, f32[64]{0:T(128)S(1)} %div.10), kind=kOutput, calls=%fused_computation.29 | convolution fusion | flops 1074135040 | bytes 18874624 | tf_op jit(solution)/shard_map/dot_general | solution.py:34
  414.4 0.0 all-reduce.12.cloned.1.call-update
  414.4 0.2 all-reduce.10.cloned.1.call-start
  414.6 21.6 %all-gather.9.cloned.1.call-done = bf16[64,32768]{1,0:T(8,128)(2,1)} async-done(((bf16[64,2048]{1,0:T(8,128)(2,1)}), bf16[64,32768]{1,0:T(8,128)(2,1)}) %all-gather.9.cloned.1.call-update) | async-done | bytes 4194320 | tf_op jit(solution)/shard_map/all_gather | solution.py:28
  436.2 9.8 %fusion.8 = f32[64,2048]{1,0:T(8,128)} fusion(bf16[4096,2048]{1,0:T(8,128)(2,1)} %param.4, bf16[64,32768]{1,0:T(8,128)(2,1)} %all-gather.9.cloned.1.call-done, s32[]{:T(128)S(6)} %select_n.8), kind=kOutput, calls=%fused_computation.16 | convolution fusion | flops 1073741824 | bytes 17825796 | tf_op jit(solution)/shard_map/dot_general | solution.py:30
  446.0 0.0 all-reduce.10.cloned.1.call-update
  446.0 0.0 all-gather.11.cloned.1.call-start
  446.1 112.0 %all-reduce.12.cloned.1.call-done = f32[64,4096]{1,0:T(8,128)} async-done(((f32[64,4096]{1,0:T(8,128)}), f32[64,4096]{1,0:T(8,128)}) %all-reduce.12.cloned.1.call-update) | async-done | bytes 1048592 | tf_op jit(solution)/shard_map/psum | solution.py:37
  558.1 0.0 all-gather.11.cloned.1.call-update
  558.1 89.6 %all-reduce.10.cloned.1.call-done = f32[64,2048]{1,0:T(8,128)} async-done(((f32[64,2048]{1,0:T(8,128)}), f32[64,2048]{1,0:T(8,128)}) %all-reduce.10.cloned.1.call-update) | async-done | bytes 524304 | tf_op jit(solution)/shard_map/psum | solution.py:31
  647.6 1.4 multiply_reduce_fusion
  649.1 27.3 %psum.62 = f32[64]{0:T(128)S(1)} all-reduce(f32[64]{0:T(128)S(1)} %get-tuple-element.8), channel_id=1, replica_groups=mesh['row'=8,'col'=16] {'col'}, use_global_device_ids=true, to_apply=%region_10.0 | all-reduce | flops 64 | bytes 512 | tf_op jit(solution)/shard_map/psum | solution.py:45
  676.4 80.3 %all-gather.11.cloned.1.call-done = f32[64,32768]{1,0:T(8,128)} async-done(((f32[64,4096]{1,0:T(8,128)}), f32[64,32768]{1,0:T(8,128)}) %all-gather.11.cloned.1.call-update) | async-done | bytes 8388624 | tf_op jit(solution)/shard_map/all_gather | solution.py:38
  756.7 2.7 multiply_subtract_fusion.4
  (3 shorter events, 0.0 us)
Async XLA Ops:
  7.2 43.0 %all-gather.5.cloned.1.call-start = ((), (), s32[]{:S(2)}) async-start(), calls=%async_computation | async-start | bytes 4456448 | tf_op jit(solution)/shard_map/all_gather | solution.py:28
  9.3 162.9 %all-reduce.8.cloned.1.call-start = ((), (), s32[]{:S(2)}) async-start(), calls=%async_computation.2 | async-start | bytes 2097152 | tf_op jit(solution)/shard_map/psum | solution.py:37
  21.5 240.3 %copy-start = (f32[64,2048]{1,0:T(8,128)S(1)}, f32[64,2048]{1,0:T(8,128)}, u32[]{:S(2)}) copy-start(f32[64,2048]{1,0:T(8,128)} %param.7) | copy-start | bytes 1572868
  21.5 240.3 %copy-start.1 = (f32[64,2048]{1,0:T(8,128)S(1)}, f32[64,2048]{1,0:T(8,128)}, u32[]{:S(2)}) copy-start(f32[64,2048]{1,0:T(8,128)} %param.6) | copy-start | bytes 1572868
  21.5 240.3 %copy-start.2 = (f32[64,2048]{1,0:T(8,128)S(1)}, f32[64,2048]{1,0:T(8,128)}, u32[]{:S(2)}) copy-start(f32[64,2048]{1,0:T(8,128)} %param.5) | copy-start | bytes 1572868
  21.5 240.3 %all-reduce.6.cloned.1.call-start = ((), (), s32[]{:S(2)}) async-start(), calls=%async_computation.1 | async-start | bytes 1048576 | tf_op jit(solution)/shard_map/psum | solution.py:31
  60.0 310.7 %all-gather.7.cloned.1.call-start = ((), (), s32[]{:S(2)}) async-start(), calls=%async_computation.3 | async-start | bytes 9437184 | tf_op jit(solution)/shard_map/all_gather | solution.py:38
  172.2 264.0 %all-gather.9.cloned.1.call-start = ((), (), s32[]{:S(2)}) async-start(), calls=%async_computation.4 | async-start | bytes 4456448 | tf_op jit(solution)/shard_map/all_gather | solution.py:28
  402.3 155.7 %all-reduce.12.cloned.1.call-start = ((), (), s32[]{:S(2)}) async-start(), calls=%async_computation.6 | async-start | bytes 2097152 | tf_op jit(solution)/shard_map/psum | solution.py:37
  414.4 233.2 %all-reduce.10.cloned.1.call-start = ((), (), s32[]{:S(2)}) async-start(), calls=%async_computation.5 | async-start | bytes 1048576 | tf_op jit(solution)/shard_map/psum | solution.py:31
  446.0 310.7 %all-gather.11.cloned.1.call-start = ((), (), s32[]{:S(2)}) async-start(), calls=%async_computation.7 | async-start | bytes 9437184 | tf_op jit(solution)/shard_map/all_gather | solution.py:38
Sparse Core Ops, SparseCore 0:
  10.2 39.9 all-gather.4
  52.7 119.4 all-reduce.7
  175.4 86.3 all-reduce.5
  264.0 106.6 all-gather.6
  402.5 33.6 all-gather.8
  438.5 119.4 all-reduce.11
  561.3 86.3 all-reduce.9
  650.0 106.6 all-gather.10
where the time goes:
time: 767 us; the launch traced here: 766 us
  waiting for transfers between devices  614 us (80%)
  blocking collectives  83.7 us (11%)
  matrix products  43.6 us (6%)
  between operations  14.2 us (2%)
  other arithmetic  10 us (1%)
    psum x2, waiting for transfers between devices, on_device(): summed = lax.psum(partial_value, 'col')  224 us
    psum x2, waiting for transfers between devices, on_device(): product = lax.psum(primary_partial_value, 'row')  179 us
    all_gather x2, waiting for transfers between devices, on_device(): gathered = lax.all_gather(summed, 'row', axis=1, tiled=True)  161 us
    all_gather x2, waiting for transfers between devices, on_device(): primary_gathered = lax.all_gather(scaled, 'col', axis=1, tiled=True)  50.2 us
    psum x1, blocking collectives, on_device(): align_next = lax.psum(jnp.sum(shadow_residual * residual, axis=1), 'col')  29.1 us
    psum x1, blocking collectives, on_device(): curve = lax.psum(jnp.sum(shadow_direction * image, axis=1), 'col')  27.3 us
    psum x1, blocking collectives, on_device(): align = lax.psum(jnp.sum(shadow_residual * residual, axis=1), 'col')  27.3 us
    dot_general x2, matrix products, on_device(): lax.dot_general(shadow_scaled, coupling, (((1,), (1,)), ((), ())), prefer...  24.1 us
  transfers between devices with their start and end apart: 8, of which 8 were waited for; matrix products, arithmetic and copies ran while one was open for 6% of the time, Pallas kernels for 0%

commit v1 on v0

v1 whole, which is shorter than its diff:
```python
import jax
import jax.numpy as jnp
from jax import lax
from jax.sharding import PartitionSpec as P

SELF_GAIN = 0.5
COUPLE_GAIN = 0.3

F32 = jnp.float32
BF16 = jnp.bfloat16
WIRE = jnp.float16
AXES = ("row", "col")

FIRST_SCALE = 32.0
SECOND_SCALE = 1.0 / 16.0


def split(d):
    row, col = divmod(d, 16)
    return row // 2, row % 2, col // 8, (col // 2) % 4, col % 2


def join(x, yh, yl, z, h):
    return (x * 2 + yh) * 16 + yl * 8 + z * 2 + h


def sends(source_of):
    return [(join(*source_of(*split(d))), d) for d in range(128)]


def flip_x(x, yh, yl, z, h):
    return x ^ 1, yh, yl, z, h


def mirror_x(x, yh, yl, z, h):
    return 3 - x, yh, yl, z, h


def flip_yh(x, yh, yl, z, h):
    return x, yh ^ 1, yl, z, h


def flip_yl(x, yh, yl, z, h):
    return x, yh, yl ^ 1, z, h


def flip_z(x, yh, yl, z, h):
    return x, yh, yl, z ^ 1, h


def mirror_z(x, yh, yl, z, h):
    return x, yh, yl, 3 - z, h


def flip_core(x, yh, yl, z, h):
    return x, yh, yl, z, h ^ 1


def by_core(first, second):
    return sends(lambda *d: (second if d[4] else first)(*d))


STEP = ({0: 2, 1: 1, 2: 0, 3: 3}, {0: 2, 1: 3, 2: 0, 3: 1})


def from_rows(x, yh, yl, z, h):
    xs, yhs = 2 * yl + z // 2, z % 2
    return xs, yhs, yl ^ yh ^ yhs, (z + STEP[h][(x - xs) % 4]) % 4, h


def from_cols(x, yh, yl, z, h):
    yls, zs = x // 2, (x % 2) * 2 + yh
    return (x + STEP[h][(z - zs) % 4]) % 4, yh ^ yl ^ yls, yls, zs, h


CORE = sends(flip_core)
TO_COLS = sends(from_rows)
TO_ROWS = sends(from_cols)
ROW_STEPS = (
    by_core(flip_x, flip_yh),
    by_core(mirror_x, flip_x),
    by_core(flip_yh, mirror_x),
)
COL_STEPS = (
    by_core(flip_yl, flip_z),
    by_core(flip_z, mirror_z),
    by_core(mirror_z, flip_yl),
)
SMALL_COL = (CORE, sends(flip_yl), sends(flip_z), sends(mirror_z))


def move(value, pairs):
    return lax.ppermute(value, AXES, pairs)


def chip_sum(value, steps):
    for pairs in steps:
        held = value.astype(WIRE)
        value = held.astype(F32) + move(held, pairs).astype(F32)
    return value


def on_device(coupling, amplitude, target, shadow_target):
    core = lax.axis_index("col") % 2
    first = core == 0
    g, gs = target, shadow_target
    slope = 1.0 - amplitude * amplitude
    keep = 1.0 - SELF_GAIN * slope

    tops = jnp.stack([jnp.max(jnp.abs(g), axis=1), jnp.max(jnp.abs(gs), axis=1)])
    sums = jnp.stack([jnp.sum(gs * g, axis=1), jnp.sum(gs * (keep * g), axis=1)])
    stats = jnp.concatenate([tops, sums])
    for pairs in SMALL_COL:
        other = move(stats, pairs)
        stats = jnp.concatenate(
            [jnp.maximum(stats[:2], other[:2]), stats[2:] + other[2:]]
        )
    tiny = 1e-30
    top = jnp.maximum(stats[0], tiny)[:, None]
    shadow_top = jnp.maximum(stats[1], tiny)[:, None]
    align = stats[2]
    alpha = jnp.clip(stats[2] / stats[3], 1.0, 2.05)
    alpha = jnp.where(jnp.isnan(alpha), 1.4, alpha)
    alpha_c = alpha[:, None]

    def rows_of(vector):
        scaled = (slope * vector).astype(BF16)
        mine = move(scaled, TO_ROWS)
        other = move(mine, CORE)
        low = jnp.where(first, mine, other)
        high = jnp.where(first, other, mine)
        return jnp.concatenate([low, high], axis=1)

    def primary(row_block):
        return jnp.dot(row_block, coupling, preferred_element_type=F32)

    def shadow(vector):
        return lax.dot_general(
            vector.astype(BF16),
            coupling,
            (((1,), (1,)), ((), ())),
            preferred_element_type=F32,
        )

    def primary_sum(partial, scale):
        return chip_sum(partial * scale, ROW_STEPS) * (1.0 / scale)

    def shadow_sum(partial, scale):
        low, high = partial[:, :2048] * scale, partial[:, 2048:] * scale
        mine = jnp.where(first, low, high)
        other = jnp.where(first, high, low).astype(WIRE)
        mine = mine + move(other, CORE).astype(F32)
        total = chip_sum(mine, COL_STEPS).astype(WIRE)
        return move(total, TO_COLS).astype(F32) * (1.0 / scale)

    shadow_partial = shadow(gs)
    primary_partial = primary(rows_of(g))
    product = primary_sum(primary_partial, FIRST_SCALE / top)
    shadow_product = shadow_sum(shadow_partial, FIRST_SCALE / shadow_top)
    p1 = keep * g - COUPLE_GAIN * product
    q1 = keep * gs - COUPLE_GAIN * slope * shadow_product
    u = g - alpha_c * p1
    us = gs - alpha_c * q1

    shadow_partial = shadow(us)
    primary_partial = primary(rows_of(u))
    product = primary_sum(primary_partial, SECOND_SCALE / top)
    shadow_product = shadow_sum(shadow_partial, SECOND_SCALE / shadow_top)
    p2 = keep * u - COUPLE_GAIN * product
    q2 = keep * us - COUPLE_GAIN * slope * shadow_product

    dots = jnp.stack(
        [
            jnp.sum(gs * p1, axis=1),
            jnp.sum(us * g, axis=1),
            jnp.sum(gs * u, axis=1),
            jnp.sum(us * u, axis=1),
            jnp.sum(us * p1, axis=1),
            jnp.sum(q1 * u, axis=1),
            jnp.sum(us * p2, axis=1),
        ]
    )
    for pairs in SMALL_COL:
        dots = dots + move(dots, pairs)
    curve, us_g, gs_u, us_u, us_p1, q1_u, us_p2 = (dots[i] for i in range(7))
    step = align / curve
    kappa = step / alpha
    rest = 1.0 - kappa
    align_next = rest * rest * align + kappa * rest * (us_g + gs_u) + kappa * kappa * us_u
    blend = align_next / align
    lead = rest + blend
    curve_next = (
        lead * lead * curve + lead * kappa * (us_p1 + q1_u) + kappa * kappa * us_p2
    )
    step_next = align_next / curve_next

    def column(value):
        return value[:, None]

    step, kappa, lead, step_next = map(column, (step, kappa, lead, step_next))
    direction = lead * g + kappa * u
    shadow_direction = lead * gs + kappa * us
    solution = step * g + step_next * direction
    shadow_solution = step * gs + step_next * shadow_direction
    residual = g - step * p1 - step_next * (lead * p1 + kappa * p2)
    shadow_residual = gs - step * q1 - step_next * (lead * q1 + kappa * q2)
    return (solution, shadow_solution, residual, shadow_residual)


def solution(mesh):
    return jax.shard_map(
        on_device,
        mesh=mesh,
        in_specs=(P("row", "col"), P(None, "col"), P(None, "col"), P(None, "col")),
        out_specs=(P(None, "col"), P(None, "col"), P(None, "col"), P(None, "col")),
        check_vma=False,
    )
```

time: 767 us -> 194 us (0.25)
  waiting for transfers between devices: 614 us -> 80.7 us
  blocking collectives: 83.7 us -> 0 us
  starting transfers between devices: 0.51 us -> 61.9 us
  between operations: 14.2 us -> 0.88 us
    psum x4 -> x0, waiting for transfers between devices: 403 us -> none  [the longest x2 224 us: on_device(): summed = lax.psum(partial_value, 'col')]
    all_gather x4 -> x0, waiting for transfers between devices: 211 us -> none  [the longest x2 161 us: on_device(): gathered = lax.all_gather(summed, 'row', axis=1, tiled=True)]
    psum x3 -> x0, blocking collectives: 83.7 us -> none  [the longest x1 29.1 us: on_device(): align_next = lax.psum(jnp.sum(shadow_residual * residual, axis=1), 'col')]
    ppermute x0 -> x28, waiting for transfers between devices: none -> 80.7 us  [move(): return lax.ppermute(value, AXES, pairs)]
    ppermute x0 -> x28, starting transfers between devices: none -> 61.9 us  [move(): return lax.ppermute(value, AXES, pairs)]
  transfers between devices with their start and end apart: 8 -> 28, of which waited for: 8 -> 18; matrix products, arithmetic and copies ran while one was open for 6% -> 11% of each run, Pallas kernels for 0% -> 0%
where the time goes in v1:
time: 194 us; the launch traced here: 193 us
  waiting for transfers between devices  80.7 us (42%)
  starting transfers between devices  61.9 us (32%)
  matrix products  39.5 us (20%)
  other arithmetic  10.3 us (5%)
    ppermute x28, waiting for transfers between devices, move(): return lax.ppermute(value, AXES, pairs)  80.7 us
    ppermute x28, starting transfers between devices, move(): return lax.ppermute(value, AXES, pairs)  61.9 us
    dot_general x2, matrix products, shadow(): lax.dot_general(vector.astype(BF16), coupling, (((1,), (1,)), ((), ())),...  21.9 us
    dot_general x2, matrix products, primary(): return jnp.dot(row_block, coupling, preferred_element_type=F32)  17.6 us
  transfers between devices with their start and end apart: 28, of which 18 were waited for; matrix products, arithmetic and copies ran while one was open for 11% of the time, Pallas kernels for 0%

profile of v1, /device:TPU:0, one launch (start us, length us, event | category | flops | bytes accessed | tf_op | source)
XLA Modules:
  0.0 193.3 jit_solution(9077678277587806926)
XLA Ops:
  0.6 1.8 multiply_reduce_fusion.8
  2.5 0.1 collective-permute-start
  2.6 1.1 collective-permute-done
  3.7 1.7 collective-permute-start.1
  5.5 1.9 collective-permute-done.1
  7.4 2.1 %collective-permute-start.2 = (f32[4,64]{1,0:T(4,128)S(1)}, f32[4,64]{1,0:T(4,128)S(1)}, u32[]{:S(2)}, u32[]{:S(2)}) collective-permute-start(f32[4,64]{1,0:T(4,128)S(1)} %pad_maximum_fusion.2), channel_id=1, source_target_pairs={{2,0},{3,1},{0,2},{1,3},{6,4},{7,5},{4,6},{5,7},{10,8},{11,9},{8,1... | collective-permute-start | bytes 3080 | tf_op jit(solution)/shard_map/ppermute | solution.py:93
  9.5 3.6 %collective-permute-start.4 = (bf16[64,2048]{1,0:T(8,128)(2,1)S(1)}, bf16[64,2048]{1,0:T(8,128)(2,1)S(1)}, u32[]{:S(2)}, u32[]{:S(2)}) collective-permute-start(bf16[64,2048]{1,0:T(8,128)(2,1)S(1)} %get-tuple-element.28), channel_id=1, source_target_pairs={{64,0},{65,1},{32,2},{97,3},{0,4},{1,5},{96,6},{33,7},{80,8},{81,9... | collective-permute-start | bytes 786440 | tf_op jit(solution)/shard_map/ppermute | solution.py:93
  13.1 4.0 %collective-permute-start.3 = (f32[4,64]{1,0:T(4,128)S(1)}, f32[4,64]{1,0:T(4,128)S(1)}, u32[]{:S(2)}, u32[]{:S(2)}) collective-permute-start(f32[4,64]{1,0:T(4,128)S(1)} %pad_maximum_fusion.3), channel_id=1, source_target_pairs={{6,0},{7,1},{4,2},{5,3},{2,4},{3,5},{0,6},{1,7},{14,8},{15,9},{12,... | collective-permute-start | bytes 3080 | tf_op jit(solution)/shard_map/ppermute | solution.py:93
  17.1 5.2 %collective-permute-done.4 = bf16[64,2048]{1,0:T(8,128)(2,1)S(1)} collective-permute-done((bf16[64,2048]{1,0:T(8,128)(2,1)S(1)}, bf16[64,2048]{1,0:T(8,128)(2,1)S(1)}, u32[]{:S(2)}, u32[]{:S(2)}) %collective-permute-start.4) | collective-permute-done | bytes 262176 | tf_op jit(solution)/shard_map/ppermute | solution.py:93
  22.3 1.5 collective-permute-done.5
  23.8 8.8 %fusion = f16[64,2048]{1,0:T(8,128)(2,1)S(1)} fusion(bf16[4096,2048]{1,0:T(8,128)(2,1)} %param.4, bf16[64,2048]{1,0:T(8,128)(2,1)S(1)} %get-tuple-element.34, bf16[64,2048]{1,0:T(8,128)(2,1)S(1)} %get-tuple-element.33, f32[64]{0:T(128)S(1)} %get-tuple-element.53), kind=kOutput, calls=%fused_computation.2 | convolution fusion | flops 1075052544 | bytes 17563904 | tf_op jit(solution)/shard_map/dot_general | solution.py:135
  32.7 0.4 collective-permute-start.6
  33.1 6.0 %collective-permute-done.6 = f16[64,2048]{1,0:T(8,128)(2,1)S(1)} collective-permute-done((f16[64,2048]{1,0:T(8,128)(2,1)S(1)}, f16[64,2048]{1,0:T(8,128)(2,1)S(1)}, u32[]{:S(2)}, u32[]{:S(2)}) %collective-permute-start.6) | collective-permute-done | bytes 262176 | tf_op jit(solution)/shard_map/ppermute | solution.py:93
  39.1 0.1 add_convert_fusion.11
  39.2 18.1 %collective-permute-start.7 = (f16[64,2048]{1,0:T(8,128)(2,1)S(1)}, f16[64,2048]{1,0:T(8,128)(2,1)S(1)}, u32[]{:S(2)}, u32[]{:S(2)}) collective-permute-start(f16[64,2048]{1,0:T(8,128)(2,1)S(1)} %add_convert_fusion.11), channel_id=1, source_target_pairs={{96,0},{33,1},{98,2},{35,3},{100,4},{37,5},{102,6},{39,7},{104,8},... | collective-permute-start | bytes 786440 | tf_op jit(solution)/shard_map/ppermute | solution.py:93
  57.4 10.9 %fusion.11 = f32[64,4096]{1,0:T(8,128)S(1)} fusion(bf16[4096,2048]{1,0:T(8,128)(2,1)} %param.4, f32[64,2048]{1,0:T(8,128)S(1)} %copy-done), kind=kOutput, calls=%fused_computation.55 | convolution fusion | flops 1073872896 | bytes 18350080 | tf_op jit(solution)/shard_map/dot_general | solution.py:138
  68.3 0.1 add_convert_fusion.10
  68.4 0.1 collective-permute-start.8
  68.5 0.1 select_convert_fusion.1
  68.6 0.3 collective-permute-start.9
  68.9 7.4 %collective-permute-done.8 = f16[64,2048]{1,0:T(8,128)(2,1)S(1)} collective-permute-done((f16[64,2048]{1,0:T(8,128)(2,1)S(1)}, f16[64,2048]{1,0:T(8,128)(2,1)S(1)}, u32[]{:S(2)}, u32[]{:S(2)}) %collective-permute-start.8) | collective-permute-done | bytes 262176 | tf_op jit(solution)/shard_map/ppermute | solution.py:93
  76.4 0.3 multiply_convert_fusion
  76.8 0.2 add_convert_fusion.9
  76.9 1.0 collective-permute-start.10
  77.9 10.4 %collective-permute-done.14 = bf16[64,2048]{1,0:T(8,128)(2,1)S(1)} collective-permute-done((bf16[64,2048]{1,0:T(8,128)(2,1)S(1)}, bf16[64,2048]{1,0:T(8,128)(2,1)S(1)}, u32[]{:S(2)}, u32[]{:S(2)}) %collective-permute-start.14) | collective-permute-done | bytes 262176 | tf_op jit(solution)/shard_map/ppermute | solution.py:93
  88.3 0.1 add_convert_fusion.8
  88.4 10.7 %collective-permute-start.11 = (f16[64,2048]{1,0:T(8,128)(2,1)S(1)}, f16[64,2048]{1,0:T(8,128)(2,1)S(1)}, u32[]{:S(2)}, u32[]{:S(2)}) collective-permute-start(f16[64,2048]{1,0:T(8,128)(2,1)S(1)} %add_convert_fusion.8), channel_id=1, source_target_pairs={{2,0},{7,1},{0,2},{5,3},{6,4},{3,5},{4,6},{1,7},{10,8},{15,9},{8,1... | collective-permute-start | bytes 786440 | tf_op jit(solution)/shard_map/ppermute | solution.py:93
  99.2 8.8 %fusion.1 = f16[64,2048]{1,0:T(8,128)(2,1)S(1)} fusion(bf16[4096,2048]{1,0:T(8,128)(2,1)} %param.4, bf16[64,2048]{1,0:T(8,128)(2,1)S(1)} %get-tuple-element.32, bf16[64,2048]{1,0:T(8,128)(2,1)S(1)} %get-tuple-element.31, f32[64]{0:T(128)S(1)} %get-tuple-element.50), kind=kOutput, calls=%fused_computation.3 | convolution fusion | flops 1075052544 | bytes 17563904 | tf_op jit(solution)/shard_map/dot_general | solution.py:135
  108.0 0.1 collective-permute-start.16
  108.1 0.1 add_convert_fusion.7
  108.2 1.5 collective-permute-start.12
  109.7 4.7 %collective-permute-done.16 = f16[64,2048]{1,0:T(8,128)(2,1)S(1)} collective-permute-done((f16[64,2048]{1,0:T(8,128)(2,1)S(1)}, f16[64,2048]{1,0:T(8,128)(2,1)S(1)}, u32[]{:S(2)}, u32[]{:S(2)}) %collective-permute-start.16) | collective-permute-done | bytes 262176 | tf_op jit(solution)/shard_map/ppermute | solution.py:93
  114.4 0.1 add_convert_fusion.5
  114.5 6.4 %collective-permute-start.17 = (f16[64,2048]{1,0:T(8,128)(2,1)S(1)}, f16[64,2048]{1,0:T(8,128)(2,1)S(1)}, u32[]{:S(2)}, u32[]{:S(2)}) collective-permute-start(f16[64,2048]{1,0:T(8,128)(2,1)S(1)} %add_convert_fusion.5), channel_id=1, source_target_pairs={{96,0},{33,1},{98,2},{35,3},{100,4},{37,5},{102,6},{39,7},{104,8},... | collective-permute-start | bytes 786440 | tf_op jit(solution)/shard_map/ppermute | solution.py:93
  120.9 0.1 add_convert_fusion.6
  121.0 2.7 %collective-permute-start.13 = (f16[64,2048]{1,0:T(8,128)(2,1)S(1)}, f16[64,2048]{1,0:T(8,128)(2,1)S(1)}, u32[]{:S(2)}, u32[]{:S(2)}) collective-permute-start(f16[64,2048]{1,0:T(8,128)(2,1)S(1)} %add_convert_fusion.6), channel_id=1, source_target_pairs={{4,0},{5,1},{30,2},{31,3},{34,4},{39,5},{60,6},{57,7},{72,8},{73,9... | collective-permute-start | bytes 786440 | tf_op jit(solution)/shard_map/ppermute | solution.py:93
  123.8 1.5 collective-permute-done.17
  125.3 0.1 add_convert_fusion.4
  125.4 0.1 collective-permute-start.18
  125.5 8.2 %collective-permute-done.13 = f16[64,2048]{1,0:T(8,128)(2,1)S(1)} collective-permute-done((f16[64,2048]{1,0:T(8,128)(2,1)S(1)}, f16[64,2048]{1,0:T(8,128)(2,1)S(1)}, u32[]{:S(2)}, u32[]{:S(2)}) %collective-permute-start.13) | collective-permute-done | bytes 262176 | tf_op jit(solution)/shard_map/ppermute | solution.py:93
  133.7 1.7 multiply_reduce_fusion
  135.4 10.9 %fusion.9 = f32[64,4096]{1,0:T(8,128)S(1)} fusion(bf16[4096,2048]{1,0:T(8,128)(2,1)} %param.4, f32[64,2048]{1,0:T(8,128)S(1)} %get-tuple-element.22), kind=kOutput, calls=%fused_computation.53 | convolution fusion | flops 1073872896 | bytes 18350080 | tf_op jit(solution)/shard_map/dot_general | solution.py:138
  146.4 0.1 select_convert_fusion
  146.5 0.9 collective-permute-start.23
  147.4 1.2 collective-permute-done.23
  148.6 0.2 add_convert_fusion.3
  148.8 0.1 collective-permute-start.24
  148.9 6.4 %collective-permute-done.24 = f16[64,2048]{1,0:T(8,128)(2,1)S(1)} collective-permute-done((f16[64,2048]{1,0:T(8,128)(2,1)S(1)}, f16[64,2048]{1,0:T(8,128)(2,1)S(1)}, u32[]{:S(2)}, u32[]{:S(2)}) %collective-permute-start.24) | collective-permute-done | bytes 262176 | tf_op jit(solution)/shard_map/ppermute | solution.py:93
  155.2 0.1 add_convert_fusion.2
  155.3 2.2 %collective-permute-start.25 = (f16[64,2048]{1,0:T(8,128)(2,1)S(1)}, f16[64,2048]{1,0:T(8,128)(2,1)S(1)}, u32[]{:S(2)}, u32[]{:S(2)}) collective-permute-start(f16[64,2048]{1,0:T(8,128)(2,1)S(1)} %add_convert_fusion.2), channel_id=1, source_target_pairs={{2,0},{7,1},{0,2},{5,3},{6,4},{3,5},{4,6},{1,7},{10,8},{15,9},{8,1... | collective-permute-start | bytes 786440 | tf_op jit(solution)/shard_map/ppermute | solution.py:93
  157.5 4.4 %collective-permute-done.25 = f16[64,2048]{1,0:T(8,128)(2,1)S(1)} collective-permute-done((f16[64,2048]{1,0:T(8,128)(2,1)S(1)}, f16[64,2048]{1,0:T(8,128)(2,1)S(1)}, u32[]{:S(2)}, u32[]{:S(2)}) %collective-permute-start.25) | collective-permute-done | bytes 262176 | tf_op jit(solution)/shard_map/ppermute | solution.py:93
  161.8 0.8 add_convert_fusion.1
  162.6 2.6 %collective-permute-start.26 = (f16[64,2048]{1,0:T(8,128)(2,1)}, f16[64,2048]{1,0:T(8,128)(2,1)}, u32[]{:S(2)}, u32[]{:S(2)}) collective-permute-start(f16[64,2048]{1,0:T(8,128)(2,1)} %add_convert_fusion.1), channel_id=1, source_target_pairs={{6,0},{9,1},{4,2},{11,3},{2,4},{13,5},{0,6},{15,7},{14,8},{1,9},{1... | collective-permute-start | bytes 786440 | tf_op jit(solution)/shard_map/ppermute | solution.py:93
  165.2 0.1 collective-permute-start.19
  165.3 1.2 collective-permute-done.19
  166.4 3.6 %collective-permute-done.20 = f32[7,64]{1,0:T(8,128)S(1)} collective-permute-done((f32[7,64]{1,0:T(8,128)S(1)}, f32[7,64]{1,0:T(8,128)S(1)}, u32[]{:S(2)}, u32[]{:S(2)}) %collective-permute-start.20) | collective-permute-done | bytes 1824 | tf_op jit(solution)/shard_map/ppermute | solution.py:93
  170.0 1.4 collective-permute-start.21
  171.4 2.2 %collective-permute-done.21 = f32[7,64]{1,0:T(8,128)S(1)} collective-permute-done((f32[7,64]{1,0:T(8,128)S(1)}, f32[7,64]{1,0:T(8,128)S(1)}, u32[]{:S(2)}, u32[]{:S(2)}) %collective-permute-start.21) | collective-permute-done | bytes 1824 | tf_op jit(solution)/shard_map/ppermute | solution.py:93
  173.6 0.7 collective-permute-start.22
  174.3 4.1 %collective-permute-done.22 = f32[7,64]{1,0:T(8,128)S(1)} collective-permute-done((f32[7,64]{1,0:T(8,128)S(1)}, f32[7,64]{1,0:T(8,128)S(1)}, u32[]{:S(2)}, u32[]{:S(2)}) %collective-permute-start.22) | collective-permute-done | bytes 1824 | tf_op jit(solution)/shard_map/ppermute | solution.py:93
  178.5 1.1 add_convert_fusion
  179.6 1.0 collective-permute-start.27
  180.6 9.7 %collective-permute-done.27 = f16[64,2048]{1,0:T(8,128)(2,1)S(1)} collective-permute-done((f16[64,2048]{1,0:T(8,128)(2,1)S(1)}, f16[64,2048]{1,0:T(8,128)(2,1)S(1)}, u32[]{:S(2)}, u32[]{:S(2)}) %collective-permute-start.27) | collective-permute-done | bytes 262176 | tf_op jit(solution)/shard_map/ppermute | solution.py:93
  190.3 3.0 %multiply_subtract_fusion = (f32[64,2048]{1,0:T(8,128)}, f32[64,2048]{1,0:T(8,128)}, f32[64,2048]{1,0:T(8,128)}, f32[64,2048]{1,0:T(8,128)}) fusion(f16[64,2048]{1,0:T(8,128)(2,1)S(1)} %collective-permute-done.27, f32[64,2048]{1,0:T(8,128)S(1)} %get-tuple-element.22, f32[64,2048]{1,0:T(8,128)S(1)} %copy-done, ...), kind=kLoop, calls=%fused_computation.14 | loop fusion | flops 5373952 | bytes 6292992 | tf_op jit(solution)/shard_map/sub | solution.py:206
  (39 shorter events, 0.4 us)
Async XLA Ops:
  0.6 56.7 %copy-start = (f32[64,2048]{1,0:T(8,128)S(1)}, f32[64,2048]{1,0:T(8,128)}, u32[]{:S(2)}) copy-start(f32[64,2048]{1,0:T(8,128)} %param.7) | copy-start | bytes 1572868
  2.5 1.2 collective-permute-start
  3.7 3.7 %collective-permute-start.1 = (f32[4,64]{1,0:T(4,128)S(1)}, f32[4,64]{1,0:T(4,128)S(1)}, u32[]{:S(2)}, u32[]{:S(2)}) collective-permute-start(f32[4,64]{1,0:T(4,128)S(1)} %pad_maximum_fusion.1), channel_id=1, source_target_pairs={{8,0},{9,1},{10,2},{11,3},{12,4},{13,5},{14,6},{15,7},{0,8},{1,9},... | collective-permute-start | bytes 3080 | tf_op jit(solution)/shard_map/ppermute | solution.py:93
  7.4 5.7 %collective-permute-start.2 = (f32[4,64]{1,0:T(4,128)S(1)}, f32[4,64]{1,0:T(4,128)S(1)}, u32[]{:S(2)}, u32[]{:S(2)}) collective-permute-start(f32[4,64]{1,0:T(4,128)S(1)} %pad_maximum_fusion.2), channel_id=1, source_target_pairs={{2,0},{3,1},{0,2},{1,3},{6,4},{7,5},{4,6},{5,7},{10,8},{11,9},{8,1... | collective-permute-start | bytes 3080 | tf_op jit(solution)/shard_map/ppermute | solution.py:93
  9.5 12.8 %collective-permute-start.4 = (bf16[64,2048]{1,0:T(8,128)(2,1)S(1)}, bf16[64,2048]{1,0:T(8,128)(2,1)S(1)}, u32[]{:S(2)}, u32[]{:S(2)}) collective-permute-start(bf16[64,2048]{1,0:T(8,128)(2,1)S(1)} %get-tuple-element.28), channel_id=1, source_target_pairs={{64,0},{65,1},{32,2},{97,3},{0,4},{1,5},{96,6},{33,7},{80,8},{81,9... | collective-permute-start | bytes 786440 | tf_op jit(solution)/shard_map/ppermute | solution.py:93
  13.1 9.2 %collective-permute-start.3 = (f32[4,64]{1,0:T(4,128)S(1)}, f32[4,64]{1,0:T(4,128)S(1)}, u32[]{:S(2)}, u32[]{:S(2)}) collective-permute-start(f32[4,64]{1,0:T(4,128)S(1)} %pad_maximum_fusion.3), channel_id=1, source_target_pairs={{6,0},{7,1},{4,2},{5,3},{2,4},{3,5},{0,6},{1,7},{14,8},{15,9},{12,... | collective-permute-start | bytes 3080 | tf_op jit(solution)/shard_map/ppermute | solution.py:93
  22.3 1.5 collective-permute-start.5
  32.6 43.7 %copy-start.1 = (f32[64,2048]{1,0:T(8,128)S(1)}, f32[64,2048]{1,0:T(8,128)}, u32[]{:S(2)}) copy-start(f32[64,2048]{1,0:T(8,128)} %param.5) | copy-start | bytes 1572868
  32.7 43.7 %copy-start.2 = (f32[64,2048]{1,0:T(8,128)S(1)}, f32[64,2048]{1,0:T(8,128)}, u32[]{:S(2)}) copy-start(f32[64,2048]{1,0:T(8,128)} %param.6) | copy-start | bytes 1572868
  32.7 6.5 %collective-permute-start.6 = (f16[64,2048]{1,0:T(8,128)(2,1)S(1)}, f16[64,2048]{1,0:T(8,128)(2,1)S(1)}, u32[]{:S(2)}, u32[]{:S(2)}) collective-permute-start(f16[64,2048]{1,0:T(8,128)(2,1)S(1)} %fusion), channel_id=1, source_target_pairs={{32,0},{17,1},{34,2},{19,3},{36,4},{21,5},{38,6},{23,7},{40,8},{25... | collective-permute-start | bytes 786440 | tf_op jit(solution)/shard_map/ppermute | solution.py:93
  39.2 29.1 %collective-permute-start.7 = (f16[64,2048]{1,0:T(8,128)(2,1)S(1)}, f16[64,2048]{1,0:T(8,128)(2,1)S(1)}, u32[]{:S(2)}, u32[]{:S(2)}) collective-permute-start(f16[64,2048]{1,0:T(8,128)(2,1)S(1)} %add_convert_fusion.11), channel_id=1, source_target_pairs={{96,0},{33,1},{98,2},{35,3},{100,4},{37,5},{102,6},{39,7},{104,8},... | collective-permute-start | bytes 786440 | tf_op jit(solution)/shard_map/ppermute | solution.py:93
  68.4 8.0 %collective-permute-start.8 = (f16[64,2048]{1,0:T(8,128)(2,1)S(1)}, f16[64,2048]{1,0:T(8,128)(2,1)S(1)}, u32[]{:S(2)}, u32[]{:S(2)}) collective-permute-start(f16[64,2048]{1,0:T(8,128)(2,1)S(1)} %add_convert_fusion.10), channel_id=1, source_target_pairs={{16,0},{97,1},{18,2},{99,3},{20,4},{101,5},{22,6},{103,7},{24,8},{... | collective-permute-start | bytes 786440 | tf_op jit(solution)/shard_map/ppermute | solution.py:93
  68.6 8.1 %collective-permute-start.9 = (f16[64,2048]{1,0:T(8,128)(2,1)S(1)}, f16[64,2048]{1,0:T(8,128)(2,1)S(1)}, u32[]{:S(2)}, u32[]{:S(2)}) collective-permute-start(f16[64,2048]{1,0:T(8,128)(2,1)S(1)} %select_convert_fusion.1), channel_id=1, source_target_pairs={{1,0},{0,1},{3,2},{2,3},{5,4},{4,5},{7,6},{6,7},{9,8},{8,9},{11,10... | collective-permute-start | bytes 786440 | tf_op jit(solution)/shard_map/ppermute | solution.py:93
  76.7 11.7 %collective-permute-start.14 = (bf16[64,2048]{1,0:T(8,128)(2,1)S(1)}, bf16[64,2048]{1,0:T(8,128)(2,1)S(1)}, u32[]{:S(2)}, u32[]{:S(2)}) collective-permute-start(bf16[64,2048]{1,0:T(8,128)(2,1)S(1)} %get-tuple-element.23), channel_id=1, source_target_pairs={{64,0},{65,1},{32,2},{97,3},{0,4},{1,5},{96,6},{33,7},{80,8},{81,9... | collective-permute-start | bytes 786440 | tf_op jit(solution)/shard_map/ppermute | solution.py:93
  76.9 11.4 %collective-permute-start.10 = (f16[64,2048]{1,0:T(8,128)(2,1)S(1)}, f16[64,2048]{1,0:T(8,128)(2,1)S(1)}, u32[]{:S(2)}, u32[]{:S(2)}) collective-permute-start(f16[64,2048]{1,0:T(8,128)(2,1)S(1)} %add_convert_fusion.9), channel_id=1, source_target_pairs={{8,0},{3,1},{10,2},{1,3},{12,4},{7,5},{14,6},{5,7},{0,8},{11,9},{2... | collective-permute-start | bytes 786440 | tf_op jit(solution)/shard_map/ppermute | solution.py:93
  88.3 10.8 %collective-permute-start.15 = (bf16[64,2048]{1,0:T(8,128)(2,1)S(1)}, bf16[64,2048]{1,0:T(8,128)(2,1)S(1)}, u32[]{:S(2)}, u32[]{:S(2)}) collective-permute-start(bf16[64,2048]{1,0:T(8,128)(2,1)S(1)} %collective-permute-done.14), channel_id=1, source_target_pairs={{1,0},{0,1},{3,2},{2,3},{5,4},{4,5},{7,6},{6,7},{9,8},{8,9},{11,10... | collective-permute-start | bytes 786440 | tf_op jit(solution)/shard_map/ppermute | solution.py:93
  88.4 19.7 %collective-permute-start.11 = (f16[64,2048]{1,0:T(8,128)(2,1)S(1)}, f16[64,2048]{1,0:T(8,128)(2,1)S(1)}, u32[]{:S(2)}, u32[]{:S(2)}) collective-permute-start(f16[64,2048]{1,0:T(8,128)(2,1)S(1)} %add_convert_fusion.8), channel_id=1, source_target_pairs={{2,0},{7,1},{0,2},{5,3},{6,4},{3,5},{4,6},{1,7},{10,8},{15,9},{8,1... | collective-permute-start | bytes 786440 | tf_op jit(solution)/shard_map/ppermute | solution.py:93
  108.0 6.5 %collective-permute-start.16 = (f16[64,2048]{1,0:T(8,128)(2,1)S(1)}, f16[64,2048]{1,0:T(8,128)(2,1)S(1)}, u32[]{:S(2)}, u32[]{:S(2)}) collective-permute-start(f16[64,2048]{1,0:T(8,128)(2,1)S(1)} %fusion.1), channel_id=1, source_target_pairs={{32,0},{17,1},{34,2},{19,3},{36,4},{21,5},{38,6},{23,7},{40,8},{25... | collective-permute-start | bytes 786440 | tf_op jit(solution)/shard_map/ppermute | solution.py:93
  108.2 12.8 %collective-permute-start.12 = (f16[64,2048]{1,0:T(8,128)(2,1)S(1)}, f16[64,2048]{1,0:T(8,128)(2,1)S(1)}, u32[]{:S(2)}, u32[]{:S(2)}) collective-permute-start(f16[64,2048]{1,0:T(8,128)(2,1)S(1)} %add_convert_fusion.7), channel_id=1, source_target_pairs={{6,0},{9,1},{4,2},{11,3},{2,4},{13,5},{0,6},{15,7},{14,8},{1,9},{1... | collective-permute-start | bytes 786440 | tf_op jit(solution)/shard_map/ppermute | solution.py:93
  114.5 10.8 %collective-permute-start.17 = (f16[64,2048]{1,0:T(8,128)(2,1)S(1)}, f16[64,2048]{1,0:T(8,128)(2,1)S(1)}, u32[]{:S(2)}, u32[]{:S(2)}) collective-permute-start(f16[64,2048]{1,0:T(8,128)(2,1)S(1)} %add_convert_fusion.5), channel_id=1, source_target_pairs={{96,0},{33,1},{98,2},{35,3},{100,4},{37,5},{102,6},{39,7},{104,8},... | collective-permute-start | bytes 786440 | tf_op jit(solution)/shard_map/ppermute | solution.py:93
  121.0 12.7 %collective-permute-start.13 = (f16[64,2048]{1,0:T(8,128)(2,1)S(1)}, f16[64,2048]{1,0:T(8,128)(2,1)S(1)}, u32[]{:S(2)}, u32[]{:S(2)}) collective-permute-start(f16[64,2048]{1,0:T(8,128)(2,1)S(1)} %add_convert_fusion.6), channel_id=1, source_target_pairs={{4,0},{5,1},{30,2},{31,3},{34,4},{39,5},{60,6},{57,7},{72,8},{73,9... | collective-permute-start | bytes 786440 | tf_op jit(solution)/shard_map/ppermute | solution.py:93
  125.4 8.3 %collective-permute-start.18 = (f16[64,2048]{1,0:T(8,128)(2,1)S(1)}, f16[64,2048]{1,0:T(8,128)(2,1)S(1)}, u32[]{:S(2)}, u32[]{:S(2)}) collective-permute-start(f16[64,2048]{1,0:T(8,128)(2,1)S(1)} %add_convert_fusion.4), channel_id=1, source_target_pairs={{16,0},{97,1},{18,2},{99,3},{20,4},{101,5},{22,6},{103,7},{24,8},{... | collective-permute-start | bytes 786440 | tf_op jit(solution)/shard_map/ppermute | solution.py:93
  146.5 2.1 %collective-permute-start.23 = (f16[64,2048]{1,0:T(8,128)(2,1)S(1)}, f16[64,2048]{1,0:T(8,128)(2,1)S(1)}, u32[]{:S(2)}, u32[]{:S(2)}) collective-permute-start(f16[64,2048]{1,0:T(8,128)(2,1)S(1)} %select_convert_fusion), channel_id=1, source_target_pairs={{1,0},{0,1},{3,2},{2,3},{5,4},{4,5},{7,6},{6,7},{9,8},{8,9},{11,10... | collective-permute-start | bytes 786440 | tf_op jit(solution)/shard_map/ppermute | solution.py:93
  148.8 6.5 %collective-permute-start.24 = (f16[64,2048]{1,0:T(8,128)(2,1)S(1)}, f16[64,2048]{1,0:T(8,128)(2,1)S(1)}, u32[]{:S(2)}, u32[]{:S(2)}) collective-permute-start(f16[64,2048]{1,0:T(8,128)(2,1)S(1)} %add_convert_fusion.3), channel_id=1, source_target_pairs={{8,0},{3,1},{10,2},{1,3},{12,4},{7,5},{14,6},{5,7},{0,8},{11,9},{2... | collective-permute-start | bytes 786440 | tf_op jit(solution)/shard_map/ppermute | solution.py:93
  155.3 6.5 %collective-permute-start.25 = (f16[64,2048]{1,0:T(8,128)(2,1)S(1)}, f16[64,2048]{1,0:T(8,128)(2,1)S(1)}, u32[]{:S(2)}, u32[]{:S(2)}) collective-permute-start(f16[64,2048]{1,0:T(8,128)(2,1)S(1)} %add_convert_fusion.2), channel_id=1, source_target_pairs={{2,0},{7,1},{0,2},{5,3},{6,4},{3,5},{4,6},{1,7},{10,8},{15,9},{8,1... | collective-permute-start | bytes 786440 | tf_op jit(solution)/shard_map/ppermute | solution.py:93
  162.6 15.9 %collective-permute-start.26 = (f16[64,2048]{1,0:T(8,128)(2,1)}, f16[64,2048]{1,0:T(8,128)(2,1)}, u32[]{:S(2)}, u32[]{:S(2)}) collective-permute-start(f16[64,2048]{1,0:T(8,128)(2,1)} %add_convert_fusion.1), channel_id=1, source_target_pairs={{6,0},{9,1},{4,2},{11,3},{2,4},{13,5},{0,6},{15,7},{14,8},{1,9},{1... | collective-permute-start | bytes 786440 | tf_op jit(solution)/shard_map/ppermute | solution.py:93
  165.2 1.2 collective-permute-start.19
  166.4 3.6 %collective-permute-start.20 = (f32[7,64]{1,0:T(8,128)S(1)}, f32[7,64]{1,0:T(8,128)S(1)}, u32[]{:S(2)}, u32[]{:S(2)}) collective-permute-start(f32[7,64]{1,0:T(8,128)S(1)} %add.170), channel_id=1, source_target_pairs={{8,0},{9,1},{10,2},{11,3},{12,4},{13,5},{14,6},{15,7},{0,8},{1,9},... | collective-permute-start | bytes 5384 | tf_op jit(solution)/shard_map/ppermute | solution.py:93
  170.0 3.6 %collective-permute-start.21 = (f32[7,64]{1,0:T(8,128)S(1)}, f32[7,64]{1,0:T(8,128)S(1)}, u32[]{:S(2)}, u32[]{:S(2)}) collective-permute-start(f32[7,64]{1,0:T(8,128)S(1)} %add.171), channel_id=1, source_target_pairs={{2,0},{3,1},{0,2},{1,3},{6,4},{7,5},{4,6},{5,7},{10,8},{11,9},{8,1... | collective-permute-start | bytes 5384 | tf_op jit(solution)/shard_map/ppermute | solution.py:93
  173.6 4.8 %collective-permute-start.22 = (f32[7,64]{1,0:T(8,128)S(1)}, f32[7,64]{1,0:T(8,128)S(1)}, u32[]{:S(2)}, u32[]{:S(2)}) collective-permute-start(f32[7,64]{1,0:T(8,128)S(1)} %add.172), channel_id=1, source_target_pairs={{6,0},{7,1},{4,2},{5,3},{2,4},{3,5},{0,6},{1,7},{14,8},{15,9},{12,... | collective-permute-start | bytes 5384 | tf_op jit(solution)/shard_map/ppermute | solution.py:93
  179.6 10.8 %collective-permute-start.27 = (f16[64,2048]{1,0:T(8,128)(2,1)S(1)}, f16[64,2048]{1,0:T(8,128)(2,1)S(1)}, u32[]{:S(2)}, u32[]{:S(2)}) collective-permute-start(f16[64,2048]{1,0:T(8,128)(2,1)S(1)} %add_convert_fusion), channel_id=1, source_target_pairs={{4,0},{5,1},{30,2},{31,3},{34,4},{39,5},{60,6},{57,7},{72,8},{73,9... | collective-permute-start | bytes 786440 | tf_op jit(solution)/shard_map/ppermute | solution.py:93

commit v2 on v1

--- a/solution.py
+++ b/solution.py
@@ -1,6 +1,8 @@
 import jax
 import jax.numpy as jnp
 from jax import lax
+from jax.experimental import pallas as pl
+from jax.experimental.pallas import tpu as pltpu
 from jax.sharding import PartitionSpec as P
 
 SELF_GAIN = 0.5
@@ -73,9 +75,23 @@
     return (x + STEP[h][(z - zs) % 4]) % 4, yh ^ yl ^ yls, yls, zs, h
 
 
+HALF_SOURCE = (
+    7, 4, 3, 7, 0, 2, 4, 1, 6, 6, 2, 3, 1, 0, 5, 5,
+    7, 0, 2, 5, 0, 6, 5, 7, 6, 2, 4, 3, 1, 4, 3, 1,
+    6, 0, 4, 1, 1, 6, 3, 3, 0, 2, 2, 7, 7, 4, 5, 5,
+    0, 4, 5, 1, 7, 2, 2, 7, 1, 0, 3, 3, 6, 6, 4, 5,
+    0, 6, 3, 7, 7, 4, 4, 1, 1, 0, 5, 3, 6, 2, 2, 5,
+    7, 2, 3, 7, 0, 0, 4, 5, 1, 6, 2, 1, 6, 4, 5, 3,
+    6, 6, 4, 3, 1, 0, 3, 5, 0, 4, 5, 7, 7, 2, 2, 1,
+    0, 4, 5, 7, 7, 2, 2, 1, 6, 0, 3, 5, 1, 6, 4, 3,
+)
+
 CORE = sends(flip_core)
 TO_COLS = sends(from_rows)
 TO_ROWS = sends(from_cols)
+HALF_TO_ROWS = [
+    (HALF_SOURCE[d] * 16 + (d // 16) * 2 + d % 2, d) for d in range(128)
+]
 ROW_STEPS = (
     by_core(flip_x, flip_yh),
     by_core(mirror_x, flip_x),
@@ -86,7 +102,75 @@
     by_core(flip_z, mirror_z),
     by_core(mirror_z, flip_yl),
 )
+Z_PAIR = sends(flip_z)
 SMALL_COL = (CORE, sends(flip_yl), sends(flip_z), sends(mirror_z))
+SMALL_ROW = (CORE, sends(flip_x), sends(mirror_x), sends(flip_yh))
+
+TILE = 512
+
+
+def primary_kernel(left_ref, coupling_ref, out_ref):
+    @pl.when(pl.program_id(0) == 0)
+    def _():
+        out_ref[...] = jnp.zeros_like(out_ref)
+
+    out_ref[...] += jnp.dot(
+        left_ref[...], coupling_ref[...], preferred_element_type=F32
+    )
+
+
+def shadow_kernel(left_ref, coupling_ref, out_ref):
+    out_ref[...] = lax.dot_general(
+        left_ref[...],
+        coupling_ref[...],
+        (((1,), (1,)), ((), ())),
+        preferred_element_type=F32,
+    )
+
+
+def call(kernel, name, left, coupling, left_spec, out_spec, width):
+    rows, columns = coupling.shape
+    reps = left.shape[0]
+    return pl.pallas_call(
+        kernel,
+        name=name,
+        grid=(rows // TILE,),
+        in_specs=[left_spec, pl.BlockSpec((TILE, columns), lambda i: (i, 0))],
+        out_specs=out_spec,
+        out_shape=jax.ShapeDtypeStruct((reps, width), F32),
+        compiler_params=pltpu.CompilerParams(vmem_limit_bytes=52 << 20),
+        cost_estimate=pl.CostEstimate(
+            flops=2 * reps * rows * columns,
+            bytes_accessed=2 * rows * columns,
+            transcendentals=0,
+        ),
+    )(left, coupling)
+
+
+def primary(left, coupling):
+    reps, columns = left.shape[0], coupling.shape[1]
+    return call(
+        primary_kernel,
+        "primary",
+        left,
+        coupling,
+        pl.BlockSpec((reps, TILE), lambda i: (0, i)),
+        pl.BlockSpec((reps, columns), lambda i: (0, 0)),
+        columns,
+    )
+
+
+def shadow(left, coupling):
+    reps, columns = left.shape
+    return call(
+        shadow_kernel,
+        "shadow",
+        left,
+        coupling,
+        pl.BlockSpec((reps, columns), lambda i: (0, 0)),
+        pl.BlockSpec((reps, TILE), lambda i: (0, i)),
+        coupling.shape[0],
+    )
 
 
 def move(value, pairs):
@@ -100,16 +184,53 @@
     return value
 
 
+def pick(flag, value):
+    width = value.shape[1] // 2
+    low, high = value[:, :width], value[:, width:]
+    return jnp.where(flag, low, high), jnp.where(flag, high, low)
+
+
+def put(flag, mine, other):
+    low = jnp.where(flag, mine, other)
+    high = jnp.where(flag, other, mine)
+    return jnp.concatenate([low, high], axis=1)
+
+
+SENDS_LOW = [0] * 128
+for source, destination in TO_ROWS:
+    SENDS_LOW[source] = int(split(destination)[3] % 2 == 0)
+
+
+def z_even_source(row, col):
+    return jnp.array(SENDS_LOW, jnp.int32)[row * 16 + col] == 1
+
+
+def total(value):
+    return jnp.sum(value, axis=1)
+
+
 def on_device(coupling, amplitude, target, shadow_target):
-    core = lax.axis_index("col") % 2
-    first = core == 0
+    row, col = lax.axis_index("row"), lax.axis_index("col")
+    x, yh = row >> 1, row & 1
+    first = (col & 1) == 0
+    z_even = (col & 2) == 0
+    low_half = jnp.where(first, (x ^ (x >> 1)) & 1, yh) == 0
+
     g, gs = target, shadow_target
     slope = 1.0 - amplitude * amplitude
     keep = 1.0 - SELF_GAIN * slope
 
+    def spread(half):
+        mine = put(z_even, half, move(half, Z_PAIR))
+        return mine, put(first, mine, move(mine, CORE))
+
+    half = pick(z_even_source(row, col), (slope * g).astype(BF16))[0]
+    half = move(half, TO_ROWS)
+    shadow_partial = shadow(gs.astype(BF16), coupling)
+    half, shadow_partial = lax.optimization_barrier((half, shadow_partial))
+
     tops = jnp.stack([jnp.max(jnp.abs(g), axis=1), jnp.max(jnp.abs(gs), axis=1)])
-    sums = jnp.stack([jnp.sum(gs * g, axis=1), jnp.sum(gs * (keep * g), axis=1)])
-    stats = jnp.concatenate([tops, sums])
+    stats = jnp.concatenate([tops, jnp.stack([total(gs * g), total(gs * (keep * g))])])
     for pairs in SMALL_COL:
         other = move(stats, pairs)
         stats = jnp.concatenate(
@@ -123,70 +244,71 @@
     alpha = jnp.where(jnp.isnan(alpha), 1.4, alpha)
     alpha_c = alpha[:, None]
 
-    def rows_of(vector):
-        scaled = (slope * vector).astype(BF16)
-        mine = move(scaled, TO_ROWS)
-        other = move(mine, CORE)
-        low = jnp.where(first, mine, other)
-        high = jnp.where(first, other, mine)
-        return jnp.concatenate([low, high], axis=1)
-
-    def primary(row_block):
-        return jnp.dot(row_block, coupling, preferred_element_type=F32)
-
-    def shadow(vector):
-        return lax.dot_general(
-            vector.astype(BF16),
-            coupling,
-            (((1,), (1,)), ((), ())),
-            preferred_element_type=F32,
-        )
-
-    def primary_sum(partial, scale):
-        return chip_sum(partial * scale, ROW_STEPS) * (1.0 / scale)
-
     def shadow_sum(partial, scale):
-        low, high = partial[:, :2048] * scale, partial[:, 2048:] * scale
-        mine = jnp.where(first, low, high)
-        other = jnp.where(first, high, low).astype(WIRE)
-        mine = mine + move(other, CORE).astype(F32)
-        total = chip_sum(mine, COL_STEPS).astype(WIRE)
-        return move(total, TO_COLS).astype(F32) * (1.0 / scale)
-
-    shadow_partial = shadow(gs)
-    primary_partial = primary(rows_of(g))
-    product = primary_sum(primary_partial, FIRST_SCALE / top)
-    shadow_product = shadow_sum(shadow_partial, FIRST_SCALE / shadow_top)
-    p1 = keep * g - COUPLE_GAIN * product
-    q1 = keep * gs - COUPLE_GAIN * slope * shadow_product
-    u = g - alpha_c * p1
+        mine, other = pick(first, partial)
+        mine = mine * scale + move((other * scale).astype(WIRE), CORE).astype(F32)
+        rows = chip_sum(mine, COL_STEPS).astype(WIRE)
+        return rows, move(rows, TO_COLS)
+
+    _, left = spread(half)
+    primary_partial = primary(left, coupling)
+    scale = FIRST_SCALE / top
+    mine, other = pick(low_half, primary_partial * scale)
+    mine = mine + move(other.astype(WIRE), ROW_STEPS[0]).astype(F32)
+    mine = chip_sum(mine, ROW_STEPS[1:]).astype(WIRE)
+    unscale = COUPLE_GAIN / scale
+
+    def first_step(kept, value, product):
+        image = kept * value - product.astype(F32) * unscale
+        return image, value - alpha_c * image
+
+    g_half, keep_half = pick(low_half, g)[0], pick(low_half, keep)[0]
+    slope_half = pick(low_half, slope)[0]
+    _, u_half = first_step(keep_half, g_half, mine)
+    u_half = (slope_half * u_half).astype(BF16)
+    u_half = move(u_half, HALF_TO_ROWS)
+    product = put(low_half, mine, move(mine, ROW_STEPS[0]))
+    p1, u = first_step(keep, g, product)
+
+    scale = FIRST_SCALE / shadow_top
+    _, columns = shadow_sum(shadow_partial, scale)
+    q1 = keep * gs - (COUPLE_GAIN / scale) * slope * columns.astype(F32)
     us = gs - alpha_c * q1
 
-    shadow_partial = shadow(us)
-    primary_partial = primary(rows_of(u))
-    product = primary_sum(primary_partial, SECOND_SCALE / top)
-    shadow_product = shadow_sum(shadow_partial, SECOND_SCALE / shadow_top)
-    p2 = keep * u - COUPLE_GAIN * product
-    q2 = keep * us - COUPLE_GAIN * slope * shadow_product
-
+    shadow_partial = shadow(us.astype(BF16), coupling)
+    u_rows, left = spread(u_half)
+    primary_partial = primary(left, coupling)
+    scale = SECOND_SCALE / shadow_top
+    rows, columns = shadow_sum(shadow_partial, scale)
+    last = total(u_rows.astype(F32) * rows.astype(F32)) / scale[:, 0]
+    q2 = keep * us - (COUPLE_GAIN / scale) * slope * columns.astype(F32)
+    scale = SECOND_SCALE / top
+    product = chip_sum(primary_partial * scale, ROW_STEPS)
+    p2 = keep * u - (COUPLE_GAIN / scale) * product
+
+    for pairs in SMALL_ROW:
+        last = last + move(last, pairs)
     dots = jnp.stack(
         [
-            jnp.sum(gs * p1, axis=1),
-            jnp.sum(us * g, axis=1),
-            jnp.sum(gs * u, axis=1),
-            jnp.sum(us * u, axis=1),
-            jnp.sum(us * p1, axis=1),
-            jnp.sum(q1 * u, axis=1),
-            jnp.sum(us * p2, axis=1),
+            total(gs * p1),
+            total(us * g),
+            total(us * u),
+            total(us * p1),
+            total(q1 * u),
+            total(us * (keep * u)),
         ]
     )
     for pairs in SMALL_COL:
         dots = dots + move(dots, pairs)
-    curve, us_g, gs_u, us_u, us_p1, q1_u, us_p2 = (dots[i] for i in range(7))
+    curve, us_g, us_u, us_p1, q1_u, us_kept = (dots[i] for i in range(6))
+    us_p2 = us_kept - COUPLE_GAIN * last
+    gs_u = align - alpha * curve
     step = align / curve
     kappa = step / alpha
     rest = 1.0 - kappa
-    align_next = rest * rest * align + kappa * rest * (us_g + gs_u) + kappa * kappa * us_u
+    align_next = (
+        rest * rest * align + kappa * rest * (us_g + gs_u) + kappa * kappa * us_u
+    )
     blend = align_next / align
     lead = rest + blend
     curve_next = (

time: 194 us -> 162 us (0.84)
  Pallas kernels: 0 us -> 40.4 us
  matrix products: 39.5 us -> 0 us
  starting transfers between devices: 61.9 us -> 35.1 us
  waiting for transfers between devices: 80.7 us -> 62.2 us
  other arithmetic: 10.3 us -> 19.5 us
  local copies, waits for them, and re-layouts: 0.04 us -> 2 us
    pallas_call x0 -> x4, Pallas kernels: none -> 40.4 us  [call(): pl.pallas_call(kernel, name=name, grid=(rows // TILE,), in_specs=[left_sp...]
    dot_general x4 -> x0, matrix products: 39.5 us -> none  [the longest x2 21.9 us: shadow(): lax.dot_general(vector.astype(BF16), coupling, (((1,), (1,)), ((), ())),...]
    ppermute x28 -> x35, starting transfers between devices: 61.9 us -> 35.1 us  [move(): return lax.ppermute(value, AXES, pairs)]
    ppermute x28 -> x35, waiting for transfers between devices: 80.7 us -> 62.2 us  [move(): return lax.ppermute(value, AXES, pairs)]
    sub x0 -> x1, other arithmetic: none -> 2.39 us  [on_device(): residual = g - step * p1 - step_next * (lead * p1 + kappa * p2)]
    reduce_sum x2 -> x3, other arithmetic: 3.51 us -> 4.34 us  [total(): return jnp.sum(value, axis=1)]
  transfers between devices with their start and end apart: 28 -> 35, of which waited for: 18 -> 20; matrix products, arithmetic and copies ran while one was open for 11% -> 10% of each run, Pallas kernels for 0% -> 18%
where the time goes in v2:
time: 162 us; the launch traced here: 161 us
  waiting for transfers between devices  62.2 us (38%)
  Pallas kernels  40.4 us (25%)
  starting transfers between devices  35.1 us (22%)
  other arithmetic  19.5 us (12%)
  local copies, waits for them, and re-layouts  2 us (1%)
  between operations  1.78 us (1%)
    ppermute x35, waiting for transfers between devices, move(): return lax.ppermute(value, AXES, pairs)  62.2 us
    pallas_call x4, Pallas kernels, call(): pl.pallas_call(kernel, name=name, grid=(rows // TILE,), in_specs=[left_sp...  40.4 us
    ppermute x35, starting transfers between devices, move(): return lax.ppermute(value, AXES, pairs)  35.1 us
    reduce_sum x3, other arithmetic, total(): return jnp.sum(value, axis=1)  4.34 us
    convert_element_type x11, other arithmetic, chip_sum(): held = value.astype(WIRE)  3.29 us
  transfers between devices with their start and end apart: 35, of which 20 were waited for; matrix products, arithmetic and copies ran while one was open for 10% of the time, Pallas kernels for 18%

profile of v2, /device:TPU:0, one launch (start us, length us, event | category | flops | bytes accessed | tf_op | source)
XLA Modules:
  0.0 160.9 jit_solution(13279912972683879477)
XLA Ops:
  0.6 2.7 %multiply_reduce_fusion.8 = (f32[64]{0:T(128)S(1)}, f32[64]{0:T(128)S(1)}, f32[64]{0:T(128)S(1)}, f32[64]{0:T(128)S(1)}, bf16[64,2048]{1,0:T(8,128)(2,1)S(1)}, /...) fusion(f32[64,2048]{1,0:T(8,128)} %param.8, f32[64,2048]{1,0:T(8,128)} %param.7, ...), kind=kLoop, calls=%fused_computation.36 | loop fusion | flops 2096896 | bytes 3146752 | tf_op jit(solution)/shard_map/reduce_sum | solution.py:209
  3.5 1.1 collective-permute-done
  4.6 1.7 %collective-permute-start.1 = (f32[4,64]{1,0:T(4,128)S(1)}, f32[4,64]{1,0:T(4,128)S(1)}, u32[]{:S(2)}, u32[]{:S(2)}) collective-permute-start(f32[4,64]{1,0:T(4,128)S(1)} %pad_maximum_fusion.6), channel_id=1, source_target_pairs={{8,0},{9,1},{10,2},{11,3},{12,4},{13,5},{14,6},{15,7},{0,8},{1,9},... | collective-permute-start | bytes 3080 | tf_op jit(solution)/shard_map/ppermute | solution.py:177
  6.4 1.2 dynamic_slice.3
  8.3 2.1 %collective-permute-start.2 = (f32[4,64]{1,0:T(4,128)S(1)}, f32[4,64]{1,0:T(4,128)S(1)}, u32[]{:S(2)}, u32[]{:S(2)}) collective-permute-start(f32[4,64]{1,0:T(4,128)S(1)} %pad_maximum_fusion.7), channel_id=1, source_target_pairs={{2,0},{3,1},{0,2},{1,3},{6,4},{7,5},{4,6},{5,7},{10,8},{11,9},{8,1... | collective-permute-start | bytes 3080 | tf_op jit(solution)/shard_map/ppermute | solution.py:177
  10.4 3.7 %collective-permute-start.4 = (bf16[64,1024]{1,0:T(8,128)(2,1)S(1)}, bf16[64,1024]{1,0:T(8,128)(2,1)S(1)}, u32[]{:S(2)}, u32[]{:S(2)}) collective-permute-start(bf16[64,1024]{1,0:T(8,128)(2,1)S(1)} %slice_select_fusion.2), channel_id=1, source_target_pairs={{64,0},{65,1},{32,2},{97,3},{0,4},{1,5},{96,6},{33,7},{80,8},{81,9... | collective-permute-start | bytes 393224 | tf_op jit(solution)/shard_map/ppermute | solution.py:177
  14.1 4.0 %collective-permute-start.3 = (f32[4,64]{1,0:T(4,128)S(1)}, f32[4,64]{1,0:T(4,128)S(1)}, u32[]{:S(2)}, u32[]{:S(2)}) collective-permute-start(f32[4,64]{1,0:T(4,128)S(1)} %pad_maximum_fusion.8), channel_id=1, source_target_pairs={{6,0},{7,1},{4,2},{5,3},{2,4},{3,5},{0,6},{1,7},{14,8},{15,9},{12,... | collective-permute-start | bytes 3080 | tf_op jit(solution)/shard_map/ppermute | solution.py:177
  18.1 10.7 %shadow.2 = f32[64,4096]{1,0:T(8,128)S(1)} custom-call(bf16[64,2048]{1,0:T(8,128)(2,1)S(1)} %get-tuple-element.40.left_ref, bf16[4096,2048]{1,0:T(8,128)(2,1)} %coupling_ref.7), custom_call_target="tpu_custom_call" | custom-call | flops 1073741824 | bytes 16777216 | tf_op jit(solution)/shard_map/shadow/pallas_call | solution.py:134
  28.9 0.6 multiply_bitcast_fusion
  29.5 4.9 %collective-permute-done.5 = bf16[64,1024]{1,0:T(8,128)(2,1)S(1)} collective-permute-done((bf16[64,1024]{1,0:T(8,128)(2,1)S(1)}, bf16[64,1024]{1,0:T(8,128)(2,1)S(1)}, u32[]{:S(2)}, u32[]{:S(2)}) %collective-permute-start.5) | collective-permute-done | bytes 131104 | tf_op jit(solution)/shard_map/ppermute | solution.py:177
  34.7 0.6 collective-permute-start.11
  35.3 0.8 collective-permute-done.6
  36.2 9.5 %primary.2 = f32[64,2048]{1,0:T(8,128)S(1)} custom-call(bf16[64,4096]{1,0:T(8,128)(2,1)S(1)} %pad_maximum_fusion.left_ref, bf16[4096,2048]{1,0:T(8,128)(2,1)} %coupling_ref.7), custom_call_target="tpu_custom_call" | custom-call | flops 1073741824 | bytes 16777216 | tf_op jit(solution)/shard_map/primary/pallas_call | solution.py:134
  46.2 1.4 collective-permute-start.12
  47.6 3.4 %collective-permute-done.7 = f16[64,1024]{1,0:T(8,128)(2,1)S(1)} collective-permute-done((f16[64,1024]{1,0:T(8,128)(2,1)S(1)}, f16[64,1024]{1,0:T(8,128)(2,1)S(1)}, u32[]{:S(2)}, u32[]{:S(2)}) %collective-permute-start.7) | collective-permute-done | bytes 131104 | tf_op jit(solution)/shard_map/ppermute | solution.py:177
  51.0 1.7 %collective-permute-start.8 = (f16[64,1024]{1,0:T(8,128)(2,1)S(1)}, f16[64,1024]{1,0:T(8,128)(2,1)S(1)}, u32[]{:S(2)}, u32[]{:S(2)}) collective-permute-start(f16[64,1024]{1,0:T(8,128)(2,1)S(1)} %add_convert_fusion.12), channel_id=1, source_target_pairs={{96,0},{33,1},{98,2},{35,3},{100,4},{37,5},{102,6},{39,7},{104,8},... | collective-permute-start | bytes 393224 | tf_op jit(solution)/shard_map/ppermute | solution.py:177
  53.0 0.3 collective-permute-start.13
  53.2 4.0 %collective-permute-done.8 = f16[64,1024]{1,0:T(8,128)(2,1)S(1)} collective-permute-done((f16[64,1024]{1,0:T(8,128)(2,1)S(1)}, f16[64,1024]{1,0:T(8,128)(2,1)S(1)}, u32[]{:S(2)}, u32[]{:S(2)}) %collective-permute-start.8) | collective-permute-done | bytes 131104 | tf_op jit(solution)/shard_map/ppermute | solution.py:177
  57.3 1.4 collective-permute-start.9
  58.7 5.2 %collective-permute-done.9 = f16[64,1024]{1,0:T(8,128)(2,1)S(1)} collective-permute-done((f16[64,1024]{1,0:T(8,128)(2,1)S(1)}, f16[64,1024]{1,0:T(8,128)(2,1)S(1)}, u32[]{:S(2)}, u32[]{:S(2)}) %collective-permute-start.9) | collective-permute-done | bytes 131104 | tf_op jit(solution)/shard_map/ppermute | solution.py:177
  63.9 1.2 fusion.7
  65.1 0.4 collective-permute-start.20
  65.5 1.3 collective-permute-start.10
  66.9 2.1 %collective-permute-start.14 = (f16[64,2048]{1,0:T(8,128)(2,1)S(1)}, f16[64,2048]{1,0:T(8,128)(2,1)S(1)}, u32[]{:S(2)}, u32[]{:S(2)}) collective-permute-start(f16[64,2048]{1,0:T(8,128)(2,1)S(1)} %add_convert_fusion.7), channel_id=1, source_target_pairs={{6,0},{9,1},{4,2},{11,3},{2,4},{13,5},{0,6},{15,7},{14,8},{1,9},{1... | collective-permute-start | bytes 786440 | tf_op jit(solution)/shard_map/ppermute | solution.py:177
  69.0 5.3 %collective-permute-done.20 = bf16[64,1024]{1,0:T(8,128)(2,1)S(1)} collective-permute-done((bf16[64,1024]{1,0:T(8,128)(2,1)S(1)}, bf16[64,1024]{1,0:T(8,128)(2,1)S(1)}, u32[]{:S(2)}, u32[]{:S(2)}) %collective-permute-start.20) | collective-permute-done | bytes 131104 | tf_op jit(solution)/shard_map/ppermute | solution.py:177
  74.4 4.9 %collective-permute-done.21 = bf16[64,1024]{1,0:T(8,128)(2,1)S(1)} collective-permute-done((bf16[64,1024]{1,0:T(8,128)(2,1)S(1)}, bf16[64,1024]{1,0:T(8,128)(2,1)S(1)}, u32[]{:S(2)}, u32[]{:S(2)}) %collective-permute-start.21) | collective-permute-done | bytes 131104 | tf_op jit(solution)/shard_map/ppermute | solution.py:177
  79.5 1.3 collective-permute-start.15
  80.9 0.9 broadcast_select_fusion.1
  81.8 10.8 %collective-permute-done.15 = f16[64,2048]{1,0:T(8,128)(2,1)S(1)} collective-permute-done((f16[64,2048]{1,0:T(8,128)(2,1)S(1)}, f16[64,2048]{1,0:T(8,128)(2,1)S(1)}, u32[]{:S(2)}, u32[]{:S(2)}) %collective-permute-start.15) | collective-permute-done | bytes 262176 | tf_op jit(solution)/shard_map/ppermute | solution.py:177
  92.6 0.3 fusion.20
  92.8 10.7 %shadow.3 = f32[64,4096]{1,0:T(8,128)S(1)} custom-call(bf16[64,2048]{1,0:T(8,128)(2,1)S(1)} %get-tuple-element.26.left_ref, bf16[4096,2048]{1,0:T(8,128)(2,1)} %coupling_ref.7), custom_call_target="tpu_custom_call" | custom-call | flops 1073741824 | bytes 16777216 | tf_op jit(solution)/shard_map/shadow/pallas_call | solution.py:134
  103.6 0.8 multiply_convert_fusion.1
  104.4 1.4 multiply_reduce_fusion.1
  105.8 0.7 stack.51
  106.5 0.6 collective-permute-start.16
  107.1 1.1 add_convert_fusion.5
  108.3 1.1 pad_maximum_fusion.1.left_ref
  109.4 2.1 %collective-permute-start.17 = (f32[6,64]{1,0:T(8,128)S(1)}, f32[6,64]{1,0:T(8,128)S(1)}, u32[]{:S(2)}, u32[]{:S(2)}) collective-permute-start(f32[6,64]{1,0:T(8,128)S(1)} %add.155), channel_id=1, source_target_pairs={{8,0},{9,1},{10,2},{11,3},{12,4},{13,5},{14,6},{15,7},{0,8},{1,9},... | collective-permute-start | bytes 4616 | tf_op jit(solution)/shard_map/ppermute | solution.py:177
  111.5 9.5 %primary.3 = f32[64,2048]{1,0:T(8,128)S(1)} custom-call(bf16[64,4096]{1,0:T(8,128)(2,1)S(1)} %pad_maximum_fusion.1.left_ref, bf16[4096,2048]{1,0:T(8,128)(2,1)} %coupling_ref.7), custom_call_target="tpu_custom_call" | custom-call | flops 1073741824 | bytes 16777216 | tf_op jit(solution)/shard_map/primary/pallas_call | solution.py:134
  121.0 0.3 collective-permute-start.18
  121.4 2.1 %collective-permute-start.24 = (f16[64,2048]{1,0:T(8,128)(2,1)S(1)}, f16[64,2048]{1,0:T(8,128)(2,1)S(1)}, u32[]{:S(2)}, u32[]{:S(2)}) collective-permute-start(f16[64,2048]{1,0:T(8,128)(2,1)S(1)} %add_convert_fusion.4), channel_id=1, source_target_pairs={{2,0},{7,1},{0,2},{5,3},{6,4},{3,5},{4,6},{1,7},{10,8},{15,9},{8,1... | collective-permute-start | bytes 786440 | tf_op jit(solution)/shard_map/ppermute | solution.py:177
  123.5 0.7 multiply_convert_fusion
  124.3 0.6 collective-permute-done.18
  124.9 0.6 collective-permute-start.19
  125.4 2.4 %collective-permute-done.24 = f16[64,2048]{1,0:T(8,128)(2,1)S(1)} collective-permute-done((f16[64,2048]{1,0:T(8,128)(2,1)S(1)}, f16[64,2048]{1,0:T(8,128)(2,1)S(1)}, u32[]{:S(2)}, u32[]{:S(2)}) %collective-permute-start.24) | collective-permute-done | bytes 262176 | tf_op jit(solution)/shard_map/ppermute | solution.py:177
  127.9 0.4 collective-permute-start.25
  128.3 2.4 %collective-permute-done.31 = f16[64,2048]{1,0:T(8,128)(2,1)S(1)} collective-permute-done((f16[64,2048]{1,0:T(8,128)(2,1)S(1)}, f16[64,2048]{1,0:T(8,128)(2,1)S(1)}, u32[]{:S(2)}, u32[]{:S(2)}) %collective-permute-start.31) | collective-permute-done | bytes 262176 | tf_op jit(solution)/shard_map/ppermute | solution.py:177
  130.7 0.8 add_convert_fusion.1
  131.4 0.8 collective-permute-start.32
  132.2 3.3 %collective-permute-done.25 = f16[64,2048]{1,0:T(8,128)(2,1)S(1)} collective-permute-done((f16[64,2048]{1,0:T(8,128)(2,1)S(1)}, f16[64,2048]{1,0:T(8,128)(2,1)S(1)}, u32[]{:S(2)}, u32[]{:S(2)}) %collective-permute-start.25) | collective-permute-done | bytes 262176 | tf_op jit(solution)/shard_map/ppermute | solution.py:177
  135.8 0.7 fusion.17
  136.5 1.1 collective-permute-done.26
  137.7 3.5 %collective-permute-done.27 = f32[64]{0:T(128)S(1)} collective-permute-done((f32[64]{0:T(128)S(1)}, f32[64]{0:T(128)S(1)}, u32[]{:S(2)}, u32[]{:S(2)}) %collective-permute-start.27) | collective-permute-done | bytes 288 | tf_op jit(solution)/shard_map/ppermute | solution.py:177
  141.2 1.1 collective-permute-start.28
  142.3 2.1 %collective-permute-start.33 = (f16[64,2048]{1,0:T(8,128)(2,1)S(1)}, f16[64,2048]{1,0:T(8,128)(2,1)S(1)}, u32[]{:S(2)}, u32[]{:S(2)}) collective-permute-start(f16[64,2048]{1,0:T(8,128)(2,1)S(1)} %add_convert_fusion), channel_id=1, source_target_pairs={{16,0},{97,1},{18,2},{99,3},{20,4},{101,5},{22,6},{103,7},{24,8},{... | collective-permute-start | bytes 786440 | tf_op jit(solution)/shard_map/ppermute | solution.py:177
  144.4 1.5 collective-permute-done.28
  145.9 1.7 %collective-permute-start.29 = (f32[64]{0:T(128)S(1)}, f32[64]{0:T(128)S(1)}, u32[]{:S(2)}, u32[]{:S(2)}) collective-permute-start(f32[64]{0:T(128)S(1)} %add.172), channel_id=1, source_target_pairs={{16,0},{17,1},{18,2},{19,3},{20,4},{21,5},{22,6},{23,7},{24,8},{25... | collective-permute-start | bytes 776 | tf_op jit(solution)/shard_map/ppermute | solution.py:177
  147.6 0.8 fusion.12
  148.4 1.1 collective-permute-start.34
  149.5 1.5 collective-permute-done.29
  151.0 0.7 fusion.10
  151.7 2.4 %multiply_subtract_fusion.1 = (f32[64,2048]{1,0:T(8,128)}, f32[64,2048]{1,0:T(8,128)}) fusion(f16[64,2048]{1,0:T(8,128)(2,1)S(1)} %collective-permute-done.33, f16[64,2048]{1,0:T(8,128)(2,1)S(1)} %add_convert_fusion, f32[64,2048]{1,0:T(8,128)S(1)} %copy-done.1, f32[64]{0:T(128)} %get-tuple-element.59, f32[64]{0:T(128)S(1)} %get-tuple-element.29, ...), kind=kLoop, calls=%fused_computation.3 | loop fusion | flops 3932160 | bytes 2885376 | tf_op jit(solution)/shard_map/sub | solution.py:327
  154.1 5.0 %collective-permute-done.34 = f16[64,2048]{1,0:T(8,128)(2,1)S(1)} collective-permute-done((f16[64,2048]{1,0:T(8,128)(2,1)S(1)}, f16[64,2048]{1,0:T(8,128)(2,1)S(1)}, u32[]{:S(2)}, u32[]{:S(2)}) %collective-permute-start.34) | collective-permute-done | bytes 262176 | tf_op jit(solution)/shard_map/ppermute | solution.py:177
  159.1 1.8 %multiply_subtract_fusion = (f32[64,2048]{1,0:T(8,128)}, f32[64,2048]{1,0:T(8,128)}) fusion(f16[64,2048]{1,0:T(8,128)(2,1)S(1)} %collective-permute-done.34, f32[64,2048]{1,0:T(8,128)S(1)} %get-tuple-element.27, f32[64,2048]{1,0:T(8,128)S(1)} %copy-done.2, f16[64,2048]{1,0:T(8,128)(2,1)S(1)} %collective-permute-done.15, f32[64]{0:T(128)S(1)} %get-tuple-element.57, ...), kind=kLoop, calls=%fused_computation.2 | loop fusion | flops 3538944 | bytes 3147264 | tf_op jit(solution)/shard_map/sub | solution.py:328
  (90 shorter events, 2.6 us)
Async XLA Ops:
  3.4 1.2 collective-permute-start
  4.6 3.7 %collective-permute-start.1 = (f32[4,64]{1,0:T(4,128)S(1)}, f32[4,64]{1,0:T(4,128)S(1)}, u32[]{:S(2)}, u32[]{:S(2)}) collective-permute-start(f32[4,64]{1,0:T(4,128)S(1)} %pad_maximum_fusion.6), channel_id=1, source_target_pairs={{8,0},{9,1},{10,2},{11,3},{12,4},{13,5},{14,6},{15,7},{0,8},{1,9},... | collective-permute-start | bytes 3080 | tf_op jit(solution)/shard_map/ppermute | solution.py:177
  8.3 5.8 %collective-permute-start.2 = (f32[4,64]{1,0:T(4,128)S(1)}, f32[4,64]{1,0:T(4,128)S(1)}, u32[]{:S(2)}, u32[]{:S(2)}) collective-permute-start(f32[4,64]{1,0:T(4,128)S(1)} %pad_maximum_fusion.7), channel_id=1, source_target_pairs={{2,0},{3,1},{0,2},{1,3},{6,4},{7,5},{4,6},{5,7},{10,8},{11,9},{8,1... | collective-permute-start | bytes 3080 | tf_op jit(solution)/shard_map/ppermute | solution.py:177
  10.4 19.0 %collective-permute-start.4 = (bf16[64,1024]{1,0:T(8,128)(2,1)S(1)}, bf16[64,1024]{1,0:T(8,128)(2,1)S(1)}, u32[]{:S(2)}, u32[]{:S(2)}) collective-permute-start(bf16[64,1024]{1,0:T(8,128)(2,1)S(1)} %slice_select_fusion.2), channel_id=1, source_target_pairs={{64,0},{65,1},{32,2},{97,3},{0,4},{1,5},{96,6},{33,7},{80,8},{81,9... | collective-permute-start | bytes 393224 | tf_op jit(solution)/shard_map/ppermute | solution.py:177
  14.1 14.7 %collective-permute-start.3 = (f32[4,64]{1,0:T(4,128)S(1)}, f32[4,64]{1,0:T(4,128)S(1)}, u32[]{:S(2)}, u32[]{:S(2)}) collective-permute-start(f32[4,64]{1,0:T(4,128)S(1)} %pad_maximum_fusion.8), channel_id=1, source_target_pairs={{6,0},{7,1},{4,2},{5,3},{2,4},{3,5},{0,6},{1,7},{14,8},{15,9},{12,... | collective-permute-start | bytes 3080 | tf_op jit(solution)/shard_map/ppermute | solution.py:177
  28.8 35.1 %copy-start.1 = (f32[64,2048]{1,0:T(8,128)S(1)}, f32[64,2048]{1,0:T(8,128)}, u32[]{:S(2)}) copy-start(f32[64,2048]{1,0:T(8,128)} %param.7) | copy-start | bytes 1572868
  28.8 5.6 %copy-start.9 = (f32[2,64]{1,0:T(2,128)}, f32[2,64]{1,0:T(2,128)S(1)}, u32[]{:S(2)}) copy-start(f32[2,64]{1,0:T(2,128)S(1)} %get-tuple-element.50) | copy-start | bytes 1540
  28.8 53.0 %copy-start.10 = (f32[2,64]{1,0:T(2,128)}, f32[2,64]{1,0:T(2,128)S(1)}, u32[]{:S(2)}) copy-start(f32[2,64]{1,0:T(2,128)S(1)} %get-tuple-element.49) | copy-start | bytes 1540
  29.4 5.0 %collective-permute-start.5 = (bf16[64,1024]{1,0:T(8,128)(2,1)S(1)}, bf16[64,1024]{1,0:T(8,128)(2,1)S(1)}, u32[]{:S(2)}, u32[]{:S(2)}) collective-permute-start(bf16[64,1024]{1,0:T(8,128)(2,1)S(1)} %collective-permute-done.4), channel_id=1, source_target_pairs={{2,0},{3,1},{0,2},{1,3},{6,4},{7,5},{4,6},{5,7},{10,8},{11,9},{8,1... | collective-permute-start | bytes 393224 | tf_op jit(solution)/shard_map/ppermute | solution.py:177
  29.4 74.1 %copy-start.11 = (f32[64]{0:T(128)}, f32[64]{0:T(128)S(1)}, u32[]{:S(2)}) copy-start(f32[64]{0:T(128)S(1)} %get-tuple-element.63) | copy-start | bytes 772
  34.4 58.1 %copy-start = (f32[64,2048]{1,0:T(8,128)S(1)}, f32[64,2048]{1,0:T(8,128)}, u32[]{:S(2)}) copy-start(f32[64,2048]{1,0:T(8,128)} %param.6) | copy-start | bytes 1572868
  34.4 58.1 %copy-start.2 = (f32[64,2048]{1,0:T(8,128)S(1)}, f32[64,2048]{1,0:T(8,128)}, u32[]{:S(2)}) copy-start(f32[64,2048]{1,0:T(8,128)} %param.8) | copy-start | bytes 1572868
  34.5 1.6 %collective-permute-start.6 = (bf16[64,2048]{1,0:T(8,128)(2,1)S(1)}, bf16[64,2048]{1,0:T(8,128)(2,1)S(1)}, u32[]{:S(2)}, u32[]{:S(2)}) collective-permute-start(bf16[64,2048]{1,0:T(8,128)(2,1)S(1)} %pad_maximum_fusion.2), channel_id=1, source_target_pairs={{1,0},{0,1},{3,2},{2,3},{5,4},{4,5},{7,6},{6,7},{9,8},{8,9},{11,10... | collective-permute-start | bytes 786440 | tf_op jit(solution)/shard_map/ppermute | solution.py:177
  34.7 11.3 %collective-permute-start.11 = (f16[64,2048]{1,0:T(8,128)(2,1)S(1)}, f16[64,2048]{1,0:T(8,128)(2,1)S(1)}, u32[]{:S(2)}, u32[]{:S(2)}) collective-permute-start(f16[64,2048]{1,0:T(8,128)(2,1)S(1)} %multiply_convert_fusion.2), channel_id=1, source_target_pairs={{1,0},{0,1},{3,2},{2,3},{5,4},{4,5},{7,6},{6,7},{9,8},{8,9},{11,10... | collective-permute-start | bytes 786440 | tf_op jit(solution)/shard_map/ppermute | solution.py:177
  45.9 5.0 %collective-permute-start.7 = (f16[64,1024]{1,0:T(8,128)(2,1)S(1)}, f16[64,1024]{1,0:T(8,128)(2,1)S(1)}, u32[]{:S(2)}, u32[]{:S(2)}) collective-permute-start(f16[64,1024]{1,0:T(8,128)(2,1)S(1)} %select_convert_fusion), channel_id=1, source_target_pairs={{32,0},{17,1},{34,2},{19,3},{36,4},{21,5},{38,6},{23,7},{40,8},{25... | collective-permute-start | bytes 393224 | tf_op jit(solution)/shard_map/ppermute | solution.py:177
  46.2 6.7 %collective-permute-start.12 = (f16[64,2048]{1,0:T(8,128)(2,1)S(1)}, f16[64,2048]{1,0:T(8,128)(2,1)S(1)}, u32[]{:S(2)}, u32[]{:S(2)}) collective-permute-start(f16[64,2048]{1,0:T(8,128)(2,1)S(1)} %add_convert_fusion.9), channel_id=1, source_target_pairs={{8,0},{3,1},{10,2},{1,3},{12,4},{7,5},{14,6},{5,7},{0,8},{11,9},{2... | collective-permute-start | bytes 786440 | tf_op jit(solution)/shard_map/ppermute | solution.py:177
  51.0 6.3 %collective-permute-start.8 = (f16[64,1024]{1,0:T(8,128)(2,1)S(1)}, f16[64,1024]{1,0:T(8,128)(2,1)S(1)}, u32[]{:S(2)}, u32[]{:S(2)}) collective-permute-start(f16[64,1024]{1,0:T(8,128)(2,1)S(1)} %add_convert_fusion.12), channel_id=1, source_target_pairs={{96,0},{33,1},{98,2},{35,3},{100,4},{37,5},{102,6},{39,7},{104,8},... | collective-permute-start | bytes 393224 | tf_op jit(solution)/shard_map/ppermute | solution.py:177
  53.0 13.9 %collective-permute-start.13 = (f16[64,2048]{1,0:T(8,128)(2,1)S(1)}, f16[64,2048]{1,0:T(8,128)(2,1)S(1)}, u32[]{:S(2)}, u32[]{:S(2)}) collective-permute-start(f16[64,2048]{1,0:T(8,128)(2,1)S(1)} %add_convert_fusion.8), channel_id=1, source_target_pairs={{2,0},{7,1},{0,2},{5,3},{6,4},{3,5},{4,6},{1,7},{10,8},{15,9},{8,1... | collective-permute-start | bytes 786440 | tf_op jit(solution)/shard_map/ppermute | solution.py:177
  57.3 6.6 %collective-permute-start.9 = (f16[64,1024]{1,0:T(8,128)(2,1)S(1)}, f16[64,1024]{1,0:T(8,128)(2,1)S(1)}, u32[]{:S(2)}, u32[]{:S(2)}) collective-permute-start(f16[64,1024]{1,0:T(8,128)(2,1)S(1)} %add_convert_fusion.11), channel_id=1, source_target_pairs={{16,0},{97,1},{18,2},{99,3},{20,4},{101,5},{22,6},{103,7},{24,8},{... | collective-permute-start | bytes 393224 | tf_op jit(solution)/shard_map/ppermute | solution.py:177
  65.1 9.2 %collective-permute-start.20 = (bf16[64,1024]{1,0:T(8,128)(2,1)S(1)}, bf16[64,1024]{1,0:T(8,128)(2,1)S(1)}, u32[]{:S(2)}, u32[]{:S(2)}) collective-permute-start(bf16[64,1024]{1,0:T(8,128)(2,1)S(1)} %get-tuple-element.24), channel_id=1, source_target_pairs={{112,0},{65,1},{48,2},{113,3},{0,4},{33,5},{64,6},{17,7},{96,8},{9... | collective-permute-start | bytes 393224 | tf_op jit(solution)/shard_map/ppermute | solution.py:177
  65.5 8.7 %collective-permute-start.10 = (f16[64,1024]{1,0:T(8,128)(2,1)S(1)}, f16[64,1024]{1,0:T(8,128)(2,1)S(1)}, u32[]{:S(2)}, u32[]{:S(2)}) collective-permute-start(f16[64,1024]{1,0:T(8,128)(2,1)S(1)} %get-tuple-element.25), channel_id=1, source_target_pairs={{32,0},{17,1},{34,2},{19,3},{36,4},{21,5},{38,6},{23,7},{40,8},{25... | collective-permute-start | bytes 393224 | tf_op jit(solution)/shard_map/ppermute | solution.py:177
  66.9 12.5 %collective-permute-start.14 = (f16[64,2048]{1,0:T(8,128)(2,1)S(1)}, f16[64,2048]{1,0:T(8,128)(2,1)S(1)}, u32[]{:S(2)}, u32[]{:S(2)}) collective-permute-start(f16[64,2048]{1,0:T(8,128)(2,1)S(1)} %add_convert_fusion.7), channel_id=1, source_target_pairs={{6,0},{9,1},{4,2},{11,3},{2,4},{13,5},{0,6},{15,7},{14,8},{1,9},{1... | collective-permute-start | bytes 786440 | tf_op jit(solution)/shard_map/ppermute | solution.py:177
  74.3 5.0 %collective-permute-start.21 = (bf16[64,1024]{1,0:T(8,128)(2,1)S(1)}, bf16[64,1024]{1,0:T(8,128)(2,1)S(1)}, u32[]{:S(2)}, u32[]{:S(2)}) collective-permute-start(bf16[64,1024]{1,0:T(8,128)(2,1)S(1)} %collective-permute-done.20), channel_id=1, source_target_pairs={{2,0},{3,1},{0,2},{1,3},{6,4},{7,5},{4,6},{5,7},{10,8},{11,9},{8,1... | collective-permute-start | bytes 393224 | tf_op jit(solution)/shard_map/ppermute | solution.py:177
  74.3 30.1 %copy-start.5 = (f16[64,1024]{1,0:T(8,128)(2,1)}, f16[64,1024]{1,0:T(8,128)(2,1)S(1)}, u32[]{:S(2)}) copy-start(f16[64,1024]{1,0:T(8,128)(2,1)S(1)} %get-tuple-element.44) | copy-start | bytes 393220
  74.3 31.4 %copy-start.7 = (f16[64,1024]{1,0:T(8,128)(2,1)}, f16[64,1024]{1,0:T(8,128)(2,1)S(1)}, u32[]{:S(2)}) copy-start(f16[64,1024]{1,0:T(8,128)(2,1)S(1)} %get-tuple-element.45) | copy-start | bytes 393220
  79.3 13.3 %copy-start.3 = (bf16[64,1024]{1,0:T(8,128)(2,1)}, bf16[64,1024]{1,0:T(8,128)(2,1)S(1)}, u32[]{:S(2)}) copy-start(bf16[64,1024]{1,0:T(8,128)(2,1)S(1)} %get-tuple-element.43) | copy-start | bytes 393220
  79.3 1.6 %collective-permute-start.30 = (bf16[64,2048]{1,0:T(8,128)(2,1)S(1)}, bf16[64,2048]{1,0:T(8,128)(2,1)S(1)}, u32[]{:S(2)}, u32[]{:S(2)}) collective-permute-start(bf16[64,2048]{1,0:T(8,128)(2,1)S(1)} %pad_maximum_fusion.4), channel_id=1, source_target_pairs={{1,0},{0,1},{3,2},{2,3},{5,4},{4,5},{7,6},{6,7},{9,8},{8,9},{11,10... | collective-permute-start | bytes 786440 | tf_op jit(solution)/shard_map/ppermute | solution.py:177
  79.5 13.1 %collective-permute-start.15 = (f16[64,2048]{1,0:T(8,128)(2,1)S(1)}, f16[64,2048]{1,0:T(8,128)(2,1)S(1)}, u32[]{:S(2)}, u32[]{:S(2)}) collective-permute-start(f16[64,2048]{1,0:T(8,128)(2,1)S(1)} %add_convert_fusion.6), channel_id=1, source_target_pairs={{4,0},{5,1},{30,2},{31,3},{34,4},{39,5},{60,6},{57,7},{72,8},{73,9... | collective-permute-start | bytes 786440 | tf_op jit(solution)/shard_map/ppermute | solution.py:177
  104.4 2.7 %collective-permute-start.22 = (f16[64,2048]{1,0:T(8,128)(2,1)}, f16[64,2048]{1,0:T(8,128)(2,1)}, u32[]{:S(2)}, u32[]{:S(2)}) collective-permute-start(f16[64,2048]{1,0:T(8,128)(2,1)} %multiply_convert_fusion.1), channel_id=1, source_target_pairs={{1,0},{0,1},{3,2},{2,3},{5,4},{4,5},{7,6},{6,7},{9,8},{8,9},{11,10... | collective-permute-start | bytes 786440 | tf_op jit(solution)/shard_map/ppermute | solution.py:177
  106.5 29.1 %copy-start.4 = (bf16[64,1024]{1,0:T(8,128)(2,1)S(1)}, bf16[64,1024]{1,0:T(8,128)(2,1)}, u32[]{:S(2)}) copy-start(bf16[64,1024]{1,0:T(8,128)(2,1)} %copy-done.3) | copy-start | bytes 393220
  106.5 45.2 %copy-start.6 = (f16[64,1024]{1,0:T(8,128)(2,1)S(1)}, f16[64,1024]{1,0:T(8,128)(2,1)}, u32[]{:S(2)}) copy-start(f16[64,1024]{1,0:T(8,128)(2,1)} %copy-done.5) | copy-start | bytes 393220
  106.5 45.2 %copy-start.8 = (f16[64,1024]{1,0:T(8,128)(2,1)S(1)}, f16[64,1024]{1,0:T(8,128)(2,1)}, u32[]{:S(2)}) copy-start(f16[64,1024]{1,0:T(8,128)(2,1)} %copy-done.7) | copy-start | bytes 393220
  106.5 2.9 %collective-permute-start.16 = (f32[6,64]{1,0:T(8,128)S(1)}, f32[6,64]{1,0:T(8,128)S(1)}, u32[]{:S(2)}, u32[]{:S(2)}) collective-permute-start(f32[6,64]{1,0:T(8,128)S(1)} %stack.51), channel_id=1, source_target_pairs={{1,0},{0,1},{3,2},{2,3},{5,4},{4,5},{7,6},{6,7},{9,8},{8,9},{11,10... | collective-permute-start | bytes 4616 | tf_op jit(solution)/shard_map/ppermute | solution.py:177
  108.2 13.1 %collective-permute-start.23 = (f16[64,2048]{1,0:T(8,128)(2,1)S(1)}, f16[64,2048]{1,0:T(8,128)(2,1)S(1)}, u32[]{:S(2)}, u32[]{:S(2)}) collective-permute-start(f16[64,2048]{1,0:T(8,128)(2,1)S(1)} %add_convert_fusion.5), channel_id=1, source_target_pairs={{8,0},{3,1},{10,2},{1,3},{12,4},{7,5},{14,6},{5,7},{0,8},{11,9},{2... | collective-permute-start | bytes 786440 | tf_op jit(solution)/shard_map/ppermute | solution.py:177
  109.4 11.6 %collective-permute-start.17 = (f32[6,64]{1,0:T(8,128)S(1)}, f32[6,64]{1,0:T(8,128)S(1)}, u32[]{:S(2)}, u32[]{:S(2)}) collective-permute-start(f32[6,64]{1,0:T(8,128)S(1)} %add.155), channel_id=1, source_target_pairs={{8,0},{9,1},{10,2},{11,3},{12,4},{13,5},{14,6},{15,7},{0,8},{1,9},... | collective-permute-start | bytes 4616 | tf_op jit(solution)/shard_map/ppermute | solution.py:177
  121.0 3.9 %collective-permute-start.18 = (f32[6,64]{1,0:T(8,128)S(1)}, f32[6,64]{1,0:T(8,128)S(1)}, u32[]{:S(2)}, u32[]{:S(2)}) collective-permute-start(f32[6,64]{1,0:T(8,128)S(1)} %add.156), channel_id=1, source_target_pairs={{2,0},{3,1},{0,2},{1,3},{6,4},{7,5},{4,6},{5,7},{10,8},{11,9},{8,1... | collective-permute-start | bytes 4616 | tf_op jit(solution)/shard_map/ppermute | solution.py:177
  121.4 6.5 %collective-permute-start.24 = (f16[64,2048]{1,0:T(8,128)(2,1)S(1)}, f16[64,2048]{1,0:T(8,128)(2,1)S(1)}, u32[]{:S(2)}, u32[]{:S(2)}) collective-permute-start(f16[64,2048]{1,0:T(8,128)(2,1)S(1)} %add_convert_fusion.4), channel_id=1, source_target_pairs={{2,0},{7,1},{0,2},{5,3},{6,4},{3,5},{4,6},{1,7},{10,8},{15,9},{8,1... | collective-permute-start | bytes 786440 | tf_op jit(solution)/shard_map/ppermute | solution.py:177
  124.2 6.5 %collective-permute-start.31 = (f16[64,2048]{1,0:T(8,128)(2,1)S(1)}, f16[64,2048]{1,0:T(8,128)(2,1)S(1)}, u32[]{:S(2)}, u32[]{:S(2)}) collective-permute-start(f16[64,2048]{1,0:T(8,128)(2,1)S(1)} %multiply_convert_fusion), channel_id=1, source_target_pairs={{32,0},{17,1},{34,2},{19,3},{36,4},{21,5},{38,6},{23,7},{40,8},{25... | collective-permute-start | bytes 786440 | tf_op jit(solution)/shard_map/ppermute | solution.py:177
  124.9 12.8 %collective-permute-start.19 = (f32[6,64]{1,0:T(8,128)S(1)}, f32[6,64]{1,0:T(8,128)S(1)}, u32[]{:S(2)}, u32[]{:S(2)}) collective-permute-start(f32[6,64]{1,0:T(8,128)S(1)} %add.157), channel_id=1, source_target_pairs={{6,0},{7,1},{4,2},{5,3},{2,4},{3,5},{0,6},{1,7},{14,8},{15,9},{12,... | collective-permute-start | bytes 4616 | tf_op jit(solution)/shard_map/ppermute | solution.py:177
  127.9 7.7 %collective-permute-start.25 = (f16[64,2048]{1,0:T(8,128)(2,1)S(1)}, f16[64,2048]{1,0:T(8,128)(2,1)S(1)}, u32[]{:S(2)}, u32[]{:S(2)}) collective-permute-start(f16[64,2048]{1,0:T(8,128)(2,1)S(1)} %add_convert_fusion.3), channel_id=1, source_target_pairs={{6,0},{9,1},{4,2},{11,3},{2,4},{13,5},{0,6},{15,7},{14,8},{1,9},{1... | collective-permute-start | bytes 786440 | tf_op jit(solution)/shard_map/ppermute | solution.py:177
  131.4 10.8 %collective-permute-start.32 = (f16[64,2048]{1,0:T(8,128)(2,1)S(1)}, f16[64,2048]{1,0:T(8,128)(2,1)S(1)}, u32[]{:S(2)}, u32[]{:S(2)}) collective-permute-start(f16[64,2048]{1,0:T(8,128)(2,1)S(1)} %add_convert_fusion.1), channel_id=1, source_target_pairs={{96,0},{33,1},{98,2},{35,3},{100,4},{37,5},{102,6},{39,7},{104,8},... | collective-permute-start | bytes 786440 | tf_op jit(solution)/shard_map/ppermute | solution.py:177
  136.5 1.1 collective-permute-start.26
  137.6 3.5 %collective-permute-start.27 = (f32[64]{0:T(128)S(1)}, f32[64]{0:T(128)S(1)}, u32[]{:S(2)}, u32[]{:S(2)}) collective-permute-start(f32[64]{0:T(128)S(1)} %add.170), channel_id=1, source_target_pairs={{32,0},{33,1},{34,2},{35,3},{36,4},{37,5},{38,6},{39,7},{40,8},{41... | collective-permute-start | bytes 776 | tf_op jit(solution)/shard_map/ppermute | solution.py:177
  141.2 4.8 %collective-permute-start.28 = (f32[64]{0:T(128)S(1)}, f32[64]{0:T(128)S(1)}, u32[]{:S(2)}, u32[]{:S(2)}) collective-permute-start(f32[64]{0:T(128)S(1)} %add.171), channel_id=1, source_target_pairs={{96,0},{97,1},{98,2},{99,3},{100,4},{101,5},{102,6},{103,7},{104,8... | collective-permute-start | bytes 776 | tf_op jit(solution)/shard_map/ppermute | solution.py:177
  142.3 9.3 %collective-permute-start.33 = (f16[64,2048]{1,0:T(8,128)(2,1)S(1)}, f16[64,2048]{1,0:T(8,128)(2,1)S(1)}, u32[]{:S(2)}, u32[]{:S(2)}) collective-permute-start(f16[64,2048]{1,0:T(8,128)(2,1)S(1)} %add_convert_fusion), channel_id=1, source_target_pairs={{16,0},{97,1},{18,2},{99,3},{20,4},{101,5},{22,6},{103,7},{24,8},{... | collective-permute-start | bytes 786440 | tf_op jit(solution)/shard_map/ppermute | solution.py:177
  145.9 5.0 %collective-permute-start.29 = (f32[64]{0:T(128)S(1)}, f32[64]{0:T(128)S(1)}, u32[]{:S(2)}, u32[]{:S(2)}) collective-permute-start(f32[64]{0:T(128)S(1)} %add.172), channel_id=1, source_target_pairs={{16,0},{17,1},{18,2},{19,3},{20,4},{21,5},{22,6},{23,7},{24,8},{25... | collective-permute-start | bytes 776 | tf_op jit(solution)/shard_map/ppermute | solution.py:177
  148.4 10.8 %collective-permute-start.34 = (f16[64,2048]{1,0:T(8,128)(2,1)S(1)}, f16[64,2048]{1,0:T(8,128)(2,1)S(1)}, u32[]{:S(2)}, u32[]{:S(2)}) collective-permute-start(f16[64,2048]{1,0:T(8,128)(2,1)S(1)} %get-tuple-element.23), channel_id=1, source_target_pairs={{4,0},{5,1},{30,2},{31,3},{34,4},{39,5},{60,6},{57,7},{72,8},{73,9... | collective-permute-start | bytes 786440 | tf_op jit(solution)/shard_map/ppermute | solution.py:177

commit v3 on v2

--- a/solution.py
+++ b/solution.py
@@ -68,11 +68,6 @@
 def from_rows(x, yh, yl, z, h):
     xs, yhs = 2 * yl + z // 2, z % 2
     return xs, yhs, yl ^ yh ^ yhs, (z + STEP[h][(x - xs) % 4]) % 4, h
-
-
-def from_cols(x, yh, yl, z, h):
-    yls, zs = x // 2, (x % 2) * 2 + yh
-    return (x + STEP[h][(z - zs) % 4]) % 4, yh ^ yl ^ yls, yls, zs, h
 
 
 HALF_SOURCE = (
@@ -88,7 +83,6 @@
 
 CORE = sends(flip_core)
 TO_COLS = sends(from_rows)
-TO_ROWS = sends(from_cols)
 HALF_TO_ROWS = [
     (HALF_SOURCE[d] * 16 + (d // 16) * 2 + d % 2, d) for d in range(128)
 ]
@@ -104,41 +98,56 @@
 )
 Z_PAIR = sends(flip_z)
 SMALL_COL = (CORE, sends(flip_yl), sends(flip_z), sends(mirror_z))
-SMALL_ROW = (CORE, sends(flip_x), sends(mirror_x), sends(flip_yh))
-
-TILE = 512
-
-
-def primary_kernel(left_ref, coupling_ref, out_ref):
-    @pl.when(pl.program_id(0) == 0)
-    def _():
-        out_ref[...] = jnp.zeros_like(out_ref)
-
-    out_ref[...] += jnp.dot(
-        left_ref[...], coupling_ref[...], preferred_element_type=F32
-    )
-
-
-def shadow_kernel(left_ref, coupling_ref, out_ref):
-    out_ref[...] = lax.dot_general(
-        left_ref[...],
-        coupling_ref[...],
-        (((1,), (1,)), ((), ())),
-        preferred_element_type=F32,
-    )
-
-
-def call(kernel, name, left, coupling, left_spec, out_spec, width):
+
+def fetch(source_ref, held_ref, sems):
+    chunks = sems.shape[0]
+    size = source_ref.shape[0] // chunks
+    copies = []
+    for i in range(chunks):
+        at = pl.ds(i * size, size)
+        copies.append(
+            pltpu.make_async_copy(source_ref.at[at], held_ref.at[at], sems.at[i])
+        )
+        copies[-1].start()
+    for i, copy in enumerate(copies):
+        copy.wait()
+        yield i, pl.ds(i * size, size)
+
+
+def primary_kernel(left_ref, coupling_ref, out_ref, held_ref, sems):
+    for i, at in fetch(coupling_ref, held_ref, sems):
+        term = jnp.dot(left_ref[:, at], held_ref[at, :], preferred_element_type=F32)
+        if i == 0:
+            out_ref[...] = term
+        else:
+            out_ref[...] += term
+
+
+def shadow_kernel(left_ref, coupling_ref, out_ref, held_ref, sems):
+    for _, at in fetch(coupling_ref, held_ref, sems):
+        out_ref[:, at] = lax.dot_general(
+            left_ref[...],
+            held_ref[at, :],
+            (((1,), (1,)), ((), ())),
+            preferred_element_type=F32,
+        )
+
+
+def call(kernel, name, left, coupling, width, chunks):
     rows, columns = coupling.shape
     reps = left.shape[0]
+    spec = pl.BlockSpec(memory_space=pltpu.VMEM)
     return pl.pallas_call(
         kernel,
         name=name,
-        grid=(rows // TILE,),
-        in_specs=[left_spec, pl.BlockSpec((TILE, columns), lambda i: (i, 0))],
-        out_specs=out_spec,
+        in_specs=[spec, pl.BlockSpec(memory_space=pltpu.HBM)],
+        out_specs=spec,
         out_shape=jax.ShapeDtypeStruct((reps, width), F32),
-        compiler_params=pltpu.CompilerParams(vmem_limit_bytes=52 << 20),
+        scratch_shapes=[
+            pltpu.VMEM((rows, columns), BF16),
+            pltpu.SemaphoreType.DMA((chunks,)),
+        ],
+        compiler_params=pltpu.CompilerParams(vmem_limit_bytes=24 << 20),
         cost_estimate=pl.CostEstimate(
             flops=2 * reps * rows * columns,
             bytes_accessed=2 * rows * columns,
@@ -148,29 +157,11 @@
 
 
 def primary(left, coupling):
-    reps, columns = left.shape[0], coupling.shape[1]
-    return call(
-        primary_kernel,
-        "primary",
-        left,
-        coupling,
-        pl.BlockSpec((reps, TILE), lambda i: (0, i)),
-        pl.BlockSpec((reps, columns), lambda i: (0, 0)),
-        columns,
-    )
+    return call(primary_kernel, "primary", left, coupling, coupling.shape[1], 16)
 
 
 def shadow(left, coupling):
-    reps, columns = left.shape
-    return call(
-        shadow_kernel,
-        "shadow",
-        left,
-        coupling,
-        pl.BlockSpec((reps, columns), lambda i: (0, 0)),
-        pl.BlockSpec((reps, TILE), lambda i: (0, i)),
-        coupling.shape[0],
-    )
+    return call(shadow_kernel, "shadow", left, coupling, coupling.shape[0], 8)
 
 
 def move(value, pairs):
@@ -194,15 +185,6 @@
     low = jnp.where(flag, mine, other)
     high = jnp.where(flag, other, mine)
     return jnp.concatenate([low, high], axis=1)
-
-
-SENDS_LOW = [0] * 128
-for source, destination in TO_ROWS:
-    SENDS_LOW[source] = int(split(destination)[3] % 2 == 0)
-
-
-def z_even_source(row, col):
-    return jnp.array(SENDS_LOW, jnp.int32)[row * 16 + col] == 1
 
 
 def total(value):
@@ -216,22 +198,26 @@
     z_even = (col & 2) == 0
     low_half = jnp.where(first, (x ^ (x >> 1)) & 1, yh) == 0
 
+    coupling = pltpu.with_memory_space_constraint(coupling, pltpu.HBM)
     g, gs = target, shadow_target
     slope = 1.0 - amplitude * amplitude
     keep = 1.0 - SELF_GAIN * slope
 
     def spread(half):
         mine = put(z_even, half, move(half, Z_PAIR))
-        return mine, put(first, mine, move(mine, CORE))
-
-    half = pick(z_even_source(row, col), (slope * g).astype(BF16))[0]
-    half = move(half, TO_ROWS)
+        return put(first, mine, move(mine, CORE))
+
+    half = pick(low_half, (slope * g).astype(BF16))[0]
+    half = move(half, HALF_TO_ROWS)
     shadow_partial = shadow(gs.astype(BF16), coupling)
-    half, shadow_partial = lax.optimization_barrier((half, shadow_partial))
 
     tops = jnp.stack([jnp.max(jnp.abs(g), axis=1), jnp.max(jnp.abs(gs), axis=1)])
     stats = jnp.concatenate([tops, jnp.stack([total(gs * g), total(gs * (keep * g))])])
     for pairs in SMALL_COL:
+        if pairs is SMALL_COL[2]:
+            stats, half, shadow_partial = lax.optimization_barrier(
+                (stats, half, shadow_partial)
+            )
         other = move(stats, pairs)
         stats = jnp.concatenate(
             [jnp.maximum(stats[:2], other[:2]), stats[2:] + other[2:]]
@@ -244,13 +230,11 @@
     alpha = jnp.where(jnp.isnan(alpha), 1.4, alpha)
     alpha_c = alpha[:, None]
 
-    def shadow_sum(partial, scale):
+    def core_sum(partial, scale):
         mine, other = pick(first, partial)
-        mine = mine * scale + move((other * scale).astype(WIRE), CORE).astype(F32)
-        rows = chip_sum(mine, COL_STEPS).astype(WIRE)
-        return rows, move(rows, TO_COLS)
-
-    _, left = spread(half)
+        return mine * scale + move((other * scale).astype(WIRE), CORE).astype(F32)
+
+    left = spread(half)
     primary_partial = primary(left, coupling)
     scale = FIRST_SCALE / top
     mine, other = pick(low_half, primary_partial * scale)
@@ -267,27 +251,24 @@
     _, u_half = first_step(keep_half, g_half, mine)
     u_half = (slope_half * u_half).astype(BF16)
     u_half = move(u_half, HALF_TO_ROWS)
+    scale = FIRST_SCALE / shadow_top
+    columns = chip_sum(core_sum(shadow_partial, scale), COL_STEPS)
+    columns = move(columns.astype(WIRE), TO_COLS)
+    q1 = keep * gs - (COUPLE_GAIN / scale) * slope * columns.astype(F32)
+    us = gs - alpha_c * q1
+
+    left = spread(u_half)
+    primary_partial = primary(left, coupling)
+    us_sent, mine, primary_partial = lax.optimization_barrier(
+        (us.astype(BF16), mine, primary_partial)
+    )
+    shadow_partial = shadow(us_sent, coupling)
+    scale = SECOND_SCALE / top
+    second = chip_sum(primary_partial * scale, ROW_STEPS) * (COUPLE_GAIN / scale)
     product = put(low_half, mine, move(mine, ROW_STEPS[0]))
     p1, u = first_step(keep, g, product)
-
-    scale = FIRST_SCALE / shadow_top
-    _, columns = shadow_sum(shadow_partial, scale)
-    q1 = keep * gs - (COUPLE_GAIN / scale) * slope * columns.astype(F32)
-    us = gs - alpha_c * q1
-
-    shadow_partial = shadow(us.astype(BF16), coupling)
-    u_rows, left = spread(u_half)
-    primary_partial = primary(left, coupling)
-    scale = SECOND_SCALE / shadow_top
-    rows, columns = shadow_sum(shadow_partial, scale)
-    last = total(u_rows.astype(F32) * rows.astype(F32)) / scale[:, 0]
-    q2 = keep * us - (COUPLE_GAIN / scale) * slope * columns.astype(F32)
-    scale = SECOND_SCALE / top
-    product = chip_sum(primary_partial * scale, ROW_STEPS)
-    p2 = keep * u - (COUPLE_GAIN / scale) * product
-
-    for pairs in SMALL_ROW:
-        last = last + move(last, pairs)
+    p2 = keep * u - second
+
     dots = jnp.stack(
         [
             total(gs * p1),
@@ -295,13 +276,20 @@
             total(us * u),
             total(us * p1),
             total(q1 * u),
-            total(us * (keep * u)),
+            total(us * p2),
         ]
     )
-    for pairs in SMALL_COL:
+    for pairs in SMALL_COL[:2]:
         dots = dots + move(dots, pairs)
-    curve, us_g, us_u, us_p1, q1_u, us_kept = (dots[i] for i in range(6))
-    us_p2 = us_kept - COUPLE_GAIN * last
+    scale = SECOND_SCALE / shadow_top
+    held = chip_sum(core_sum(shadow_partial, scale), COL_STEPS[:2]).astype(WIRE)
+    held, dots = lax.optimization_barrier((held, dots))
+    columns = move(chip_sum(held, COL_STEPS[2:]).astype(WIRE), TO_COLS)
+    for pairs in SMALL_COL[2:]:
+        dots = dots + move(dots, pairs)
+    curve, us_g, us_u, us_p1, q1_u, us_p2 = (dots[i] for i in range(6))
+    q2 = keep * us - (COUPLE_GAIN / scale) * slope * columns.astype(F32)
+
     gs_u = align - alpha * curve
     step = align / curve
     kappa = step / alpha

time: 162 us -> 153 us (0.944)
  Pallas kernels: 40.4 us -> 27.9 us
  waiting for transfers between devices: 62.2 us -> 74.2 us
  other arithmetic: 19.5 us -> 11.5 us
  starting transfers between devices: 35.1 us -> 38.2 us
  local copies, waits for them, and re-layouts: 2 us -> 0.05 us
    pallas_call x4, Pallas kernels: 40.4 us -> 27.9 us  [call(): pl.pallas_call(kernel, name=name, in_specs=[spec, pl.BlockSpec(memory_spa...]
    ppermute x35 -> x31, waiting for transfers between devices: 62.2 us -> 74.2 us  [move(): return lax.ppermute(value, AXES, pairs)]
    ppermute x35 -> x31, starting transfers between devices: 35.1 us -> 38.2 us  [move(): return lax.ppermute(value, AXES, pairs)]
    convert_element_type x11 -> x10, other arithmetic: 3.29 us -> 0.99 us  [chip_sum(): held = value.astype(WIRE)]
    reduce_sum x3 -> x2, other arithmetic: 4.34 us -> 3.55 us  [total(): return jnp.sum(value, axis=1)]
  transfers between devices with their start and end apart: 35 -> 31, of which waited for: 20 -> 20; matrix products, arithmetic and copies ran while one was open for 10% -> 4% of each run, Pallas kernels for 18% -> 18%
where the time goes in v3:
time: 153 us
  waiting for transfers between devices  74.2 us (48%)
  starting transfers between devices  38.2 us (25%)
  Pallas kernels  27.9 us (18%)
  other arithmetic  11.5 us (8%)
    ppermute x31, waiting for transfers between devices, move(): return lax.ppermute(value, AXES, pairs)  74.2 us
    ppermute x31, starting transfers between devices, move(): return lax.ppermute(value, AXES, pairs)  38.2 us
    pallas_call x4, Pallas kernels, call(): pl.pallas_call(kernel, name=name, in_specs=[spec, pl.BlockSpec(memory_spa...  27.9 us
    reduce_sum x2, other arithmetic, total(): return jnp.sum(value, axis=1)  3.55 us
  transfers between devices with their start and end apart: 31, of which 20 were waited for; matrix products, arithmetic and copies ran while one was open for 4% of the time, Pallas kernels for 18%

profile of v3, /device:TPU:0, one launch (start us, length us, event | category | flops | bytes accessed | tf_op | source)
XLA Modules:
  0.0 152.8 jit_solution(13432539893183139151)
XLA Ops:
  0.6 2.7 %multiply_reduce_fusion.7 = (f32[64]{0:T(128)S(1)}, f32[64]{0:T(128)S(1)}, f32[64]{0:T(128)S(1)}, f32[64]{0:T(128)S(1)}, bf16[64,2048]{1,0:T(8,128)(2,1)S(1)}, /...) fusion(f32[64,2048]{1,0:T(8,128)} %param.7, f32[64,2048]{1,0:T(8,128)} %param.6, ...), kind=kLoop, calls=%fused_computation.34 | loop fusion | flops 2096896 | bytes 3146752 | tf_op jit(solution)/shard_map/reduce_sum | solution.py:191
  3.4 0.1 collective-permute-start
  3.5 4.0 %collective-permute-start.2 = (bf16[64,1024]{1,0:T(8,128)(2,1)S(1)}, bf16[64,1024]{1,0:T(8,128)(2,1)S(1)}, u32[]{:S(2)}, u32[]{:S(2)}) collective-permute-start(bf16[64,1024]{1,0:T(8,128)(2,1)S(1)} %slice_select_fusion.2), channel_id=1, source_target_pairs={{112,0},{65,1},{48,2},{113,3},{0,4},{33,5},{64,6},{17,7},{96,8},{9... | collective-permute-start | bytes 393224 | tf_op jit(solution)/shard_map/ppermute | solution.py:168
  7.6 0.7 collective-permute-start.1
  8.3 7.7 %shadow.2 = f32[64,4096]{1,0:T(8,128)S(1)} custom-call(bf16[64,2048]{1,0:T(8,128)(2,1)S(1)} %get-tuple-element.45.left_ref, bf16[4096,2048]{1,0:T(8,128)(2,1)} %coupling_ref.7), custom_call_target="tpu_custom_call" | custom-call | flops 1073741824 | bytes 16777216 | tf_op jit(solution)/shard_map/shadow/pallas_call | solution.py:140
  16.0 4.5 %collective-permute-start.3 = (f32[4,64]{1,0:T(4,128)S(1)}, f32[4,64]{1,0:T(4,128)S(1)}, u32[]{:S(2)}, u32[]{:S(2)}) collective-permute-start(f32[4,64]{1,0:T(4,128)S(1)} %pad_maximum_fusion.7), channel_id=1, source_target_pairs={{2,0},{3,1},{0,2},{1,3},{6,4},{7,5},{4,6},{5,7},{10,8},{11,9},{8,1... | collective-permute-start | bytes 3080 | tf_op jit(solution)/shard_map/ppermute | solution.py:168
  20.5 1.6 %collective-permute-done.3 = f32[4,64]{1,0:T(4,128)S(1)} collective-permute-done((f32[4,64]{1,0:T(4,128)S(1)}, f32[4,64]{1,0:T(4,128)S(1)}, u32[]{:S(2)}, u32[]{:S(2)}) %collective-permute-start.3) | collective-permute-done | bytes 1056 | tf_op jit(solution)/shard_map/ppermute | solution.py:168
  22.1 1.2 collective-permute-start.4
  23.3 1.0 collective-permute-start.10
  24.3 2.7 %collective-permute-done.4 = f32[4,64]{1,0:T(4,128)S(1)} collective-permute-done((f32[4,64]{1,0:T(4,128)S(1)}, f32[4,64]{1,0:T(4,128)S(1)}, u32[]{:S(2)}, u32[]{:S(2)}) %collective-permute-start.4) | collective-permute-done | bytes 1056 | tf_op jit(solution)/shard_map/ppermute | solution.py:168
  27.0 1.3 collective-permute-done.10
  28.4 0.1 collective-permute-start.11
  28.5 0.1 multiply_convert_fusion.2
  28.6 0.6 collective-permute-start.5
  29.2 0.8 collective-permute-done.11
  30.0 0.1 broadcast_select_fusion.3
  30.1 6.2 %primary.2 = f32[64,2048]{1,0:T(8,128)S(1)} custom-call(bf16[64,4096]{1,0:T(8,128)(2,1)S(1)} %pad_maximum_fusion.left_ref, bf16[4096,2048]{1,0:T(8,128)(2,1)} %coupling_ref.7), custom_call_target="tpu_custom_call" | custom-call | flops 1073741824 | bytes 16777216 | tf_op jit(solution)/shard_map/primary/pallas_call | solution.py:140
  36.4 0.1 broadcast_multiply_fusion
  36.5 2.3 %collective-permute-start.12 = (f16[64,1024]{1,0:T(8,128)(2,1)S(1)}, f16[64,1024]{1,0:T(8,128)(2,1)S(1)}, u32[]{:S(2)}, u32[]{:S(2)}) collective-permute-start(f16[64,1024]{1,0:T(8,128)(2,1)S(1)} %select_convert_fusion), channel_id=1, source_target_pairs={{32,0},{17,1},{34,2},{19,3},{36,4},{21,5},{38,6},{23,7},{40,8},{25... | collective-permute-start | bytes 393224 | tf_op jit(solution)/shard_map/ppermute | solution.py:168
  38.8 0.2 add_convert_fusion.9
  39.0 0.6 collective-permute-start.6
  39.6 2.2 %collective-permute-done.12 = f16[64,1024]{1,0:T(8,128)(2,1)S(1)} collective-permute-done((f16[64,1024]{1,0:T(8,128)(2,1)S(1)}, f16[64,1024]{1,0:T(8,128)(2,1)S(1)}, u32[]{:S(2)}, u32[]{:S(2)}) %collective-permute-start.12) | collective-permute-done | bytes 131104 | tf_op jit(solution)/shard_map/ppermute | solution.py:168
  41.8 2.4 %collective-permute-start.13 = (f16[64,1024]{1,0:T(8,128)(2,1)S(1)}, f16[64,1024]{1,0:T(8,128)(2,1)S(1)}, u32[]{:S(2)}, u32[]{:S(2)}) collective-permute-start(f16[64,1024]{1,0:T(8,128)(2,1)S(1)} %add_convert_fusion.12), channel_id=1, source_target_pairs={{96,0},{33,1},{98,2},{35,3},{100,4},{37,5},{102,6},{39,7},{104,8},... | collective-permute-start | bytes 393224 | tf_op jit(solution)/shard_map/ppermute | solution.py:168
  44.2 3.9 %collective-permute-done.13 = f16[64,1024]{1,0:T(8,128)(2,1)S(1)} collective-permute-done((f16[64,1024]{1,0:T(8,128)(2,1)S(1)}, f16[64,1024]{1,0:T(8,128)(2,1)S(1)}, u32[]{:S(2)}, u32[]{:S(2)}) %collective-permute-start.13) | collective-permute-done | bytes 131104 | tf_op jit(solution)/shard_map/ppermute | solution.py:168
  48.1 3.0 %collective-permute-start.14 = (f16[64,1024]{1,0:T(8,128)(2,1)S(1)}, f16[64,1024]{1,0:T(8,128)(2,1)S(1)}, u32[]{:S(2)}, u32[]{:S(2)}) collective-permute-start(f16[64,1024]{1,0:T(8,128)(2,1)S(1)} %add_convert_fusion.11), channel_id=1, source_target_pairs={{16,0},{97,1},{18,2},{99,3},{20,4},{101,5},{22,6},{103,7},{24,8},{... | collective-permute-start | bytes 393224 | tf_op jit(solution)/shard_map/ppermute | solution.py:168
  51.2 0.7 collective-permute-start.7
  51.9 2.8 %collective-permute-done.14 = f16[64,1024]{1,0:T(8,128)(2,1)S(1)} collective-permute-done((f16[64,1024]{1,0:T(8,128)(2,1)S(1)}, f16[64,1024]{1,0:T(8,128)(2,1)S(1)}, u32[]{:S(2)}, u32[]{:S(2)}) %collective-permute-start.14) | collective-permute-done | bytes 131104 | tf_op jit(solution)/shard_map/ppermute | solution.py:168
  54.7 1.2 fusion.6
  55.9 2.8 %collective-permute-start.15 = (bf16[64,1024]{1,0:T(8,128)(2,1)S(1)}, bf16[64,1024]{1,0:T(8,128)(2,1)S(1)}, u32[]{:S(2)}, u32[]{:S(2)}) collective-permute-start(bf16[64,1024]{1,0:T(8,128)(2,1)S(1)} %get-tuple-element.34), channel_id=1, source_target_pairs={{112,0},{65,1},{48,2},{113,3},{0,4},{33,5},{64,6},{17,7},{96,8},{9... | collective-permute-start | bytes 393224 | tf_op jit(solution)/shard_map/ppermute | solution.py:168
  58.7 7.4 %collective-permute-done.15 = bf16[64,1024]{1,0:T(8,128)(2,1)S(1)} collective-permute-done((bf16[64,1024]{1,0:T(8,128)(2,1)S(1)}, bf16[64,1024]{1,0:T(8,128)(2,1)S(1)}, u32[]{:S(2)}, u32[]{:S(2)}) %collective-permute-start.15) | collective-permute-done | bytes 131104 | tf_op jit(solution)/shard_map/ppermute | solution.py:168
  66.1 1.6 %collective-permute-start.8 = (f16[64,2048]{1,0:T(8,128)(2,1)S(1)}, f16[64,2048]{1,0:T(8,128)(2,1)S(1)}, u32[]{:S(2)}, u32[]{:S(2)}) collective-permute-start(f16[64,2048]{1,0:T(8,128)(2,1)S(1)} %add_convert_fusion.7), channel_id=1, source_target_pairs={{6,0},{9,1},{4,2},{11,3},{2,4},{13,5},{0,6},{15,7},{14,8},{1,9},{1... | collective-permute-start | bytes 786440 | tf_op jit(solution)/shard_map/ppermute | solution.py:168
  67.7 3.3 %collective-permute-done.16 = bf16[64,1024]{1,0:T(8,128)(2,1)S(1)} collective-permute-done((bf16[64,1024]{1,0:T(8,128)(2,1)S(1)}, bf16[64,1024]{1,0:T(8,128)(2,1)S(1)}, u32[]{:S(2)}, u32[]{:S(2)}) %collective-permute-start.16) | collective-permute-done | bytes 131104 | tf_op jit(solution)/shard_map/ppermute | solution.py:168
  71.2 2.6 %collective-permute-done.8 = f16[64,2048]{1,0:T(8,128)(2,1)S(1)} collective-permute-done((f16[64,2048]{1,0:T(8,128)(2,1)S(1)}, f16[64,2048]{1,0:T(8,128)(2,1)S(1)}, u32[]{:S(2)}, u32[]{:S(2)}) %collective-permute-start.8) | collective-permute-done | bytes 262176 | tf_op jit(solution)/shard_map/ppermute | solution.py:168
  73.9 0.8 collective-permute-start.9
  74.7 0.1 broadcast_select_fusion.1
  74.9 6.2 %primary.3 = f32[64,2048]{1,0:T(8,128)S(1)} custom-call(bf16[64,4096]{1,0:T(8,128)(2,1)S(1)} %pad_maximum_fusion.1.left_ref, bf16[4096,2048]{1,0:T(8,128)(2,1)} %coupling_ref.7), custom_call_target="tpu_custom_call" | custom-call | flops 1073741824 | bytes 16777216 | tf_op jit(solution)/shard_map/primary/pallas_call | solution.py:140
  81.1 3.7 %collective-permute-done.9 = f16[64,2048]{1,0:T(8,128)(2,1)S(1)} collective-permute-done((f16[64,2048]{1,0:T(8,128)(2,1)S(1)}, f16[64,2048]{1,0:T(8,128)(2,1)S(1)}, u32[]{:S(2)}, u32[]{:S(2)}) %collective-permute-start.9) | collective-permute-done | bytes 262176 | tf_op jit(solution)/shard_map/ppermute | solution.py:168
  84.8 0.2 fusion.15
  85.1 0.1 multiply_convert_fusion
  85.2 0.7 collective-permute-start.22
  85.9 7.7 %shadow.3 = f32[64,4096]{1,0:T(8,128)S(1)} custom-call(bf16[64,2048]{1,0:T(8,128)(2,1)S(1)} %get-tuple-element.15.left_ref, bf16[4096,2048]{1,0:T(8,128)(2,1)} %coupling_ref.7), custom_call_target="tpu_custom_call" | custom-call | flops 1073741824 | bytes 16777216 | tf_op jit(solution)/shard_map/shadow/pallas_call | solution.py:140
  93.6 1.5 collective-permute-start.21
  95.1 0.1 multiply_convert_fusion.1
  95.3 3.4 %collective-permute-done.21 = f16[64,1024]{1,0:T(8,128)(2,1)S(1)} collective-permute-done((f16[64,1024]{1,0:T(8,128)(2,1)S(1)}, f16[64,1024]{1,0:T(8,128)(2,1)S(1)}, u32[]{:S(2)}, u32[]{:S(2)}) %collective-permute-start.21) | collective-permute-done | bytes 131104 | tf_op jit(solution)/shard_map/ppermute | solution.py:168
  98.8 0.1 add_convert_fusion.2
  98.9 0.4 collective-permute-start.23
  99.3 0.2 add_convert_fusion.5
  99.5 1.8 %collective-permute-start.19 = (f16[64,2048]{1,0:T(8,128)(2,1)S(1)}, f16[64,2048]{1,0:T(8,128)(2,1)S(1)}, u32[]{:S(2)}, u32[]{:S(2)}) collective-permute-start(f16[64,2048]{1,0:T(8,128)(2,1)S(1)} %add_convert_fusion.5), channel_id=1, source_target_pairs={{8,0},{3,1},{10,2},{1,3},{12,4},{7,5},{14,6},{5,7},{0,8},{11,9},{2... | collective-permute-start | bytes 786440 | tf_op jit(solution)/shard_map/ppermute | solution.py:168
  101.3 6.4 %collective-permute-done.23 = f16[64,2048]{1,0:T(8,128)(2,1)S(1)} collective-permute-done((f16[64,2048]{1,0:T(8,128)(2,1)S(1)}, f16[64,2048]{1,0:T(8,128)(2,1)S(1)}, u32[]{:S(2)}, u32[]{:S(2)}) %collective-permute-start.23) | collective-permute-done | bytes 262176 | tf_op jit(solution)/shard_map/ppermute | solution.py:168
  107.8 1.6 %collective-permute-start.24 = (f16[64,2048]{1,0:T(8,128)(2,1)S(1)}, f16[64,2048]{1,0:T(8,128)(2,1)S(1)}, u32[]{:S(2)}, u32[]{:S(2)}) collective-permute-start(f16[64,2048]{1,0:T(8,128)(2,1)S(1)} %add_convert_fusion.1), channel_id=1, source_target_pairs={{16,0},{97,1},{18,2},{99,3},{20,4},{101,5},{22,6},{103,7},{24,8},{... | collective-permute-start | bytes 786440 | tf_op jit(solution)/shard_map/ppermute | solution.py:168
  109.5 0.1 collective-permute-start.20
  109.6 6.2 %collective-permute-done.24 = f16[64,2048]{1,0:T(8,128)(2,1)S(1)} collective-permute-done((f16[64,2048]{1,0:T(8,128)(2,1)S(1)}, f16[64,2048]{1,0:T(8,128)(2,1)S(1)}, u32[]{:S(2)}, u32[]{:S(2)}) %collective-permute-start.24) | collective-permute-done | bytes 262176 | tf_op jit(solution)/shard_map/ppermute | solution.py:168
  115.8 0.8 multiply_reduce_fusion
  116.7 1.2 collective-permute-done.25
  117.9 1.0 add_convert_fusion.3
  118.9 2.6 %collective-permute-done.26 = f32[6,64]{1,0:T(8,128)S(1)} collective-permute-done((f32[6,64]{1,0:T(8,128)S(1)}, f32[6,64]{1,0:T(8,128)S(1)}, u32[]{:S(2)}, u32[]{:S(2)}) %collective-permute-start.26) | collective-permute-done | bytes 1568 | tf_op jit(solution)/shard_map/ppermute | solution.py:168
  121.5 0.7 collective-permute-start.27
  122.2 2.9 %collective-permute-done.27 = f32[6,64]{1,0:T(8,128)S(1)} collective-permute-done((f32[6,64]{1,0:T(8,128)S(1)}, f32[6,64]{1,0:T(8,128)S(1)}, u32[]{:S(2)}, u32[]{:S(2)}) %collective-permute-start.27) | collective-permute-done | bytes 1568 | tf_op jit(solution)/shard_map/ppermute | solution.py:168
  125.1 4.7 %collective-permute-start.28 = (f32[6,64]{1,0:T(8,128)S(1)}, f32[6,64]{1,0:T(8,128)S(1)}, u32[]{:S(2)}, u32[]{:S(2)}) collective-permute-start(f32[6,64]{1,0:T(8,128)S(1)} %add.167), channel_id=1, source_target_pairs={{6,0},{7,1},{4,2},{5,3},{2,4},{3,5},{0,6},{1,7},{14,8},{15,9},{12,... | collective-permute-start | bytes 4616 | tf_op jit(solution)/shard_map/ppermute | solution.py:168
  129.9 1.6 %collective-permute-done.28 = f32[6,64]{1,0:T(8,128)S(1)} collective-permute-done((f32[6,64]{1,0:T(8,128)S(1)}, f32[6,64]{1,0:T(8,128)S(1)}, u32[]{:S(2)}, u32[]{:S(2)}) %collective-permute-start.28) | collective-permute-done | bytes 1568 | tf_op jit(solution)/shard_map/ppermute | solution.py:168
  131.5 8.8 %collective-permute-done.29 = f16[64,2048]{1,0:T(8,128)(2,1)S(1)} collective-permute-done((f16[64,2048]{1,0:T(8,128)(2,1)S(1)}, f16[64,2048]{1,0:T(8,128)(2,1)S(1)}, u32[]{:S(2)}, u32[]{:S(2)}) %collective-permute-start.29) | collective-permute-done | bytes 262176 | tf_op jit(solution)/shard_map/ppermute | solution.py:168
  140.4 1.7 %multiply_subtract_fusion.1 = (f32[64,2048]{1,0:T(8,128)}, f32[64,2048]{1,0:T(8,128)}) fusion(f32[64,2048]{1,0:T(8,128)S(1)} %copy-done.1, f16[64,2048]{1,0:T(8,128)(2,1)S(1)} %collective-permute-done.24, f16[64,2048]{1,0:T(8,128)(2,1)S(1)} %add_convert_fusion.1, f32[64]{0:T(128)S(1)} %get-tuple-element.33, f32[64]{0:T(128)S(1)} %get-tuple-element.31, ...), kind=kLoop, calls=%fused_computation.4 | loop fusion | flops 3932160 | bytes 2885376 | tf_op jit(solution)/shard_map/sub | solution.py:315
  142.1 9.0 %collective-permute-done.30 = f16[64,2048]{1,0:T(8,128)(2,1)S(1)} collective-permute-done((f16[64,2048]{1,0:T(8,128)(2,1)S(1)}, f16[64,2048]{1,0:T(8,128)(2,1)S(1)}, u32[]{:S(2)}, u32[]{:S(2)}) %collective-permute-start.30) | collective-permute-done | bytes 262176 | tf_op jit(solution)/shard_map/ppermute | solution.py:168
  151.1 1.8 %multiply_subtract_fusion = (f32[64,2048]{1,0:T(8,128)}, f32[64,2048]{1,0:T(8,128)}) fusion(f16[64,2048]{1,0:T(8,128)(2,1)S(1)} %collective-permute-done.30, f32[64,2048]{1,0:T(8,128)S(1)} %get-tuple-element.37, f32[64,2048]{1,0:T(8,128)S(1)} %copy-done.2, f16[64,2048]{1,0:T(8,128)(2,1)S(1)} %collective-permute-done.9, f32[64]{0:T(128)S(1)} %get-tuple-element.67, ...), kind=kLoop, calls=%fused_computation.2 | loop fusion | flops 3538944 | bytes 3147264 | tf_op jit(solution)/shard_map/sub | solution.py:316
  (58 shorter events, 1.4 us)
Async XLA Ops:
  3.4 4.2 %collective-permute-start = (f32[4,64]{1,0:T(4,128)S(1)}, f32[4,64]{1,0:T(4,128)S(1)}, u32[]{:S(2)}, u32[]{:S(2)}) collective-permute-start(f32[4,64]{1,0:T(4,128)S(1)} %pad_maximum_fusion.5), channel_id=1, source_target_pairs={{1,0},{0,1},{3,2},{2,3},{5,4},{4,5},{7,6},{6,7},{9,8},{8,9},{11,10... | collective-permute-start | bytes 3080 | tf_op jit(solution)/shard_map/ppermute | solution.py:168
  3.5 12.5 %collective-permute-start.2 = (bf16[64,1024]{1,0:T(8,128)(2,1)S(1)}, bf16[64,1024]{1,0:T(8,128)(2,1)S(1)}, u32[]{:S(2)}, u32[]{:S(2)}) collective-permute-start(bf16[64,1024]{1,0:T(8,128)(2,1)S(1)} %slice_select_fusion.2), channel_id=1, source_target_pairs={{112,0},{65,1},{48,2},{113,3},{0,4},{33,5},{64,6},{17,7},{96,8},{9... | collective-permute-start | bytes 393224 | tf_op jit(solution)/shard_map/ppermute | solution.py:168
  7.6 8.4 %collective-permute-start.1 = (f32[4,64]{1,0:T(4,128)S(1)}, f32[4,64]{1,0:T(4,128)S(1)}, u32[]{:S(2)}, u32[]{:S(2)}) collective-permute-start(f32[4,64]{1,0:T(4,128)S(1)} %pad_maximum_fusion.6), channel_id=1, source_target_pairs={{8,0},{9,1},{10,2},{11,3},{12,4},{13,5},{14,6},{15,7},{0,8},{1,9},... | collective-permute-start | bytes 3080 | tf_op jit(solution)/shard_map/ppermute | solution.py:168
  16.0 38.7 %copy-start.1 = (f32[64,2048]{1,0:T(8,128)S(1)}, f32[64,2048]{1,0:T(8,128)}, u32[]{:S(2)}) copy-start(f32[64,2048]{1,0:T(8,128)} %param.6) | copy-start | bytes 1572868
  16.0 6.0 %collective-permute-start.3 = (f32[4,64]{1,0:T(4,128)S(1)}, f32[4,64]{1,0:T(4,128)S(1)}, u32[]{:S(2)}, u32[]{:S(2)}) collective-permute-start(f32[4,64]{1,0:T(4,128)S(1)} %pad_maximum_fusion.7), channel_id=1, source_target_pairs={{2,0},{3,1},{0,2},{1,3},{6,4},{7,5},{4,6},{5,7},{10,8},{11,9},{8,1... | collective-permute-start | bytes 3080 | tf_op jit(solution)/shard_map/ppermute | solution.py:168
  22.1 4.9 %collective-permute-start.4 = (f32[4,64]{1,0:T(4,128)S(1)}, f32[4,64]{1,0:T(4,128)S(1)}, u32[]{:S(2)}, u32[]{:S(2)}) collective-permute-start(f32[4,64]{1,0:T(4,128)S(1)} %pad_maximum_fusion.8), channel_id=1, source_target_pairs={{6,0},{7,1},{4,2},{5,3},{2,4},{3,5},{0,6},{1,7},{14,8},{15,9},{12,... | collective-permute-start | bytes 3080 | tf_op jit(solution)/shard_map/ppermute | solution.py:168
  23.3 5.0 %collective-permute-start.10 = (bf16[64,1024]{1,0:T(8,128)(2,1)S(1)}, bf16[64,1024]{1,0:T(8,128)(2,1)S(1)}, u32[]{:S(2)}, u32[]{:S(2)}) collective-permute-start(bf16[64,1024]{1,0:T(8,128)(2,1)S(1)} %collective-permute-done.2), channel_id=1, source_target_pairs={{2,0},{3,1},{0,2},{1,3},{6,4},{7,5},{4,6},{5,7},{10,8},{11,9},{8,1... | collective-permute-start | bytes 393224 | tf_op jit(solution)/shard_map/ppermute | solution.py:168
  28.4 1.6 %collective-permute-start.11 = (bf16[64,2048]{1,0:T(8,128)(2,1)S(1)}, bf16[64,2048]{1,0:T(8,128)(2,1)S(1)}, u32[]{:S(2)}, u32[]{:S(2)}) collective-permute-start(bf16[64,2048]{1,0:T(8,128)(2,1)S(1)} %pad_maximum_fusion.2), channel_id=1, source_target_pairs={{1,0},{0,1},{3,2},{2,3},{5,4},{4,5},{7,6},{6,7},{9,8},{8,9},{11,10... | collective-permute-start | bytes 786440 | tf_op jit(solution)/shard_map/ppermute | solution.py:168
  28.6 10.3 %collective-permute-start.5 = (f16[64,2048]{1,0:T(8,128)(2,1)S(1)}, f16[64,2048]{1,0:T(8,128)(2,1)S(1)}, u32[]{:S(2)}, u32[]{:S(2)}) collective-permute-start(f16[64,2048]{1,0:T(8,128)(2,1)S(1)} %multiply_convert_fusion.2), channel_id=1, source_target_pairs={{1,0},{0,1},{3,2},{2,3},{5,4},{4,5},{7,6},{6,7},{9,8},{8,9},{11,10... | collective-permute-start | bytes 786440 | tf_op jit(solution)/shard_map/ppermute | solution.py:168
  36.4 48.5 %copy-start = (f32[64,2048]{1,0:T(8,128)S(1)}, f32[64,2048]{1,0:T(8,128)}, u32[]{:S(2)}) copy-start(f32[64,2048]{1,0:T(8,128)} %param.5) | copy-start | bytes 1572868
  36.4 48.4 %copy-start.2 = (f32[64,2048]{1,0:T(8,128)S(1)}, f32[64,2048]{1,0:T(8,128)}, u32[]{:S(2)}) copy-start(f32[64,2048]{1,0:T(8,128)} %param.7) | copy-start | bytes 1572868
  36.5 5.2 %collective-permute-start.12 = (f16[64,1024]{1,0:T(8,128)(2,1)S(1)}, f16[64,1024]{1,0:T(8,128)(2,1)S(1)}, u32[]{:S(2)}, u32[]{:S(2)}) collective-permute-start(f16[64,1024]{1,0:T(8,128)(2,1)S(1)} %select_convert_fusion), channel_id=1, source_target_pairs={{32,0},{17,1},{34,2},{19,3},{36,4},{21,5},{38,6},{23,7},{40,8},{25... | collective-permute-start | bytes 393224 | tf_op jit(solution)/shard_map/ppermute | solution.py:168
  39.0 12.1 %collective-permute-start.6 = (f16[64,2048]{1,0:T(8,128)(2,1)S(1)}, f16[64,2048]{1,0:T(8,128)(2,1)S(1)}, u32[]{:S(2)}, u32[]{:S(2)}) collective-permute-start(f16[64,2048]{1,0:T(8,128)(2,1)S(1)} %add_convert_fusion.9), channel_id=1, source_target_pairs={{8,0},{3,1},{10,2},{1,3},{12,4},{7,5},{14,6},{5,7},{0,8},{11,9},{2... | collective-permute-start | bytes 786440 | tf_op jit(solution)/shard_map/ppermute | solution.py:168
  41.8 6.3 %collective-permute-start.13 = (f16[64,1024]{1,0:T(8,128)(2,1)S(1)}, f16[64,1024]{1,0:T(8,128)(2,1)S(1)}, u32[]{:S(2)}, u32[]{:S(2)}) collective-permute-start(f16[64,1024]{1,0:T(8,128)(2,1)S(1)} %add_convert_fusion.12), channel_id=1, source_target_pairs={{96,0},{33,1},{98,2},{35,3},{100,4},{37,5},{102,6},{39,7},{104,8},... | collective-permute-start | bytes 393224 | tf_op jit(solution)/shard_map/ppermute | solution.py:168
  48.1 6.6 %collective-permute-start.14 = (f16[64,1024]{1,0:T(8,128)(2,1)S(1)}, f16[64,1024]{1,0:T(8,128)(2,1)S(1)}, u32[]{:S(2)}, u32[]{:S(2)}) collective-permute-start(f16[64,1024]{1,0:T(8,128)(2,1)S(1)} %add_convert_fusion.11), channel_id=1, source_target_pairs={{16,0},{97,1},{18,2},{99,3},{20,4},{101,5},{22,6},{103,7},{24,8},{... | collective-permute-start | bytes 393224 | tf_op jit(solution)/shard_map/ppermute | solution.py:168
  51.2 14.9 %collective-permute-start.7 = (f16[64,2048]{1,0:T(8,128)(2,1)S(1)}, f16[64,2048]{1,0:T(8,128)(2,1)S(1)}, u32[]{:S(2)}, u32[]{:S(2)}) collective-permute-start(f16[64,2048]{1,0:T(8,128)(2,1)S(1)} %add_convert_fusion.8), channel_id=1, source_target_pairs={{2,0},{7,1},{0,2},{5,3},{6,4},{3,5},{4,6},{1,7},{10,8},{15,9},{8,1... | collective-permute-start | bytes 786440 | tf_op jit(solution)/shard_map/ppermute | solution.py:168
  55.9 10.2 %collective-permute-start.15 = (bf16[64,1024]{1,0:T(8,128)(2,1)S(1)}, bf16[64,1024]{1,0:T(8,128)(2,1)S(1)}, u32[]{:S(2)}, u32[]{:S(2)}) collective-permute-start(bf16[64,1024]{1,0:T(8,128)(2,1)S(1)} %get-tuple-element.34), channel_id=1, source_target_pairs={{112,0},{65,1},{48,2},{113,3},{0,4},{33,5},{64,6},{17,7},{96,8},{9... | collective-permute-start | bytes 393224 | tf_op jit(solution)/shard_map/ppermute | solution.py:168
  66.1 5.0 %collective-permute-start.16 = (bf16[64,1024]{1,0:T(8,128)(2,1)S(1)}, bf16[64,1024]{1,0:T(8,128)(2,1)S(1)}, u32[]{:S(2)}, u32[]{:S(2)}) collective-permute-start(bf16[64,1024]{1,0:T(8,128)(2,1)S(1)} %collective-permute-done.15), channel_id=1, source_target_pairs={{2,0},{3,1},{0,2},{1,3},{6,4},{7,5},{4,6},{5,7},{10,8},{11,9},{8,1... | collective-permute-start | bytes 393224 | tf_op jit(solution)/shard_map/ppermute | solution.py:168
  66.1 7.7 %collective-permute-start.8 = (f16[64,2048]{1,0:T(8,128)(2,1)S(1)}, f16[64,2048]{1,0:T(8,128)(2,1)S(1)}, u32[]{:S(2)}, u32[]{:S(2)}) collective-permute-start(f16[64,2048]{1,0:T(8,128)(2,1)S(1)} %add_convert_fusion.7), channel_id=1, source_target_pairs={{6,0},{9,1},{4,2},{11,3},{2,4},{13,5},{0,6},{15,7},{14,8},{1,9},{1... | collective-permute-start | bytes 786440 | tf_op jit(solution)/shard_map/ppermute | solution.py:168
  71.1 3.7 %collective-permute-start.17 = (bf16[64,2048]{1,0:T(8,128)(2,1)S(1)}, bf16[64,2048]{1,0:T(8,128)(2,1)S(1)}, u32[]{:S(2)}, u32[]{:S(2)}) collective-permute-start(bf16[64,2048]{1,0:T(8,128)(2,1)S(1)} %pad_maximum_fusion.3), channel_id=1, source_target_pairs={{1,0},{0,1},{3,2},{2,3},{5,4},{4,5},{7,6},{6,7},{9,8},{8,9},{11,10... | collective-permute-start | bytes 786440 | tf_op jit(solution)/shard_map/ppermute | solution.py:168
  73.9 10.9 %collective-permute-start.9 = (f16[64,2048]{1,0:T(8,128)(2,1)S(1)}, f16[64,2048]{1,0:T(8,128)(2,1)S(1)}, u32[]{:S(2)}, u32[]{:S(2)}) collective-permute-start(f16[64,2048]{1,0:T(8,128)(2,1)S(1)} %add_convert_fusion.6), channel_id=1, source_target_pairs={{4,0},{5,1},{30,2},{31,3},{34,4},{39,5},{60,6},{57,7},{72,8},{73,9... | collective-permute-start | bytes 786440 | tf_op jit(solution)/shard_map/ppermute | solution.py:168
  85.2 13.6 %collective-permute-start.22 = (f16[64,2048]{1,0:T(8,128)(2,1)S(1)}, f16[64,2048]{1,0:T(8,128)(2,1)S(1)}, u32[]{:S(2)}, u32[]{:S(2)}) collective-permute-start(f16[64,2048]{1,0:T(8,128)(2,1)S(1)} %multiply_convert_fusion), channel_id=1, source_target_pairs={{32,0},{17,1},{34,2},{19,3},{36,4},{21,5},{38,6},{23,7},{40,8},{25... | collective-permute-start | bytes 786440 | tf_op jit(solution)/shard_map/ppermute | solution.py:168
  93.6 5.0 %collective-permute-start.21 = (f16[64,1024]{1,0:T(8,128)(2,1)S(1)}, f16[64,1024]{1,0:T(8,128)(2,1)S(1)}, u32[]{:S(2)}, u32[]{:S(2)}) collective-permute-start(f16[64,1024]{1,0:T(8,128)(2,1)S(1)} %get-tuple-element.16), channel_id=1, source_target_pairs={{32,0},{17,1},{34,2},{19,3},{36,4},{21,5},{38,6},{23,7},{40,8},{25... | collective-permute-start | bytes 393224 | tf_op jit(solution)/shard_map/ppermute | solution.py:168
  95.2 4.1 %collective-permute-start.18 = (f16[64,2048]{1,0:T(8,128)(2,1)S(1)}, f16[64,2048]{1,0:T(8,128)(2,1)S(1)}, u32[]{:S(2)}, u32[]{:S(2)}) collective-permute-start(f16[64,2048]{1,0:T(8,128)(2,1)S(1)} %multiply_convert_fusion.1), channel_id=1, source_target_pairs={{1,0},{0,1},{3,2},{2,3},{5,4},{4,5},{7,6},{6,7},{9,8},{8,9},{11,10... | collective-permute-start | bytes 786440 | tf_op jit(solution)/shard_map/ppermute | solution.py:168
  98.9 8.8 %collective-permute-start.23 = (f16[64,2048]{1,0:T(8,128)(2,1)S(1)}, f16[64,2048]{1,0:T(8,128)(2,1)S(1)}, u32[]{:S(2)}, u32[]{:S(2)}) collective-permute-start(f16[64,2048]{1,0:T(8,128)(2,1)S(1)} %add_convert_fusion.2), channel_id=1, source_target_pairs={{96,0},{33,1},{98,2},{35,3},{100,4},{37,5},{102,6},{39,7},{104,8},... | collective-permute-start | bytes 786440 | tf_op jit(solution)/shard_map/ppermute | solution.py:168
  99.5 9.9 %collective-permute-start.19 = (f16[64,2048]{1,0:T(8,128)(2,1)S(1)}, f16[64,2048]{1,0:T(8,128)(2,1)S(1)}, u32[]{:S(2)}, u32[]{:S(2)}) collective-permute-start(f16[64,2048]{1,0:T(8,128)(2,1)S(1)} %add_convert_fusion.5), channel_id=1, source_target_pairs={{8,0},{3,1},{10,2},{1,3},{12,4},{7,5},{14,6},{5,7},{0,8},{11,9},{2... | collective-permute-start | bytes 786440 | tf_op jit(solution)/shard_map/ppermute | solution.py:168
  107.8 8.0 %collective-permute-start.24 = (f16[64,2048]{1,0:T(8,128)(2,1)S(1)}, f16[64,2048]{1,0:T(8,128)(2,1)S(1)}, u32[]{:S(2)}, u32[]{:S(2)}) collective-permute-start(f16[64,2048]{1,0:T(8,128)(2,1)S(1)} %add_convert_fusion.1), channel_id=1, source_target_pairs={{16,0},{97,1},{18,2},{99,3},{20,4},{101,5},{22,6},{103,7},{24,8},{... | collective-permute-start | bytes 786440 | tf_op jit(solution)/shard_map/ppermute | solution.py:168
  109.5 8.4 %collective-permute-start.20 = (f16[64,2048]{1,0:T(8,128)(2,1)S(1)}, f16[64,2048]{1,0:T(8,128)(2,1)}, u32[]{:S(2)}, u32[]{:S(2)}) collective-permute-start(f16[64,2048]{1,0:T(8,128)(2,1)S(1)} %add_convert_fusion.4), channel_id=1, source_target_pairs={{2,0},{7,1},{0,2},{5,3},{6,4},{3,5},{4,6},{1,7},{10,8},{15,9},{8,1... | collective-permute-start | bytes 786440 | tf_op jit(solution)/shard_map/ppermute | solution.py:168
  116.6 1.2 collective-permute-start.25
  117.9 3.6 %collective-permute-start.26 = (f32[6,64]{1,0:T(8,128)S(1)}, f32[6,64]{1,0:T(8,128)S(1)}, u32[]{:S(2)}, u32[]{:S(2)}) collective-permute-start(f32[6,64]{1,0:T(8,128)S(1)} %add.165), channel_id=1, source_target_pairs={{8,0},{9,1},{10,2},{11,3},{12,4},{13,5},{14,6},{15,7},{0,8},{1,9},... | collective-permute-start | bytes 4616 | tf_op jit(solution)/shard_map/ppermute | solution.py:168
  121.5 3.6 %collective-permute-start.27 = (f32[6,64]{1,0:T(8,128)S(1)}, f32[6,64]{1,0:T(8,128)S(1)}, u32[]{:S(2)}, u32[]{:S(2)}) collective-permute-start(f32[6,64]{1,0:T(8,128)S(1)} %add.166), channel_id=1, source_target_pairs={{2,0},{3,1},{0,2},{1,3},{6,4},{7,5},{4,6},{5,7},{10,8},{11,9},{8,1... | collective-permute-start | bytes 4616 | tf_op jit(solution)/shard_map/ppermute | solution.py:168
  125.1 6.3 %collective-permute-start.28 = (f32[6,64]{1,0:T(8,128)S(1)}, f32[6,64]{1,0:T(8,128)S(1)}, u32[]{:S(2)}, u32[]{:S(2)}) collective-permute-start(f32[6,64]{1,0:T(8,128)S(1)} %add.167), channel_id=1, source_target_pairs={{6,0},{7,1},{4,2},{5,3},{2,4},{3,5},{0,6},{1,7},{14,8},{15,9},{12,... | collective-permute-start | bytes 4616 | tf_op jit(solution)/shard_map/ppermute | solution.py:168
  129.9 10.4 %collective-permute-start.29 = (f16[64,2048]{1,0:T(8,128)(2,1)S(1)}, f16[64,2048]{1,0:T(8,128)(2,1)S(1)}, u32[]{:S(2)}, u32[]{:S(2)}) collective-permute-start(f16[64,2048]{1,0:T(8,128)(2,1)S(1)} %add_convert_fusion.3), channel_id=1, source_target_pairs={{6,0},{9,1},{4,2},{11,3},{2,4},{13,5},{0,6},{15,7},{14,8},{1,9},{1... | collective-permute-start | bytes 786440 | tf_op jit(solution)/shard_map/ppermute | solution.py:168
  140.3 10.8 %collective-permute-start.30 = (f16[64,2048]{1,0:T(8,128)(2,1)S(1)}, f16[64,2048]{1,0:T(8,128)(2,1)S(1)}, u32[]{:S(2)}, u32[]{:S(2)}) collective-permute-start(f16[64,2048]{1,0:T(8,128)(2,1)S(1)} %add_convert_fusion), channel_id=1, source_target_pairs={{4,0},{5,1},{30,2},{31,3},{34,4},{39,5},{60,6},{57,7},{72,8},{73,9... | collective-permute-start | bytes 786440 | tf_op jit(solution)/shard_map/ppermute | solution.py:168

commit v4 on v3

--- a/solution.py
+++ b/solution.py
@@ -168,11 +168,12 @@
     return lax.ppermute(value, AXES, pairs)
 
 
-def chip_sum(value, steps):
-    for pairs in steps:
-        held = value.astype(WIRE)
-        value = held.astype(F32) + move(held, pairs).astype(F32)
-    return value
+def exchange(held, pairs):
+    return (held.astype(F32) + move(held, pairs).astype(F32)).astype(WIRE)
+
+
+def tie(*values):
+    return lax.optimization_barrier(values)
 
 
 def pick(flag, value):
@@ -203,9 +204,12 @@
     slope = 1.0 - amplitude * amplitude
     keep = 1.0 - SELF_GAIN * slope
 
-    def spread(half):
-        mine = put(z_even, half, move(half, Z_PAIR))
-        return put(first, mine, move(mine, CORE))
+    def send_core(partial, scale):
+        mine, other = pick(first, partial * scale)
+        return (mine + move(other.astype(WIRE), CORE).astype(F32)).astype(WIRE)
+
+    def send_half(mine, other):
+        return (mine + move(other.astype(WIRE), ROW_STEPS[0]).astype(F32)).astype(WIRE)
 
     half = pick(low_half, (slope * g).astype(BF16))[0]
     half = move(half, HALF_TO_ROWS)
@@ -215,9 +219,7 @@
     stats = jnp.concatenate([tops, jnp.stack([total(gs * g), total(gs * (keep * g))])])
     for pairs in SMALL_COL:
         if pairs is SMALL_COL[2]:
-            stats, half, shadow_partial = lax.optimization_barrier(
-                (stats, half, shadow_partial)
-            )
+            stats, half, shadow_partial = tie(stats, half, shadow_partial)
         other = move(stats, pairs)
         stats = jnp.concatenate(
             [jnp.maximum(stats[:2], other[:2]), stats[2:] + other[2:]]
@@ -230,16 +232,24 @@
     alpha = jnp.where(jnp.isnan(alpha), 1.4, alpha)
     alpha_c = alpha[:, None]
 
-    def core_sum(partial, scale):
-        mine, other = pick(first, partial)
-        return mine * scale + move((other * scale).astype(WIRE), CORE).astype(F32)
-
-    left = spread(half)
-    primary_partial = primary(left, coupling)
+    block = put(z_even, half, move(half, Z_PAIR))
+    left = put(first, block, move(block, CORE))
+    shadow_held = send_core(shadow_partial, FIRST_SCALE / shadow_top)
+    left, shadow_held = tie(left, shadow_held)
+    partial = primary(left, coupling)
+    shadow_held = exchange(shadow_held, COL_STEPS[0])
+    partial, shadow_held = tie(partial, shadow_held)
     scale = FIRST_SCALE / top
-    mine, other = pick(low_half, primary_partial * scale)
-    mine = mine + move(other.astype(WIRE), ROW_STEPS[0]).astype(F32)
-    mine = chip_sum(mine, ROW_STEPS[1:]).astype(WIRE)
+    held = send_half(*pick(low_half, partial * scale))
+    shadow_held = exchange(shadow_held, COL_STEPS[1])
+    held, shadow_held = tie(held, shadow_held)
+    held = exchange(held, ROW_STEPS[1])
+    shadow_held = exchange(shadow_held, COL_STEPS[2])
+    held, shadow_held = tie(held, shadow_held)
+    columns = move(shadow_held, TO_COLS)
+    held = exchange(held, ROW_STEPS[2])
+    held, columns = tie(held, columns)
+
     unscale = COUPLE_GAIN / scale
 
     def first_step(kept, value, product):
@@ -248,27 +258,34 @@
 
     g_half, keep_half = pick(low_half, g)[0], pick(low_half, keep)[0]
     slope_half = pick(low_half, slope)[0]
-    _, u_half = first_step(keep_half, g_half, mine)
-    u_half = (slope_half * u_half).astype(BF16)
-    u_half = move(u_half, HALF_TO_ROWS)
+    _, u_half = first_step(keep_half, g_half, held)
+    half = move((slope_half * u_half).astype(BF16), HALF_TO_ROWS)
     scale = FIRST_SCALE / shadow_top
-    columns = chip_sum(core_sum(shadow_partial, scale), COL_STEPS)
-    columns = move(columns.astype(WIRE), TO_COLS)
     q1 = keep * gs - (COUPLE_GAIN / scale) * slope * columns.astype(F32)
     us = gs - alpha_c * q1
 
-    left = spread(u_half)
-    primary_partial = primary(left, coupling)
-    us_sent, mine, primary_partial = lax.optimization_barrier(
-        (us.astype(BF16), mine, primary_partial)
-    )
-    shadow_partial = shadow(us_sent, coupling)
-    scale = SECOND_SCALE / top
-    second = chip_sum(primary_partial * scale, ROW_STEPS) * (COUPLE_GAIN / scale)
-    product = put(low_half, mine, move(mine, ROW_STEPS[0]))
+    shadow_partial = shadow(us.astype(BF16), coupling)
+    half, shadow_partial, held = tie(half, shadow_partial, held)
+    block = put(z_even, half, move(half, Z_PAIR))
+    scale = SECOND_SCALE / shadow_top
+    shadow_held = send_core(shadow_partial, scale)
+    product = put(low_half, held, move(held, ROW_STEPS[0]))
+    block, shadow_held, product = tie(block, shadow_held, product)
+    left = put(first, block, move(block, CORE))
+    partial = primary(left, coupling)
+    shadow_held = exchange(shadow_held, COL_STEPS[0])
+    partial, shadow_held = tie(partial, shadow_held)
+    held = exchange((partial * (SECOND_SCALE / top)).astype(WIRE), ROW_STEPS[0])
+    shadow_held = exchange(shadow_held, COL_STEPS[1])
+    held, shadow_held = tie(held, shadow_held)
+    held = exchange(held, ROW_STEPS[1])
+    shadow_held = exchange(shadow_held, COL_STEPS[2])
+    held, shadow_held = tie(held, shadow_held)
+    columns = move(shadow_held, TO_COLS)
+    held = exchange(held, ROW_STEPS[2])
+
     p1, u = first_step(keep, g, product)
-    p2 = keep * u - second
-
+    p2 = keep * u - held.astype(F32) * (COUPLE_GAIN * top / SECOND_SCALE)
     dots = jnp.stack(
         [
             total(gs * p1),
@@ -279,13 +296,9 @@
             total(us * p2),
         ]
     )
-    for pairs in SMALL_COL[:2]:
-        dots = dots + move(dots, pairs)
-    scale = SECOND_SCALE / shadow_top
-    held = chip_sum(core_sum(shadow_partial, scale), COL_STEPS[:2]).astype(WIRE)
-    held, dots = lax.optimization_barrier((held, dots))
-    columns = move(chip_sum(held, COL_STEPS[2:]).astype(WIRE), TO_COLS)
-    for pairs in SMALL_COL[2:]:
+    for pairs in SMALL_COL:
+        if pairs is SMALL_COL[1]:
+            dots, columns = tie(dots, columns)
         dots = dots + move(dots, pairs)
     curve, us_g, us_u, us_p1, q1_u, us_p2 = (dots[i] for i in range(6))
     q2 = keep * us - (COUPLE_GAIN / scale) * slope * columns.astype(F32)

time: 153 us -> 140 us (0.915)
  waiting for transfers between devices: 74.2 us -> 65.3 us
  starting transfers between devices: 38.2 us -> 35.1 us
  other arithmetic: 11.5 us -> 8.95 us
    ppermute x31, waiting for transfers between devices: 74.2 us -> 65.3 us  [move(): return lax.ppermute(value, AXES, pairs)]
    ppermute x31, starting transfers between devices: 38.2 us -> 35.1 us  [move(): return lax.ppermute(value, AXES, pairs)]
    sub x1 -> x0, other arithmetic: 1.69 us -> none  [on_device(): residual = g - step * p1 - step_next * (lead * p1 + kappa * p2)]
    convert_element_type x18 -> x19, other arithmetic: 3.87 us -> 2.44 us  [the longest x10 1.5 us: exchange(): return (held.astype(F32) + move(held, pairs).astype(F32)).astype(WIRE)]
  transfers between devices with their start and end apart: 31 -> 31, of which waited for: 20 -> 23; matrix products, arithmetic and copies ran while one was open for 4% -> 1% of each run, Pallas kernels for 18% -> 20%
where the time goes in v4:
time: 140 us; the launch traced here: 138 us
  waiting for transfers between devices  65.3 us (47%)
  starting transfers between devices  35.1 us (25%)
  Pallas kernels  27.9 us (20%)
  other arithmetic  8.95 us (6%)
    ppermute x31, waiting for transfers between devices, move(): return lax.ppermute(value, AXES, pairs)  65.3 us
    ppermute x31, starting transfers between devices, move(): return lax.ppermute(value, AXES, pairs)  35.1 us
    pallas_call x4, Pallas kernels, call(): pl.pallas_call(kernel, name=name, in_specs=[spec, pl.BlockSpec(memory_spa...  27.9 us
    sub x1, other arithmetic, on_device(): shadow_residual = gs - step * q1 - step_next * (lead * q1 + kappa * q2)  2.83 us
  transfers between devices with their start and end apart: 31, of which 23 were waited for; matrix products, arithmetic and copies ran while one was open for 1% of the time, Pallas kernels for 20%

profile of v4, /device:TPU:0, one launch (start us, length us, event | category | flops | bytes accessed | tf_op | source)
XLA Modules:
  0.0 138.4 jit_solution(13637585852781754524)
XLA Ops:
  0.6 1.9 %multiply_reduce_fusion.7 = (f32[64]{0:T(128)S(1)}, f32[64]{0:T(128)S(1)}, f32[64]{0:T(128)S(1)}, f32[64]{0:T(128)S(1)}, bf16[64,2048]{1,0:T(8,128)(2,1)S(1)}, /*index=5*/bf16[64,2048]{1,0:T(8,128)(2,1)S(1)}) fusion(f32[64,2048]{1,0:T(8,128)} %param.7, f32[64,2048]{1,0:T(8,128)} %param.6, f32[64,2048]{1,0:T(8,128)} %param.5), kind=kLoop, calls=%fused_computation.37 | loop fusion | flops 2096896 | bytes 2098176 | tf_op jit(solution)/shard_map/reduce_sum | solution.py:192
  2.6 0.1 collective-permute-start
  2.7 4.0 %collective-permute-start.2 = (bf16[64,1024]{1,0:T(8,128)(2,1)S(1)}, bf16[64,1024]{1,0:T(8,128)(2,1)S(1)}, u32[]{:S(2)}, u32[]{:S(2)}) collective-permute-start(bf16[64,1024]{1,0:T(8,128)(2,1)S(1)} %slice_select_fusion.2), channel_id=1, source_target_pairs={{112,0},{65,1},{48,2},{113,3},{0,4},{33,5},{64,6},{17,7},{96,8},{9... | collective-permute-start | bytes 393224 | tf_op jit(solution)/shard_map/ppermute | solution.py:168
  6.8 0.7 collective-permute-start.1
  7.4 7.7 %shadow.2 = f32[64,4096]{1,0:T(8,128)S(1)} custom-call(bf16[64,2048]{1,0:T(8,128)(2,1)S(1)} %get-tuple-element.83.left_ref, bf16[4096,2048]{1,0:T(8,128)(2,1)} %coupling_ref.7), custom_call_target="tpu_custom_call" | custom-call | flops 1073741824 | bytes 16777216 | tf_op jit(solution)/shard_map/shadow/pallas_call | solution.py:140
  15.3 4.5 %collective-permute-start.3 = (f32[4,64]{1,0:T(4,128)S(1)}, f32[4,64]{1,0:T(4,128)S(1)}, u32[]{:S(2)}, u32[]{:S(2)}) collective-permute-start(f32[4,64]{1,0:T(4,128)S(1)} %pad_maximum_fusion.7), channel_id=1, source_target_pairs={{2,0},{3,1},{0,2},{1,3},{6,4},{7,5},{4,6},{5,7},{10,8},{11,9},{8,1... | collective-permute-start | bytes 3080 | tf_op jit(solution)/shard_map/ppermute | solution.py:168
  19.7 1.6 %collective-permute-done.3 = f32[4,64]{1,0:T(4,128)S(1)} collective-permute-done((f32[4,64]{1,0:T(4,128)S(1)}, f32[4,64]{1,0:T(4,128)S(1)}, u32[]{:S(2)}, u32[]{:S(2)}) %collective-permute-start.3) | collective-permute-done | bytes 1056 | tf_op jit(solution)/shard_map/ppermute | solution.py:168
  21.3 1.2 collective-permute-start.4
  22.5 1.0 collective-permute-start.5
  23.5 2.7 %collective-permute-done.4 = f32[4,64]{1,0:T(4,128)S(1)} collective-permute-done((f32[4,64]{1,0:T(4,128)S(1)}, f32[4,64]{1,0:T(4,128)S(1)}, u32[]{:S(2)}, u32[]{:S(2)}) %collective-permute-start.4) | collective-permute-done | bytes 1056 | tf_op jit(solution)/shard_map/ppermute | solution.py:168
  26.2 0.1 broadcast_multiply_fusion.1
  26.4 0.1 collective-permute-start.7
  26.5 1.0 collective-permute-done.5
  27.7 0.4 collective-permute-done.7
  28.0 0.1 add_convert_fusion.10
  28.1 1.0 collective-permute-done.6
  29.2 0.1 broadcast_select_fusion.3
  29.3 0.9 collective-permute-start.8
  30.2 6.2 %primary.2 = f32[64,2048]{1,0:T(8,128)S(1)} custom-call(bf16[64,4096]{1,0:T(8,128)(2,1)S(1)} %pad_maximum_fusion.left_ref, bf16[4096,2048]{1,0:T(8,128)(2,1)} %coupling_ref.7), custom_call_target="tpu_custom_call" | custom-call | flops 1073741824 | bytes 16777216 | tf_op jit(solution)/shard_map/primary/pallas_call | solution.py:140
  36.5 0.1 broadcast_multiply_fusion.2
  36.7 2.0 %collective-permute-start.9 = (f16[64,1024]{1,0:T(8,128)(2,1)S(1)}, f16[64,1024]{1,0:T(8,128)(2,1)S(1)}, u32[]{:S(2)}, u32[]{:S(2)}) collective-permute-start(f16[64,1024]{1,0:T(8,128)(2,1)S(1)} %select_convert_fusion.2), channel_id=1, source_target_pairs={{32,0},{17,1},{34,2},{19,3},{36,4},{21,5},{38,6},{23,7},{40,8},{25... | collective-permute-start | bytes 393224 | tf_op jit(solution)/shard_map/ppermute | solution.py:168
  38.7 3.0 %collective-permute-done.9 = f16[64,1024]{1,0:T(8,128)(2,1)S(1)} collective-permute-done((f16[64,1024]{1,0:T(8,128)(2,1)S(1)}, f16[64,1024]{1,0:T(8,128)(2,1)S(1)}, u32[]{:S(2)}, u32[]{:S(2)}) %collective-permute-start.9) | collective-permute-done | bytes 131104 | tf_op jit(solution)/shard_map/ppermute | solution.py:168
  41.8 3.3 %collective-permute-done.10 = f16[64,2048]{1,0:T(8,128)(2,1)S(1)} collective-permute-done((f16[64,2048]{1,0:T(8,128)(2,1)S(1)}, f16[64,2048]{1,0:T(8,128)(2,1)S(1)}, u32[]{:S(2)}, u32[]{:S(2)}) %collective-permute-start.10) | collective-permute-done | bytes 262176 | tf_op jit(solution)/shard_map/ppermute | solution.py:168
  45.2 2.0 %collective-permute-start.11 = (f16[64,1024]{1,0:T(8,128)(2,1)S(1)}, f16[64,1024]{1,0:T(8,128)(2,1)S(1)}, u32[]{:S(2)}, u32[]{:S(2)}) collective-permute-start(f16[64,1024]{1,0:T(8,128)(2,1)S(1)} %add_convert_fusion.13), channel_id=1, source_target_pairs={{96,0},{33,1},{98,2},{35,3},{100,4},{37,5},{102,6},{39,7},{104,8},... | collective-permute-start | bytes 393224 | tf_op jit(solution)/shard_map/ppermute | solution.py:168
  47.1 0.4 collective-permute-start.12
  47.5 3.9 %collective-permute-done.11 = f16[64,1024]{1,0:T(8,128)(2,1)S(1)} collective-permute-done((f16[64,1024]{1,0:T(8,128)(2,1)S(1)}, f16[64,1024]{1,0:T(8,128)(2,1)S(1)}, u32[]{:S(2)}, u32[]{:S(2)}) %collective-permute-start.11) | collective-permute-done | bytes 131104 | tf_op jit(solution)/shard_map/ppermute | solution.py:168
  51.5 3.2 %collective-permute-done.12 = f16[64,2048]{1,0:T(8,128)(2,1)S(1)} collective-permute-done((f16[64,2048]{1,0:T(8,128)(2,1)S(1)}, f16[64,2048]{1,0:T(8,128)(2,1)S(1)}, u32[]{:S(2)}, u32[]{:S(2)}) %collective-permute-start.12) | collective-permute-done | bytes 262176 | tf_op jit(solution)/shard_map/ppermute | solution.py:168
  54.8 2.0 %collective-permute-start.13 = (f16[64,1024]{1,0:T(8,128)(2,1)S(1)}, f16[64,1024]{1,0:T(8,128)(2,1)S(1)}, u32[]{:S(2)}, u32[]{:S(2)}) collective-permute-start(f16[64,1024]{1,0:T(8,128)(2,1)S(1)} %add_convert_fusion.12), channel_id=1, source_target_pairs={{16,0},{97,1},{18,2},{99,3},{20,4},{101,5},{22,6},{103,7},{24,8},{... | collective-permute-start | bytes 393224 | tf_op jit(solution)/shard_map/ppermute | solution.py:168
  56.8 0.7 collective-permute-start.14
  57.6 5.2 %collective-permute-done.13 = f16[64,1024]{1,0:T(8,128)(2,1)S(1)} collective-permute-done((f16[64,1024]{1,0:T(8,128)(2,1)S(1)}, f16[64,1024]{1,0:T(8,128)(2,1)S(1)}, u32[]{:S(2)}, u32[]{:S(2)}) %collective-permute-start.13) | collective-permute-done | bytes 131104 | tf_op jit(solution)/shard_map/ppermute | solution.py:168
  62.8 4.7 %collective-permute-done.14 = f16[64,2048]{1,0:T(8,128)(2,1)S(1)} collective-permute-done((f16[64,2048]{1,0:T(8,128)(2,1)S(1)}, f16[64,2048]{1,0:T(8,128)(2,1)S(1)}, u32[]{:S(2)}, u32[]{:S(2)}) %collective-permute-start.14) | collective-permute-done | bytes 262176 | tf_op jit(solution)/shard_map/ppermute | solution.py:168
  67.5 0.3 fusion.15
  67.8 0.2 fusion.6
  68.0 0.3 collective-permute-start.15
  68.2 7.7 %shadow.3 = f32[64,4096]{1,0:T(8,128)S(1)} custom-call(bf16[64,2048]{1,0:T(8,128)(2,1)S(1)} %get-tuple-element.74.left_ref, bf16[4096,2048]{1,0:T(8,128)(2,1)} %coupling_ref.7), custom_call_target="tpu_custom_call" | custom-call | flops 1073741824 | bytes 16777216 | tf_op jit(solution)/shard_map/shadow/pallas_call | solution.py:140
  76.0 2.2 %collective-permute-done.15 = bf16[64,1024]{1,0:T(8,128)(2,1)S(1)} collective-permute-done((bf16[64,1024]{1,0:T(8,128)(2,1)S(1)}, bf16[64,1024]{1,0:T(8,128)(2,1)S(1)}, u32[]{:S(2)}, u32[]{:S(2)}) %collective-permute-start.15) | collective-permute-done | bytes 131104 | tf_op jit(solution)/shard_map/ppermute | solution.py:168
  78.2 0.3 collective-permute-start.18
  78.5 0.1 broadcast_multiply_fusion
  78.8 4.3 %collective-permute-done.16 = bf16[64,1024]{1,0:T(8,128)(2,1)S(1)} collective-permute-done((bf16[64,1024]{1,0:T(8,128)(2,1)S(1)}, bf16[64,1024]{1,0:T(8,128)(2,1)S(1)}, u32[]{:S(2)}, u32[]{:S(2)}) %collective-permute-start.16) | collective-permute-done | bytes 131104 | tf_op jit(solution)/shard_map/ppermute | solution.py:168
  83.3 0.1 add_convert_fusion.6
  83.5 0.1 collective-permute-start.20
  83.6 1.4 %collective-permute-done.19 = bf16[64,2048]{1,0:T(8,128)(2,1)S(1)} collective-permute-done((bf16[64,2048]{1,0:T(8,128)(2,1)S(1)}, bf16[64,2048]{1,0:T(8,128)(2,1)S(1)}, u32[]{:S(2)}, u32[]{:S(2)}) %collective-permute-start.19) | collective-permute-done | bytes 262176 | tf_op jit(solution)/shard_map/ppermute | solution.py:168
  85.2 6.2 %primary.3 = f32[64,2048]{1,0:T(8,128)S(1)} custom-call(bf16[64,4096]{1,0:T(8,128)(2,1)S(1)} %pad_maximum_fusion.1.left_ref, bf16[4096,2048]{1,0:T(8,128)(2,1)} %coupling_ref.7), custom_call_target="tpu_custom_call" | custom-call | flops 1073741824 | bytes 16777216 | tf_op jit(solution)/shard_map/primary/pallas_call | solution.py:140
  91.5 0.1 multiply_convert_fusion
  91.6 0.4 collective-permute-start.21
  92.0 1.8 %collective-permute-start.22 = (f16[64,2048]{1,0:T(8,128)(2,1)S(1)}, f16[64,2048]{1,0:T(8,128)(2,1)S(1)}, u32[]{:S(2)}, u32[]{:S(2)}) collective-permute-start(f16[64,2048]{1,0:T(8,128)(2,1)S(1)} %add_convert_fusion.5), channel_id=1, source_target_pairs={{2,0},{7,1},{0,2},{5,3},{6,4},{3,5},{4,6},{1,7},{10,8},{15,9},{8,1... | collective-permute-start | bytes 786440 | tf_op jit(solution)/shard_map/ppermute | solution.py:168
  93.8 4.3 %collective-permute-done.21 = f16[64,2048]{1,0:T(8,128)(2,1)S(1)} collective-permute-done((f16[64,2048]{1,0:T(8,128)(2,1)S(1)}, f16[64,2048]{1,0:T(8,128)(2,1)S(1)}, u32[]{:S(2)}, u32[]{:S(2)}) %collective-permute-start.21) | collective-permute-done | bytes 262176 | tf_op jit(solution)/shard_map/ppermute | solution.py:168
  98.1 0.1 add_convert_fusion.4
  98.2 0.2 collective-permute-done.22
  98.5 5.0 %collective-permute-start.23 = (f16[64,2048]{1,0:T(8,128)(2,1)S(1)}, f16[64,2048]{1,0:T(8,128)(2,1)S(1)}, u32[]{:S(2)}, u32[]{:S(2)}) collective-permute-start(f16[64,2048]{1,0:T(8,128)(2,1)S(1)} %add_convert_fusion.4), channel_id=1, source_target_pairs={{96,0},{33,1},{98,2},{35,3},{100,4},{37,5},{102,6},{39,7},{104,8},... | collective-permute-start | bytes 786440 | tf_op jit(solution)/shard_map/ppermute | solution.py:168
  103.4 4.3 %collective-permute-done.23 = f16[64,2048]{1,0:T(8,128)(2,1)S(1)} collective-permute-done((f16[64,2048]{1,0:T(8,128)(2,1)S(1)}, f16[64,2048]{1,0:T(8,128)(2,1)S(1)}, u32[]{:S(2)}, u32[]{:S(2)}) %collective-permute-start.23) | collective-permute-done | bytes 262176 | tf_op jit(solution)/shard_map/ppermute | solution.py:168
  107.9 3.1 %collective-permute-done.24 = f16[64,2048]{1,0:T(8,128)(2,1)S(1)} collective-permute-done((f16[64,2048]{1,0:T(8,128)(2,1)S(1)}, f16[64,2048]{1,0:T(8,128)(2,1)S(1)}, u32[]{:S(2)}, u32[]{:S(2)}) %collective-permute-start.24) | collective-permute-done | bytes 262176 | tf_op jit(solution)/shard_map/ppermute | solution.py:168
  111.0 0.8 add_convert_fusion.1
  111.8 3.1 %collective-permute-start.27 = (f16[64,2048]{1,0:T(8,128)(2,1)}, f16[64,2048]{1,0:T(8,128)(2,1)S(1)}, u32[]{:S(2)}, u32[]{:S(2)}) collective-permute-start(f16[64,2048]{1,0:T(8,128)(2,1)} %add_convert_fusion.1), channel_id=1, source_target_pairs={{4,0},{5,1},{30,2},{31,3},{34,4},{39,5},{60,6},{57,7},{72,8},{73,9... | collective-permute-start | bytes 786440 | tf_op jit(solution)/shard_map/ppermute | solution.py:168
  114.9 5.9 %collective-permute-done.25 = f16[64,2048]{1,0:T(8,128)(2,1)S(1)} collective-permute-done((f16[64,2048]{1,0:T(8,128)(2,1)S(1)}, f16[64,2048]{1,0:T(8,128)(2,1)S(1)}, u32[]{:S(2)}, u32[]{:S(2)}) %collective-permute-start.25) | collective-permute-done | bytes 262176 | tf_op jit(solution)/shard_map/ppermute | solution.py:168
  120.9 0.8 multiply_reduce_fusion
  121.8 1.2 collective-permute-done.26
  122.9 1.5 %collective-permute-start.28 = (f32[6,64]{1,0:T(8,128)S(1)}, f32[6,64]{1,0:T(8,128)S(1)}, u32[]{:S(2)}, u32[]{:S(2)}) collective-permute-start(f32[6,64]{1,0:T(8,128)S(1)} %add.166), channel_id=1, source_target_pairs={{8,0},{9,1},{10,2},{11,3},{12,4},{13,5},{14,6},{15,7},{0,8},{1,9},... | collective-permute-start | bytes 4616 | tf_op jit(solution)/shard_map/ppermute | solution.py:168
  124.4 2.1 %collective-permute-done.28 = f32[6,64]{1,0:T(8,128)S(1)} collective-permute-done((f32[6,64]{1,0:T(8,128)S(1)}, f32[6,64]{1,0:T(8,128)S(1)}, u32[]{:S(2)}, u32[]{:S(2)}) %collective-permute-start.28) | collective-permute-done | bytes 1568 | tf_op jit(solution)/shard_map/ppermute | solution.py:168
  126.6 2.5 %collective-permute-start.29 = (f32[6,64]{1,0:T(8,128)S(1)}, f32[6,64]{1,0:T(8,128)S(1)}, u32[]{:S(2)}, u32[]{:S(2)}) collective-permute-start(f32[6,64]{1,0:T(8,128)S(1)} %add.167), channel_id=1, source_target_pairs={{2,0},{3,1},{0,2},{1,3},{6,4},{7,5},{4,6},{5,7},{10,8},{11,9},{8,1... | collective-permute-start | bytes 4616 | tf_op jit(solution)/shard_map/ppermute | solution.py:168
  129.1 1.6 %collective-permute-done.29 = f32[6,64]{1,0:T(8,128)S(1)} collective-permute-done((f32[6,64]{1,0:T(8,128)S(1)}, f32[6,64]{1,0:T(8,128)S(1)}, u32[]{:S(2)}, u32[]{:S(2)}) %collective-permute-start.29) | collective-permute-done | bytes 1568 | tf_op jit(solution)/shard_map/ppermute | solution.py:168
  130.7 0.3 collective-permute-start.30
  131.0 4.5 %collective-permute-done.30 = f32[6,64]{1,0:T(8,128)S(1)} collective-permute-done((f32[6,64]{1,0:T(8,128)S(1)}, f32[6,64]{1,0:T(8,128)S(1)}, u32[]{:S(2)}, u32[]{:S(2)}) %collective-permute-start.30) | collective-permute-done | bytes 1568 | tf_op jit(solution)/shard_map/ppermute | solution.py:168
  135.5 2.8 %multiply_subtract_fusion = (f32[64,2048]{1,0:T(8,128)}, f32[64,2048]{1,0:T(8,128)}, f32[64,2048]{1,0:T(8,128)}, f32[64,2048]{1,0:T(8,128)}) fusion(f16[64,2048]{1,0:T(8,128)(2,1)S(1)} %collective-permute-done.27, f32[64,2048]{1,0:T(8,128)S(1)} %get-tuple-element.75, f32[64,2048]{1,0:T(8,128)S(1)} %copy-done, f16[64,2048]{1,0:T(8,128)(2,1)S(1)} %collective-permute-done.14, ...), kind=kLoop, calls=%fused_computation.2 | loop fusion | flops 7077888 | bytes 5507328 | tf_op jit(solution)/shard_map/sub | solution.py:329
  (61 shorter events, 1.7 us)
Async XLA Ops:
  2.6 4.2 %collective-permute-start = (f32[4,64]{1,0:T(4,128)S(1)}, f32[4,64]{1,0:T(4,128)S(1)}, u32[]{:S(2)}, u32[]{:S(2)}) collective-permute-start(f32[4,64]{1,0:T(4,128)S(1)} %pad_maximum_fusion.5), channel_id=1, source_target_pairs={{1,0},{0,1},{3,2},{2,3},{5,4},{4,5},{7,6},{6,7},{9,8},{8,9},{11,10... | collective-permute-start | bytes 3080 | tf_op jit(solution)/shard_map/ppermute | solution.py:168
  2.7 12.5 %collective-permute-start.2 = (bf16[64,1024]{1,0:T(8,128)(2,1)S(1)}, bf16[64,1024]{1,0:T(8,128)(2,1)S(1)}, u32[]{:S(2)}, u32[]{:S(2)}) collective-permute-start(bf16[64,1024]{1,0:T(8,128)(2,1)S(1)} %slice_select_fusion.2), channel_id=1, source_target_pairs={{112,0},{65,1},{48,2},{113,3},{0,4},{33,5},{64,6},{17,7},{96,8},{9... | collective-permute-start | bytes 393224 | tf_op jit(solution)/shard_map/ppermute | solution.py:168
  6.8 8.4 %collective-permute-start.1 = (f32[4,64]{1,0:T(4,128)S(1)}, f32[4,64]{1,0:T(4,128)S(1)}, u32[]{:S(2)}, u32[]{:S(2)}) collective-permute-start(f32[4,64]{1,0:T(4,128)S(1)} %pad_maximum_fusion.6), channel_id=1, source_target_pairs={{8,0},{9,1},{10,2},{11,3},{12,4},{13,5},{14,6},{15,7},{0,8},{1,9},... | collective-permute-start | bytes 3080 | tf_op jit(solution)/shard_map/ppermute | solution.py:168
  15.2 52.3 %copy-start = (f32[64,2048]{1,0:T(8,128)S(1)}, f32[64,2048]{1,0:T(8,128)}, u32[]{:S(2)}) copy-start(f32[64,2048]{1,0:T(8,128)} %param.7) | copy-start | bytes 1572868
  15.2 52.3 %copy-start.2 = (f32[64,2048]{1,0:T(8,128)S(1)}, f32[64,2048]{1,0:T(8,128)}, u32[]{:S(2)}) copy-start(f32[64,2048]{1,0:T(8,128)} %param.5) | copy-start | bytes 1572868
  15.3 6.0 %collective-permute-start.3 = (f32[4,64]{1,0:T(4,128)S(1)}, f32[4,64]{1,0:T(4,128)S(1)}, u32[]{:S(2)}, u32[]{:S(2)}) collective-permute-start(f32[4,64]{1,0:T(4,128)S(1)} %pad_maximum_fusion.7), channel_id=1, source_target_pairs={{2,0},{3,1},{0,2},{1,3},{6,4},{7,5},{4,6},{5,7},{10,8},{11,9},{8,1... | collective-permute-start | bytes 3080 | tf_op jit(solution)/shard_map/ppermute | solution.py:168
  21.3 4.9 %collective-permute-start.4 = (f32[4,64]{1,0:T(4,128)S(1)}, f32[4,64]{1,0:T(4,128)S(1)}, u32[]{:S(2)}, u32[]{:S(2)}) collective-permute-start(f32[4,64]{1,0:T(4,128)S(1)} %pad_maximum_fusion.8), channel_id=1, source_target_pairs={{6,0},{7,1},{4,2},{5,3},{2,4},{3,5},{0,6},{1,7},{14,8},{15,9},{12,... | collective-permute-start | bytes 3080 | tf_op jit(solution)/shard_map/ppermute | solution.py:168
  22.5 5.0 %collective-permute-start.5 = (bf16[64,1024]{1,0:T(8,128)(2,1)S(1)}, bf16[64,1024]{1,0:T(8,128)(2,1)S(1)}, u32[]{:S(2)}, u32[]{:S(2)}) collective-permute-start(bf16[64,1024]{1,0:T(8,128)(2,1)S(1)} %collective-permute-done.2), channel_id=1, source_target_pairs={{2,0},{3,1},{0,2},{1,3},{6,4},{7,5},{4,6},{5,7},{10,8},{11,9},{8,1... | collective-permute-start | bytes 393224 | tf_op jit(solution)/shard_map/ppermute | solution.py:168
  26.4 41.4 %copy-start.1 = (f32[64,2048]{1,0:T(8,128)S(1)}, f32[64,2048]{1,0:T(8,128)}, u32[]{:S(2)}) copy-start(f32[64,2048]{1,0:T(8,128)} %param.6) | copy-start | bytes 1572868
  26.4 1.6 %collective-permute-start.7 = (f16[64,2048]{1,0:T(8,128)(2,1)S(1)}, f16[64,2048]{1,0:T(8,128)(2,1)S(1)}, u32[]{:S(2)}, u32[]{:S(2)}) collective-permute-start(f16[64,2048]{1,0:T(8,128)(2,1)S(1)} %select_convert_fusion.1), channel_id=1, source_target_pairs={{1,0},{0,1},{3,2},{2,3},{5,4},{4,5},{7,6},{6,7},{9,8},{8,9},{11,10... | collective-permute-start | bytes 786440 | tf_op jit(solution)/shard_map/ppermute | solution.py:168
  27.6 1.6 %collective-permute-start.6 = (bf16[64,2048]{1,0:T(8,128)(2,1)S(1)}, bf16[64,2048]{1,0:T(8,128)(2,1)S(1)}, u32[]{:S(2)}, u32[]{:S(2)}) collective-permute-start(bf16[64,2048]{1,0:T(8,128)(2,1)S(1)} %pad_maximum_fusion.2), channel_id=1, source_target_pairs={{1,0},{0,1},{3,2},{2,3},{5,4},{4,5},{7,6},{6,7},{9,8},{8,9},{11,10... | collective-permute-start | bytes 786440 | tf_op jit(solution)/shard_map/ppermute | solution.py:168
  29.3 7.1 %collective-permute-start.8 = (f16[64,2048]{1,0:T(8,128)(2,1)S(1)}, f16[64,2048]{1,0:T(8,128)(2,1)S(1)}, u32[]{:S(2)}, u32[]{:S(2)}) collective-permute-start(f16[64,2048]{1,0:T(8,128)(2,1)S(1)} %add_convert_fusion.10), channel_id=1, source_target_pairs={{8,0},{3,1},{10,2},{1,3},{12,4},{7,5},{14,6},{5,7},{0,8},{11,9},{2... | collective-permute-start | bytes 786440 | tf_op jit(solution)/shard_map/ppermute | solution.py:168
  36.7 5.0 %collective-permute-start.9 = (f16[64,1024]{1,0:T(8,128)(2,1)S(1)}, f16[64,1024]{1,0:T(8,128)(2,1)S(1)}, u32[]{:S(2)}, u32[]{:S(2)}) collective-permute-start(f16[64,1024]{1,0:T(8,128)(2,1)S(1)} %select_convert_fusion.2), channel_id=1, source_target_pairs={{32,0},{17,1},{34,2},{19,3},{36,4},{21,5},{38,6},{23,7},{40,8},{25... | collective-permute-start | bytes 393224 | tf_op jit(solution)/shard_map/ppermute | solution.py:168
  38.7 6.4 %collective-permute-start.10 = (f16[64,2048]{1,0:T(8,128)(2,1)S(1)}, f16[64,2048]{1,0:T(8,128)(2,1)S(1)}, u32[]{:S(2)}, u32[]{:S(2)}) collective-permute-start(f16[64,2048]{1,0:T(8,128)(2,1)S(1)} %add_convert_fusion.9), channel_id=1, source_target_pairs={{2,0},{7,1},{0,2},{5,3},{6,4},{3,5},{4,6},{1,7},{10,8},{15,9},{8,1... | collective-permute-start | bytes 786440 | tf_op jit(solution)/shard_map/ppermute | solution.py:168
  45.2 6.3 %collective-permute-start.11 = (f16[64,1024]{1,0:T(8,128)(2,1)S(1)}, f16[64,1024]{1,0:T(8,128)(2,1)S(1)}, u32[]{:S(2)}, u32[]{:S(2)}) collective-permute-start(f16[64,1024]{1,0:T(8,128)(2,1)S(1)} %add_convert_fusion.13), channel_id=1, source_target_pairs={{96,0},{33,1},{98,2},{35,3},{100,4},{37,5},{102,6},{39,7},{104,8},... | collective-permute-start | bytes 393224 | tf_op jit(solution)/shard_map/ppermute | solution.py:168
  47.1 7.6 %collective-permute-start.12 = (f16[64,2048]{1,0:T(8,128)(2,1)S(1)}, f16[64,2048]{1,0:T(8,128)(2,1)S(1)}, u32[]{:S(2)}, u32[]{:S(2)}) collective-permute-start(f16[64,2048]{1,0:T(8,128)(2,1)S(1)} %add_convert_fusion.8), channel_id=1, source_target_pairs={{6,0},{9,1},{4,2},{11,3},{2,4},{13,5},{0,6},{15,7},{14,8},{1,9},{1... | collective-permute-start | bytes 786440 | tf_op jit(solution)/shard_map/ppermute | solution.py:168
  54.8 8.0 %collective-permute-start.13 = (f16[64,1024]{1,0:T(8,128)(2,1)S(1)}, f16[64,1024]{1,0:T(8,128)(2,1)S(1)}, u32[]{:S(2)}, u32[]{:S(2)}) collective-permute-start(f16[64,1024]{1,0:T(8,128)(2,1)S(1)} %add_convert_fusion.12), channel_id=1, source_target_pairs={{16,0},{97,1},{18,2},{99,3},{20,4},{101,5},{22,6},{103,7},{24,8},{... | collective-permute-start | bytes 393224 | tf_op jit(solution)/shard_map/ppermute | solution.py:168
  56.8 10.7 %collective-permute-start.14 = (f16[64,2048]{1,0:T(8,128)(2,1)S(1)}, f16[64,2048]{1,0:T(8,128)(2,1)S(1)}, u32[]{:S(2)}, u32[]{:S(2)}) collective-permute-start(f16[64,2048]{1,0:T(8,128)(2,1)S(1)} %add_convert_fusion.7), channel_id=1, source_target_pairs={{4,0},{5,1},{30,2},{31,3},{34,4},{39,5},{60,6},{57,7},{72,8},{73,9... | collective-permute-start | bytes 786440 | tf_op jit(solution)/shard_map/ppermute | solution.py:168
  68.0 10.2 %collective-permute-start.15 = (bf16[64,1024]{1,0:T(8,128)(2,1)S(1)}, bf16[64,1024]{1,0:T(8,128)(2,1)S(1)}, u32[]{:S(2)}, u32[]{:S(2)}) collective-permute-start(bf16[64,1024]{1,0:T(8,128)(2,1)S(1)} %fusion.6), channel_id=1, source_target_pairs={{112,0},{65,1},{48,2},{113,3},{0,4},{33,5},{64,6},{17,7},{96,8},{9... | collective-permute-start | bytes 393224 | tf_op jit(solution)/shard_map/ppermute | solution.py:168
  78.2 5.0 %collective-permute-start.16 = (bf16[64,1024]{1,0:T(8,128)(2,1)S(1)}, bf16[64,1024]{1,0:T(8,128)(2,1)S(1)}, u32[]{:S(2)}, u32[]{:S(2)}) collective-permute-start(bf16[64,1024]{1,0:T(8,128)(2,1)S(1)} %collective-permute-done.15), channel_id=1, source_target_pairs={{2,0},{3,1},{0,2},{1,3},{6,4},{7,5},{4,6},{5,7},{10,8},{11,9},{8,1... | collective-permute-start | bytes 393224 | tf_op jit(solution)/shard_map/ppermute | solution.py:168
  78.2 5.0 %collective-permute-start.18 = (f16[64,1024]{1,0:T(8,128)(2,1)S(1)}, f16[64,1024]{1,0:T(8,128)(2,1)S(1)}, u32[]{:S(2)}, u32[]{:S(2)}) collective-permute-start(f16[64,1024]{1,0:T(8,128)(2,1)S(1)} %add_convert_fusion.11), channel_id=1, source_target_pairs={{32,0},{17,1},{34,2},{19,3},{36,4},{21,5},{38,6},{23,7},{40,8},{25... | collective-permute-start | bytes 393224 | tf_op jit(solution)/shard_map/ppermute | solution.py:168
  78.7 4.6 %collective-permute-start.17 = (f16[64,2048]{1,0:T(8,128)(2,1)S(1)}, f16[64,2048]{1,0:T(8,128)(2,1)S(1)}, u32[]{:S(2)}, u32[]{:S(2)}) collective-permute-start(f16[64,2048]{1,0:T(8,128)(2,1)S(1)} %select_convert_fusion), channel_id=1, source_target_pairs={{1,0},{0,1},{3,2},{2,3},{5,4},{4,5},{7,6},{6,7},{9,8},{8,9},{11,10... | collective-permute-start | bytes 786440 | tf_op jit(solution)/shard_map/ppermute | solution.py:168
  83.4 1.6 %collective-permute-start.19 = (bf16[64,2048]{1,0:T(8,128)(2,1)S(1)}, bf16[64,2048]{1,0:T(8,128)(2,1)S(1)}, u32[]{:S(2)}, u32[]{:S(2)}) collective-permute-start(bf16[64,2048]{1,0:T(8,128)(2,1)S(1)} %pad_maximum_fusion.3), channel_id=1, source_target_pairs={{1,0},{0,1},{3,2},{2,3},{5,4},{4,5},{7,6},{6,7},{9,8},{8,9},{11,10... | collective-permute-start | bytes 786440 | tf_op jit(solution)/shard_map/ppermute | solution.py:168
  83.5 7.9 %collective-permute-start.20 = (f16[64,2048]{1,0:T(8,128)(2,1)S(1)}, f16[64,2048]{1,0:T(8,128)(2,1)S(1)}, u32[]{:S(2)}, u32[]{:S(2)}) collective-permute-start(f16[64,2048]{1,0:T(8,128)(2,1)S(1)} %add_convert_fusion.6), channel_id=1, source_target_pairs={{8,0},{3,1},{10,2},{1,3},{12,4},{7,5},{14,6},{5,7},{0,8},{11,9},{2... | collective-permute-start | bytes 786440 | tf_op jit(solution)/shard_map/ppermute | solution.py:168
  91.6 6.5 %collective-permute-start.21 = (f16[64,2048]{1,0:T(8,128)(2,1)S(1)}, f16[64,2048]{1,0:T(8,128)(2,1)S(1)}, u32[]{:S(2)}, u32[]{:S(2)}) collective-permute-start(f16[64,2048]{1,0:T(8,128)(2,1)S(1)} %multiply_convert_fusion), channel_id=1, source_target_pairs={{32,0},{17,1},{34,2},{19,3},{36,4},{21,5},{38,6},{23,7},{40,8},{25... | collective-permute-start | bytes 786440 | tf_op jit(solution)/shard_map/ppermute | solution.py:168
  92.0 6.4 %collective-permute-start.22 = (f16[64,2048]{1,0:T(8,128)(2,1)S(1)}, f16[64,2048]{1,0:T(8,128)(2,1)S(1)}, u32[]{:S(2)}, u32[]{:S(2)}) collective-permute-start(f16[64,2048]{1,0:T(8,128)(2,1)S(1)} %add_convert_fusion.5), channel_id=1, source_target_pairs={{2,0},{7,1},{0,2},{5,3},{6,4},{3,5},{4,6},{1,7},{10,8},{15,9},{8,1... | collective-permute-start | bytes 786440 | tf_op jit(solution)/shard_map/ppermute | solution.py:168
  98.5 9.3 %collective-permute-start.23 = (f16[64,2048]{1,0:T(8,128)(2,1)S(1)}, f16[64,2048]{1,0:T(8,128)(2,1)S(1)}, u32[]{:S(2)}, u32[]{:S(2)}) collective-permute-start(f16[64,2048]{1,0:T(8,128)(2,1)S(1)} %add_convert_fusion.4), channel_id=1, source_target_pairs={{96,0},{33,1},{98,2},{35,3},{100,4},{37,5},{102,6},{39,7},{104,8},... | collective-permute-start | bytes 786440 | tf_op jit(solution)/shard_map/ppermute | solution.py:168
  103.4 7.6 %collective-permute-start.24 = (f16[64,2048]{1,0:T(8,128)(2,1)S(1)}, f16[64,2048]{1,0:T(8,128)(2,1)S(1)}, u32[]{:S(2)}, u32[]{:S(2)}) collective-permute-start(f16[64,2048]{1,0:T(8,128)(2,1)S(1)} %add_convert_fusion.3), channel_id=1, source_target_pairs={{6,0},{9,1},{4,2},{11,3},{2,4},{13,5},{0,6},{15,7},{14,8},{1,9},{1... | collective-permute-start | bytes 786440 | tf_op jit(solution)/shard_map/ppermute | solution.py:168
  111.8 9.1 %collective-permute-start.25 = (f16[64,2048]{1,0:T(8,128)(2,1)S(1)}, f16[64,2048]{1,0:T(8,128)(2,1)S(1)}, u32[]{:S(2)}, u32[]{:S(2)}) collective-permute-start(f16[64,2048]{1,0:T(8,128)(2,1)S(1)} %add_convert_fusion.2), channel_id=1, source_target_pairs={{16,0},{97,1},{18,2},{99,3},{20,4},{101,5},{22,6},{103,7},{24,8},{... | collective-permute-start | bytes 786440 | tf_op jit(solution)/shard_map/ppermute | solution.py:168
  111.8 11.1 %collective-permute-start.27 = (f16[64,2048]{1,0:T(8,128)(2,1)}, f16[64,2048]{1,0:T(8,128)(2,1)S(1)}, u32[]{:S(2)}, u32[]{:S(2)}) collective-permute-start(f16[64,2048]{1,0:T(8,128)(2,1)} %add_convert_fusion.1), channel_id=1, source_target_pairs={{4,0},{5,1},{30,2},{31,3},{34,4},{39,5},{60,6},{57,7},{72,8},{73,9... | collective-permute-start | bytes 786440 | tf_op jit(solution)/shard_map/ppermute | solution.py:168
  121.7 1.2 collective-permute-start.26
  122.9 3.6 %collective-permute-start.28 = (f32[6,64]{1,0:T(8,128)S(1)}, f32[6,64]{1,0:T(8,128)S(1)}, u32[]{:S(2)}, u32[]{:S(2)}) collective-permute-start(f32[6,64]{1,0:T(8,128)S(1)} %add.166), channel_id=1, source_target_pairs={{8,0},{9,1},{10,2},{11,3},{12,4},{13,5},{14,6},{15,7},{0,8},{1,9},... | collective-permute-start | bytes 4616 | tf_op jit(solution)/shard_map/ppermute | solution.py:168
  126.6 4.1 %collective-permute-start.29 = (f32[6,64]{1,0:T(8,128)S(1)}, f32[6,64]{1,0:T(8,128)S(1)}, u32[]{:S(2)}, u32[]{:S(2)}) collective-permute-start(f32[6,64]{1,0:T(8,128)S(1)} %add.167), channel_id=1, source_target_pairs={{2,0},{3,1},{0,2},{1,3},{6,4},{7,5},{4,6},{5,7},{10,8},{11,9},{8,1... | collective-permute-start | bytes 4616 | tf_op jit(solution)/shard_map/ppermute | solution.py:168
  130.7 4.8 %collective-permute-start.30 = (f32[6,64]{1,0:T(8,128)S(1)}, f32[6,64]{1,0:T(8,128)S(1)}, u32[]{:S(2)}, u32[]{:S(2)}) collective-permute-start(f32[6,64]{1,0:T(8,128)S(1)} %add.168), channel_id=1, source_target_pairs={{6,0},{7,1},{4,2},{5,3},{2,4},{3,5},{0,6},{1,7},{14,8},{15,9},{12,... | collective-permute-start | bytes 4616 | tf_op jit(solution)/shard_map/ppermute | solution.py:168

commit v5 on v4

--- a/solution.py
+++ b/solution.py
@@ -97,6 +97,7 @@
     by_core(mirror_z, flip_yl),
 )
 Z_PAIR = sends(flip_z)
+SMALL_ROW = (CORE, sends(flip_x), sends(mirror_x), sends(flip_yh))
 SMALL_COL = (CORE, sends(flip_yl), sends(flip_z), sends(mirror_z))
 
 def fetch(source_ref, held_ref, sems):
@@ -264,28 +265,15 @@
     q1 = keep * gs - (COUPLE_GAIN / scale) * slope * columns.astype(F32)
     us = gs - alpha_c * q1
 
+    product = put(low_half, held, move(held, ROW_STEPS[0]))
     shadow_partial = shadow(us.astype(BF16), coupling)
-    half, shadow_partial, held = tie(half, shadow_partial, held)
-    block = put(z_even, half, move(half, Z_PAIR))
+    half, shadow_partial, product = tie(half, shadow_partial, product)
+
     scale = SECOND_SCALE / shadow_top
     shadow_held = send_core(shadow_partial, scale)
-    product = put(low_half, held, move(held, ROW_STEPS[0]))
-    block, shadow_held, product = tie(block, shadow_held, product)
-    left = put(first, block, move(block, CORE))
-    partial = primary(left, coupling)
     shadow_held = exchange(shadow_held, COL_STEPS[0])
-    partial, shadow_held = tie(partial, shadow_held)
-    held = exchange((partial * (SECOND_SCALE / top)).astype(WIRE), ROW_STEPS[0])
-    shadow_held = exchange(shadow_held, COL_STEPS[1])
-    held, shadow_held = tie(held, shadow_held)
-    held = exchange(held, ROW_STEPS[1])
-    shadow_held = exchange(shadow_held, COL_STEPS[2])
-    held, shadow_held = tie(held, shadow_held)
-    columns = move(shadow_held, TO_COLS)
-    held = exchange(held, ROW_STEPS[2])
-
+    block = put(z_even, half, move(half, Z_PAIR))
     p1, u = first_step(keep, g, product)
-    p2 = keep * u - held.astype(F32) * (COUPLE_GAIN * top / SECOND_SCALE)
     dots = jnp.stack(
         [
             total(gs * p1),
@@ -293,16 +281,39 @@
             total(us * u),
             total(us * p1),
             total(q1 * u),
-            total(us * p2),
+            total(us * (keep * u)),
         ]
     )
-    for pairs in SMALL_COL:
-        if pairs is SMALL_COL[1]:
-            dots, columns = tie(dots, columns)
-        dots = dots + move(dots, pairs)
-    curve, us_g, us_u, us_p1, q1_u, us_p2 = (dots[i] for i in range(6))
+    dots = dots + move(dots, SMALL_COL[0])
+    block, shadow_held, dots = tie(block, shadow_held, dots)
+
+    left = put(first, block, move(block, CORE))
+    shadow_held = exchange(shadow_held, COL_STEPS[1])
+    dots = dots + move(dots, SMALL_COL[1])
+    partial = primary(left, coupling)
+    partial, shadow_held, dots = tie(partial, shadow_held, dots)
+
+    held = exchange((partial * (SECOND_SCALE / top)).astype(WIRE), ROW_STEPS[0])
+    shadow_held = exchange(shadow_held, COL_STEPS[2])
+    dots = dots + move(dots, SMALL_COL[2])
+    held, shadow_held, dots = tie(held, shadow_held, dots)
+
+    columns = move(shadow_held, TO_COLS)
+    last = total(block.astype(F32) * shadow_held.astype(F32)) / scale[:, 0]
+    held = exchange(held, ROW_STEPS[1])
+    dots = dots + move(dots, SMALL_COL[3])
+    for pairs in SMALL_ROW[:2]:
+        last = last + move(last, pairs)
+    held, columns, dots, last = tie(held, columns, dots, last)
+
+    held = exchange(held, ROW_STEPS[2])
+    for pairs in SMALL_ROW[2:]:
+        last = last + move(last, pairs)
+
+    p2 = keep * u - held.astype(F32) * (COUPLE_GAIN * top / SECOND_SCALE)
     q2 = keep * us - (COUPLE_GAIN / scale) * slope * columns.astype(F32)
-
+    curve, us_g, us_u, us_p1, q1_u, us_kept = (dots[i] for i in range(6))
+    us_p2 = us_kept - COUPLE_GAIN * last
     gs_u = align - alpha * curve
     step = align / curve
     kappa = step / alpha

time: 140 us -> 146 us (1.043)
  starting transfers between devices: 35.1 us -> 40.6 us
  other arithmetic: 8.95 us -> 14 us
  waiting for transfers between devices: 65.3 us -> 61.5 us
    ppermute x31 -> x35, starting transfers between devices: 35.1 us -> 40.6 us  [move(): return lax.ppermute(value, AXES, pairs)]
    ppermute x31 -> x35, waiting for transfers between devices: 65.3 us -> 61.5 us  [move(): return lax.ppermute(value, AXES, pairs)]
    convert_element_type x4, other arithmetic: 0.29 us -> 1.96 us  [send_core(): return (mine + move(other.astype(WIRE), CORE).astype(F32)).astype(WIRE)]
    reduce_sum x2 -> x3, other arithmetic: 2.7 us -> 3.49 us  [total(): return jnp.sum(value, axis=1)]
  transfers between devices with their start and end apart: 31 -> 35, of which waited for: 23 -> 22; matrix products, arithmetic and copies ran while one was open for 1% -> 5% of each run, Pallas kernels for 20% -> 19%
where the time goes in v5:
time: 146 us
  waiting for transfers between devices  61.5 us (42%)
  starting transfers between devices  40.6 us (28%)
  Pallas kernels  27.9 us (19%)
  other arithmetic  14 us (10%)
    ppermute x35, waiting for transfers between devices, move(): return lax.ppermute(value, AXES, pairs)  61.5 us
    ppermute x35, starting transfers between devices, move(): return lax.ppermute(value, AXES, pairs)  40.6 us
    pallas_call x4, Pallas kernels, call(): pl.pallas_call(kernel, name=name, in_specs=[spec, pl.BlockSpec(memory_spa...  27.9 us
    sub x1, other arithmetic, on_device(): shadow_residual = gs - step * q1 - step_next * (lead * q1 + kappa * q2)  3.64 us
    reduce_sum x3, other arithmetic, total(): return jnp.sum(value, axis=1)  3.49 us
  transfers between devices with their start and end apart: 35, of which 22 were waited for; matrix products, arithmetic and copies ran while one was open for 5% of the time, Pallas kernels for 19%

profile of v5, /device:TPU:0, one launch (start us, length us, event | category | flops | bytes accessed | tf_op | source)
XLA Modules:
  0.0 145.8 jit_solution(10780435013249458811)
XLA Ops:
  0.6 1.9 %multiply_reduce_fusion.8 = (f32[64]{0:T(128)S(1)}, f32[64]{0:T(128)S(1)}, f32[64]{0:T(128)S(1)}, f32[64]{0:T(128)S(1)}, bf16[64,2048]{1,0:T(8,128)(2,1)S(1)}, /*index=5*/bf16[64,2048]{1,0:T(8,128)(2,1)S(1)}) fusion(f32[64,2048]{1,0:T(8,128)} %param.7, f32[64,2048]{1,0:T(8,128)} %param.6, f32[64,2048]{1,0:T(8,128)} %param.5), kind=kLoop, calls=%fused_computation.37 | loop fusion | flops 2096896 | bytes 2098176 | tf_op jit(solution)/shard_map/reduce_sum | solution.py:193
  2.7 4.0 %collective-permute-start.2 = (bf16[64,1024]{1,0:T(8,128)(2,1)S(1)}, bf16[64,1024]{1,0:T(8,128)(2,1)S(1)}, u32[]{:S(2)}, u32[]{:S(2)}) collective-permute-start(bf16[64,1024]{1,0:T(8,128)(2,1)S(1)} %slice_select_fusion.2), channel_id=1, source_target_pairs={{112,0},{65,1},{48,2},{113,3},{0,4},{33,5},{64,6},{17,7},{96,8},{9... | collective-permute-start | bytes 393224 | tf_op jit(solution)/shard_map/ppermute | solution.py:169
  6.8 0.7 collective-permute-start.1
  7.4 7.7 %shadow.2 = f32[64,4096]{1,0:T(8,128)S(1)} custom-call(bf16[64,2048]{1,0:T(8,128)(2,1)S(1)} %get-tuple-element.87.left_ref, bf16[4096,2048]{1,0:T(8,128)(2,1)} %coupling_ref.7), custom_call_target="tpu_custom_call" | custom-call | flops 1073741824 | bytes 16777216 | tf_op jit(solution)/shard_map/shadow/pallas_call | solution.py:141
  15.3 4.5 %collective-permute-start.3 = (f32[4,64]{1,0:T(4,128)S(1)}, f32[4,64]{1,0:T(4,128)S(1)}, u32[]{:S(2)}, u32[]{:S(2)}) collective-permute-start(f32[4,64]{1,0:T(4,128)S(1)} %pad_maximum_fusion.7), channel_id=1, source_target_pairs={{2,0},{3,1},{0,2},{1,3},{6,4},{7,5},{4,6},{5,7},{10,8},{11,9},{8,1... | collective-permute-start | bytes 3080 | tf_op jit(solution)/shard_map/ppermute | solution.py:169
  19.7 1.6 %collective-permute-done.3 = f32[4,64]{1,0:T(4,128)S(1)} collective-permute-done((f32[4,64]{1,0:T(4,128)S(1)}, f32[4,64]{1,0:T(4,128)S(1)}, u32[]{:S(2)}, u32[]{:S(2)}) %collective-permute-start.3) | collective-permute-done | bytes 1056 | tf_op jit(solution)/shard_map/ppermute | solution.py:169
  21.3 1.2 collective-permute-start.4
  22.5 1.0 collective-permute-start.5
  23.5 2.7 %collective-permute-done.4 = f32[4,64]{1,0:T(4,128)S(1)} collective-permute-done((f32[4,64]{1,0:T(4,128)S(1)}, f32[4,64]{1,0:T(4,128)S(1)}, u32[]{:S(2)}, u32[]{:S(2)}) %collective-permute-start.4) | collective-permute-done | bytes 1056 | tf_op jit(solution)/shard_map/ppermute | solution.py:169
  26.5 1.0 collective-permute-done.5
  27.7 0.4 collective-permute-done.7
  28.1 1.0 collective-permute-done.6
  29.3 0.9 collective-permute-start.8
  30.2 0.5 multiply_bitcast_fusion
  30.7 6.2 %primary.2 = f32[64,2048]{1,0:T(8,128)S(1)} custom-call(bf16[64,4096]{1,0:T(8,128)(2,1)S(1)} %pad_maximum_fusion.left_ref, bf16[4096,2048]{1,0:T(8,128)(2,1)} %coupling_ref.7), custom_call_target="tpu_custom_call" | custom-call | flops 1073741824 | bytes 16777216 | tf_op jit(solution)/shard_map/primary/pallas_call | solution.py:141
  37.2 2.0 %collective-permute-start.9 = (f16[64,1024]{1,0:T(8,128)(2,1)S(1)}, f16[64,1024]{1,0:T(8,128)(2,1)S(1)}, u32[]{:S(2)}, u32[]{:S(2)}) collective-permute-start(f16[64,1024]{1,0:T(8,128)(2,1)S(1)} %select_convert_fusion.2), channel_id=1, source_target_pairs={{32,0},{17,1},{34,2},{19,3},{36,4},{21,5},{38,6},{23,7},{40,8},{25... | collective-permute-start | bytes 393224 | tf_op jit(solution)/shard_map/ppermute | solution.py:169
  39.2 3.0 %collective-permute-done.9 = f16[64,1024]{1,0:T(8,128)(2,1)S(1)} collective-permute-done((f16[64,1024]{1,0:T(8,128)(2,1)S(1)}, f16[64,1024]{1,0:T(8,128)(2,1)S(1)}, u32[]{:S(2)}, u32[]{:S(2)}) %collective-permute-start.9) | collective-permute-done | bytes 131104 | tf_op jit(solution)/shard_map/ppermute | solution.py:169
  42.3 3.3 %collective-permute-done.10 = f16[64,2048]{1,0:T(8,128)(2,1)S(1)} collective-permute-done((f16[64,2048]{1,0:T(8,128)(2,1)S(1)}, f16[64,2048]{1,0:T(8,128)(2,1)S(1)}, u32[]{:S(2)}, u32[]{:S(2)}) %collective-permute-start.10) | collective-permute-done | bytes 262176 | tf_op jit(solution)/shard_map/ppermute | solution.py:169
  45.7 2.0 %collective-permute-start.11 = (f16[64,1024]{1,0:T(8,128)(2,1)S(1)}, f16[64,1024]{1,0:T(8,128)(2,1)S(1)}, u32[]{:S(2)}, u32[]{:S(2)}) collective-permute-start(f16[64,1024]{1,0:T(8,128)(2,1)S(1)} %add_convert_fusion.13), channel_id=1, source_target_pairs={{96,0},{33,1},{98,2},{35,3},{100,4},{37,5},{102,6},{39,7},{104,8},... | collective-permute-start | bytes 393224 | tf_op jit(solution)/shard_map/ppermute | solution.py:169
  47.6 0.4 collective-permute-start.12
  48.0 3.9 %collective-permute-done.11 = f16[64,1024]{1,0:T(8,128)(2,1)S(1)} collective-permute-done((f16[64,1024]{1,0:T(8,128)(2,1)S(1)}, f16[64,1024]{1,0:T(8,128)(2,1)S(1)}, u32[]{:S(2)}, u32[]{:S(2)}) %collective-permute-start.11) | collective-permute-done | bytes 131104 | tf_op jit(solution)/shard_map/ppermute | solution.py:169
  52.0 3.2 %collective-permute-done.12 = f16[64,2048]{1,0:T(8,128)(2,1)S(1)} collective-permute-done((f16[64,2048]{1,0:T(8,128)(2,1)S(1)}, f16[64,2048]{1,0:T(8,128)(2,1)S(1)}, u32[]{:S(2)}, u32[]{:S(2)}) %collective-permute-start.12) | collective-permute-done | bytes 262176 | tf_op jit(solution)/shard_map/ppermute | solution.py:169
  55.3 2.0 %collective-permute-start.13 = (f16[64,1024]{1,0:T(8,128)(2,1)S(1)}, f16[64,1024]{1,0:T(8,128)(2,1)S(1)}, u32[]{:S(2)}, u32[]{:S(2)}) collective-permute-start(f16[64,1024]{1,0:T(8,128)(2,1)S(1)} %add_convert_fusion.12), channel_id=1, source_target_pairs={{16,0},{97,1},{18,2},{99,3},{20,4},{101,5},{22,6},{103,7},{24,8},{... | collective-permute-start | bytes 393224 | tf_op jit(solution)/shard_map/ppermute | solution.py:169
  57.3 0.6 collective-permute-start.14
  58.0 5.3 %collective-permute-done.13 = f16[64,1024]{1,0:T(8,128)(2,1)S(1)} collective-permute-done((f16[64,1024]{1,0:T(8,128)(2,1)S(1)}, f16[64,1024]{1,0:T(8,128)(2,1)S(1)}, u32[]{:S(2)}, u32[]{:S(2)}) %collective-permute-start.13) | collective-permute-done | bytes 131104 | tf_op jit(solution)/shard_map/ppermute | solution.py:169
  63.3 2.6 %collective-permute-done.14 = f16[64,2048]{1,0:T(8,128)(2,1)S(1)} collective-permute-done((f16[64,2048]{1,0:T(8,128)(2,1)S(1)}, f16[64,2048]{1,0:T(8,128)(2,1)S(1)}, u32[]{:S(2)}, u32[]{:S(2)}) %collective-permute-start.14) | collective-permute-done | bytes 262176 | tf_op jit(solution)/shard_map/ppermute | solution.py:169
  65.9 2.2 %collective-permute-start.16 = (f16[64,1024]{1,0:T(8,128)(2,1)S(1)}, f16[64,1024]{1,0:T(8,128)(2,1)S(1)}, u32[]{:S(2)}, u32[]{:S(2)}) collective-permute-start(f16[64,1024]{1,0:T(8,128)(2,1)S(1)} %add_convert_fusion.11), channel_id=1, source_target_pairs={{32,0},{17,1},{34,2},{19,3},{36,4},{21,5},{38,6},{23,7},{40,8},{25... | collective-permute-start | bytes 393224 | tf_op jit(solution)/shard_map/ppermute | solution.py:169
  68.1 0.3 fusion.20
  68.4 0.2 fusion.7
  68.5 0.5 collective-permute-start.15
  69.0 7.7 %shadow.3 = f32[64,4096]{1,0:T(8,128)S(1)} custom-call(bf16[64,2048]{1,0:T(8,128)(2,1)S(1)} %get-tuple-element.78.left_ref, bf16[4096,2048]{1,0:T(8,128)(2,1)} %coupling_ref.7), custom_call_target="tpu_custom_call" | custom-call | flops 1073741824 | bytes 16777216 | tf_op jit(solution)/shard_map/shadow/pallas_call | solution.py:141
  76.9 2.3 %collective-permute-done.15 = bf16[64,1024]{1,0:T(8,128)(2,1)S(1)} collective-permute-done((bf16[64,1024]{1,0:T(8,128)(2,1)S(1)}, bf16[64,1024]{1,0:T(8,128)(2,1)S(1)}, u32[]{:S(2)}, u32[]{:S(2)}) %collective-permute-start.15) | collective-permute-done | bytes 131104 | tf_op jit(solution)/shard_map/ppermute | solution.py:169
  79.4 0.8 select_convert_fusion
  80.1 1.4 multiply_reduce_fusion.1
  81.6 0.7 stack.51
  82.3 0.6 collective-permute-start.20
  82.9 0.8 collective-permute-done.20
  83.7 1.1 add_convert_fusion.6
  84.7 0.2 collective-permute-start.19
  85.0 3.9 %collective-permute-done.17 = bf16[64,1024]{1,0:T(8,128)(2,1)S(1)} collective-permute-done((bf16[64,1024]{1,0:T(8,128)(2,1)S(1)}, bf16[64,1024]{1,0:T(8,128)(2,1)S(1)}, u32[]{:S(2)}, u32[]{:S(2)}) %collective-permute-start.17) | collective-permute-done | bytes 131104 | tf_op jit(solution)/shard_map/ppermute | solution.py:169
  88.9 2.3 %collective-permute-done.19 = f16[64,2048]{1,0:T(8,128)(2,1)S(1)} collective-permute-done((f16[64,2048]{1,0:T(8,128)(2,1)S(1)}, f16[64,2048]{1,0:T(8,128)(2,1)S(1)}, u32[]{:S(2)}, u32[]{:S(2)}) %collective-permute-start.19) | collective-permute-done | bytes 262176 | tf_op jit(solution)/shard_map/ppermute | solution.py:169
  91.3 0.2 collective-permute-start.21
  91.6 1.2 collective-permute-start.22
  92.8 2.3 %collective-permute-done.23 = f32[6,64]{1,0:T(8,128)S(1)} collective-permute-done((f32[6,64]{1,0:T(8,128)S(1)}, f32[6,64]{1,0:T(8,128)S(1)}, u32[]{:S(2)}, u32[]{:S(2)}) %collective-permute-start.23) | collective-permute-done | bytes 1568 | tf_op jit(solution)/shard_map/ppermute | solution.py:169
  95.2 6.2 %primary.3 = f32[64,2048]{1,0:T(8,128)S(1)} custom-call(bf16[64,4096]{1,0:T(8,128)(2,1)S(1)} %pad_maximum_fusion.1.left_ref, bf16[4096,2048]{1,0:T(8,128)(2,1)} %coupling_ref.7), custom_call_target="tpu_custom_call" | custom-call | flops 1073741824 | bytes 16777216 | tf_op jit(solution)/shard_map/primary/pallas_call | solution.py:141
  101.5 0.8 multiply_convert_fusion
  102.3 0.4 collective-permute-start.24
  102.7 1.2 collective-permute-start.26
  104.0 4.1 %collective-permute-start.25 = (f16[64,2048]{1,0:T(8,128)(2,1)S(1)}, f16[64,2048]{1,0:T(8,128)(2,1)S(1)}, u32[]{:S(2)}, u32[]{:S(2)}) collective-permute-start(f16[64,2048]{1,0:T(8,128)(2,1)S(1)} %add_convert_fusion.4), channel_id=1, source_target_pairs={{6,0},{9,1},{4,2},{11,3},{2,4},{13,5},{0,6},{15,7},{14,8},{1,9},{1... | collective-permute-start | bytes 786440 | tf_op jit(solution)/shard_map/ppermute | solution.py:169
  108.1 0.7 collective-permute-done.24
  108.8 0.8 add_convert_fusion.3
  109.6 2.9 %collective-permute-done.25 = f16[64,2048]{1,0:T(8,128)(2,1)S(1)} collective-permute-done((f16[64,2048]{1,0:T(8,128)(2,1)S(1)}, f16[64,2048]{1,0:T(8,128)(2,1)S(1)}, u32[]{:S(2)}, u32[]{:S(2)}) %collective-permute-start.25) | collective-permute-done | bytes 262176 | tf_op jit(solution)/shard_map/ppermute | solution.py:169
  112.5 3.6 %collective-permute-start.27 = (f16[64,2048]{1,0:T(8,128)(2,1)S(1)}, f16[64,2048]{1,0:T(8,128)(2,1)S(1)}, u32[]{:S(2)}, u32[]{:S(2)}) collective-permute-start(f16[64,2048]{1,0:T(8,128)(2,1)S(1)} %add_convert_fusion.3), channel_id=1, source_target_pairs={{96,0},{33,1},{98,2},{35,3},{100,4},{37,5},{102,6},{39,7},{104,8},... | collective-permute-start | bytes 786440 | tf_op jit(solution)/shard_map/ppermute | solution.py:169
  116.1 0.2 multiply_reduce_fusion
  116.4 0.7 fusion.17
  117.1 1.1 collective-permute-done.30
  118.2 1.6 %collective-permute-start.31 = (f32[64]{0:T(128)S(1)}, f32[64]{0:T(128)S(1)}, u32[]{:S(2)}, u32[]{:S(2)}) collective-permute-start(f32[64]{0:T(128)S(1)} %add.157), channel_id=1, source_target_pairs={{32,0},{33,1},{34,2},{35,3},{36,4},{37,5},{38,6},{39,7},{40,8},{41... | collective-permute-start | bytes 776 | tf_op jit(solution)/shard_map/ppermute | solution.py:169
  119.8 2.8 %collective-permute-start.28 = (f16[64,2048]{1,0:T(8,128)(2,1)S(1)}, f16[64,2048]{1,0:T(8,128)(2,1)S(1)}, u32[]{:S(2)}, u32[]{:S(2)}) collective-permute-start(f16[64,2048]{1,0:T(8,128)(2,1)S(1)} %add_convert_fusion.2), channel_id=1, source_target_pairs={{4,0},{5,1},{30,2},{31,3},{34,4},{39,5},{60,6},{57,7},{72,8},{73,9... | collective-permute-start | bytes 786440 | tf_op jit(solution)/shard_map/ppermute | solution.py:169
  122.7 9.6 %collective-permute-done.28 = f16[64,2048]{1,0:T(8,128)(2,1)S(1)} collective-permute-done((f16[64,2048]{1,0:T(8,128)(2,1)S(1)}, f16[64,2048]{1,0:T(8,128)(2,1)S(1)}, u32[]{:S(2)}, u32[]{:S(2)}) %collective-permute-start.28) | collective-permute-done | bytes 262176 | tf_op jit(solution)/shard_map/ppermute | solution.py:169
  132.3 1.1 collective-permute-start.34
  133.3 3.8 %collective-permute-done.32 = f32[64]{0:T(128)S(1)} collective-permute-done((f32[64]{0:T(128)S(1)}, f32[64]{0:T(128)S(1)}, u32[]{:S(2)}, u32[]{:S(2)}) %collective-permute-start.32) | collective-permute-done | bytes 288 | tf_op jit(solution)/shard_map/ppermute | solution.py:169
  137.1 1.1 collective-permute-start.33
  138.2 4.0 %collective-permute-done.33 = f32[64]{0:T(128)S(1)} collective-permute-done((f32[64]{0:T(128)S(1)}, f32[64]{0:T(128)S(1)}, u32[]{:S(2)}, u32[]{:S(2)}) %collective-permute-start.33) | collective-permute-done | bytes 288 | tf_op jit(solution)/shard_map/ppermute | solution.py:169
  142.2 3.6 %multiply_subtract_fusion = (f32[64,2048]{1,0:T(8,128)}, f32[64,2048]{1,0:T(8,128)}, f32[64,2048]{1,0:T(8,128)}, f32[64,2048]{1,0:T(8,128)}) fusion(f16[64,2048]{1,0:T(8,128)(2,1)S(1)} %collective-permute-done.28, f32[64,2048]{1,0:T(8,128)S(1)} %get-tuple-element.79, f32[64,2048]{1,0:T(8,128)S(1)} %copy-done, f16[64,2048]{1,0:T(8,128)(2,1)S(1)} %collective-permute-done.14, ...), kind=kLoop, calls=%fused_computation.2 | loop fusion | flops 7077888 | bytes 5507328 | tf_op jit(solution)/shard_map/sub | solution.py:340
  (84 shorter events, 2.4 us)
Async XLA Ops:
  2.6 4.2 %collective-permute-start = (f32[4,64]{1,0:T(4,128)S(1)}, f32[4,64]{1,0:T(4,128)S(1)}, u32[]{:S(2)}, u32[]{:S(2)}) collective-permute-start(f32[4,64]{1,0:T(4,128)S(1)} %pad_maximum_fusion.5), channel_id=1, source_target_pairs={{1,0},{0,1},{3,2},{2,3},{5,4},{4,5},{7,6},{6,7},{9,8},{8,9},{11,10... | collective-permute-start | bytes 3080 | tf_op jit(solution)/shard_map/ppermute | solution.py:169
  2.7 12.5 %collective-permute-start.2 = (bf16[64,1024]{1,0:T(8,128)(2,1)S(1)}, bf16[64,1024]{1,0:T(8,128)(2,1)S(1)}, u32[]{:S(2)}, u32[]{:S(2)}) collective-permute-start(bf16[64,1024]{1,0:T(8,128)(2,1)S(1)} %slice_select_fusion.2), channel_id=1, source_target_pairs={{112,0},{65,1},{48,2},{113,3},{0,4},{33,5},{64,6},{17,7},{96,8},{9... | collective-permute-start | bytes 393224 | tf_op jit(solution)/shard_map/ppermute | solution.py:169
  6.8 8.4 %collective-permute-start.1 = (f32[4,64]{1,0:T(4,128)S(1)}, f32[4,64]{1,0:T(4,128)S(1)}, u32[]{:S(2)}, u32[]{:S(2)}) collective-permute-start(f32[4,64]{1,0:T(4,128)S(1)} %pad_maximum_fusion.6), channel_id=1, source_target_pairs={{8,0},{9,1},{10,2},{11,3},{12,4},{13,5},{14,6},{15,7},{0,8},{1,9},... | collective-permute-start | bytes 3080 | tf_op jit(solution)/shard_map/ppermute | solution.py:169
  15.2 52.9 %copy-start = (f32[64,2048]{1,0:T(8,128)S(1)}, f32[64,2048]{1,0:T(8,128)}, u32[]{:S(2)}) copy-start(f32[64,2048]{1,0:T(8,128)} %param.7) | copy-start | bytes 1572868
  15.2 52.9 %copy-start.2 = (f32[64,2048]{1,0:T(8,128)S(1)}, f32[64,2048]{1,0:T(8,128)}, u32[]{:S(2)}) copy-start(f32[64,2048]{1,0:T(8,128)} %param.5) | copy-start | bytes 1572868
  15.3 6.0 %collective-permute-start.3 = (f32[4,64]{1,0:T(4,128)S(1)}, f32[4,64]{1,0:T(4,128)S(1)}, u32[]{:S(2)}, u32[]{:S(2)}) collective-permute-start(f32[4,64]{1,0:T(4,128)S(1)} %pad_maximum_fusion.7), channel_id=1, source_target_pairs={{2,0},{3,1},{0,2},{1,3},{6,4},{7,5},{4,6},{5,7},{10,8},{11,9},{8,1... | collective-permute-start | bytes 3080 | tf_op jit(solution)/shard_map/ppermute | solution.py:169
  21.3 4.9 %collective-permute-start.4 = (f32[4,64]{1,0:T(4,128)S(1)}, f32[4,64]{1,0:T(4,128)S(1)}, u32[]{:S(2)}, u32[]{:S(2)}) collective-permute-start(f32[4,64]{1,0:T(4,128)S(1)} %pad_maximum_fusion.8), channel_id=1, source_target_pairs={{6,0},{7,1},{4,2},{5,3},{2,4},{3,5},{0,6},{1,7},{14,8},{15,9},{12,... | collective-permute-start | bytes 3080 | tf_op jit(solution)/shard_map/ppermute | solution.py:169
  22.5 5.0 %collective-permute-start.5 = (bf16[64,1024]{1,0:T(8,128)(2,1)S(1)}, bf16[64,1024]{1,0:T(8,128)(2,1)S(1)}, u32[]{:S(2)}, u32[]{:S(2)}) collective-permute-start(bf16[64,1024]{1,0:T(8,128)(2,1)S(1)} %collective-permute-done.2), channel_id=1, source_target_pairs={{2,0},{3,1},{0,2},{1,3},{6,4},{7,5},{4,6},{5,7},{10,8},{11,9},{8,1... | collective-permute-start | bytes 393224 | tf_op jit(solution)/shard_map/ppermute | solution.py:169
  26.2 4.0 %copy-start.7 = (f32[2,64]{1,0:T(2,128)}, f32[2,64]{1,0:T(2,128)S(1)}, u32[]{:S(2)}) copy-start(f32[2,64]{1,0:T(2,128)S(1)} %get-tuple-element.104) | copy-start | bytes 1540
  26.4 42.0 %copy-start.1 = (f32[64,2048]{1,0:T(8,128)S(1)}, f32[64,2048]{1,0:T(8,128)}, u32[]{:S(2)}) copy-start(f32[64,2048]{1,0:T(8,128)} %param.6) | copy-start | bytes 1572868
  26.4 1.6 %collective-permute-start.7 = (f16[64,2048]{1,0:T(8,128)(2,1)S(1)}, f16[64,2048]{1,0:T(8,128)(2,1)S(1)}, u32[]{:S(2)}, u32[]{:S(2)}) collective-permute-start(f16[64,2048]{1,0:T(8,128)(2,1)S(1)} %select_convert_fusion.1), channel_id=1, source_target_pairs={{1,0},{0,1},{3,2},{2,3},{5,4},{4,5},{7,6},{6,7},{9,8},{8,9},{11,10... | collective-permute-start | bytes 786440 | tf_op jit(solution)/shard_map/ppermute | solution.py:169
  27.6 1.6 %collective-permute-start.6 = (bf16[64,2048]{1,0:T(8,128)(2,1)S(1)}, bf16[64,2048]{1,0:T(8,128)(2,1)S(1)}, u32[]{:S(2)}, u32[]{:S(2)}) collective-permute-start(bf16[64,2048]{1,0:T(8,128)(2,1)S(1)} %pad_maximum_fusion.2), channel_id=1, source_target_pairs={{1,0},{0,1},{3,2},{2,3},{5,4},{4,5},{7,6},{6,7},{9,8},{8,9},{11,10... | collective-permute-start | bytes 786440 | tf_op jit(solution)/shard_map/ppermute | solution.py:169
  29.3 7.7 %collective-permute-start.8 = (f16[64,2048]{1,0:T(8,128)(2,1)S(1)}, f16[64,2048]{1,0:T(8,128)(2,1)S(1)}, u32[]{:S(2)}, u32[]{:S(2)}) collective-permute-start(f16[64,2048]{1,0:T(8,128)(2,1)S(1)} %add_convert_fusion.10), channel_id=1, source_target_pairs={{8,0},{3,1},{10,2},{1,3},{12,4},{7,5},{14,6},{5,7},{0,8},{11,9},{2... | collective-permute-start | bytes 786440 | tf_op jit(solution)/shard_map/ppermute | solution.py:169
  30.7 49.4 %copy-start.5 = (f32[64]{0:T(128)}, f32[64]{0:T(128)S(1)}, u32[]{:S(2)}) copy-start(f32[64]{0:T(128)S(1)} %get-tuple-element.112) | copy-start | bytes 772
  37.2 5.0 %collective-permute-start.9 = (f16[64,1024]{1,0:T(8,128)(2,1)S(1)}, f16[64,1024]{1,0:T(8,128)(2,1)S(1)}, u32[]{:S(2)}, u32[]{:S(2)}) collective-permute-start(f16[64,1024]{1,0:T(8,128)(2,1)S(1)} %select_convert_fusion.2), channel_id=1, source_target_pairs={{32,0},{17,1},{34,2},{19,3},{36,4},{21,5},{38,6},{23,7},{40,8},{25... | collective-permute-start | bytes 393224 | tf_op jit(solution)/shard_map/ppermute | solution.py:169
  39.2 6.4 %collective-permute-start.10 = (f16[64,2048]{1,0:T(8,128)(2,1)S(1)}, f16[64,2048]{1,0:T(8,128)(2,1)S(1)}, u32[]{:S(2)}, u32[]{:S(2)}) collective-permute-start(f16[64,2048]{1,0:T(8,128)(2,1)S(1)} %add_convert_fusion.9), channel_id=1, source_target_pairs={{2,0},{7,1},{0,2},{5,3},{6,4},{3,5},{4,6},{1,7},{10,8},{15,9},{8,1... | collective-permute-start | bytes 786440 | tf_op jit(solution)/shard_map/ppermute | solution.py:169
  45.7 6.3 %collective-permute-start.11 = (f16[64,1024]{1,0:T(8,128)(2,1)S(1)}, f16[64,1024]{1,0:T(8,128)(2,1)S(1)}, u32[]{:S(2)}, u32[]{:S(2)}) collective-permute-start(f16[64,1024]{1,0:T(8,128)(2,1)S(1)} %add_convert_fusion.13), channel_id=1, source_target_pairs={{96,0},{33,1},{98,2},{35,3},{100,4},{37,5},{102,6},{39,7},{104,8},... | collective-permute-start | bytes 393224 | tf_op jit(solution)/shard_map/ppermute | solution.py:169
  47.6 7.6 %collective-permute-start.12 = (f16[64,2048]{1,0:T(8,128)(2,1)S(1)}, f16[64,2048]{1,0:T(8,128)(2,1)S(1)}, u32[]{:S(2)}, u32[]{:S(2)}) collective-permute-start(f16[64,2048]{1,0:T(8,128)(2,1)S(1)} %add_convert_fusion.8), channel_id=1, source_target_pairs={{6,0},{9,1},{4,2},{11,3},{2,4},{13,5},{0,6},{15,7},{14,8},{1,9},{1... | collective-permute-start | bytes 786440 | tf_op jit(solution)/shard_map/ppermute | solution.py:169
  55.3 8.0 %collective-permute-start.13 = (f16[64,1024]{1,0:T(8,128)(2,1)S(1)}, f16[64,1024]{1,0:T(8,128)(2,1)S(1)}, u32[]{:S(2)}, u32[]{:S(2)}) collective-permute-start(f16[64,1024]{1,0:T(8,128)(2,1)S(1)} %add_convert_fusion.12), channel_id=1, source_target_pairs={{16,0},{97,1},{18,2},{99,3},{20,4},{101,5},{22,6},{103,7},{24,8},{... | collective-permute-start | bytes 393224 | tf_op jit(solution)/shard_map/ppermute | solution.py:169
  57.3 8.6 %collective-permute-start.14 = (f16[64,2048]{1,0:T(8,128)(2,1)S(1)}, f16[64,2048]{1,0:T(8,128)(2,1)S(1)}, u32[]{:S(2)}, u32[]{:S(2)}) collective-permute-start(f16[64,2048]{1,0:T(8,128)(2,1)S(1)} %add_convert_fusion.7), channel_id=1, source_target_pairs={{4,0},{5,1},{30,2},{31,3},{34,4},{39,5},{60,6},{57,7},{72,8},{73,9... | collective-permute-start | bytes 786440 | tf_op jit(solution)/shard_map/ppermute | solution.py:169
  65.9 10.9 %collective-permute-start.16 = (f16[64,1024]{1,0:T(8,128)(2,1)S(1)}, f16[64,1024]{1,0:T(8,128)(2,1)S(1)}, u32[]{:S(2)}, u32[]{:S(2)}) collective-permute-start(f16[64,1024]{1,0:T(8,128)(2,1)S(1)} %add_convert_fusion.11), channel_id=1, source_target_pairs={{32,0},{17,1},{34,2},{19,3},{36,4},{21,5},{38,6},{23,7},{40,8},{25... | collective-permute-start | bytes 393224 | tf_op jit(solution)/shard_map/ppermute | solution.py:169
  68.5 10.7 %collective-permute-start.15 = (bf16[64,1024]{1,0:T(8,128)(2,1)S(1)}, bf16[64,1024]{1,0:T(8,128)(2,1)S(1)}, u32[]{:S(2)}, u32[]{:S(2)}) collective-permute-start(bf16[64,1024]{1,0:T(8,128)(2,1)S(1)} %fusion.7), channel_id=1, source_target_pairs={{112,0},{65,1},{48,2},{113,3},{0,4},{33,5},{64,6},{17,7},{96,8},{9... | collective-permute-start | bytes 393224 | tf_op jit(solution)/shard_map/ppermute | solution.py:169
  76.9 3.2 %copy-start.3 = (f16[64,2048]{1,0:T(8,128)(2,1)}, f16[64,2048]{1,0:T(8,128)(2,1)S(1)}, u32[]{:S(2)}) copy-start(f16[64,2048]{1,0:T(8,128)(2,1)S(1)} %pad_maximum_fusion.3) | copy-start | bytes 786436
  80.1 3.5 %collective-permute-start.18 = (f16[64,2048]{1,0:T(8,128)(2,1)}, f16[64,2048]{1,0:T(8,128)(2,1)}, u32[]{:S(2)}, u32[]{:S(2)}) collective-permute-start(f16[64,2048]{1,0:T(8,128)(2,1)} %select_convert_fusion), channel_id=1, source_target_pairs={{1,0},{0,1},{3,2},{2,3},{5,4},{4,5},{7,6},{6,7},{9,8},{8,9},{11,10... | collective-permute-start | bytes 786440 | tf_op jit(solution)/shard_map/ppermute | solution.py:169
  82.3 59.9 %copy-start.4 = (f16[64,2048]{1,0:T(8,128)(2,1)S(1)}, f16[64,2048]{1,0:T(8,128)(2,1)}, u32[]{:S(2)}) copy-start(f16[64,2048]{1,0:T(8,128)(2,1)} %copy-done.3) | copy-start | bytes 786436
  82.3 59.9 %copy-start.6 = (f32[64]{0:T(128)S(1)}, f32[64]{0:T(128)}, u32[]{:S(2)}) copy-start(f32[64]{0:T(128)} %copy-done.5) | copy-start | bytes 772
  82.3 1.4 collective-permute-start.20
  82.9 6.0 %collective-permute-start.17 = (bf16[64,1024]{1,0:T(8,128)(2,1)S(1)}, bf16[64,1024]{1,0:T(8,128)(2,1)S(1)}, u32[]{:S(2)}, u32[]{:S(2)}) collective-permute-start(bf16[64,1024]{1,0:T(8,128)(2,1)S(1)} %collective-permute-done.15), channel_id=1, source_target_pairs={{2,0},{3,1},{0,2},{1,3},{6,4},{7,5},{4,6},{5,7},{10,8},{11,9},{8,1... | collective-permute-start | bytes 393224 | tf_op jit(solution)/shard_map/ppermute | solution.py:169
  84.7 6.5 %collective-permute-start.19 = (f16[64,2048]{1,0:T(8,128)(2,1)S(1)}, f16[64,2048]{1,0:T(8,128)(2,1)S(1)}, u32[]{:S(2)}, u32[]{:S(2)}) collective-permute-start(f16[64,2048]{1,0:T(8,128)(2,1)S(1)} %add_convert_fusion.6), channel_id=1, source_target_pairs={{8,0},{3,1},{10,2},{1,3},{12,4},{7,5},{14,6},{5,7},{0,8},{11,9},{2... | collective-permute-start | bytes 786440 | tf_op jit(solution)/shard_map/ppermute | solution.py:169
  91.3 3.8 %collective-permute-start.21 = (bf16[64,2048]{1,0:T(8,128)(2,1)S(1)}, bf16[64,2048]{1,0:T(8,128)(2,1)S(1)}, u32[]{:S(2)}, u32[]{:S(2)}) collective-permute-start(bf16[64,2048]{1,0:T(8,128)(2,1)S(1)} %pad_maximum_fusion.4), channel_id=1, source_target_pairs={{1,0},{0,1},{3,2},{2,3},{5,4},{4,5},{7,6},{6,7},{9,8},{8,9},{11,10... | collective-permute-start | bytes 786440 | tf_op jit(solution)/shard_map/ppermute | solution.py:169
  91.4 3.6 %collective-permute-start.23 = (f32[6,64]{1,0:T(8,128)S(1)}, f32[6,64]{1,0:T(8,128)S(1)}, u32[]{:S(2)}, u32[]{:S(2)}) collective-permute-start(f32[6,64]{1,0:T(8,128)S(1)} %add.149), channel_id=1, source_target_pairs={{8,0},{9,1},{10,2},{11,3},{12,4},{13,5},{14,6},{15,7},{0,8},{1,9},... | collective-permute-start | bytes 4616 | tf_op jit(solution)/shard_map/ppermute | solution.py:169
  91.6 9.8 %collective-permute-start.22 = (f16[64,2048]{1,0:T(8,128)(2,1)S(1)}, f16[64,2048]{1,0:T(8,128)(2,1)S(1)}, u32[]{:S(2)}, u32[]{:S(2)}) collective-permute-start(f16[64,2048]{1,0:T(8,128)(2,1)S(1)} %add_convert_fusion.5), channel_id=1, source_target_pairs={{2,0},{7,1},{0,2},{5,3},{6,4},{3,5},{4,6},{1,7},{10,8},{15,9},{8,1... | collective-permute-start | bytes 786440 | tf_op jit(solution)/shard_map/ppermute | solution.py:169
  102.3 6.5 %collective-permute-start.24 = (f16[64,2048]{1,0:T(8,128)(2,1)S(1)}, f16[64,2048]{1,0:T(8,128)(2,1)S(1)}, u32[]{:S(2)}, u32[]{:S(2)}) collective-permute-start(f16[64,2048]{1,0:T(8,128)(2,1)S(1)} %multiply_convert_fusion), channel_id=1, source_target_pairs={{32,0},{17,1},{34,2},{19,3},{36,4},{21,5},{38,6},{23,7},{40,8},{25... | collective-permute-start | bytes 786440 | tf_op jit(solution)/shard_map/ppermute | solution.py:169
  102.7 5.3 %collective-permute-start.26 = (f32[6,64]{1,0:T(8,128)S(1)}, f32[6,64]{1,0:T(8,128)S(1)}, u32[]{:S(2)}, u32[]{:S(2)}) collective-permute-start(f32[6,64]{1,0:T(8,128)S(1)} %add.151), channel_id=1, source_target_pairs={{2,0},{3,1},{0,2},{1,3},{6,4},{7,5},{4,6},{5,7},{10,8},{11,9},{8,1... | collective-permute-start | bytes 4616 | tf_op jit(solution)/shard_map/ppermute | solution.py:169
  104.0 8.5 %collective-permute-start.25 = (f16[64,2048]{1,0:T(8,128)(2,1)S(1)}, f16[64,2048]{1,0:T(8,128)(2,1)S(1)}, u32[]{:S(2)}, u32[]{:S(2)}) collective-permute-start(f16[64,2048]{1,0:T(8,128)(2,1)S(1)} %add_convert_fusion.4), channel_id=1, source_target_pairs={{6,0},{9,1},{4,2},{11,3},{2,4},{13,5},{0,6},{15,7},{14,8},{1,9},{1... | collective-permute-start | bytes 786440 | tf_op jit(solution)/shard_map/ppermute | solution.py:169
  112.5 10.1 %collective-permute-start.27 = (f16[64,2048]{1,0:T(8,128)(2,1)S(1)}, f16[64,2048]{1,0:T(8,128)(2,1)S(1)}, u32[]{:S(2)}, u32[]{:S(2)}) collective-permute-start(f16[64,2048]{1,0:T(8,128)(2,1)S(1)} %add_convert_fusion.3), channel_id=1, source_target_pairs={{96,0},{33,1},{98,2},{35,3},{100,4},{37,5},{102,6},{39,7},{104,8},... | collective-permute-start | bytes 786440 | tf_op jit(solution)/shard_map/ppermute | solution.py:169
  116.3 6.3 %collective-permute-start.29 = (f32[6,64]{1,0:T(8,128)S(1)}, f32[6,64]{1,0:T(8,128)S(1)}, u32[]{:S(2)}, u32[]{:S(2)}) collective-permute-start(f32[6,64]{1,0:T(8,128)S(1)} %add.154), channel_id=1, source_target_pairs={{6,0},{7,1},{4,2},{5,3},{2,4},{3,5},{0,6},{1,7},{14,8},{15,9},{12,... | collective-permute-start | bytes 4616 | tf_op jit(solution)/shard_map/ppermute | solution.py:169
  117.1 1.1 collective-permute-start.30
  118.2 4.4 %collective-permute-start.31 = (f32[64]{0:T(128)S(1)}, f32[64]{0:T(128)S(1)}, u32[]{:S(2)}, u32[]{:S(2)}) collective-permute-start(f32[64]{0:T(128)S(1)} %add.157), channel_id=1, source_target_pairs={{32,0},{33,1},{34,2},{35,3},{36,4},{37,5},{38,6},{39,7},{40,8},{41... | collective-permute-start | bytes 776 | tf_op jit(solution)/shard_map/ppermute | solution.py:169
  119.8 12.5 %collective-permute-start.28 = (f16[64,2048]{1,0:T(8,128)(2,1)S(1)}, f16[64,2048]{1,0:T(8,128)(2,1)S(1)}, u32[]{:S(2)}, u32[]{:S(2)}) collective-permute-start(f16[64,2048]{1,0:T(8,128)(2,1)S(1)} %add_convert_fusion.2), channel_id=1, source_target_pairs={{4,0},{5,1},{30,2},{31,3},{34,4},{39,5},{60,6},{57,7},{72,8},{73,9... | collective-permute-start | bytes 786440 | tf_op jit(solution)/shard_map/ppermute | solution.py:169
  132.3 4.8 %collective-permute-start.32 = (f32[64]{0:T(128)S(1)}, f32[64]{0:T(128)S(1)}, u32[]{:S(2)}, u32[]{:S(2)}) collective-permute-start(f32[64]{0:T(128)S(1)} %add.158), channel_id=1, source_target_pairs={{96,0},{97,1},{98,2},{99,3},{100,4},{101,5},{102,6},{103,7},{104,8... | collective-permute-start | bytes 776 | tf_op jit(solution)/shard_map/ppermute | solution.py:169
  132.3 9.9 %collective-permute-start.34 = (f16[64,2048]{1,0:T(8,128)(2,1)S(1)}, f16[64,2048]{1,0:T(8,128)(2,1)S(1)}, u32[]{:S(2)}, u32[]{:S(2)}) collective-permute-start(f16[64,2048]{1,0:T(8,128)(2,1)S(1)} %add_convert_fusion.1), channel_id=1, source_target_pairs={{16,0},{97,1},{18,2},{99,3},{20,4},{101,5},{22,6},{103,7},{24,8},{... | collective-permute-start | bytes 786440 | tf_op jit(solution)/shard_map/ppermute | solution.py:169
  137.1 5.0 %collective-permute-start.33 = (f32[64]{0:T(128)S(1)}, f32[64]{0:T(128)S(1)}, u32[]{:S(2)}, u32[]{:S(2)}) collective-permute-start(f32[64]{0:T(128)S(1)} %add.166), channel_id=1, source_target_pairs={{16,0},{17,1},{18,2},{19,3},{20,4},{21,5},{22,6},{23,7},{24,8},{25... | collective-permute-start | bytes 776 | tf_op jit(solution)/shard_map/ppermute | solution.py:169

commit v6 on v4

--- a/solution.py
+++ b/solution.py
@@ -164,6 +164,44 @@
     return call(shadow_kernel, "shadow", left, coupling, coupling.shape[0], 8)
 
 
+def half_kernel(offset_ref, left_ref, coupling_ref, out_ref, held_ref, sems):
+    width = out_ref.shape[1]
+    columns = pl.ds(pl.multiple_of(offset_ref[0], width), width)
+    for i, at in fetch(coupling_ref.at[:, columns], held_ref, sems):
+        term = jnp.dot(left_ref[:, at], held_ref[at, :], preferred_element_type=F32)
+        if i == 0:
+            out_ref[...] = term
+        else:
+            out_ref[...] += term
+
+
+def primary_half(left, coupling, offset):
+    rows, columns = coupling.shape
+    reps, width = left.shape[0], columns // 2
+    spec = pl.BlockSpec(memory_space=pltpu.VMEM)
+    return pl.pallas_call(
+        half_kernel,
+        name="primary_half",
+        in_specs=[
+            pl.BlockSpec(memory_space=pltpu.SMEM),
+            spec,
+            pl.BlockSpec(memory_space=pltpu.HBM),
+        ],
+        out_specs=spec,
+        out_shape=jax.ShapeDtypeStruct((reps, width), F32),
+        scratch_shapes=[
+            pltpu.VMEM((rows, width), BF16),
+            pltpu.SemaphoreType.DMA((16,)),
+        ],
+        compiler_params=pltpu.CompilerParams(vmem_limit_bytes=16 << 20),
+        cost_estimate=pl.CostEstimate(
+            flops=2 * reps * rows * width,
+            bytes_accessed=2 * rows * width,
+            transcendentals=0,
+        ),
+    )(offset.reshape(1), left, coupling)
+
+
 def move(value, pairs):
     return lax.ppermute(value, AXES, pairs)
 
@@ -208,9 +246,6 @@
         mine, other = pick(first, partial * scale)
         return (mine + move(other.astype(WIRE), CORE).astype(F32)).astype(WIRE)
 
-    def send_half(mine, other):
-        return (mine + move(other.astype(WIRE), ROW_STEPS[0]).astype(F32)).astype(WIRE)
-
     half = pick(low_half, (slope * g).astype(BF16))[0]
     half = move(half, HALF_TO_ROWS)
     shadow_partial = shadow(gs.astype(BF16), coupling)
@@ -220,6 +255,9 @@
     for pairs in SMALL_COL:
         if pairs is SMALL_COL[2]:
             stats, half, shadow_partial = tie(stats, half, shadow_partial)
+            block = put(z_even, half, move(half, Z_PAIR))
+        if pairs is SMALL_COL[3]:
+            stats, block = tie(stats, block)
         other = move(stats, pairs)
         stats = jnp.concatenate(
             [jnp.maximum(stats[:2], other[:2]), stats[2:] + other[2:]]
@@ -232,15 +270,17 @@
     alpha = jnp.where(jnp.isnan(alpha), 1.4, alpha)
     alpha_c = alpha[:, None]
 
-    block = put(z_even, half, move(half, Z_PAIR))
     left = put(first, block, move(block, CORE))
     shadow_held = send_core(shadow_partial, FIRST_SCALE / shadow_top)
     left, shadow_held = tie(left, shadow_held)
-    partial = primary(left, coupling)
+    scale = FIRST_SCALE / top
+    offset = jnp.where(low_half, 1024, 0)
+    other = primary_half(left, coupling, offset)
+    other = move((other * scale).astype(WIRE), ROW_STEPS[0])
     shadow_held = exchange(shadow_held, COL_STEPS[0])
-    partial, shadow_held = tie(partial, shadow_held)
-    scale = FIRST_SCALE / top
-    held = send_half(*pick(low_half, partial * scale))
+    mine = primary_half(left, coupling, 1024 - offset)
+    mine, shadow_held = tie(mine, shadow_held)
+    held = (mine * scale + other.astype(F32)).astype(WIRE)
     shadow_held = exchange(shadow_held, COL_STEPS[1])
     held, shadow_held = tie(held, shadow_held)
     held = exchange(held, ROW_STEPS[1])
@@ -248,7 +288,6 @@
     held, shadow_held = tie(held, shadow_held)
     columns = move(shadow_held, TO_COLS)
     held = exchange(held, ROW_STEPS[2])
-    held, columns = tie(held, columns)
 
     unscale = COUPLE_GAIN / scale
 
@@ -259,7 +298,9 @@
     g_half, keep_half = pick(low_half, g)[0], pick(low_half, keep)[0]
     slope_half = pick(low_half, slope)[0]
     _, u_half = first_step(keep_half, g_half, held)
-    half = move((slope_half * u_half).astype(BF16), HALF_TO_ROWS)
+    u_half = (slope_half * u_half).astype(BF16)
+    half = move(u_half, HALF_TO_ROWS)
+    columns, _ = tie(columns, u_half)
     scale = FIRST_SCALE / shadow_top
     q1 = keep * gs - (COUPLE_GAIN / scale) * slope * columns.astype(F32)
     us = gs - alpha_c * q1

time: 140 us -> 139 us (level)
  waiting for transfers between devices: 65.3 us -> 63.8 us
  Pallas kernels: 27.9 us -> 29.3 us
    pallas_call x0 -> x2, Pallas kernels: none -> 7.57 us  [primary_half(): pl.pallas_call(half_kernel, name='primary_half', in_specs=[pl.BlockSpec(m...]
    pallas_call x4 -> x3, Pallas kernels: 27.9 us -> 21.7 us  [call(): pl.pallas_call(kernel, name=name, in_specs=[spec, pl.BlockSpec(memory_spa...]
    ppermute x31, waiting for transfers between devices: 65.3 us -> 63.8 us  [move(): return lax.ppermute(value, AXES, pairs)]
  transfers between devices with their start and end apart: 31 -> 31, of which waited for: 23 -> 22; matrix products, arithmetic and copies ran while one was open for 1% -> 2% of each run, Pallas kernels for 20% -> 21%
where the time goes in v6:
time: 139 us; the launch traced here: 138 us
  waiting for transfers between devices  63.8 us (46%)
  starting transfers between devices  34.7 us (25%)
  Pallas kernels  29.3 us (21%)
  other arithmetic  8.82 us (6%)
    ppermute x31, waiting for transfers between devices, move(): return lax.ppermute(value, AXES, pairs)  63.8 us
    ppermute x31, starting transfers between devices, move(): return lax.ppermute(value, AXES, pairs)  34.7 us
    pallas_call x3, Pallas kernels, call(): pl.pallas_call(kernel, name=name, in_specs=[spec, pl.BlockSpec(memory_spa...  21.7 us
    pallas_call x2, Pallas kernels, primary_half(): pl.pallas_call(half_kernel, name='primary_half', in_specs=[pl.BlockSpec(m...  7.57 us
    sub x1, other arithmetic, on_device(): shadow_residual = gs - step * q1 - step_next * (lead * q1 + kappa * q2)  2.83 us
  transfers between devices with their start and end apart: 31, of which 22 were waited for; matrix products, arithmetic and copies ran while one was open for 2% of the time, Pallas kernels for 21%

profile of v6, /device:TPU:0, one launch (start us, length us, event | category | flops | bytes accessed | tf_op | source)
XLA Modules:
  0.0 137.7 jit_solution(8296018385469747422)
XLA Ops:
  0.6 1.9 %multiply_reduce_fusion.7 = (f32[64]{0:T(128)S(1)}, f32[64]{0:T(128)S(1)}, f32[64]{0:T(128)S(1)}, f32[64]{0:T(128)S(1)}, bf16[64,2048]{1,0:T(8,128)(2,1)S(1)}, /...) fusion(f32[64,2048]{1,0:T(8,128)} %param.7, f32[64,2048]{1,0:T(8,128)} %param.6, ...), kind=kLoop, calls=%fused_computation.37 | loop fusion | flops 2096896 | bytes 3146752 | tf_op jit(solution)/shard_map/reduce_sum | solution.py:230
  2.6 0.1 collective-permute-start
  2.7 4.0 %collective-permute-start.2 = (bf16[64,1024]{1,0:T(8,128)(2,1)S(1)}, bf16[64,1024]{1,0:T(8,128)(2,1)S(1)}, u32[]{:S(2)}, u32[]{:S(2)}) collective-permute-start(bf16[64,1024]{1,0:T(8,128)(2,1)S(1)} %slice_select_fusion.2), channel_id=1, source_target_pairs={{112,0},{65,1},{48,2},{113,3},{0,4},{33,5},{64,6},{17,7},{96,8},{9... | collective-permute-start | bytes 393224 | tf_op jit(solution)/shard_map/ppermute | solution.py:206
  6.8 0.7 collective-permute-start.1
  7.5 7.7 %shadow.2 = f32[64,4096]{1,0:T(8,128)S(1)} custom-call(bf16[64,2048]{1,0:T(8,128)(2,1)S(1)} %get-tuple-element.87.left_ref, bf16[4096,2048]{1,0:T(8,128)(2,1)} %coupling_ref.9), custom_call_target="tpu_custom_call" | custom-call | flops 1073741824 | bytes 16777216 | tf_op jit(solution)/shard_map/shadow/pallas_call | solution.py:140
  15.3 4.5 %collective-permute-start.3 = (f32[4,64]{1,0:T(4,128)S(1)}, f32[4,64]{1,0:T(4,128)S(1)}, u32[]{:S(2)}, u32[]{:S(2)}) collective-permute-start(f32[4,64]{1,0:T(4,128)S(1)} %pad_maximum_fusion.7), channel_id=1, source_target_pairs={{2,0},{3,1},{0,2},{1,3},{6,4},{7,5},{4,6},{5,7},{10,8},{11,9},{8,1... | collective-permute-start | bytes 3080 | tf_op jit(solution)/shard_map/ppermute | solution.py:206
  19.7 0.1 collective-permute-start.4
  19.8 1.5 %collective-permute-done.3 = f32[4,64]{1,0:T(4,128)S(1)} collective-permute-done((f32[4,64]{1,0:T(4,128)S(1)}, f32[4,64]{1,0:T(4,128)S(1)}, u32[]{:S(2)}, u32[]{:S(2)}) %collective-permute-start.3) | collective-permute-done | bytes 1056 | tf_op jit(solution)/shard_map/ppermute | solution.py:206
  21.3 3.5 %collective-permute-done.4 = bf16[64,1024]{1,0:T(8,128)(2,1)S(1)} collective-permute-done((bf16[64,1024]{1,0:T(8,128)(2,1)S(1)}, bf16[64,1024]{1,0:T(8,128)(2,1)S(1)}, u32[]{:S(2)}, u32[]{:S(2)}) %collective-permute-start.4) | collective-permute-done | bytes 131104 | tf_op jit(solution)/shard_map/ppermute | solution.py:206
  24.8 0.3 collective-permute-start.5
  25.2 4.5 %collective-permute-done.5 = f32[4,64]{1,0:T(4,128)S(1)} collective-permute-done((f32[4,64]{1,0:T(4,128)S(1)}, f32[4,64]{1,0:T(4,128)S(1)}, u32[]{:S(2)}, u32[]{:S(2)}) %collective-permute-start.5) | collective-permute-done | bytes 1056 | tf_op jit(solution)/shard_map/ppermute | solution.py:206
  29.7 0.1 broadcast_multiply_fusion.1
  29.9 0.1 collective-permute-start.7
  30.1 1.4 %collective-permute-done.7 = f16[64,2048]{1,0:T(8,128)(2,1)S(1)} collective-permute-done((f16[64,2048]{1,0:T(8,128)(2,1)S(1)}, f16[64,2048]{1,0:T(8,128)(2,1)S(1)}, u32[]{:S(2)}, u32[]{:S(2)}) %collective-permute-start.7) | collective-permute-done | bytes 262176 | tf_op jit(solution)/shard_map/ppermute | solution.py:206
  31.5 0.1 add_convert_fusion.10
  31.6 0.4 collective-permute-start.8
  32.0 3.8 %primary_half.3 = f32[64,1024]{1,0:T(8,128)S(1)} custom-call(s32[1]{0:T(128)} %bitcast.9.offset_ref, bf16[64,4096]{1,0:T(8,128)(2,1)S(1)} %pad_maximum_fusion.left_ref, bf16[4096,2048]{1,0:T(8,128)(2,1)} %coupling_ref.9), custom_call_target="tpu_custom_call" | custom-call | flops 536870912 | bytes 8388608 | tf_op jit(solution)/shard_map/primary_half/pallas_call | solution.py:182
  35.9 0.1 multiply_convert_fusion.2
  36.0 0.1 collective-permute-start.9
  36.0 3.7 %primary_half.2 = f32[64,1024]{1,0:T(8,128)S(1)} custom-call(s32[1]{0:T(128)} %bitcast.6.offset_ref, bf16[64,4096]{1,0:T(8,128)(2,1)S(1)} %pad_maximum_fusion.left_ref, bf16[4096,2048]{1,0:T(8,128)(2,1)} %coupling_ref.9), custom_call_target="tpu_custom_call" | custom-call | flops 536870912 | bytes 8388608 | tf_op jit(solution)/shard_map/primary_half/pallas_call | solution.py:182
  39.9 0.1 collective-permute-start.10
  40.0 1.0 collective-permute-done.9
  41.0 0.1 add_convert_fusion.13
  41.1 5.2 %collective-permute-done.10 = f16[64,2048]{1,0:T(8,128)(2,1)S(1)} collective-permute-done((f16[64,2048]{1,0:T(8,128)(2,1)S(1)}, f16[64,2048]{1,0:T(8,128)(2,1)S(1)}, u32[]{:S(2)}, u32[]{:S(2)}) %collective-permute-start.10) | collective-permute-done | bytes 262176 | tf_op jit(solution)/shard_map/ppermute | solution.py:206
  46.4 2.7 %collective-permute-start.11 = (f16[64,1024]{1,0:T(8,128)(2,1)S(1)}, f16[64,1024]{1,0:T(8,128)(2,1)S(1)}, u32[]{:S(2)}, u32[]{:S(2)}) collective-permute-start(f16[64,1024]{1,0:T(8,128)(2,1)S(1)} %add_convert_fusion.13), channel_id=1, source_target_pairs={{96,0},{33,1},{98,2},{35,3},{100,4},{37,5},{102,6},{39,7},{104,8},... | collective-permute-start | bytes 393224 | tf_op jit(solution)/shard_map/ppermute | solution.py:206
  49.1 1.1 collective-permute-start.12
  50.2 2.4 %collective-permute-done.11 = f16[64,1024]{1,0:T(8,128)(2,1)S(1)} collective-permute-done((f16[64,1024]{1,0:T(8,128)(2,1)S(1)}, f16[64,1024]{1,0:T(8,128)(2,1)S(1)}, u32[]{:S(2)}, u32[]{:S(2)}) %collective-permute-start.11) | collective-permute-done | bytes 131104 | tf_op jit(solution)/shard_map/ppermute | solution.py:206
  52.7 4.0 %collective-permute-done.12 = f16[64,2048]{1,0:T(8,128)(2,1)S(1)} collective-permute-done((f16[64,2048]{1,0:T(8,128)(2,1)S(1)}, f16[64,2048]{1,0:T(8,128)(2,1)S(1)}, u32[]{:S(2)}, u32[]{:S(2)}) %collective-permute-start.12) | collective-permute-done | bytes 262176 | tf_op jit(solution)/shard_map/ppermute | solution.py:206
  56.8 1.8 %collective-permute-start.13 = (f16[64,1024]{1,0:T(8,128)(2,1)S(1)}, f16[64,1024]{1,0:T(8,128)(2,1)S(1)}, u32[]{:S(2)}, u32[]{:S(2)}) collective-permute-start(f16[64,1024]{1,0:T(8,128)(2,1)S(1)} %add_convert_fusion.12), channel_id=1, source_target_pairs={{16,0},{97,1},{18,2},{99,3},{20,4},{101,5},{22,6},{103,7},{24,8},{... | collective-permute-start | bytes 393224 | tf_op jit(solution)/shard_map/ppermute | solution.py:206
  58.6 1.5 %collective-permute-start.15 = (f16[64,2048]{1,0:T(8,128)(2,1)S(1)}, f16[64,2048]{1,0:T(8,128)(2,1)S(1)}, u32[]{:S(2)}, u32[]{:S(2)}) collective-permute-start(f16[64,2048]{1,0:T(8,128)(2,1)S(1)} %add_convert_fusion.7), channel_id=1, source_target_pairs={{4,0},{5,1},{30,2},{31,3},{34,4},{39,5},{60,6},{57,7},{72,8},{73,9... | collective-permute-start | bytes 786440 | tf_op jit(solution)/shard_map/ppermute | solution.py:206
  60.1 4.7 %collective-permute-done.13 = f16[64,1024]{1,0:T(8,128)(2,1)S(1)} collective-permute-done((f16[64,1024]{1,0:T(8,128)(2,1)S(1)}, f16[64,1024]{1,0:T(8,128)(2,1)S(1)}, u32[]{:S(2)}, u32[]{:S(2)}) %collective-permute-start.13) | collective-permute-done | bytes 131104 | tf_op jit(solution)/shard_map/ppermute | solution.py:206
  64.8 0.2 fusion.6
  64.9 0.3 collective-permute-start.14
  65.2 2.6 %collective-permute-done.15 = f16[64,2048]{1,0:T(8,128)(2,1)S(1)} collective-permute-done((f16[64,2048]{1,0:T(8,128)(2,1)S(1)}, f16[64,2048]{1,0:T(8,128)(2,1)S(1)}, u32[]{:S(2)}, u32[]{:S(2)}) %collective-permute-start.15) | collective-permute-done | bytes 262176 | tf_op jit(solution)/shard_map/ppermute | solution.py:206
  67.8 0.2 fusion.15
  68.0 7.7 %shadow.3 = f32[64,4096]{1,0:T(8,128)S(1)} custom-call(bf16[64,2048]{1,0:T(8,128)(2,1)S(1)} %get-tuple-element.76.left_ref, bf16[4096,2048]{1,0:T(8,128)(2,1)} %coupling_ref.9), custom_call_target="tpu_custom_call" | custom-call | flops 1073741824 | bytes 16777216 | tf_op jit(solution)/shard_map/shadow/pallas_call | solution.py:140
  75.7 1.6 %collective-permute-start.16 = (bf16[64,1024]{1,0:T(8,128)(2,1)S(1)}, bf16[64,1024]{1,0:T(8,128)(2,1)S(1)}, u32[]{:S(2)}, u32[]{:S(2)}) collective-permute-start(bf16[64,1024]{1,0:T(8,128)(2,1)S(1)} %collective-permute-done.14), channel_id=1, source_target_pairs={{2,0},{3,1},{0,2},{1,3},{6,4},{7,5},{4,6},{5,7},{10,8},{11,9},{8,1... | collective-permute-start | bytes 393224 | tf_op jit(solution)/shard_map/ppermute | solution.py:206
  77.3 0.1 broadcast_multiply_fusion
  77.6 3.1 %collective-permute-done.16 = bf16[64,1024]{1,0:T(8,128)(2,1)S(1)} collective-permute-done((bf16[64,1024]{1,0:T(8,128)(2,1)S(1)}, bf16[64,1024]{1,0:T(8,128)(2,1)S(1)}, u32[]{:S(2)}, u32[]{:S(2)}) %collective-permute-start.16) | collective-permute-done | bytes 131104 | tf_op jit(solution)/shard_map/ppermute | solution.py:206
  80.8 1.5 %collective-permute-done.18 = f16[64,1024]{1,0:T(8,128)(2,1)S(1)} collective-permute-done((f16[64,1024]{1,0:T(8,128)(2,1)S(1)}, f16[64,1024]{1,0:T(8,128)(2,1)S(1)}, u32[]{:S(2)}, u32[]{:S(2)}) %collective-permute-start.18) | collective-permute-done | bytes 131104 | tf_op jit(solution)/shard_map/ppermute | solution.py:206
  82.5 0.1 add_convert_fusion.6
  82.8 1.4 %collective-permute-done.19 = bf16[64,2048]{1,0:T(8,128)(2,1)S(1)} collective-permute-done((bf16[64,2048]{1,0:T(8,128)(2,1)S(1)}, bf16[64,2048]{1,0:T(8,128)(2,1)S(1)}, u32[]{:S(2)}, u32[]{:S(2)}) %collective-permute-start.19) | collective-permute-done | bytes 262176 | tf_op jit(solution)/shard_map/ppermute | solution.py:206
  84.3 6.2 %primary.1 = f32[64,2048]{1,0:T(8,128)S(1)} custom-call(bf16[64,4096]{1,0:T(8,128)(2,1)S(1)} %pad_maximum_fusion.1.left_ref, bf16[4096,2048]{1,0:T(8,128)(2,1)} %coupling_ref.9), custom_call_target="tpu_custom_call" | custom-call | flops 1073741824 | bytes 16777216 | tf_op jit(solution)/shard_map/primary/pallas_call | solution.py:140
  90.6 0.1 multiply_convert_fusion
  90.8 1.9 %collective-permute-start.22 = (f16[64,2048]{1,0:T(8,128)(2,1)S(1)}, f16[64,2048]{1,0:T(8,128)(2,1)S(1)}, u32[]{:S(2)}, u32[]{:S(2)}) collective-permute-start(f16[64,2048]{1,0:T(8,128)(2,1)S(1)} %add_convert_fusion.5), channel_id=1, source_target_pairs={{2,0},{7,1},{0,2},{5,3},{6,4},{3,5},{4,6},{1,7},{10,8},{15,9},{8,1... | collective-permute-start | bytes 786440 | tf_op jit(solution)/shard_map/ppermute | solution.py:206
  92.7 4.5 %collective-permute-done.21 = f16[64,2048]{1,0:T(8,128)(2,1)S(1)} collective-permute-done((f16[64,2048]{1,0:T(8,128)(2,1)S(1)}, f16[64,2048]{1,0:T(8,128)(2,1)S(1)}, u32[]{:S(2)}, u32[]{:S(2)}) %collective-permute-start.21) | collective-permute-done | bytes 262176 | tf_op jit(solution)/shard_map/ppermute | solution.py:206
  97.2 0.1 add_convert_fusion.4
  97.4 2.4 %collective-permute-start.23 = (f16[64,2048]{1,0:T(8,128)(2,1)S(1)}, f16[64,2048]{1,0:T(8,128)(2,1)S(1)}, u32[]{:S(2)}, u32[]{:S(2)}) collective-permute-start(f16[64,2048]{1,0:T(8,128)(2,1)S(1)} %add_convert_fusion.4), channel_id=1, source_target_pairs={{96,0},{33,1},{98,2},{35,3},{100,4},{37,5},{102,6},{39,7},{104,8},... | collective-permute-start | bytes 786440 | tf_op jit(solution)/shard_map/ppermute | solution.py:206
  99.9 2.3 %collective-permute-start.24 = (f16[64,2048]{1,0:T(8,128)(2,1)S(1)}, f16[64,2048]{1,0:T(8,128)(2,1)S(1)}, u32[]{:S(2)}, u32[]{:S(2)}) collective-permute-start(f16[64,2048]{1,0:T(8,128)(2,1)S(1)} %add_convert_fusion.3), channel_id=1, source_target_pairs={{6,0},{9,1},{4,2},{11,3},{2,4},{13,5},{0,6},{15,7},{14,8},{1,9},{1... | collective-permute-start | bytes 786440 | tf_op jit(solution)/shard_map/ppermute | solution.py:206
  102.1 3.0 %collective-permute-done.23 = f16[64,2048]{1,0:T(8,128)(2,1)S(1)} collective-permute-done((f16[64,2048]{1,0:T(8,128)(2,1)S(1)}, f16[64,2048]{1,0:T(8,128)(2,1)S(1)}, u32[]{:S(2)}, u32[]{:S(2)}) %collective-permute-start.23) | collective-permute-done | bytes 262176 | tf_op jit(solution)/shard_map/ppermute | solution.py:206
  105.2 2.2 %collective-permute-done.24 = f16[64,2048]{1,0:T(8,128)(2,1)S(1)} collective-permute-done((f16[64,2048]{1,0:T(8,128)(2,1)S(1)}, f16[64,2048]{1,0:T(8,128)(2,1)S(1)}, u32[]{:S(2)}, u32[]{:S(2)}) %collective-permute-start.24) | collective-permute-done | bytes 262176 | tf_op jit(solution)/shard_map/ppermute | solution.py:206
  107.4 0.8 add_convert_fusion.1
  108.2 3.6 %collective-permute-start.25 = (f16[64,2048]{1,0:T(8,128)(2,1)S(1)}, f16[64,2048]{1,0:T(8,128)(2,1)S(1)}, u32[]{:S(2)}, u32[]{:S(2)}) collective-permute-start(f16[64,2048]{1,0:T(8,128)(2,1)S(1)} %add_convert_fusion.2), channel_id=1, source_target_pairs={{16,0},{97,1},{18,2},{99,3},{20,4},{101,5},{22,6},{103,7},{24,8},{... | collective-permute-start | bytes 786440 | tf_op jit(solution)/shard_map/ppermute | solution.py:206
  111.9 2.1 %collective-permute-start.27 = (f16[64,2048]{1,0:T(8,128)(2,1)}, f16[64,2048]{1,0:T(8,128)(2,1)S(1)}, u32[]{:S(2)}, u32[]{:S(2)}) collective-permute-start(f16[64,2048]{1,0:T(8,128)(2,1)} %add_convert_fusion.1), channel_id=1, source_target_pairs={{4,0},{5,1},{30,2},{31,3},{34,4},{39,5},{60,6},{57,7},{72,8},{73,9... | collective-permute-start | bytes 786440 | tf_op jit(solution)/shard_map/ppermute | solution.py:206
  114.0 4.9 %collective-permute-done.25 = f16[64,2048]{1,0:T(8,128)(2,1)S(1)} collective-permute-done((f16[64,2048]{1,0:T(8,128)(2,1)S(1)}, f16[64,2048]{1,0:T(8,128)(2,1)S(1)}, u32[]{:S(2)}, u32[]{:S(2)}) %collective-permute-start.25) | collective-permute-done | bytes 262176 | tf_op jit(solution)/shard_map/ppermute | solution.py:206
  118.9 0.8 multiply_reduce_fusion
  119.8 1.2 collective-permute-done.26
  120.9 1.8 %collective-permute-done.27 = f16[64,2048]{1,0:T(8,128)(2,1)S(1)} collective-permute-done((f16[64,2048]{1,0:T(8,128)(2,1)}, f16[64,2048]{1,0:T(8,128)(2,1)S(1)}, u32[]{:S(2)}, u32[]{:S(2)}) %collective-permute-start.27) | collective-permute-done | bytes 262176 | tf_op jit(solution)/shard_map/ppermute | solution.py:206
  122.8 1.4 %collective-permute-start.28 = (f32[6,64]{1,0:T(8,128)S(1)}, f32[6,64]{1,0:T(8,128)S(1)}, u32[]{:S(2)}, u32[]{:S(2)}) collective-permute-start(f32[6,64]{1,0:T(8,128)S(1)} %add.166), channel_id=1, source_target_pairs={{8,0},{9,1},{10,2},{11,3},{12,4},{13,5},{14,6},{15,7},{0,8},{1,9},... | collective-permute-start | bytes 4616 | tf_op jit(solution)/shard_map/ppermute | solution.py:206
  124.1 2.2 %collective-permute-done.28 = f32[6,64]{1,0:T(8,128)S(1)} collective-permute-done((f32[6,64]{1,0:T(8,128)S(1)}, f32[6,64]{1,0:T(8,128)S(1)}, u32[]{:S(2)}, u32[]{:S(2)}) %collective-permute-start.28) | collective-permute-done | bytes 1568 | tf_op jit(solution)/shard_map/ppermute | solution.py:206
  126.4 1.2 collective-permute-start.29
  127.6 2.4 %collective-permute-done.29 = f32[6,64]{1,0:T(8,128)S(1)} collective-permute-done((f32[6,64]{1,0:T(8,128)S(1)}, f32[6,64]{1,0:T(8,128)S(1)}, u32[]{:S(2)}, u32[]{:S(2)}) %collective-permute-start.29) | collective-permute-done | bytes 1568 | tf_op jit(solution)/shard_map/ppermute | solution.py:206
  130.0 4.8 %collective-permute-done.30 = f32[6,64]{1,0:T(8,128)S(1)} collective-permute-done((f32[6,64]{1,0:T(8,128)S(1)}, f32[6,64]{1,0:T(8,128)S(1)}, u32[]{:S(2)}, u32[]{:S(2)}) %collective-permute-start.30) | collective-permute-done | bytes 1568 | tf_op jit(solution)/shard_map/ppermute | solution.py:206
  134.8 2.8 %multiply_subtract_fusion = (f32[64,2048]{1,0:T(8,128)}, f32[64,2048]{1,0:T(8,128)}, f32[64,2048]{1,0:T(8,128)}, f32[64,2048]{1,0:T(8,128)}) fusion(f16[64,2048]{1,0:T(8,128)(2,1)S(1)} %collective-permute-done.27, f32[64,2048]{1,0:T(8,128)S(1)} %get-tuple-element.77, f32[64,2048]{1,0:T(8,128)S(1)} %copy-done, f16[64,2048]{1,0:T(8,128)(2,1)S(1)} %collective-permute-done.15, ...), kind=kLoop, calls=%fused_computation.2 | loop fusion | flops 7077888 | bytes 5507328 | tf_op jit(solution)/shard_map/sub | solution.py:370
  (60 shorter events, 1.7 us)
Async XLA Ops:
  2.6 4.2 %collective-permute-start = (f32[4,64]{1,0:T(4,128)S(1)}, f32[4,64]{1,0:T(4,128)S(1)}, u32[]{:S(2)}, u32[]{:S(2)}) collective-permute-start(f32[4,64]{1,0:T(4,128)S(1)} %pad_maximum_fusion.5), channel_id=1, source_target_pairs={{1,0},{0,1},{3,2},{2,3},{5,4},{4,5},{7,6},{6,7},{9,8},{8,9},{11,10... | collective-permute-start | bytes 3080 | tf_op jit(solution)/shard_map/ppermute | solution.py:206
  2.7 12.5 %collective-permute-start.2 = (bf16[64,1024]{1,0:T(8,128)(2,1)S(1)}, bf16[64,1024]{1,0:T(8,128)(2,1)S(1)}, u32[]{:S(2)}, u32[]{:S(2)}) collective-permute-start(bf16[64,1024]{1,0:T(8,128)(2,1)S(1)} %slice_select_fusion.2), channel_id=1, source_target_pairs={{112,0},{65,1},{48,2},{113,3},{0,4},{33,5},{64,6},{17,7},{96,8},{9... | collective-permute-start | bytes 393224 | tf_op jit(solution)/shard_map/ppermute | solution.py:206
  6.8 8.4 %collective-permute-start.1 = (f32[4,64]{1,0:T(4,128)S(1)}, f32[4,64]{1,0:T(4,128)S(1)}, u32[]{:S(2)}, u32[]{:S(2)}) collective-permute-start(f32[4,64]{1,0:T(4,128)S(1)} %pad_maximum_fusion.6), channel_id=1, source_target_pairs={{8,0},{9,1},{10,2},{11,3},{12,4},{13,5},{14,6},{15,7},{0,8},{1,9},... | collective-permute-start | bytes 3080 | tf_op jit(solution)/shard_map/ppermute | solution.py:206
  15.3 6.0 %collective-permute-start.3 = (f32[4,64]{1,0:T(4,128)S(1)}, f32[4,64]{1,0:T(4,128)S(1)}, u32[]{:S(2)}, u32[]{:S(2)}) collective-permute-start(f32[4,64]{1,0:T(4,128)S(1)} %pad_maximum_fusion.7), channel_id=1, source_target_pairs={{2,0},{3,1},{0,2},{1,3},{6,4},{7,5},{4,6},{5,7},{10,8},{11,9},{8,1... | collective-permute-start | bytes 3080 | tf_op jit(solution)/shard_map/ppermute | solution.py:206
  19.7 5.0 %collective-permute-start.4 = (bf16[64,1024]{1,0:T(8,128)(2,1)S(1)}, bf16[64,1024]{1,0:T(8,128)(2,1)S(1)}, u32[]{:S(2)}, u32[]{:S(2)}) collective-permute-start(bf16[64,1024]{1,0:T(8,128)(2,1)S(1)} %collective-permute-done.2), channel_id=1, source_target_pairs={{2,0},{3,1},{0,2},{1,3},{6,4},{7,5},{4,6},{5,7},{10,8},{11,9},{8,1... | collective-permute-start | bytes 393224 | tf_op jit(solution)/shard_map/ppermute | solution.py:206
  24.8 4.9 %collective-permute-start.5 = (f32[4,64]{1,0:T(4,128)S(1)}, f32[4,64]{1,0:T(4,128)S(1)}, u32[]{:S(2)}, u32[]{:S(2)}) collective-permute-start(f32[4,64]{1,0:T(4,128)S(1)} %pad_maximum_fusion.8), channel_id=1, source_target_pairs={{6,0},{7,1},{4,2},{5,3},{2,4},{3,5},{0,6},{1,7},{14,8},{15,9},{12,... | collective-permute-start | bytes 3080 | tf_op jit(solution)/shard_map/ppermute | solution.py:206
  25.2 4.9 %collective-permute-start.6 = (bf16[64,2048]{1,0:T(8,128)(2,1)S(1)}, bf16[64,2048]{1,0:T(8,128)(2,1)S(1)}, u32[]{:S(2)}, u32[]{:S(2)}) collective-permute-start(bf16[64,2048]{1,0:T(8,128)(2,1)S(1)} %pad_maximum_fusion.2), channel_id=1, source_target_pairs={{1,0},{0,1},{3,2},{2,3},{5,4},{4,5},{7,6},{6,7},{9,8},{8,9},{11,10... | collective-permute-start | bytes 786440 | tf_op jit(solution)/shard_map/ppermute | solution.py:206
  29.9 1.6 %collective-permute-start.7 = (f16[64,2048]{1,0:T(8,128)(2,1)S(1)}, f16[64,2048]{1,0:T(8,128)(2,1)S(1)}, u32[]{:S(2)}, u32[]{:S(2)}) collective-permute-start(f16[64,2048]{1,0:T(8,128)(2,1)S(1)} %select_convert_fusion.1), channel_id=1, source_target_pairs={{1,0},{0,1},{3,2},{2,3},{5,4},{4,5},{7,6},{6,7},{9,8},{8,9},{11,10... | collective-permute-start | bytes 786440 | tf_op jit(solution)/shard_map/ppermute | solution.py:206
  31.6 8.2 %collective-permute-start.8 = (f16[64,2048]{1,0:T(8,128)(2,1)S(1)}, f16[64,2048]{1,0:T(8,128)(2,1)S(1)}, u32[]{:S(2)}, u32[]{:S(2)}) collective-permute-start(f16[64,2048]{1,0:T(8,128)(2,1)S(1)} %add_convert_fusion.10), channel_id=1, source_target_pairs={{8,0},{3,1},{10,2},{1,3},{12,4},{7,5},{14,6},{5,7},{0,8},{11,9},{2... | collective-permute-start | bytes 786440 | tf_op jit(solution)/shard_map/ppermute | solution.py:206
  32.0 32.8 %copy-start.1 = (f32[64,2048]{1,0:T(8,128)S(1)}, f32[64,2048]{1,0:T(8,128)}, u32[]{:S(2)}) copy-start(f32[64,2048]{1,0:T(8,128)} %param.6) | copy-start | bytes 1572868
  32.0 35.7 %copy-start = (f32[64,2048]{1,0:T(8,128)S(1)}, f32[64,2048]{1,0:T(8,128)}, u32[]{:S(2)}) copy-start(f32[64,2048]{1,0:T(8,128)} %param.7) | copy-start | bytes 1572868
  32.0 35.7 %copy-start.2 = (f32[64,2048]{1,0:T(8,128)S(1)}, f32[64,2048]{1,0:T(8,128)}, u32[]{:S(2)}) copy-start(f32[64,2048]{1,0:T(8,128)} %param.5) | copy-start | bytes 1572868
  36.0 5.0 %collective-permute-start.9 = (f16[64,1024]{1,0:T(8,128)(2,1)S(1)}, f16[64,1024]{1,0:T(8,128)(2,1)S(1)}, u32[]{:S(2)}, u32[]{:S(2)}) collective-permute-start(f16[64,1024]{1,0:T(8,128)(2,1)S(1)} %multiply_convert_fusion.2), channel_id=1, source_target_pairs={{32,0},{17,1},{34,2},{19,3},{36,4},{21,5},{38,6},{23,7},{40,8},{25... | collective-permute-start | bytes 393224 | tf_op jit(solution)/shard_map/ppermute | solution.py:206
  39.9 6.5 %collective-permute-start.10 = (f16[64,2048]{1,0:T(8,128)(2,1)S(1)}, f16[64,2048]{1,0:T(8,128)(2,1)S(1)}, u32[]{:S(2)}, u32[]{:S(2)}) collective-permute-start(f16[64,2048]{1,0:T(8,128)(2,1)S(1)} %add_convert_fusion.9), channel_id=1, source_target_pairs={{2,0},{7,1},{0,2},{5,3},{6,4},{3,5},{4,6},{1,7},{10,8},{15,9},{8,1... | collective-permute-start | bytes 786440 | tf_op jit(solution)/shard_map/ppermute | solution.py:206
  46.4 6.3 %collective-permute-start.11 = (f16[64,1024]{1,0:T(8,128)(2,1)S(1)}, f16[64,1024]{1,0:T(8,128)(2,1)S(1)}, u32[]{:S(2)}, u32[]{:S(2)}) collective-permute-start(f16[64,1024]{1,0:T(8,128)(2,1)S(1)} %add_convert_fusion.13), channel_id=1, source_target_pairs={{96,0},{33,1},{98,2},{35,3},{100,4},{37,5},{102,6},{39,7},{104,8},... | collective-permute-start | bytes 393224 | tf_op jit(solution)/shard_map/ppermute | solution.py:206
  49.1 7.6 %collective-permute-start.12 = (f16[64,2048]{1,0:T(8,128)(2,1)S(1)}, f16[64,2048]{1,0:T(8,128)(2,1)S(1)}, u32[]{:S(2)}, u32[]{:S(2)}) collective-permute-start(f16[64,2048]{1,0:T(8,128)(2,1)S(1)} %add_convert_fusion.8), channel_id=1, source_target_pairs={{6,0},{9,1},{4,2},{11,3},{2,4},{13,5},{0,6},{15,7},{14,8},{1,9},{1... | collective-permute-start | bytes 786440 | tf_op jit(solution)/shard_map/ppermute | solution.py:206
  56.8 8.0 %collective-permute-start.13 = (f16[64,1024]{1,0:T(8,128)(2,1)S(1)}, f16[64,1024]{1,0:T(8,128)(2,1)S(1)}, u32[]{:S(2)}, u32[]{:S(2)}) collective-permute-start(f16[64,1024]{1,0:T(8,128)(2,1)S(1)} %add_convert_fusion.12), channel_id=1, source_target_pairs={{16,0},{97,1},{18,2},{99,3},{20,4},{101,5},{22,6},{103,7},{24,8},{... | collective-permute-start | bytes 393224 | tf_op jit(solution)/shard_map/ppermute | solution.py:206
  58.6 9.1 %collective-permute-start.15 = (f16[64,2048]{1,0:T(8,128)(2,1)S(1)}, f16[64,2048]{1,0:T(8,128)(2,1)S(1)}, u32[]{:S(2)}, u32[]{:S(2)}) collective-permute-start(f16[64,2048]{1,0:T(8,128)(2,1)S(1)} %add_convert_fusion.7), channel_id=1, source_target_pairs={{4,0},{5,1},{30,2},{31,3},{34,4},{39,5},{60,6},{57,7},{72,8},{73,9... | collective-permute-start | bytes 786440 | tf_op jit(solution)/shard_map/ppermute | solution.py:206
  64.9 10.8 %collective-permute-start.14 = (bf16[64,1024]{1,0:T(8,128)(2,1)S(1)}, bf16[64,1024]{1,0:T(8,128)(2,1)S(1)}, u32[]{:S(2)}, u32[]{:S(2)}) collective-permute-start(bf16[64,1024]{1,0:T(8,128)(2,1)S(1)} %get-tuple-element.78), channel_id=1, source_target_pairs={{112,0},{65,1},{48,2},{113,3},{0,4},{33,5},{64,6},{17,7},{96,8},{9... | collective-permute-start | bytes 393224 | tf_op jit(solution)/shard_map/ppermute | solution.py:206
  75.7 5.0 %collective-permute-start.16 = (bf16[64,1024]{1,0:T(8,128)(2,1)S(1)}, bf16[64,1024]{1,0:T(8,128)(2,1)S(1)}, u32[]{:S(2)}, u32[]{:S(2)}) collective-permute-start(bf16[64,1024]{1,0:T(8,128)(2,1)S(1)} %collective-permute-done.14), channel_id=1, source_target_pairs={{2,0},{3,1},{0,2},{1,3},{6,4},{7,5},{4,6},{5,7},{10,8},{11,9},{8,1... | collective-permute-start | bytes 393224 | tf_op jit(solution)/shard_map/ppermute | solution.py:206
  77.3 5.0 %collective-permute-start.18 = (f16[64,1024]{1,0:T(8,128)(2,1)S(1)}, f16[64,1024]{1,0:T(8,128)(2,1)S(1)}, u32[]{:S(2)}, u32[]{:S(2)}) collective-permute-start(f16[64,1024]{1,0:T(8,128)(2,1)S(1)} %get-tuple-element.48), channel_id=1, source_target_pairs={{32,0},{17,1},{34,2},{19,3},{36,4},{21,5},{38,6},{23,7},{40,8},{25... | collective-permute-start | bytes 393224 | tf_op jit(solution)/shard_map/ppermute | solution.py:206
  77.5 4.9 %collective-permute-start.17 = (f16[64,2048]{1,0:T(8,128)(2,1)S(1)}, f16[64,2048]{1,0:T(8,128)(2,1)S(1)}, u32[]{:S(2)}, u32[]{:S(2)}) collective-permute-start(f16[64,2048]{1,0:T(8,128)(2,1)S(1)} %select_convert_fusion), channel_id=1, source_target_pairs={{1,0},{0,1},{3,2},{2,3},{5,4},{4,5},{7,6},{6,7},{9,8},{8,9},{11,10... | collective-permute-start | bytes 786440 | tf_op jit(solution)/shard_map/ppermute | solution.py:206
  82.6 1.6 %collective-permute-start.19 = (bf16[64,2048]{1,0:T(8,128)(2,1)S(1)}, bf16[64,2048]{1,0:T(8,128)(2,1)S(1)}, u32[]{:S(2)}, u32[]{:S(2)}) collective-permute-start(bf16[64,2048]{1,0:T(8,128)(2,1)S(1)} %pad_maximum_fusion.3), channel_id=1, source_target_pairs={{1,0},{0,1},{3,2},{2,3},{5,4},{4,5},{7,6},{6,7},{9,8},{8,9},{11,10... | collective-permute-start | bytes 786440 | tf_op jit(solution)/shard_map/ppermute | solution.py:206
  82.7 7.9 %collective-permute-start.20 = (f16[64,2048]{1,0:T(8,128)(2,1)S(1)}, f16[64,2048]{1,0:T(8,128)(2,1)S(1)}, u32[]{:S(2)}, u32[]{:S(2)}) collective-permute-start(f16[64,2048]{1,0:T(8,128)(2,1)S(1)} %add_convert_fusion.6), channel_id=1, source_target_pairs={{8,0},{3,1},{10,2},{1,3},{12,4},{7,5},{14,6},{5,7},{0,8},{11,9},{2... | collective-permute-start | bytes 786440 | tf_op jit(solution)/shard_map/ppermute | solution.py:206
  90.8 6.5 %collective-permute-start.21 = (f16[64,2048]{1,0:T(8,128)(2,1)S(1)}, f16[64,2048]{1,0:T(8,128)(2,1)S(1)}, u32[]{:S(2)}, u32[]{:S(2)}) collective-permute-start(f16[64,2048]{1,0:T(8,128)(2,1)S(1)} %multiply_convert_fusion), channel_id=1, source_target_pairs={{32,0},{17,1},{34,2},{19,3},{36,4},{21,5},{38,6},{23,7},{40,8},{25... | collective-permute-start | bytes 786440 | tf_op jit(solution)/shard_map/ppermute | solution.py:206
  90.8 6.5 %collective-permute-start.22 = (f16[64,2048]{1,0:T(8,128)(2,1)S(1)}, f16[64,2048]{1,0:T(8,128)(2,1)S(1)}, u32[]{:S(2)}, u32[]{:S(2)}) collective-permute-start(f16[64,2048]{1,0:T(8,128)(2,1)S(1)} %add_convert_fusion.5), channel_id=1, source_target_pairs={{2,0},{7,1},{0,2},{5,3},{6,4},{3,5},{4,6},{1,7},{10,8},{15,9},{8,1... | collective-permute-start | bytes 786440 | tf_op jit(solution)/shard_map/ppermute | solution.py:206
  97.4 7.7 %collective-permute-start.23 = (f16[64,2048]{1,0:T(8,128)(2,1)S(1)}, f16[64,2048]{1,0:T(8,128)(2,1)S(1)}, u32[]{:S(2)}, u32[]{:S(2)}) collective-permute-start(f16[64,2048]{1,0:T(8,128)(2,1)S(1)} %add_convert_fusion.4), channel_id=1, source_target_pairs={{96,0},{33,1},{98,2},{35,3},{100,4},{37,5},{102,6},{39,7},{104,8},... | collective-permute-start | bytes 786440 | tf_op jit(solution)/shard_map/ppermute | solution.py:206
  99.9 7.6 %collective-permute-start.24 = (f16[64,2048]{1,0:T(8,128)(2,1)S(1)}, f16[64,2048]{1,0:T(8,128)(2,1)S(1)}, u32[]{:S(2)}, u32[]{:S(2)}) collective-permute-start(f16[64,2048]{1,0:T(8,128)(2,1)S(1)} %add_convert_fusion.3), channel_id=1, source_target_pairs={{6,0},{9,1},{4,2},{11,3},{2,4},{13,5},{0,6},{15,7},{14,8},{1,9},{1... | collective-permute-start | bytes 786440 | tf_op jit(solution)/shard_map/ppermute | solution.py:206
  108.2 10.6 %collective-permute-start.25 = (f16[64,2048]{1,0:T(8,128)(2,1)S(1)}, f16[64,2048]{1,0:T(8,128)(2,1)S(1)}, u32[]{:S(2)}, u32[]{:S(2)}) collective-permute-start(f16[64,2048]{1,0:T(8,128)(2,1)S(1)} %add_convert_fusion.2), channel_id=1, source_target_pairs={{16,0},{97,1},{18,2},{99,3},{20,4},{101,5},{22,6},{103,7},{24,8},{... | collective-permute-start | bytes 786440 | tf_op jit(solution)/shard_map/ppermute | solution.py:206
  111.9 10.9 %collective-permute-start.27 = (f16[64,2048]{1,0:T(8,128)(2,1)}, f16[64,2048]{1,0:T(8,128)(2,1)S(1)}, u32[]{:S(2)}, u32[]{:S(2)}) collective-permute-start(f16[64,2048]{1,0:T(8,128)(2,1)} %add_convert_fusion.1), channel_id=1, source_target_pairs={{4,0},{5,1},{30,2},{31,3},{34,4},{39,5},{60,6},{57,7},{72,8},{73,9... | collective-permute-start | bytes 786440 | tf_op jit(solution)/shard_map/ppermute | solution.py:206
  119.7 1.2 collective-permute-start.26
  122.8 3.6 %collective-permute-start.28 = (f32[6,64]{1,0:T(8,128)S(1)}, f32[6,64]{1,0:T(8,128)S(1)}, u32[]{:S(2)}, u32[]{:S(2)}) collective-permute-start(f32[6,64]{1,0:T(8,128)S(1)} %add.166), channel_id=1, source_target_pairs={{8,0},{9,1},{10,2},{11,3},{12,4},{13,5},{14,6},{15,7},{0,8},{1,9},... | collective-permute-start | bytes 4616 | tf_op jit(solution)/shard_map/ppermute | solution.py:206
  126.4 3.6 %collective-permute-start.29 = (f32[6,64]{1,0:T(8,128)S(1)}, f32[6,64]{1,0:T(8,128)S(1)}, u32[]{:S(2)}, u32[]{:S(2)}) collective-permute-start(f32[6,64]{1,0:T(8,128)S(1)} %add.167), channel_id=1, source_target_pairs={{2,0},{3,1},{0,2},{1,3},{6,4},{7,5},{4,6},{5,7},{10,8},{11,9},{8,1... | collective-permute-start | bytes 4616 | tf_op jit(solution)/shard_map/ppermute | solution.py:206
  130.0 4.8 %collective-permute-start.30 = (f32[6,64]{1,0:T(8,128)S(1)}, f32[6,64]{1,0:T(8,128)S(1)}, u32[]{:S(2)}, u32[]{:S(2)}) collective-permute-start(f32[6,64]{1,0:T(8,128)S(1)} %add.168), channel_id=1, source_target_pairs={{6,0},{7,1},{4,2},{5,3},{2,4},{3,5},{0,6},{1,7},{14,8},{15,9},{12,... | collective-permute-start | bytes 4616 | tf_op jit(solution)/shard_map/ppermute | solution.py:206

commit v7 on v6

--- a/solution.py
+++ b/solution.py
@@ -162,6 +162,34 @@
 
 def shadow(left, coupling):
     return call(shadow_kernel, "shadow", left, coupling, coupling.shape[0], 8)
+
+
+def shadow_rows(left, coupling, start, count):
+    columns = coupling.shape[1]
+    reps = left.shape[0]
+    spec = pl.BlockSpec(memory_space=pltpu.VMEM)
+
+    def kernel(left_ref, coupling_ref, out_ref, held_ref, sems):
+        rows = coupling_ref.at[pl.ds(start, count)]
+        shadow_kernel(left_ref, rows, out_ref, held_ref, sems)
+
+    return pl.pallas_call(
+        kernel,
+        name="shadow_rows",
+        in_specs=[spec, pl.BlockSpec(memory_space=pltpu.HBM)],
+        out_specs=spec,
+        out_shape=jax.ShapeDtypeStruct((reps, count), F32),
+        scratch_shapes=[
+            pltpu.VMEM((count, columns), BF16),
+            pltpu.SemaphoreType.DMA((8,)),
+        ],
+        compiler_params=pltpu.CompilerParams(vmem_limit_bytes=16 << 20),
+        cost_estimate=pl.CostEstimate(
+            flops=2 * reps * count * columns,
+            bytes_accessed=2 * count * columns,
+            transcendentals=0,
+        ),
+    )(left, coupling)
 
 
 def half_kernel(offset_ref, left_ref, coupling_ref, out_ref, held_ref, sems):
@@ -243,25 +271,33 @@
     keep = 1.0 - SELF_GAIN * slope
 
     def send_core(partial, scale):
-        mine, other = pick(first, partial * scale)
+        low, high = partial
+        mine = jnp.where(first, low, high) * scale
+        other = jnp.where(first, high, low) * scale
         return (mine + move(other.astype(WIRE), CORE).astype(F32)).astype(WIRE)
 
     half = pick(low_half, (slope * g).astype(BF16))[0]
     half = move(half, HALF_TO_ROWS)
-    shadow_partial = shadow(gs.astype(BF16), coupling)
 
     tops = jnp.stack([jnp.max(jnp.abs(g), axis=1), jnp.max(jnp.abs(gs), axis=1)])
     stats = jnp.concatenate([tops, jnp.stack([total(gs * g), total(gs * (keep * g))])])
-    for pairs in SMALL_COL:
-        if pairs is SMALL_COL[2]:
-            stats, half, shadow_partial = tie(stats, half, shadow_partial)
-            block = put(z_even, half, move(half, Z_PAIR))
-        if pairs is SMALL_COL[3]:
-            stats, block = tie(stats, block)
+
+    def widen(stats, pairs):
         other = move(stats, pairs)
-        stats = jnp.concatenate(
+        return jnp.concatenate(
             [jnp.maximum(stats[:2], other[:2]), stats[2:] + other[2:]]
         )
+
+    stats = widen(widen(stats, SMALL_COL[0]), SMALL_COL[1])
+    shadow_left = gs.astype(BF16)
+    low = shadow_rows(shadow_left, coupling, 0, 2048)
+    stats, low, shadow_left = tie(stats, low, shadow_left)
+    stats = widen(stats, SMALL_COL[2])
+    high = shadow_rows(shadow_left, coupling, 2048, 2048)
+    stats, high, half = tie(stats, high, half)
+    block = put(z_even, half, move(half, Z_PAIR))
+    stats = widen(stats, SMALL_COL[3])
+    stats, block = tie(stats, block)
     tiny = 1e-30
     top = jnp.maximum(stats[0], tiny)[:, None]
     shadow_top = jnp.maximum(stats[1], tiny)[:, None]
@@ -271,7 +307,7 @@
     alpha_c = alpha[:, None]
 
     left = put(first, block, move(block, CORE))
-    shadow_held = send_core(shadow_partial, FIRST_SCALE / shadow_top)
+    shadow_held = send_core((low, high), FIRST_SCALE / shadow_top)
     left, shadow_held = tie(left, shadow_held)
     scale = FIRST_SCALE / top
     offset = jnp.where(low_half, 1024, 0)
@@ -309,7 +345,7 @@
     half, shadow_partial, held = tie(half, shadow_partial, held)
     block = put(z_even, half, move(half, Z_PAIR))
     scale = SECOND_SCALE / shadow_top
-    shadow_held = send_core(shadow_partial, scale)
+    shadow_held = send_core(jnp.split(shadow_partial, 2, axis=1), scale)
     product = put(low_half, held, move(held, ROW_STEPS[0]))
     block, shadow_held, product = tie(block, shadow_held, product)
     left = put(first, block, move(block, CORE))

time: 139 us -> 142 us (1.022)
  waiting for transfers between devices: 63.8 us -> 52.2 us
  starting transfers between devices: 34.7 us -> 43.7 us
  Pallas kernels: 29.3 us -> 34.9 us
    pallas_call x0 -> x2, Pallas kernels: none -> 13.4 us  [shadow_rows(): pl.pallas_call(kernel, name='shadow_rows', in_specs=[spec, pl.BlockSpec(m...]
    ppermute x31, waiting for transfers between devices: 63.8 us -> 52.2 us  [move(): return lax.ppermute(value, AXES, pairs)]
    ppermute x31, starting transfers between devices: 34.7 us -> 43.7 us  [move(): return lax.ppermute(value, AXES, pairs)]
    pallas_call x3 -> x2, Pallas kernels: 21.7 us -> 14 us  [call(): pl.pallas_call(kernel, name=name, in_specs=[spec, pl.BlockSpec(memory_spa...]
  transfers between devices with their start and end apart: 31 -> 31, of which waited for: 22 -> 23; matrix products, arithmetic and copies ran while one was open for 2% -> 2% of each run, Pallas kernels for 21% -> 25%
where the time goes in v7:
time: 142 us; the launch traced here: 141 us
  waiting for transfers between devices  52.2 us (37%)
  starting transfers between devices  43.7 us (31%)
  Pallas kernels  34.9 us (25%)
  other arithmetic  8.82 us (6%)
    ppermute x31, waiting for transfers between devices, move(): return lax.ppermute(value, AXES, pairs)  52.2 us
    ppermute x31, starting transfers between devices, move(): return lax.ppermute(value, AXES, pairs)  43.7 us
    pallas_call x2, Pallas kernels, call(): pl.pallas_call(kernel, name=name, in_specs=[spec, pl.BlockSpec(memory_spa...  14 us
    pallas_call x2, Pallas kernels, shadow_rows(): pl.pallas_call(kernel, name='shadow_rows', in_specs=[spec, pl.BlockSpec(m...  13.4 us
    pallas_call x2, Pallas kernels, primary_half(): pl.pallas_call(half_kernel, name='primary_half', in_specs=[pl.BlockSpec(m...  7.56 us
  transfers between devices with their start and end apart: 31, of which 23 were waited for; matrix products, arithmetic and copies ran while one was open for 2% of the time, Pallas kernels for 25%

profile of v7, /device:TPU:0, one launch (start us, length us, event | category | flops | bytes accessed | tf_op | source)
XLA Modules:
  0.0 140.7 jit_solution(4200693603005965354)
XLA Ops:
  0.6 1.9 %multiply_reduce_fusion.7 = (f32[64]{0:T(128)S(1)}, f32[64]{0:T(128)S(1)}, f32[64]{0:T(128)S(1)}, f32[64]{0:T(128)S(1)}, bf16[64,2048]{1,0:T(8,128)(2,1)S(1)}, /...) fusion(f32[64,2048]{1,0:T(8,128)} %param.7, f32[64,2048]{1,0:T(8,128)} %param.6, ...), kind=kLoop, calls=%fused_computation.35 | loop fusion | flops 2096896 | bytes 3146752 | tf_op jit(solution)/shard_map/reduce_sum | solution.py:258
  2.7 4.0 %collective-permute-start.3 = (bf16[64,1024]{1,0:T(8,128)(2,1)S(1)}, bf16[64,1024]{1,0:T(8,128)(2,1)S(1)}, u32[]{:S(2)}, u32[]{:S(2)}) collective-permute-start(bf16[64,1024]{1,0:T(8,128)(2,1)S(1)} %slice_select_fusion.2), channel_id=1, source_target_pairs={{112,0},{65,1},{48,2},{113,3},{0,4},{33,5},{64,6},{17,7},{96,8},{9... | collective-permute-start | bytes 393224 | tf_op jit(solution)/shard_map/ppermute | solution.py:234
  6.8 0.7 collective-permute-start.1
  7.5 6.7 %shadow_rows.2 = f32[64,2048]{1,0:T(8,128)S(1)} custom-call(bf16[64,2048]{1,0:T(8,128)(2,1)S(1)} %get-tuple-element.36.left_ref, bf16[4096,2048]{1,0:T(8,128)(2,1)} %coupling_ref.11), custom_call_target="tpu_custom_call" | custom-call | flops 536870912 | bytes 8388608 | tf_op jit(solution)/shard_map/shadow_rows/pallas_call | solution.py:176
  14.2 4.5 %collective-permute-start.2 = (f32[4,64]{1,0:T(4,128)S(1)}, f32[4,64]{1,0:T(4,128)S(1)}, u32[]{:S(2)}, u32[]{:S(2)}) collective-permute-start(f32[4,64]{1,0:T(4,128)S(1)} %pad_maximum_fusion.7), channel_id=1, source_target_pairs={{2,0},{3,1},{0,2},{1,3},{6,4},{7,5},{4,6},{5,7},{10,8},{11,9},{8,1... | collective-permute-start | bytes 3080 | tf_op jit(solution)/shard_map/ppermute | solution.py:234
  18.7 6.7 %shadow_rows.3 = f32[64,2048]{1,0:T(8,128)S(1)} custom-call(bf16[64,2048]{1,0:T(8,128)(2,1)S(1)} %get-tuple-element.36.left_ref, bf16[4096,2048]{1,0:T(8,128)(2,1)} %coupling_ref.11), custom_call_target="tpu_custom_call" | custom-call | flops 536870912 | bytes 8388608 | tf_op jit(solution)/shard_map/shadow_rows/pallas_call | solution.py:176
  25.5 0.5 collective-permute-start.5
  26.1 4.2 %collective-permute-done.4 = f32[4,64]{1,0:T(4,128)S(1)} collective-permute-done((f32[4,64]{1,0:T(4,128)S(1)}, f32[4,64]{1,0:T(4,128)S(1)}, u32[]{:S(2)}, u32[]{:S(2)}) %collective-permute-start.4) | collective-permute-done | bytes 1056 | tf_op jit(solution)/shard_map/ppermute | solution.py:234
  30.3 0.3 collective-permute-done.5
  30.9 0.6 collective-permute-start.7
  31.5 0.8 collective-permute-done.6
  32.4 0.3 collective-permute-done.7
  32.7 0.2 add_convert_fusion.10
  32.9 0.4 collective-permute-start.8
  33.3 3.8 %primary_half.3 = f32[64,1024]{1,0:T(8,128)S(1)} custom-call(s32[1]{0:T(128)} %bitcast.9.offset_ref, bf16[64,4096]{1,0:T(8,128)(2,1)S(1)} %pad_maximum_fusion.left_ref, bf16[4096,2048]{1,0:T(8,128)(2,1)} %coupling_ref.11), custom_call_target="tpu_custom_call" | custom-call | flops 536870912 | bytes 8388608 | tf_op jit(solution)/shard_map/primary_half/pallas_call | solution.py:210
  37.2 1.5 %collective-permute-start.9 = (f16[64,1024]{1,0:T(8,128)(2,1)S(1)}, f16[64,1024]{1,0:T(8,128)(2,1)S(1)}, u32[]{:S(2)}, u32[]{:S(2)}) collective-permute-start(f16[64,1024]{1,0:T(8,128)(2,1)S(1)} %multiply_convert_fusion.4), channel_id=1, source_target_pairs={{32,0},{17,1},{34,2},{19,3},{36,4},{21,5},{38,6},{23,7},{40,8},{25... | collective-permute-start | bytes 393224 | tf_op jit(solution)/shard_map/ppermute | solution.py:234
  38.7 3.7 %primary_half.2 = f32[64,1024]{1,0:T(8,128)S(1)} custom-call(s32[1]{0:T(128)} %bitcast.6.offset_ref, bf16[64,4096]{1,0:T(8,128)(2,1)S(1)} %pad_maximum_fusion.left_ref, bf16[4096,2048]{1,0:T(8,128)(2,1)} %coupling_ref.11), custom_call_target="tpu_custom_call" | custom-call | flops 536870912 | bytes 8388608 | tf_op jit(solution)/shard_map/primary_half/pallas_call | solution.py:210
  42.5 1.5 %collective-permute-start.10 = (f16[64,2048]{1,0:T(8,128)(2,1)S(1)}, f16[64,2048]{1,0:T(8,128)(2,1)S(1)}, u32[]{:S(2)}, u32[]{:S(2)}) collective-permute-start(f16[64,2048]{1,0:T(8,128)(2,1)S(1)} %add_convert_fusion.9), channel_id=1, source_target_pairs={{2,0},{7,1},{0,2},{5,3},{6,4},{3,5},{4,6},{1,7},{10,8},{15,9},{8,1... | collective-permute-start | bytes 786440 | tf_op jit(solution)/shard_map/ppermute | solution.py:234
  44.1 4.9 %collective-permute-done.10 = f16[64,2048]{1,0:T(8,128)(2,1)S(1)} collective-permute-done((f16[64,2048]{1,0:T(8,128)(2,1)S(1)}, f16[64,2048]{1,0:T(8,128)(2,1)S(1)}, u32[]{:S(2)}, u32[]{:S(2)}) %collective-permute-start.10) | collective-permute-done | bytes 262176 | tf_op jit(solution)/shard_map/ppermute | solution.py:234
  49.1 2.0 %collective-permute-start.11 = (f16[64,1024]{1,0:T(8,128)(2,1)S(1)}, f16[64,1024]{1,0:T(8,128)(2,1)S(1)}, u32[]{:S(2)}, u32[]{:S(2)}) collective-permute-start(f16[64,1024]{1,0:T(8,128)(2,1)S(1)} %add_convert_fusion.13), channel_id=1, source_target_pairs={{96,0},{33,1},{98,2},{35,3},{100,4},{37,5},{102,6},{39,7},{104,8},... | collective-permute-start | bytes 393224 | tf_op jit(solution)/shard_map/ppermute | solution.py:234
  51.0 2.2 %collective-permute-start.12 = (f16[64,2048]{1,0:T(8,128)(2,1)S(1)}, f16[64,2048]{1,0:T(8,128)(2,1)S(1)}, u32[]{:S(2)}, u32[]{:S(2)}) collective-permute-start(f16[64,2048]{1,0:T(8,128)(2,1)S(1)} %add_convert_fusion.8), channel_id=1, source_target_pairs={{6,0},{9,1},{4,2},{11,3},{2,4},{13,5},{0,6},{15,7},{14,8},{1,9},{1... | collective-permute-start | bytes 786440 | tf_op jit(solution)/shard_map/ppermute | solution.py:234
  53.2 2.1 %collective-permute-done.11 = f16[64,1024]{1,0:T(8,128)(2,1)S(1)} collective-permute-done((f16[64,1024]{1,0:T(8,128)(2,1)S(1)}, f16[64,1024]{1,0:T(8,128)(2,1)S(1)}, u32[]{:S(2)}, u32[]{:S(2)}) %collective-permute-start.11) | collective-permute-done | bytes 131104 | tf_op jit(solution)/shard_map/ppermute | solution.py:234
  55.4 3.2 %collective-permute-done.12 = f16[64,2048]{1,0:T(8,128)(2,1)S(1)} collective-permute-done((f16[64,2048]{1,0:T(8,128)(2,1)S(1)}, f16[64,2048]{1,0:T(8,128)(2,1)S(1)}, u32[]{:S(2)}, u32[]{:S(2)}) %collective-permute-start.12) | collective-permute-done | bytes 262176 | tf_op jit(solution)/shard_map/ppermute | solution.py:234
  58.7 2.2 %collective-permute-start.13 = (f16[64,1024]{1,0:T(8,128)(2,1)S(1)}, f16[64,1024]{1,0:T(8,128)(2,1)S(1)}, u32[]{:S(2)}, u32[]{:S(2)}) collective-permute-start(f16[64,1024]{1,0:T(8,128)(2,1)S(1)} %add_convert_fusion.12), channel_id=1, source_target_pairs={{16,0},{97,1},{18,2},{99,3},{20,4},{101,5},{22,6},{103,7},{24,8},{... | collective-permute-start | bytes 393224 | tf_op jit(solution)/shard_map/ppermute | solution.py:234
  60.9 1.8 %collective-permute-start.15 = (f16[64,2048]{1,0:T(8,128)(2,1)S(1)}, f16[64,2048]{1,0:T(8,128)(2,1)S(1)}, u32[]{:S(2)}, u32[]{:S(2)}) collective-permute-start(f16[64,2048]{1,0:T(8,128)(2,1)S(1)} %add_convert_fusion.7), channel_id=1, source_target_pairs={{4,0},{5,1},{30,2},{31,3},{34,4},{39,5},{60,6},{57,7},{72,8},{73,9... | collective-permute-start | bytes 786440 | tf_op jit(solution)/shard_map/ppermute | solution.py:234
  62.6 3.2 %collective-permute-done.13 = f16[64,1024]{1,0:T(8,128)(2,1)S(1)} collective-permute-done((f16[64,1024]{1,0:T(8,128)(2,1)S(1)}, f16[64,1024]{1,0:T(8,128)(2,1)S(1)}, u32[]{:S(2)}, u32[]{:S(2)}) %collective-permute-start.13) | collective-permute-done | bytes 131104 | tf_op jit(solution)/shard_map/ppermute | solution.py:234
  65.8 0.2 fusion.6
  66.0 0.4 collective-permute-start.14
  66.4 2.3 %collective-permute-done.15 = f16[64,2048]{1,0:T(8,128)(2,1)S(1)} collective-permute-done((f16[64,2048]{1,0:T(8,128)(2,1)S(1)}, f16[64,2048]{1,0:T(8,128)(2,1)S(1)}, u32[]{:S(2)}, u32[]{:S(2)}) %collective-permute-start.15) | collective-permute-done | bytes 262176 | tf_op jit(solution)/shard_map/ppermute | solution.py:234
  68.7 0.2 fusion.15
  69.0 7.7 %shadow.1 = f32[64,4096]{1,0:T(8,128)S(1)} custom-call(bf16[64,2048]{1,0:T(8,128)(2,1)S(1)} %get-tuple-element.82.left_ref, bf16[4096,2048]{1,0:T(8,128)(2,1)} %coupling_ref.11), custom_call_target="tpu_custom_call" | custom-call | flops 1073741824 | bytes 16777216 | tf_op jit(solution)/shard_map/shadow/pallas_call | solution.py:140
  76.7 0.5 collective-permute-done.14
  77.2 2.8 %collective-permute-start.16 = (bf16[64,1024]{1,0:T(8,128)(2,1)S(1)}, bf16[64,1024]{1,0:T(8,128)(2,1)S(1)}, u32[]{:S(2)}, u32[]{:S(2)}) collective-permute-start(bf16[64,1024]{1,0:T(8,128)(2,1)S(1)} %collective-permute-done.14), channel_id=1, source_target_pairs={{2,0},{3,1},{0,2},{1,3},{6,4},{7,5},{4,6},{5,7},{10,8},{11,9},{8,1... | collective-permute-start | bytes 393224 | tf_op jit(solution)/shard_map/ppermute | solution.py:234
  80.0 0.4 collective-permute-start.18
  80.5 0.8 collective-permute-start.17
  81.3 1.6 %collective-permute-done.16 = bf16[64,1024]{1,0:T(8,128)(2,1)S(1)} collective-permute-done((bf16[64,1024]{1,0:T(8,128)(2,1)S(1)}, bf16[64,1024]{1,0:T(8,128)(2,1)S(1)}, u32[]{:S(2)}, u32[]{:S(2)}) %collective-permute-start.16) | collective-permute-done | bytes 131104 | tf_op jit(solution)/shard_map/ppermute | solution.py:234
  82.9 2.0 %collective-permute-done.18 = f16[64,1024]{1,0:T(8,128)(2,1)S(1)} collective-permute-done((f16[64,1024]{1,0:T(8,128)(2,1)S(1)}, f16[64,1024]{1,0:T(8,128)(2,1)S(1)}, u32[]{:S(2)}, u32[]{:S(2)}) %collective-permute-start.18) | collective-permute-done | bytes 131104 | tf_op jit(solution)/shard_map/ppermute | solution.py:234
  85.1 0.2 add_convert_fusion.6
  85.5 1.4 %collective-permute-done.19 = bf16[64,2048]{1,0:T(8,128)(2,1)S(1)} collective-permute-done((bf16[64,2048]{1,0:T(8,128)(2,1)S(1)}, bf16[64,2048]{1,0:T(8,128)(2,1)S(1)}, u32[]{:S(2)}, u32[]{:S(2)}) %collective-permute-start.19) | collective-permute-done | bytes 262176 | tf_op jit(solution)/shard_map/ppermute | solution.py:234
  87.0 6.2 %primary.1 = f32[64,2048]{1,0:T(8,128)S(1)} custom-call(bf16[64,4096]{1,0:T(8,128)(2,1)S(1)} %pad_maximum_fusion.1.left_ref, bf16[4096,2048]{1,0:T(8,128)(2,1)} %coupling_ref.11), custom_call_target="tpu_custom_call" | custom-call | flops 1073741824 | bytes 16777216 | tf_op jit(solution)/shard_map/primary/pallas_call | solution.py:140
  93.5 0.5 collective-permute-start.21
  93.9 1.2 collective-permute-start.22
  95.2 4.7 %collective-permute-done.21 = f16[64,2048]{1,0:T(8,128)(2,1)S(1)} collective-permute-done((f16[64,2048]{1,0:T(8,128)(2,1)S(1)}, f16[64,2048]{1,0:T(8,128)(2,1)S(1)}, u32[]{:S(2)}, u32[]{:S(2)}) %collective-permute-start.21) | collective-permute-done | bytes 262176 | tf_op jit(solution)/shard_map/ppermute | solution.py:234
  99.9 0.1 add_convert_fusion.4
  100.1 0.3 collective-permute-done.22
  100.4 2.3 %collective-permute-start.23 = (f16[64,2048]{1,0:T(8,128)(2,1)S(1)}, f16[64,2048]{1,0:T(8,128)(2,1)S(1)}, u32[]{:S(2)}, u32[]{:S(2)}) collective-permute-start(f16[64,2048]{1,0:T(8,128)(2,1)S(1)} %add_convert_fusion.4), channel_id=1, source_target_pairs={{96,0},{33,1},{98,2},{35,3},{100,4},{37,5},{102,6},{39,7},{104,8},... | collective-permute-start | bytes 786440 | tf_op jit(solution)/shard_map/ppermute | solution.py:234
  102.7 4.0 %collective-permute-start.24 = (f16[64,2048]{1,0:T(8,128)(2,1)S(1)}, f16[64,2048]{1,0:T(8,128)(2,1)S(1)}, u32[]{:S(2)}, u32[]{:S(2)}) collective-permute-start(f16[64,2048]{1,0:T(8,128)(2,1)S(1)} %add_convert_fusion.3), channel_id=1, source_target_pairs={{6,0},{9,1},{4,2},{11,3},{2,4},{13,5},{0,6},{15,7},{14,8},{1,9},{1... | collective-permute-start | bytes 786440 | tf_op jit(solution)/shard_map/ppermute | solution.py:234
  106.7 1.3 collective-permute-done.23
  108.2 2.9 %collective-permute-done.24 = f16[64,2048]{1,0:T(8,128)(2,1)S(1)} collective-permute-done((f16[64,2048]{1,0:T(8,128)(2,1)S(1)}, f16[64,2048]{1,0:T(8,128)(2,1)S(1)}, u32[]{:S(2)}, u32[]{:S(2)}) %collective-permute-start.24) | collective-permute-done | bytes 262176 | tf_op jit(solution)/shard_map/ppermute | solution.py:234
  111.1 0.8 add_convert_fusion.1
  111.9 3.0 %collective-permute-start.25 = (f16[64,2048]{1,0:T(8,128)(2,1)S(1)}, f16[64,2048]{1,0:T(8,128)(2,1)S(1)}, u32[]{:S(2)}, u32[]{:S(2)}) collective-permute-start(f16[64,2048]{1,0:T(8,128)(2,1)S(1)} %add_convert_fusion.2), channel_id=1, source_target_pairs={{16,0},{97,1},{18,2},{99,3},{20,4},{101,5},{22,6},{103,7},{24,8},{... | collective-permute-start | bytes 786440 | tf_op jit(solution)/shard_map/ppermute | solution.py:234
  114.9 2.1 %collective-permute-start.27 = (f16[64,2048]{1,0:T(8,128)(2,1)}, f16[64,2048]{1,0:T(8,128)(2,1)S(1)}, u32[]{:S(2)}, u32[]{:S(2)}) collective-permute-start(f16[64,2048]{1,0:T(8,128)(2,1)} %add_convert_fusion.1), channel_id=1, source_target_pairs={{4,0},{5,1},{30,2},{31,3},{34,4},{39,5},{60,6},{57,7},{72,8},{73,9... | collective-permute-start | bytes 786440 | tf_op jit(solution)/shard_map/ppermute | solution.py:234
  117.0 4.6 %collective-permute-done.25 = f16[64,2048]{1,0:T(8,128)(2,1)S(1)} collective-permute-done((f16[64,2048]{1,0:T(8,128)(2,1)S(1)}, f16[64,2048]{1,0:T(8,128)(2,1)S(1)}, u32[]{:S(2)}, u32[]{:S(2)}) %collective-permute-start.25) | collective-permute-done | bytes 262176 | tf_op jit(solution)/shard_map/ppermute | solution.py:234
  121.5 0.8 multiply_reduce_fusion
  122.3 0.8 collective-permute-start.26
  123.1 0.8 collective-permute-done.26
  124.0 1.8 %collective-permute-done.27 = f16[64,2048]{1,0:T(8,128)(2,1)S(1)} collective-permute-done((f16[64,2048]{1,0:T(8,128)(2,1)}, f16[64,2048]{1,0:T(8,128)(2,1)S(1)}, u32[]{:S(2)}, u32[]{:S(2)}) %collective-permute-start.27) | collective-permute-done | bytes 262176 | tf_op jit(solution)/shard_map/ppermute | solution.py:234
  125.8 1.4 collective-permute-start.28
  127.1 2.3 %collective-permute-done.28 = f32[6,64]{1,0:T(8,128)S(1)} collective-permute-done((f32[6,64]{1,0:T(8,128)S(1)}, f32[6,64]{1,0:T(8,128)S(1)}, u32[]{:S(2)}, u32[]{:S(2)}) %collective-permute-start.28) | collective-permute-done | bytes 1568 | tf_op jit(solution)/shard_map/ppermute | solution.py:234
  129.4 1.5 %collective-permute-start.29 = (f32[6,64]{1,0:T(8,128)S(1)}, f32[6,64]{1,0:T(8,128)S(1)}, u32[]{:S(2)}, u32[]{:S(2)}) collective-permute-start(f32[6,64]{1,0:T(8,128)S(1)} %add.167), channel_id=1, source_target_pairs={{2,0},{3,1},{0,2},{1,3},{6,4},{7,5},{4,6},{5,7},{10,8},{11,9},{8,1... | collective-permute-start | bytes 4616 | tf_op jit(solution)/shard_map/ppermute | solution.py:234
  130.9 2.1 %collective-permute-done.29 = f32[6,64]{1,0:T(8,128)S(1)} collective-permute-done((f32[6,64]{1,0:T(8,128)S(1)}, f32[6,64]{1,0:T(8,128)S(1)}, u32[]{:S(2)}, u32[]{:S(2)}) %collective-permute-start.29) | collective-permute-done | bytes 1568 | tf_op jit(solution)/shard_map/ppermute | solution.py:234
  133.0 0.3 collective-permute-start.30
  133.3 4.5 %collective-permute-done.30 = f32[6,64]{1,0:T(8,128)S(1)} collective-permute-done((f32[6,64]{1,0:T(8,128)S(1)}, f32[6,64]{1,0:T(8,128)S(1)}, u32[]{:S(2)}, u32[]{:S(2)}) %collective-permute-start.30) | collective-permute-done | bytes 1568 | tf_op jit(solution)/shard_map/ppermute | solution.py:234
  137.8 2.8 %multiply_subtract_fusion = (f32[64,2048]{1,0:T(8,128)}, f32[64,2048]{1,0:T(8,128)}, f32[64,2048]{1,0:T(8,128)}, f32[64,2048]{1,0:T(8,128)}) fusion(f16[64,2048]{1,0:T(8,128)(2,1)S(1)} %collective-permute-done.27, f32[64,2048]{1,0:T(8,128)S(1)} %get-tuple-element.83, f32[64,2048]{1,0:T(8,128)S(1)} %copy-done, f16[64,2048]{1,0:T(8,128)(2,1)S(1)} %collective-permute-done.15, ...), kind=kLoop, calls=%fused_computation.2 | loop fusion | flops 7077888 | bytes 5507328 | tf_op jit(solution)/shard_map/sub | solution.py:406
  (60 shorter events, 2.1 us)
Async XLA Ops:
  2.6 4.2 %collective-permute-start = (f32[4,64]{1,0:T(4,128)S(1)}, f32[4,64]{1,0:T(4,128)S(1)}, u32[]{:S(2)}, u32[]{:S(2)}) collective-permute-start(f32[4,64]{1,0:T(4,128)S(1)} %pad_maximum_fusion.5), channel_id=1, source_target_pairs={{1,0},{0,1},{3,2},{2,3},{5,4},{4,5},{7,6},{6,7},{9,8},{8,9},{11,10... | collective-permute-start | bytes 3080 | tf_op jit(solution)/shard_map/ppermute | solution.py:234
  2.7 22.7 %collective-permute-start.3 = (bf16[64,1024]{1,0:T(8,128)(2,1)S(1)}, bf16[64,1024]{1,0:T(8,128)(2,1)S(1)}, u32[]{:S(2)}, u32[]{:S(2)}) collective-permute-start(bf16[64,1024]{1,0:T(8,128)(2,1)S(1)} %slice_select_fusion.2), channel_id=1, source_target_pairs={{112,0},{65,1},{48,2},{113,3},{0,4},{33,5},{64,6},{17,7},{96,8},{9... | collective-permute-start | bytes 393224 | tf_op jit(solution)/shard_map/ppermute | solution.py:234
  6.8 7.4 %collective-permute-start.1 = (f32[4,64]{1,0:T(4,128)S(1)}, f32[4,64]{1,0:T(4,128)S(1)}, u32[]{:S(2)}, u32[]{:S(2)}) collective-permute-start(f32[4,64]{1,0:T(4,128)S(1)} %pad_maximum_fusion.6), channel_id=1, source_target_pairs={{8,0},{9,1},{10,2},{11,3},{12,4},{13,5},{14,6},{15,7},{0,8},{1,9},... | collective-permute-start | bytes 3080 | tf_op jit(solution)/shard_map/ppermute | solution.py:234
  14.2 11.2 %collective-permute-start.2 = (f32[4,64]{1,0:T(4,128)S(1)}, f32[4,64]{1,0:T(4,128)S(1)}, u32[]{:S(2)}, u32[]{:S(2)}) collective-permute-start(f32[4,64]{1,0:T(4,128)S(1)} %pad_maximum_fusion.7), channel_id=1, source_target_pairs={{2,0},{3,1},{0,2},{1,3},{6,4},{7,5},{4,6},{5,7},{10,8},{11,9},{8,1... | collective-permute-start | bytes 3080 | tf_op jit(solution)/shard_map/ppermute | solution.py:234
  25.4 4.9 %collective-permute-start.4 = (f32[4,64]{1,0:T(4,128)S(1)}, f32[4,64]{1,0:T(4,128)S(1)}, u32[]{:S(2)}, u32[]{:S(2)}) collective-permute-start(f32[4,64]{1,0:T(4,128)S(1)} %pad_maximum_fusion.8), channel_id=1, source_target_pairs={{6,0},{7,1},{4,2},{5,3},{2,4},{3,5},{0,6},{1,7},{14,8},{15,9},{12,... | collective-permute-start | bytes 3080 | tf_op jit(solution)/shard_map/ppermute | solution.py:234
  25.5 5.1 %collective-permute-start.5 = (bf16[64,1024]{1,0:T(8,128)(2,1)S(1)}, bf16[64,1024]{1,0:T(8,128)(2,1)S(1)}, u32[]{:S(2)}, u32[]{:S(2)}) collective-permute-start(bf16[64,1024]{1,0:T(8,128)(2,1)S(1)} %collective-permute-done.3), channel_id=1, source_target_pairs={{2,0},{3,1},{0,2},{1,3},{6,4},{7,5},{4,6},{5,7},{10,8},{11,9},{8,1... | collective-permute-start | bytes 393224 | tf_op jit(solution)/shard_map/ppermute | solution.py:234
  30.7 1.6 %collective-permute-start.6 = (bf16[64,2048]{1,0:T(8,128)(2,1)S(1)}, bf16[64,2048]{1,0:T(8,128)(2,1)S(1)}, u32[]{:S(2)}, u32[]{:S(2)}) collective-permute-start(bf16[64,2048]{1,0:T(8,128)(2,1)S(1)} %pad_maximum_fusion.2), channel_id=1, source_target_pairs={{1,0},{0,1},{3,2},{2,3},{5,4},{4,5},{7,6},{6,7},{9,8},{8,9},{11,10... | collective-permute-start | bytes 786440 | tf_op jit(solution)/shard_map/ppermute | solution.py:234
  30.9 1.8 %collective-permute-start.7 = (f16[64,2048]{1,0:T(8,128)(2,1)S(1)}, f16[64,2048]{1,0:T(8,128)(2,1)S(1)}, u32[]{:S(2)}, u32[]{:S(2)}) collective-permute-start(f16[64,2048]{1,0:T(8,128)(2,1)S(1)} %multiply_convert_fusion.2), channel_id=1, source_target_pairs={{1,0},{0,1},{3,2},{2,3},{5,4},{4,5},{7,6},{6,7},{9,8},{8,9},{11,10... | collective-permute-start | bytes 786440 | tf_op jit(solution)/shard_map/ppermute | solution.py:234
  32.9 9.5 %collective-permute-start.8 = (f16[64,2048]{1,0:T(8,128)(2,1)S(1)}, f16[64,2048]{1,0:T(8,128)(2,1)S(1)}, u32[]{:S(2)}, u32[]{:S(2)}) collective-permute-start(f16[64,2048]{1,0:T(8,128)(2,1)S(1)} %add_convert_fusion.10), channel_id=1, source_target_pairs={{8,0},{3,1},{10,2},{1,3},{12,4},{7,5},{14,6},{5,7},{0,8},{11,9},{2... | collective-permute-start | bytes 786440 | tf_op jit(solution)/shard_map/ppermute | solution.py:234
  33.3 32.5 %copy-start.1 = (f32[64,2048]{1,0:T(8,128)S(1)}, f32[64,2048]{1,0:T(8,128)}, u32[]{:S(2)}) copy-start(f32[64,2048]{1,0:T(8,128)} %param.6) | copy-start | bytes 1572868
  33.3 35.5 %copy-start = (f32[64,2048]{1,0:T(8,128)S(1)}, f32[64,2048]{1,0:T(8,128)}, u32[]{:S(2)}) copy-start(f32[64,2048]{1,0:T(8,128)} %param.7) | copy-start | bytes 1572868
  33.3 35.5 %copy-start.2 = (f32[64,2048]{1,0:T(8,128)S(1)}, f32[64,2048]{1,0:T(8,128)}, u32[]{:S(2)}) copy-start(f32[64,2048]{1,0:T(8,128)} %param.5) | copy-start | bytes 1572868
  37.2 6.8 %collective-permute-start.9 = (f16[64,1024]{1,0:T(8,128)(2,1)S(1)}, f16[64,1024]{1,0:T(8,128)(2,1)S(1)}, u32[]{:S(2)}, u32[]{:S(2)}) collective-permute-start(f16[64,1024]{1,0:T(8,128)(2,1)S(1)} %multiply_convert_fusion.4), channel_id=1, source_target_pairs={{32,0},{17,1},{34,2},{19,3},{36,4},{21,5},{38,6},{23,7},{40,8},{25... | collective-permute-start | bytes 393224 | tf_op jit(solution)/shard_map/ppermute | solution.py:234
  42.5 6.5 %collective-permute-start.10 = (f16[64,2048]{1,0:T(8,128)(2,1)S(1)}, f16[64,2048]{1,0:T(8,128)(2,1)S(1)}, u32[]{:S(2)}, u32[]{:S(2)}) collective-permute-start(f16[64,2048]{1,0:T(8,128)(2,1)S(1)} %add_convert_fusion.9), channel_id=1, source_target_pairs={{2,0},{7,1},{0,2},{5,3},{6,4},{3,5},{4,6},{1,7},{10,8},{15,9},{8,1... | collective-permute-start | bytes 786440 | tf_op jit(solution)/shard_map/ppermute | solution.py:234
  49.1 6.3 %collective-permute-start.11 = (f16[64,1024]{1,0:T(8,128)(2,1)S(1)}, f16[64,1024]{1,0:T(8,128)(2,1)S(1)}, u32[]{:S(2)}, u32[]{:S(2)}) collective-permute-start(f16[64,1024]{1,0:T(8,128)(2,1)S(1)} %add_convert_fusion.13), channel_id=1, source_target_pairs={{96,0},{33,1},{98,2},{35,3},{100,4},{37,5},{102,6},{39,7},{104,8},... | collective-permute-start | bytes 393224 | tf_op jit(solution)/shard_map/ppermute | solution.py:234
  51.0 7.6 %collective-permute-start.12 = (f16[64,2048]{1,0:T(8,128)(2,1)S(1)}, f16[64,2048]{1,0:T(8,128)(2,1)S(1)}, u32[]{:S(2)}, u32[]{:S(2)}) collective-permute-start(f16[64,2048]{1,0:T(8,128)(2,1)S(1)} %add_convert_fusion.8), channel_id=1, source_target_pairs={{6,0},{9,1},{4,2},{11,3},{2,4},{13,5},{0,6},{15,7},{14,8},{1,9},{1... | collective-permute-start | bytes 786440 | tf_op jit(solution)/shard_map/ppermute | solution.py:234
  58.7 7.1 %collective-permute-start.13 = (f16[64,1024]{1,0:T(8,128)(2,1)S(1)}, f16[64,1024]{1,0:T(8,128)(2,1)S(1)}, u32[]{:S(2)}, u32[]{:S(2)}) collective-permute-start(f16[64,1024]{1,0:T(8,128)(2,1)S(1)} %add_convert_fusion.12), channel_id=1, source_target_pairs={{16,0},{97,1},{18,2},{99,3},{20,4},{101,5},{22,6},{103,7},{24,8},{... | collective-permute-start | bytes 393224 | tf_op jit(solution)/shard_map/ppermute | solution.py:234
  60.9 7.9 %collective-permute-start.15 = (f16[64,2048]{1,0:T(8,128)(2,1)S(1)}, f16[64,2048]{1,0:T(8,128)(2,1)S(1)}, u32[]{:S(2)}, u32[]{:S(2)}) collective-permute-start(f16[64,2048]{1,0:T(8,128)(2,1)S(1)} %add_convert_fusion.7), channel_id=1, source_target_pairs={{4,0},{5,1},{30,2},{31,3},{34,4},{39,5},{60,6},{57,7},{72,8},{73,9... | collective-permute-start | bytes 786440 | tf_op jit(solution)/shard_map/ppermute | solution.py:234
  66.0 11.2 %collective-permute-start.14 = (bf16[64,1024]{1,0:T(8,128)(2,1)S(1)}, bf16[64,1024]{1,0:T(8,128)(2,1)S(1)}, u32[]{:S(2)}, u32[]{:S(2)}) collective-permute-start(bf16[64,1024]{1,0:T(8,128)(2,1)S(1)} %get-tuple-element.84), channel_id=1, source_target_pairs={{112,0},{65,1},{48,2},{113,3},{0,4},{33,5},{64,6},{17,7},{96,8},{9... | collective-permute-start | bytes 393224 | tf_op jit(solution)/shard_map/ppermute | solution.py:234
  77.2 5.7 %collective-permute-start.16 = (bf16[64,1024]{1,0:T(8,128)(2,1)S(1)}, bf16[64,1024]{1,0:T(8,128)(2,1)S(1)}, u32[]{:S(2)}, u32[]{:S(2)}) collective-permute-start(bf16[64,1024]{1,0:T(8,128)(2,1)S(1)} %collective-permute-done.14), channel_id=1, source_target_pairs={{2,0},{3,1},{0,2},{1,3},{6,4},{7,5},{4,6},{5,7},{10,8},{11,9},{8,1... | collective-permute-start | bytes 393224 | tf_op jit(solution)/shard_map/ppermute | solution.py:234
  80.0 5.0 %collective-permute-start.18 = (f16[64,1024]{1,0:T(8,128)(2,1)S(1)}, f16[64,1024]{1,0:T(8,128)(2,1)S(1)}, u32[]{:S(2)}, u32[]{:S(2)}) collective-permute-start(f16[64,1024]{1,0:T(8,128)(2,1)S(1)} %get-tuple-element.54), channel_id=1, source_target_pairs={{32,0},{17,1},{34,2},{19,3},{36,4},{21,5},{38,6},{23,7},{40,8},{25... | collective-permute-start | bytes 393224 | tf_op jit(solution)/shard_map/ppermute | solution.py:234
  80.5 4.6 %collective-permute-start.17 = (f16[64,2048]{1,0:T(8,128)(2,1)S(1)}, f16[64,2048]{1,0:T(8,128)(2,1)S(1)}, u32[]{:S(2)}, u32[]{:S(2)}) collective-permute-start(f16[64,2048]{1,0:T(8,128)(2,1)S(1)} %multiply_convert_fusion.1), channel_id=1, source_target_pairs={{1,0},{0,1},{3,2},{2,3},{5,4},{4,5},{7,6},{6,7},{9,8},{8,9},{11,10... | collective-permute-start | bytes 786440 | tf_op jit(solution)/shard_map/ppermute | solution.py:234
  85.3 1.6 %collective-permute-start.19 = (bf16[64,2048]{1,0:T(8,128)(2,1)S(1)}, bf16[64,2048]{1,0:T(8,128)(2,1)S(1)}, u32[]{:S(2)}, u32[]{:S(2)}) collective-permute-start(bf16[64,2048]{1,0:T(8,128)(2,1)S(1)} %pad_maximum_fusion.3), channel_id=1, source_target_pairs={{1,0},{0,1},{3,2},{2,3},{5,4},{4,5},{7,6},{6,7},{9,8},{8,9},{11,10... | collective-permute-start | bytes 786440 | tf_op jit(solution)/shard_map/ppermute | solution.py:234
  85.4 7.9 %collective-permute-start.20 = (f16[64,2048]{1,0:T(8,128)(2,1)S(1)}, f16[64,2048]{1,0:T(8,128)(2,1)S(1)}, u32[]{:S(2)}, u32[]{:S(2)}) collective-permute-start(f16[64,2048]{1,0:T(8,128)(2,1)S(1)} %add_convert_fusion.6), channel_id=1, source_target_pairs={{8,0},{3,1},{10,2},{1,3},{12,4},{7,5},{14,6},{5,7},{0,8},{11,9},{2... | collective-permute-start | bytes 786440 | tf_op jit(solution)/shard_map/ppermute | solution.py:234
  93.5 6.5 %collective-permute-start.21 = (f16[64,2048]{1,0:T(8,128)(2,1)S(1)}, f16[64,2048]{1,0:T(8,128)(2,1)S(1)}, u32[]{:S(2)}, u32[]{:S(2)}) collective-permute-start(f16[64,2048]{1,0:T(8,128)(2,1)S(1)} %multiply_convert_fusion), channel_id=1, source_target_pairs={{32,0},{17,1},{34,2},{19,3},{36,4},{21,5},{38,6},{23,7},{40,8},{25... | collective-permute-start | bytes 786440 | tf_op jit(solution)/shard_map/ppermute | solution.py:234
  93.9 6.4 %collective-permute-start.22 = (f16[64,2048]{1,0:T(8,128)(2,1)S(1)}, f16[64,2048]{1,0:T(8,128)(2,1)S(1)}, u32[]{:S(2)}, u32[]{:S(2)}) collective-permute-start(f16[64,2048]{1,0:T(8,128)(2,1)S(1)} %add_convert_fusion.5), channel_id=1, source_target_pairs={{2,0},{7,1},{0,2},{5,3},{6,4},{3,5},{4,6},{1,7},{10,8},{15,9},{8,1... | collective-permute-start | bytes 786440 | tf_op jit(solution)/shard_map/ppermute | solution.py:234
  100.4 7.7 %collective-permute-start.23 = (f16[64,2048]{1,0:T(8,128)(2,1)S(1)}, f16[64,2048]{1,0:T(8,128)(2,1)S(1)}, u32[]{:S(2)}, u32[]{:S(2)}) collective-permute-start(f16[64,2048]{1,0:T(8,128)(2,1)S(1)} %add_convert_fusion.4), channel_id=1, source_target_pairs={{96,0},{33,1},{98,2},{35,3},{100,4},{37,5},{102,6},{39,7},{104,8},... | collective-permute-start | bytes 786440 | tf_op jit(solution)/shard_map/ppermute | solution.py:234
  102.7 8.4 %collective-permute-start.24 = (f16[64,2048]{1,0:T(8,128)(2,1)S(1)}, f16[64,2048]{1,0:T(8,128)(2,1)S(1)}, u32[]{:S(2)}, u32[]{:S(2)}) collective-permute-start(f16[64,2048]{1,0:T(8,128)(2,1)S(1)} %add_convert_fusion.3), channel_id=1, source_target_pairs={{6,0},{9,1},{4,2},{11,3},{2,4},{13,5},{0,6},{15,7},{14,8},{1,9},{1... | collective-permute-start | bytes 786440 | tf_op jit(solution)/shard_map/ppermute | solution.py:234
  111.9 9.6 %collective-permute-start.25 = (f16[64,2048]{1,0:T(8,128)(2,1)S(1)}, f16[64,2048]{1,0:T(8,128)(2,1)S(1)}, u32[]{:S(2)}, u32[]{:S(2)}) collective-permute-start(f16[64,2048]{1,0:T(8,128)(2,1)S(1)} %add_convert_fusion.2), channel_id=1, source_target_pairs={{16,0},{97,1},{18,2},{99,3},{20,4},{101,5},{22,6},{103,7},{24,8},{... | collective-permute-start | bytes 786440 | tf_op jit(solution)/shard_map/ppermute | solution.py:234
  114.9 10.9 %collective-permute-start.27 = (f16[64,2048]{1,0:T(8,128)(2,1)}, f16[64,2048]{1,0:T(8,128)(2,1)S(1)}, u32[]{:S(2)}, u32[]{:S(2)}) collective-permute-start(f16[64,2048]{1,0:T(8,128)(2,1)} %add_convert_fusion.1), channel_id=1, source_target_pairs={{4,0},{5,1},{30,2},{31,3},{34,4},{39,5},{60,6},{57,7},{72,8},{73,9... | collective-permute-start | bytes 786440 | tf_op jit(solution)/shard_map/ppermute | solution.py:234
  122.3 1.6 %collective-permute-start.26 = (f32[6,64]{1,0:T(8,128)S(1)}, f32[6,64]{1,0:T(8,128)S(1)}, u32[]{:S(2)}, u32[]{:S(2)}) collective-permute-start(f32[6,64]{1,0:T(8,128)S(1)} %stack.51), channel_id=1, source_target_pairs={{1,0},{0,1},{3,2},{2,3},{5,4},{4,5},{7,6},{6,7},{9,8},{8,9},{11,10... | collective-permute-start | bytes 4616 | tf_op jit(solution)/shard_map/ppermute | solution.py:234
  125.8 3.6 %collective-permute-start.28 = (f32[6,64]{1,0:T(8,128)S(1)}, f32[6,64]{1,0:T(8,128)S(1)}, u32[]{:S(2)}, u32[]{:S(2)}) collective-permute-start(f32[6,64]{1,0:T(8,128)S(1)} %add.166), channel_id=1, source_target_pairs={{8,0},{9,1},{10,2},{11,3},{12,4},{13,5},{14,6},{15,7},{0,8},{1,9},... | collective-permute-start | bytes 4616 | tf_op jit(solution)/shard_map/ppermute | solution.py:234
  129.4 3.6 %collective-permute-start.29 = (f32[6,64]{1,0:T(8,128)S(1)}, f32[6,64]{1,0:T(8,128)S(1)}, u32[]{:S(2)}, u32[]{:S(2)}) collective-permute-start(f32[6,64]{1,0:T(8,128)S(1)} %add.167), channel_id=1, source_target_pairs={{2,0},{3,1},{0,2},{1,3},{6,4},{7,5},{4,6},{5,7},{10,8},{11,9},{8,1... | collective-permute-start | bytes 4616 | tf_op jit(solution)/shard_map/ppermute | solution.py:234
  133.0 4.8 %collective-permute-start.30 = (f32[6,64]{1,0:T(8,128)S(1)}, f32[6,64]{1,0:T(8,128)S(1)}, u32[]{:S(2)}, u32[]{:S(2)}) collective-permute-start(f32[6,64]{1,0:T(8,128)S(1)} %add.168), channel_id=1, source_target_pairs={{6,0},{7,1},{4,2},{5,3},{2,4},{3,5},{0,6},{1,7},{14,8},{15,9},{12,... | collective-permute-start | bytes 4616 | tf_op jit(solution)/shard_map/ppermute | solution.py:234

commit v8 on v7

--- a/solution.py
+++ b/solution.py
@@ -181,7 +181,7 @@
         out_shape=jax.ShapeDtypeStruct((reps, count), F32),
         scratch_shapes=[
             pltpu.VMEM((count, columns), BF16),
-            pltpu.SemaphoreType.DMA((8,)),
+            pltpu.SemaphoreType.DMA((count // 512,)),
         ],
         compiler_params=pltpu.CompilerParams(vmem_limit_bytes=16 << 20),
         cost_estimate=pl.CostEstimate(
@@ -336,18 +336,18 @@
     _, u_half = first_step(keep_half, g_half, held)
     u_half = (slope_half * u_half).astype(BF16)
     half = move(u_half, HALF_TO_ROWS)
-    columns, _ = tie(columns, u_half)
+    columns, _, late = tie(columns, u_half, held)
+    product = put(low_half, late, move(late, ROW_STEPS[0]))
     scale = FIRST_SCALE / shadow_top
     q1 = keep * gs - (COUPLE_GAIN / scale) * slope * columns.astype(F32)
     us = gs - alpha_c * q1
 
     shadow_partial = shadow(us.astype(BF16), coupling)
-    half, shadow_partial, held = tie(half, shadow_partial, held)
+    half, shadow_partial, product = tie(half, shadow_partial, product)
     block = put(z_even, half, move(half, Z_PAIR))
     scale = SECOND_SCALE / shadow_top
     shadow_held = send_core(jnp.split(shadow_partial, 2, axis=1), scale)
-    product = put(low_half, held, move(held, ROW_STEPS[0]))
-    block, shadow_held, product = tie(block, shadow_held, product)
+    block, shadow_held = tie(block, shadow_held)
     left = put(first, block, move(block, CORE))
     partial = primary(left, coupling)
     shadow_held = exchange(shadow_held, COL_STEPS[0])

time: 142 us -> 141 us (level)
  waiting for transfers between devices: 52.2 us -> 56.5 us
  Pallas kernels: 34.9 us -> 30.8 us
    ppermute x31, waiting for transfers between devices: 52.2 us -> 56.5 us  [move(): return lax.ppermute(value, AXES, pairs)]
    pallas_call x2, Pallas kernels: 13.4 us -> 9.31 us  [shadow_rows(): pl.pallas_call(kernel, name='shadow_rows', in_specs=[spec, pl.BlockSpec(m...]
  transfers between devices with their start and end apart: 31 -> 31, of which waited for: 23 -> 20; matrix products, arithmetic and copies ran while one was open for 2% -> 2% of each run, Pallas kernels for 25% -> 22%
where the time goes in v8:
time: 141 us; the launch traced here: 140 us
  waiting for transfers between devices  56.5 us (40%)
  starting transfers between devices  43.1 us (31%)
  Pallas kernels  30.8 us (22%)
  other arithmetic  8.82 us (6%)
    ppermute x31, waiting for transfers between devices, move(): return lax.ppermute(value, AXES, pairs)  56.5 us
    ppermute x31, starting transfers between devices, move(): return lax.ppermute(value, AXES, pairs)  43.1 us
    pallas_call x2, Pallas kernels, call(): pl.pallas_call(kernel, name=name, in_specs=[spec, pl.BlockSpec(memory_spa...  14 us
    pallas_call x2, Pallas kernels, shadow_rows(): pl.pallas_call(kernel, name='shadow_rows', in_specs=[spec, pl.BlockSpec(m...  9.31 us
    pallas_call x2, Pallas kernels, primary_half(): pl.pallas_call(half_kernel, name='primary_half', in_specs=[pl.BlockSpec(m...  7.56 us
    sub x1, other arithmetic, on_device(): shadow_residual = gs - step * q1 - step_next * (lead * q1 + kappa * q2)  2.83 us
  transfers between devices with their start and end apart: 31, of which 20 were waited for; matrix products, arithmetic and copies ran while one was open for 2% of the time, Pallas kernels for 22%

profile of v8, /device:TPU:0, one launch (start us, length us, event | category | flops | bytes accessed | tf_op | source)
XLA Modules:
  0.0 140.4 jit_solution(6601361525146938370)
XLA Ops:
  0.6 1.9 %multiply_reduce_fusion.7 = (f32[64]{0:T(128)S(1)}, f32[64]{0:T(128)S(1)}, f32[64]{0:T(128)S(1)}, f32[64]{0:T(128)S(1)}, bf16[64,2048]{1,0:T(8,128)(2,1)S(1)}, /...) fusion(f32[64,2048]{1,0:T(8,128)} %param.7, f32[64,2048]{1,0:T(8,128)} %param.6, ...), kind=kLoop, calls=%fused_computation.35 | loop fusion | flops 2096896 | bytes 3146752 | tf_op jit(solution)/shard_map/reduce_sum | solution.py:258
  2.7 4.0 %collective-permute-start.3 = (bf16[64,1024]{1,0:T(8,128)(2,1)S(1)}, bf16[64,1024]{1,0:T(8,128)(2,1)S(1)}, u32[]{:S(2)}, u32[]{:S(2)}) collective-permute-start(bf16[64,1024]{1,0:T(8,128)(2,1)S(1)} %slice_select_fusion.2), channel_id=1, source_target_pairs={{112,0},{65,1},{48,2},{113,3},{0,4},{33,5},{64,6},{17,7},{96,8},{9... | collective-permute-start | bytes 393224 | tf_op jit(solution)/shard_map/ppermute | solution.py:234
  6.8 0.7 collective-permute-start.1
  7.5 4.7 %shadow_rows.2 = f32[64,2048]{1,0:T(8,128)S(1)} custom-call(bf16[64,2048]{1,0:T(8,128)(2,1)S(1)} %get-tuple-element.36.left_ref, bf16[4096,2048]{1,0:T(8,128)(2,1)} %coupling_ref.11), custom_call_target="tpu_custom_call" | custom-call | flops 536870912 | bytes 8388608 | tf_op jit(solution)/shard_map/shadow_rows/pallas_call | solution.py:176
  12.2 4.5 %collective-permute-start.2 = (f32[4,64]{1,0:T(4,128)S(1)}, f32[4,64]{1,0:T(4,128)S(1)}, u32[]{:S(2)}, u32[]{:S(2)}) collective-permute-start(f32[4,64]{1,0:T(4,128)S(1)} %pad_maximum_fusion.7), channel_id=1, source_target_pairs={{2,0},{3,1},{0,2},{1,3},{6,4},{7,5},{4,6},{5,7},{10,8},{11,9},{8,1... | collective-permute-start | bytes 3080 | tf_op jit(solution)/shard_map/ppermute | solution.py:234
  16.7 4.7 %shadow_rows.3 = f32[64,2048]{1,0:T(8,128)S(1)} custom-call(bf16[64,2048]{1,0:T(8,128)(2,1)S(1)} %get-tuple-element.36.left_ref, bf16[4096,2048]{1,0:T(8,128)(2,1)} %coupling_ref.11), custom_call_target="tpu_custom_call" | custom-call | flops 536870912 | bytes 8388608 | tf_op jit(solution)/shard_map/shadow_rows/pallas_call | solution.py:176
  21.4 0.1 collective-permute-start.4
  21.5 0.5 collective-permute-start.5
  22.0 4.2 %collective-permute-done.4 = f32[4,64]{1,0:T(4,128)S(1)} collective-permute-done((f32[4,64]{1,0:T(4,128)S(1)}, f32[4,64]{1,0:T(4,128)S(1)}, u32[]{:S(2)}, u32[]{:S(2)}) %collective-permute-start.4) | collective-permute-done | bytes 1056 | tf_op jit(solution)/shard_map/ppermute | solution.py:234
  26.3 0.3 collective-permute-done.5
  26.8 0.1 multiply_convert_fusion.2
  26.9 0.6 collective-permute-start.7
  27.4 0.8 collective-permute-done.6
  28.4 0.3 collective-permute-done.7
  28.6 0.2 add_convert_fusion.10
  28.8 0.4 collective-permute-start.8
  29.2 3.8 %primary_half.3 = f32[64,1024]{1,0:T(8,128)S(1)} custom-call(s32[1]{0:T(128)} %bitcast.9.offset_ref, bf16[64,4096]{1,0:T(8,128)(2,1)S(1)} %pad_maximum_fusion.left_ref, bf16[4096,2048]{1,0:T(8,128)(2,1)} %coupling_ref.11), custom_call_target="tpu_custom_call" | custom-call | flops 536870912 | bytes 8388608 | tf_op jit(solution)/shard_map/primary_half/pallas_call | solution.py:210
  33.1 0.1 multiply_convert_fusion.4
  33.1 3.1 %collective-permute-start.9 = (f16[64,1024]{1,0:T(8,128)(2,1)S(1)}, f16[64,1024]{1,0:T(8,128)(2,1)S(1)}, u32[]{:S(2)}, u32[]{:S(2)}) collective-permute-start(f16[64,1024]{1,0:T(8,128)(2,1)S(1)} %multiply_convert_fusion.4), channel_id=1, source_target_pairs={{32,0},{17,1},{34,2},{19,3},{36,4},{21,5},{38,6},{23,7},{40,8},{25... | collective-permute-start | bytes 393224 | tf_op jit(solution)/shard_map/ppermute | solution.py:234
  36.3 3.7 %primary_half.2 = f32[64,1024]{1,0:T(8,128)S(1)} custom-call(s32[1]{0:T(128)} %bitcast.6.offset_ref, bf16[64,4096]{1,0:T(8,128)(2,1)S(1)} %pad_maximum_fusion.left_ref, bf16[4096,2048]{1,0:T(8,128)(2,1)} %coupling_ref.11), custom_call_target="tpu_custom_call" | custom-call | flops 536870912 | bytes 8388608 | tf_op jit(solution)/shard_map/primary_half/pallas_call | solution.py:210
  40.1 1.3 collective-permute-start.10
  41.4 0.1 add_convert_fusion.13
  41.5 5.1 %collective-permute-done.10 = f16[64,2048]{1,0:T(8,128)(2,1)S(1)} collective-permute-done((f16[64,2048]{1,0:T(8,128)(2,1)S(1)}, f16[64,2048]{1,0:T(8,128)(2,1)S(1)}, u32[]{:S(2)}, u32[]{:S(2)}) %collective-permute-start.10) | collective-permute-done | bytes 262176 | tf_op jit(solution)/shard_map/ppermute | solution.py:234
  46.7 0.3 collective-permute-start.11
  47.0 2.3 %collective-permute-start.12 = (f16[64,2048]{1,0:T(8,128)(2,1)S(1)}, f16[64,2048]{1,0:T(8,128)(2,1)S(1)}, u32[]{:S(2)}, u32[]{:S(2)}) collective-permute-start(f16[64,2048]{1,0:T(8,128)(2,1)S(1)} %add_convert_fusion.8), channel_id=1, source_target_pairs={{6,0},{9,1},{4,2},{11,3},{2,4},{13,5},{0,6},{15,7},{14,8},{1,9},{1... | collective-permute-start | bytes 786440 | tf_op jit(solution)/shard_map/ppermute | solution.py:234
  49.3 3.6 %collective-permute-done.11 = f16[64,1024]{1,0:T(8,128)(2,1)S(1)} collective-permute-done((f16[64,1024]{1,0:T(8,128)(2,1)S(1)}, f16[64,1024]{1,0:T(8,128)(2,1)S(1)}, u32[]{:S(2)}, u32[]{:S(2)}) %collective-permute-start.11) | collective-permute-done | bytes 131104 | tf_op jit(solution)/shard_map/ppermute | solution.py:234
  53.0 1.6 %collective-permute-done.12 = f16[64,2048]{1,0:T(8,128)(2,1)S(1)} collective-permute-done((f16[64,2048]{1,0:T(8,128)(2,1)S(1)}, f16[64,2048]{1,0:T(8,128)(2,1)S(1)}, u32[]{:S(2)}, u32[]{:S(2)}) %collective-permute-start.12) | collective-permute-done | bytes 262176 | tf_op jit(solution)/shard_map/ppermute | solution.py:234
  54.6 2.2 %collective-permute-start.13 = (f16[64,1024]{1,0:T(8,128)(2,1)S(1)}, f16[64,1024]{1,0:T(8,128)(2,1)S(1)}, u32[]{:S(2)}, u32[]{:S(2)}) collective-permute-start(f16[64,1024]{1,0:T(8,128)(2,1)S(1)} %add_convert_fusion.12), channel_id=1, source_target_pairs={{16,0},{97,1},{18,2},{99,3},{20,4},{101,5},{22,6},{103,7},{24,8},{... | collective-permute-start | bytes 393224 | tf_op jit(solution)/shard_map/ppermute | solution.py:234
  56.8 2.5 %collective-permute-start.15 = (f16[64,2048]{1,0:T(8,128)(2,1)S(1)}, f16[64,2048]{1,0:T(8,128)(2,1)S(1)}, u32[]{:S(2)}, u32[]{:S(2)}) collective-permute-start(f16[64,2048]{1,0:T(8,128)(2,1)S(1)} %add_convert_fusion.7), channel_id=1, source_target_pairs={{4,0},{5,1},{30,2},{31,3},{34,4},{39,5},{60,6},{57,7},{72,8},{73,9... | collective-permute-start | bytes 786440 | tf_op jit(solution)/shard_map/ppermute | solution.py:234
  59.3 2.2 %collective-permute-done.13 = f16[64,1024]{1,0:T(8,128)(2,1)S(1)} collective-permute-done((f16[64,1024]{1,0:T(8,128)(2,1)S(1)}, f16[64,1024]{1,0:T(8,128)(2,1)S(1)}, u32[]{:S(2)}, u32[]{:S(2)}) %collective-permute-start.13) | collective-permute-done | bytes 131104 | tf_op jit(solution)/shard_map/ppermute | solution.py:234
  61.5 0.2 fusion.6
  61.6 0.6 collective-permute-start.14
  62.3 2.4 %collective-permute-done.15 = f16[64,2048]{1,0:T(8,128)(2,1)S(1)} collective-permute-done((f16[64,2048]{1,0:T(8,128)(2,1)S(1)}, f16[64,2048]{1,0:T(8,128)(2,1)S(1)}, u32[]{:S(2)}, u32[]{:S(2)}) %collective-permute-start.15) | collective-permute-done | bytes 262176 | tf_op jit(solution)/shard_map/ppermute | solution.py:234
  64.7 3.1 %collective-permute-start.16 = (f16[64,1024]{1,0:T(8,128)(2,1)S(1)}, f16[64,1024]{1,0:T(8,128)(2,1)S(1)}, u32[]{:S(2)}, u32[]{:S(2)}) collective-permute-start(f16[64,1024]{1,0:T(8,128)(2,1)S(1)} %get-tuple-element.52), channel_id=1, source_target_pairs={{32,0},{17,1},{34,2},{19,3},{36,4},{21,5},{38,6},{23,7},{40,8},{25... | collective-permute-start | bytes 393224 | tf_op jit(solution)/shard_map/ppermute | solution.py:234
  67.7 0.2 fusion.15
  68.0 7.7 %shadow.1 = f32[64,4096]{1,0:T(8,128)S(1)} custom-call(bf16[64,2048]{1,0:T(8,128)(2,1)S(1)} %get-tuple-element.82.left_ref, bf16[4096,2048]{1,0:T(8,128)(2,1)} %coupling_ref.11), custom_call_target="tpu_custom_call" | custom-call | flops 1073741824 | bytes 16777216 | tf_op jit(solution)/shard_map/shadow/pallas_call | solution.py:140
  75.9 1.5 %collective-permute-start.17 = (bf16[64,1024]{1,0:T(8,128)(2,1)S(1)}, bf16[64,1024]{1,0:T(8,128)(2,1)S(1)}, u32[]{:S(2)}, u32[]{:S(2)}) collective-permute-start(bf16[64,1024]{1,0:T(8,128)(2,1)S(1)} %collective-permute-done.14), channel_id=1, source_target_pairs={{2,0},{3,1},{0,2},{1,3},{6,4},{7,5},{4,6},{5,7},{10,8},{11,9},{8,1... | collective-permute-start | bytes 393224 | tf_op jit(solution)/shard_map/ppermute | solution.py:234
  77.3 0.1 multiply_convert_fusion.1
  77.5 4.7 %collective-permute-done.17 = bf16[64,1024]{1,0:T(8,128)(2,1)S(1)} collective-permute-done((bf16[64,1024]{1,0:T(8,128)(2,1)S(1)}, bf16[64,1024]{1,0:T(8,128)(2,1)S(1)}, u32[]{:S(2)}, u32[]{:S(2)}) %collective-permute-start.17) | collective-permute-done | bytes 131104 | tf_op jit(solution)/shard_map/ppermute | solution.py:234
  82.4 0.2 add_convert_fusion.6
  82.5 0.2 collective-permute-start.19
  82.7 1.4 %collective-permute-done.19 = bf16[64,2048]{1,0:T(8,128)(2,1)S(1)} collective-permute-done((bf16[64,2048]{1,0:T(8,128)(2,1)S(1)}, bf16[64,2048]{1,0:T(8,128)(2,1)S(1)}, u32[]{:S(2)}, u32[]{:S(2)}) %collective-permute-start.19) | collective-permute-done | bytes 262176 | tf_op jit(solution)/shard_map/ppermute | solution.py:234
  84.3 6.2 %primary.1 = f32[64,2048]{1,0:T(8,128)S(1)} custom-call(bf16[64,4096]{1,0:T(8,128)(2,1)S(1)} %pad_maximum_fusion.1.left_ref, bf16[4096,2048]{1,0:T(8,128)(2,1)} %coupling_ref.11), custom_call_target="tpu_custom_call" | custom-call | flops 1073741824 | bytes 16777216 | tf_op jit(solution)/shard_map/primary/pallas_call | solution.py:140
  90.6 0.1 multiply_convert_fusion
  90.7 0.1 collective-permute-start.21
  90.8 0.7 collective-permute-start.22
  91.5 5.7 %collective-permute-done.21 = f16[64,2048]{1,0:T(8,128)(2,1)S(1)} collective-permute-done((f16[64,2048]{1,0:T(8,128)(2,1)S(1)}, f16[64,2048]{1,0:T(8,128)(2,1)S(1)}, u32[]{:S(2)}, u32[]{:S(2)}) %collective-permute-start.21) | collective-permute-done | bytes 262176 | tf_op jit(solution)/shard_map/ppermute | solution.py:234
  97.2 0.1 add_convert_fusion.4
  97.4 1.9 %collective-permute-start.23 = (f16[64,2048]{1,0:T(8,128)(2,1)S(1)}, f16[64,2048]{1,0:T(8,128)(2,1)S(1)}, u32[]{:S(2)}, u32[]{:S(2)}) collective-permute-start(f16[64,2048]{1,0:T(8,128)(2,1)S(1)} %add_convert_fusion.4), channel_id=1, source_target_pairs={{96,0},{33,1},{98,2},{35,3},{100,4},{37,5},{102,6},{39,7},{104,8},... | collective-permute-start | bytes 786440 | tf_op jit(solution)/shard_map/ppermute | solution.py:234
  99.3 5.4 %collective-permute-start.24 = (f16[64,2048]{1,0:T(8,128)(2,1)S(1)}, f16[64,2048]{1,0:T(8,128)(2,1)S(1)}, u32[]{:S(2)}, u32[]{:S(2)}) collective-permute-start(f16[64,2048]{1,0:T(8,128)(2,1)S(1)} %add_convert_fusion.3), channel_id=1, source_target_pairs={{6,0},{9,1},{4,2},{11,3},{2,4},{13,5},{0,6},{15,7},{14,8},{1,9},{1... | collective-permute-start | bytes 786440 | tf_op jit(solution)/shard_map/ppermute | solution.py:234
  104.7 0.3 collective-permute-done.23
  105.2 3.9 %collective-permute-done.24 = f16[64,2048]{1,0:T(8,128)(2,1)S(1)} collective-permute-done((f16[64,2048]{1,0:T(8,128)(2,1)S(1)}, f16[64,2048]{1,0:T(8,128)(2,1)S(1)}, u32[]{:S(2)}, u32[]{:S(2)}) %collective-permute-start.24) | collective-permute-done | bytes 262176 | tf_op jit(solution)/shard_map/ppermute | solution.py:234
  109.1 0.8 add_convert_fusion.1
  109.9 4.7 %collective-permute-start.25 = (f16[64,2048]{1,0:T(8,128)(2,1)S(1)}, f16[64,2048]{1,0:T(8,128)(2,1)S(1)}, u32[]{:S(2)}, u32[]{:S(2)}) collective-permute-start(f16[64,2048]{1,0:T(8,128)(2,1)S(1)} %add_convert_fusion.2), channel_id=1, source_target_pairs={{16,0},{97,1},{18,2},{99,3},{20,4},{101,5},{22,6},{103,7},{24,8},{... | collective-permute-start | bytes 786440 | tf_op jit(solution)/shard_map/ppermute | solution.py:234
  114.6 1.5 %collective-permute-start.27 = (f16[64,2048]{1,0:T(8,128)(2,1)}, f16[64,2048]{1,0:T(8,128)(2,1)S(1)}, u32[]{:S(2)}, u32[]{:S(2)}) collective-permute-start(f16[64,2048]{1,0:T(8,128)(2,1)} %add_convert_fusion.1), channel_id=1, source_target_pairs={{4,0},{5,1},{30,2},{31,3},{34,4},{39,5},{60,6},{57,7},{72,8},{73,9... | collective-permute-start | bytes 786440 | tf_op jit(solution)/shard_map/ppermute | solution.py:234
  116.1 5.3 %collective-permute-done.25 = f16[64,2048]{1,0:T(8,128)(2,1)S(1)} collective-permute-done((f16[64,2048]{1,0:T(8,128)(2,1)S(1)}, f16[64,2048]{1,0:T(8,128)(2,1)S(1)}, u32[]{:S(2)}, u32[]{:S(2)}) %collective-permute-start.25) | collective-permute-done | bytes 262176 | tf_op jit(solution)/shard_map/ppermute | solution.py:234
  121.3 0.8 multiply_reduce_fusion
  122.2 1.2 collective-permute-done.26
  123.4 2.1 %collective-permute-done.27 = f16[64,2048]{1,0:T(8,128)(2,1)S(1)} collective-permute-done((f16[64,2048]{1,0:T(8,128)(2,1)}, f16[64,2048]{1,0:T(8,128)(2,1)S(1)}, u32[]{:S(2)}, u32[]{:S(2)}) %collective-permute-start.27) | collective-permute-done | bytes 262176 | tf_op jit(solution)/shard_map/ppermute | solution.py:234
  125.5 3.6 %collective-permute-done.28 = f32[6,64]{1,0:T(8,128)S(1)} collective-permute-done((f32[6,64]{1,0:T(8,128)S(1)}, f32[6,64]{1,0:T(8,128)S(1)}, u32[]{:S(2)}, u32[]{:S(2)}) %collective-permute-start.28) | collective-permute-done | bytes 1568 | tf_op jit(solution)/shard_map/ppermute | solution.py:234
  129.1 0.6 collective-permute-start.29
  129.7 3.0 %collective-permute-done.29 = f32[6,64]{1,0:T(8,128)S(1)} collective-permute-done((f32[6,64]{1,0:T(8,128)S(1)}, f32[6,64]{1,0:T(8,128)S(1)}, u32[]{:S(2)}, u32[]{:S(2)}) %collective-permute-start.29) | collective-permute-done | bytes 1568 | tf_op jit(solution)/shard_map/ppermute | solution.py:234
  132.7 4.8 %collective-permute-done.30 = f32[6,64]{1,0:T(8,128)S(1)} collective-permute-done((f32[6,64]{1,0:T(8,128)S(1)}, f32[6,64]{1,0:T(8,128)S(1)}, u32[]{:S(2)}, u32[]{:S(2)}) %collective-permute-start.30) | collective-permute-done | bytes 1568 | tf_op jit(solution)/shard_map/ppermute | solution.py:234
  137.5 2.8 %multiply_subtract_fusion = (f32[64,2048]{1,0:T(8,128)}, f32[64,2048]{1,0:T(8,128)}, f32[64,2048]{1,0:T(8,128)}, f32[64,2048]{1,0:T(8,128)}) fusion(f16[64,2048]{1,0:T(8,128)(2,1)S(1)} %collective-permute-done.27, f32[64,2048]{1,0:T(8,128)S(1)} %get-tuple-element.83, f32[64,2048]{1,0:T(8,128)S(1)} %copy-done, f16[64,2048]{1,0:T(8,128)(2,1)S(1)} %collective-permute-done.15, ...), kind=kLoop, calls=%fused_computation.2 | loop fusion | flops 7077888 | bytes 5507328 | tf_op jit(solution)/shard_map/sub | solution.py:406
  (60 shorter events, 1.5 us)
Async XLA Ops:
  2.6 4.2 %collective-permute-start = (f32[4,64]{1,0:T(4,128)S(1)}, f32[4,64]{1,0:T(4,128)S(1)}, u32[]{:S(2)}, u32[]{:S(2)}) collective-permute-start(f32[4,64]{1,0:T(4,128)S(1)} %pad_maximum_fusion.5), channel_id=1, source_target_pairs={{1,0},{0,1},{3,2},{2,3},{5,4},{4,5},{7,6},{6,7},{9,8},{8,9},{11,10... | collective-permute-start | bytes 3080 | tf_op jit(solution)/shard_map/ppermute | solution.py:234
  2.7 18.6 %collective-permute-start.3 = (bf16[64,1024]{1,0:T(8,128)(2,1)S(1)}, bf16[64,1024]{1,0:T(8,128)(2,1)S(1)}, u32[]{:S(2)}, u32[]{:S(2)}) collective-permute-start(bf16[64,1024]{1,0:T(8,128)(2,1)S(1)} %slice_select_fusion.2), channel_id=1, source_target_pairs={{112,0},{65,1},{48,2},{113,3},{0,4},{33,5},{64,6},{17,7},{96,8},{9... | collective-permute-start | bytes 393224 | tf_op jit(solution)/shard_map/ppermute | solution.py:234
  6.8 5.4 %collective-permute-start.1 = (f32[4,64]{1,0:T(4,128)S(1)}, f32[4,64]{1,0:T(4,128)S(1)}, u32[]{:S(2)}, u32[]{:S(2)}) collective-permute-start(f32[4,64]{1,0:T(4,128)S(1)} %pad_maximum_fusion.6), channel_id=1, source_target_pairs={{8,0},{9,1},{10,2},{11,3},{12,4},{13,5},{14,6},{15,7},{0,8},{1,9},... | collective-permute-start | bytes 3080 | tf_op jit(solution)/shard_map/ppermute | solution.py:234
  12.2 9.1 %collective-permute-start.2 = (f32[4,64]{1,0:T(4,128)S(1)}, f32[4,64]{1,0:T(4,128)S(1)}, u32[]{:S(2)}, u32[]{:S(2)}) collective-permute-start(f32[4,64]{1,0:T(4,128)S(1)} %pad_maximum_fusion.7), channel_id=1, source_target_pairs={{2,0},{3,1},{0,2},{1,3},{6,4},{7,5},{4,6},{5,7},{10,8},{11,9},{8,1... | collective-permute-start | bytes 3080 | tf_op jit(solution)/shard_map/ppermute | solution.py:234
  21.4 4.9 %collective-permute-start.4 = (f32[4,64]{1,0:T(4,128)S(1)}, f32[4,64]{1,0:T(4,128)S(1)}, u32[]{:S(2)}, u32[]{:S(2)}) collective-permute-start(f32[4,64]{1,0:T(4,128)S(1)} %pad_maximum_fusion.8), channel_id=1, source_target_pairs={{6,0},{7,1},{4,2},{5,3},{2,4},{3,5},{0,6},{1,7},{14,8},{15,9},{12,... | collective-permute-start | bytes 3080 | tf_op jit(solution)/shard_map/ppermute | solution.py:234
  21.5 5.1 %collective-permute-start.5 = (bf16[64,1024]{1,0:T(8,128)(2,1)S(1)}, bf16[64,1024]{1,0:T(8,128)(2,1)S(1)}, u32[]{:S(2)}, u32[]{:S(2)}) collective-permute-start(bf16[64,1024]{1,0:T(8,128)(2,1)S(1)} %collective-permute-done.3), channel_id=1, source_target_pairs={{2,0},{3,1},{0,2},{1,3},{6,4},{7,5},{4,6},{5,7},{10,8},{11,9},{8,1... | collective-permute-start | bytes 393224 | tf_op jit(solution)/shard_map/ppermute | solution.py:234
  26.7 1.6 %collective-permute-start.6 = (bf16[64,2048]{1,0:T(8,128)(2,1)S(1)}, bf16[64,2048]{1,0:T(8,128)(2,1)S(1)}, u32[]{:S(2)}, u32[]{:S(2)}) collective-permute-start(bf16[64,2048]{1,0:T(8,128)(2,1)S(1)} %pad_maximum_fusion.2), channel_id=1, source_target_pairs={{1,0},{0,1},{3,2},{2,3},{5,4},{4,5},{7,6},{6,7},{9,8},{8,9},{11,10... | collective-permute-start | bytes 786440 | tf_op jit(solution)/shard_map/ppermute | solution.py:234
  26.9 1.8 %collective-permute-start.7 = (f16[64,2048]{1,0:T(8,128)(2,1)S(1)}, f16[64,2048]{1,0:T(8,128)(2,1)S(1)}, u32[]{:S(2)}, u32[]{:S(2)}) collective-permute-start(f16[64,2048]{1,0:T(8,128)(2,1)S(1)} %multiply_convert_fusion.2), channel_id=1, source_target_pairs={{1,0},{0,1},{3,2},{2,3},{5,4},{4,5},{7,6},{6,7},{9,8},{8,9},{11,10... | collective-permute-start | bytes 786440 | tf_op jit(solution)/shard_map/ppermute | solution.py:234
  28.8 11.2 %collective-permute-start.8 = (f16[64,2048]{1,0:T(8,128)(2,1)S(1)}, f16[64,2048]{1,0:T(8,128)(2,1)S(1)}, u32[]{:S(2)}, u32[]{:S(2)}) collective-permute-start(f16[64,2048]{1,0:T(8,128)(2,1)S(1)} %add_convert_fusion.10), channel_id=1, source_target_pairs={{8,0},{3,1},{10,2},{1,3},{12,4},{7,5},{14,6},{5,7},{0,8},{11,9},{2... | collective-permute-start | bytes 786440 | tf_op jit(solution)/shard_map/ppermute | solution.py:234
  29.2 32.3 %copy-start.1 = (f32[64,2048]{1,0:T(8,128)S(1)}, f32[64,2048]{1,0:T(8,128)}, u32[]{:S(2)}) copy-start(f32[64,2048]{1,0:T(8,128)} %param.6) | copy-start | bytes 1572868
  29.2 38.5 %copy-start = (f32[64,2048]{1,0:T(8,128)S(1)}, f32[64,2048]{1,0:T(8,128)}, u32[]{:S(2)}) copy-start(f32[64,2048]{1,0:T(8,128)} %param.7) | copy-start | bytes 1572868
  29.2 38.5 %copy-start.2 = (f32[64,2048]{1,0:T(8,128)S(1)}, f32[64,2048]{1,0:T(8,128)}, u32[]{:S(2)}) copy-start(f32[64,2048]{1,0:T(8,128)} %param.5) | copy-start | bytes 1572868
  33.1 8.2 %collective-permute-start.9 = (f16[64,1024]{1,0:T(8,128)(2,1)S(1)}, f16[64,1024]{1,0:T(8,128)(2,1)S(1)}, u32[]{:S(2)}, u32[]{:S(2)}) collective-permute-start(f16[64,1024]{1,0:T(8,128)(2,1)S(1)} %multiply_convert_fusion.4), channel_id=1, source_target_pairs={{32,0},{17,1},{34,2},{19,3},{36,4},{21,5},{38,6},{23,7},{40,8},{25... | collective-permute-start | bytes 393224 | tf_op jit(solution)/shard_map/ppermute | solution.py:234
  40.1 6.5 %collective-permute-start.10 = (f16[64,2048]{1,0:T(8,128)(2,1)S(1)}, f16[64,2048]{1,0:T(8,128)(2,1)S(1)}, u32[]{:S(2)}, u32[]{:S(2)}) collective-permute-start(f16[64,2048]{1,0:T(8,128)(2,1)S(1)} %add_convert_fusion.9), channel_id=1, source_target_pairs={{2,0},{7,1},{0,2},{5,3},{6,4},{3,5},{4,6},{1,7},{10,8},{15,9},{8,1... | collective-permute-start | bytes 786440 | tf_op jit(solution)/shard_map/ppermute | solution.py:234
  46.7 6.3 %collective-permute-start.11 = (f16[64,1024]{1,0:T(8,128)(2,1)S(1)}, f16[64,1024]{1,0:T(8,128)(2,1)S(1)}, u32[]{:S(2)}, u32[]{:S(2)}) collective-permute-start(f16[64,1024]{1,0:T(8,128)(2,1)S(1)} %add_convert_fusion.13), channel_id=1, source_target_pairs={{96,0},{33,1},{98,2},{35,3},{100,4},{37,5},{102,6},{39,7},{104,8},... | collective-permute-start | bytes 393224 | tf_op jit(solution)/shard_map/ppermute | solution.py:234
  47.0 7.6 %collective-permute-start.12 = (f16[64,2048]{1,0:T(8,128)(2,1)S(1)}, f16[64,2048]{1,0:T(8,128)(2,1)S(1)}, u32[]{:S(2)}, u32[]{:S(2)}) collective-permute-start(f16[64,2048]{1,0:T(8,128)(2,1)S(1)} %add_convert_fusion.8), channel_id=1, source_target_pairs={{6,0},{9,1},{4,2},{11,3},{2,4},{13,5},{0,6},{15,7},{14,8},{1,9},{1... | collective-permute-start | bytes 786440 | tf_op jit(solution)/shard_map/ppermute | solution.py:234
  54.6 6.8 %collective-permute-start.13 = (f16[64,1024]{1,0:T(8,128)(2,1)S(1)}, f16[64,1024]{1,0:T(8,128)(2,1)S(1)}, u32[]{:S(2)}, u32[]{:S(2)}) collective-permute-start(f16[64,1024]{1,0:T(8,128)(2,1)S(1)} %add_convert_fusion.12), channel_id=1, source_target_pairs={{16,0},{97,1},{18,2},{99,3},{20,4},{101,5},{22,6},{103,7},{24,8},{... | collective-permute-start | bytes 393224 | tf_op jit(solution)/shard_map/ppermute | solution.py:234
  56.8 7.9 %collective-permute-start.15 = (f16[64,2048]{1,0:T(8,128)(2,1)S(1)}, f16[64,2048]{1,0:T(8,128)(2,1)S(1)}, u32[]{:S(2)}, u32[]{:S(2)}) collective-permute-start(f16[64,2048]{1,0:T(8,128)(2,1)S(1)} %add_convert_fusion.7), channel_id=1, source_target_pairs={{4,0},{5,1},{30,2},{31,3},{34,4},{39,5},{60,6},{57,7},{72,8},{73,9... | collective-permute-start | bytes 786440 | tf_op jit(solution)/shard_map/ppermute | solution.py:234
  61.6 14.2 %collective-permute-start.14 = (bf16[64,1024]{1,0:T(8,128)(2,1)S(1)}, bf16[64,1024]{1,0:T(8,128)(2,1)S(1)}, u32[]{:S(2)}, u32[]{:S(2)}) collective-permute-start(bf16[64,1024]{1,0:T(8,128)(2,1)S(1)} %get-tuple-element.84), channel_id=1, source_target_pairs={{112,0},{65,1},{48,2},{113,3},{0,4},{33,5},{64,6},{17,7},{96,8},{9... | collective-permute-start | bytes 393224 | tf_op jit(solution)/shard_map/ppermute | solution.py:234
  64.7 11.1 %collective-permute-start.16 = (f16[64,1024]{1,0:T(8,128)(2,1)S(1)}, f16[64,1024]{1,0:T(8,128)(2,1)S(1)}, u32[]{:S(2)}, u32[]{:S(2)}) collective-permute-start(f16[64,1024]{1,0:T(8,128)(2,1)S(1)} %get-tuple-element.52), channel_id=1, source_target_pairs={{32,0},{17,1},{34,2},{19,3},{36,4},{21,5},{38,6},{23,7},{40,8},{25... | collective-permute-start | bytes 393224 | tf_op jit(solution)/shard_map/ppermute | solution.py:234
  75.9 6.4 %collective-permute-start.17 = (bf16[64,1024]{1,0:T(8,128)(2,1)S(1)}, bf16[64,1024]{1,0:T(8,128)(2,1)S(1)}, u32[]{:S(2)}, u32[]{:S(2)}) collective-permute-start(bf16[64,1024]{1,0:T(8,128)(2,1)S(1)} %collective-permute-done.14), channel_id=1, source_target_pairs={{2,0},{3,1},{0,2},{1,3},{6,4},{7,5},{4,6},{5,7},{10,8},{11,9},{8,1... | collective-permute-start | bytes 393224 | tf_op jit(solution)/shard_map/ppermute | solution.py:234
  77.5 4.9 %collective-permute-start.18 = (f16[64,2048]{1,0:T(8,128)(2,1)S(1)}, f16[64,2048]{1,0:T(8,128)(2,1)S(1)}, u32[]{:S(2)}, u32[]{:S(2)}) collective-permute-start(f16[64,2048]{1,0:T(8,128)(2,1)S(1)} %multiply_convert_fusion.1), channel_id=1, source_target_pairs={{1,0},{0,1},{3,2},{2,3},{5,4},{4,5},{7,6},{6,7},{9,8},{8,9},{11,10... | collective-permute-start | bytes 786440 | tf_op jit(solution)/shard_map/ppermute | solution.py:234
  82.5 1.6 %collective-permute-start.19 = (bf16[64,2048]{1,0:T(8,128)(2,1)S(1)}, bf16[64,2048]{1,0:T(8,128)(2,1)S(1)}, u32[]{:S(2)}, u32[]{:S(2)}) collective-permute-start(bf16[64,2048]{1,0:T(8,128)(2,1)S(1)} %pad_maximum_fusion.4), channel_id=1, source_target_pairs={{1,0},{0,1},{3,2},{2,3},{5,4},{4,5},{7,6},{6,7},{9,8},{8,9},{11,10... | collective-permute-start | bytes 786440 | tf_op jit(solution)/shard_map/ppermute | solution.py:234
  82.7 7.8 %collective-permute-start.20 = (f16[64,2048]{1,0:T(8,128)(2,1)S(1)}, f16[64,2048]{1,0:T(8,128)(2,1)S(1)}, u32[]{:S(2)}, u32[]{:S(2)}) collective-permute-start(f16[64,2048]{1,0:T(8,128)(2,1)S(1)} %add_convert_fusion.6), channel_id=1, source_target_pairs={{8,0},{3,1},{10,2},{1,3},{12,4},{7,5},{14,6},{5,7},{0,8},{11,9},{2... | collective-permute-start | bytes 786440 | tf_op jit(solution)/shard_map/ppermute | solution.py:234
  90.7 6.5 %collective-permute-start.21 = (f16[64,2048]{1,0:T(8,128)(2,1)S(1)}, f16[64,2048]{1,0:T(8,128)(2,1)S(1)}, u32[]{:S(2)}, u32[]{:S(2)}) collective-permute-start(f16[64,2048]{1,0:T(8,128)(2,1)S(1)} %multiply_convert_fusion), channel_id=1, source_target_pairs={{32,0},{17,1},{34,2},{19,3},{36,4},{21,5},{38,6},{23,7},{40,8},{25... | collective-permute-start | bytes 786440 | tf_op jit(solution)/shard_map/ppermute | solution.py:234
  90.8 6.5 %collective-permute-start.22 = (f16[64,2048]{1,0:T(8,128)(2,1)S(1)}, f16[64,2048]{1,0:T(8,128)(2,1)S(1)}, u32[]{:S(2)}, u32[]{:S(2)}) collective-permute-start(f16[64,2048]{1,0:T(8,128)(2,1)S(1)} %add_convert_fusion.5), channel_id=1, source_target_pairs={{2,0},{7,1},{0,2},{5,3},{6,4},{3,5},{4,6},{1,7},{10,8},{15,9},{8,1... | collective-permute-start | bytes 786440 | tf_op jit(solution)/shard_map/ppermute | solution.py:234
  97.4 7.7 %collective-permute-start.23 = (f16[64,2048]{1,0:T(8,128)(2,1)S(1)}, f16[64,2048]{1,0:T(8,128)(2,1)S(1)}, u32[]{:S(2)}, u32[]{:S(2)}) collective-permute-start(f16[64,2048]{1,0:T(8,128)(2,1)S(1)} %add_convert_fusion.4), channel_id=1, source_target_pairs={{96,0},{33,1},{98,2},{35,3},{100,4},{37,5},{102,6},{39,7},{104,8},... | collective-permute-start | bytes 786440 | tf_op jit(solution)/shard_map/ppermute | solution.py:234
  99.3 9.8 %collective-permute-start.24 = (f16[64,2048]{1,0:T(8,128)(2,1)S(1)}, f16[64,2048]{1,0:T(8,128)(2,1)S(1)}, u32[]{:S(2)}, u32[]{:S(2)}) collective-permute-start(f16[64,2048]{1,0:T(8,128)(2,1)S(1)} %add_convert_fusion.3), channel_id=1, source_target_pairs={{6,0},{9,1},{4,2},{11,3},{2,4},{13,5},{0,6},{15,7},{14,8},{1,9},{1... | collective-permute-start | bytes 786440 | tf_op jit(solution)/shard_map/ppermute | solution.py:234
  109.9 11.5 %collective-permute-start.25 = (f16[64,2048]{1,0:T(8,128)(2,1)S(1)}, f16[64,2048]{1,0:T(8,128)(2,1)S(1)}, u32[]{:S(2)}, u32[]{:S(2)}) collective-permute-start(f16[64,2048]{1,0:T(8,128)(2,1)S(1)} %add_convert_fusion.2), channel_id=1, source_target_pairs={{16,0},{97,1},{18,2},{99,3},{20,4},{101,5},{22,6},{103,7},{24,8},{... | collective-permute-start | bytes 786440 | tf_op jit(solution)/shard_map/ppermute | solution.py:234
  114.6 10.9 %collective-permute-start.27 = (f16[64,2048]{1,0:T(8,128)(2,1)}, f16[64,2048]{1,0:T(8,128)(2,1)S(1)}, u32[]{:S(2)}, u32[]{:S(2)}) collective-permute-start(f16[64,2048]{1,0:T(8,128)(2,1)} %add_convert_fusion.1), channel_id=1, source_target_pairs={{4,0},{5,1},{30,2},{31,3},{34,4},{39,5},{60,6},{57,7},{72,8},{73,9... | collective-permute-start | bytes 786440 | tf_op jit(solution)/shard_map/ppermute | solution.py:234
  122.1 1.2 collective-permute-start.26
  125.4 3.6 %collective-permute-start.28 = (f32[6,64]{1,0:T(8,128)S(1)}, f32[6,64]{1,0:T(8,128)S(1)}, u32[]{:S(2)}, u32[]{:S(2)}) collective-permute-start(f32[6,64]{1,0:T(8,128)S(1)} %add.166), channel_id=1, source_target_pairs={{8,0},{9,1},{10,2},{11,3},{12,4},{13,5},{14,6},{15,7},{0,8},{1,9},... | collective-permute-start | bytes 4616 | tf_op jit(solution)/shard_map/ppermute | solution.py:234
  129.1 3.6 %collective-permute-start.29 = (f32[6,64]{1,0:T(8,128)S(1)}, f32[6,64]{1,0:T(8,128)S(1)}, u32[]{:S(2)}, u32[]{:S(2)}) collective-permute-start(f32[6,64]{1,0:T(8,128)S(1)} %add.167), channel_id=1, source_target_pairs={{2,0},{3,1},{0,2},{1,3},{6,4},{7,5},{4,6},{5,7},{10,8},{11,9},{8,1... | collective-permute-start | bytes 4616 | tf_op jit(solution)/shard_map/ppermute | solution.py:234
  132.7 4.8 %collective-permute-start.30 = (f32[6,64]{1,0:T(8,128)S(1)}, f32[6,64]{1,0:T(8,128)S(1)}, u32[]{:S(2)}, u32[]{:S(2)}) collective-permute-start(f32[6,64]{1,0:T(8,128)S(1)} %add.168), channel_id=1, source_target_pairs={{6,0},{7,1},{4,2},{5,3},{2,4},{3,5},{0,6},{1,7},{14,8},{15,9},{12,... | collective-permute-start | bytes 4616 | tf_op jit(solution)/shard_map/ppermute | solution.py:234

commit v9 on v7

--- a/solution.py
+++ b/solution.py
@@ -181,7 +181,7 @@
         out_shape=jax.ShapeDtypeStruct((reps, count), F32),
         scratch_shapes=[
             pltpu.VMEM((count, columns), BF16),
-            pltpu.SemaphoreType.DMA((8,)),
+            pltpu.SemaphoreType.DMA((count // 512,)),
         ],
         compiler_params=pltpu.CompilerParams(vmem_limit_bytes=16 << 20),
         cost_estimate=pl.CostEstimate(
@@ -374,7 +374,7 @@
         ]
     )
     for pairs in SMALL_COL:
-        if pairs is SMALL_COL[1]:
+        if pairs is SMALL_COL[2]:
             dots, columns = tie(dots, columns)
         dots = dots + move(dots, pairs)
     curve, us_g, us_u, us_p1, q1_u, us_p2 = (dots[i] for i in range(6))

time: 142 us -> 137 us (0.965)
  Pallas kernels: 34.9 us -> 30.8 us
  waiting for transfers between devices: 52.2 us -> 49.9 us
  starting transfers between devices: 43.7 us -> 45.4 us
    pallas_call x2, Pallas kernels: 13.4 us -> 9.31 us  [shadow_rows(): pl.pallas_call(kernel, name='shadow_rows', in_specs=[spec, pl.BlockSpec(m...]
    ppermute x31, waiting for transfers between devices: 52.2 us -> 49.9 us  [move(): return lax.ppermute(value, AXES, pairs)]
    ppermute x31, starting transfers between devices: 43.7 us -> 45.4 us  [move(): return lax.ppermute(value, AXES, pairs)]
  transfers between devices with their start and end apart: 31 -> 31, of which waited for: 23 -> 22; matrix products, arithmetic and copies ran while one was open for 2% -> 2% of each run, Pallas kernels for 25% -> 23%
where the time goes in v9:
time: 137 us; the launch traced here: 136 us
  waiting for transfers between devices  49.9 us (36%)
  starting transfers between devices  45.4 us (33%)
  Pallas kernels  30.8 us (22%)
  other arithmetic  8.82 us (6%)
    ppermute x31, waiting for transfers between devices, move(): return lax.ppermute(value, AXES, pairs)  49.9 us
    ppermute x31, starting transfers between devices, move(): return lax.ppermute(value, AXES, pairs)  45.4 us
    pallas_call x2, Pallas kernels, call(): pl.pallas_call(kernel, name=name, in_specs=[spec, pl.BlockSpec(memory_spa...  14 us
    pallas_call x2, Pallas kernels, shadow_rows(): pl.pallas_call(kernel, name='shadow_rows', in_specs=[spec, pl.BlockSpec(m...  9.31 us
    pallas_call x2, Pallas kernels, primary_half(): pl.pallas_call(half_kernel, name='primary_half', in_specs=[pl.BlockSpec(m...  7.56 us
    sub x1, other arithmetic, on_device(): shadow_residual = gs - step * q1 - step_next * (lead * q1 + kappa * q2)  2.83 us
  transfers between devices with their start and end apart: 31, of which 22 were waited for; matrix products, arithmetic and copies ran while one was open for 2% of the time, Pallas kernels for 23%

profile of v9, /device:TPU:0, one launch (start us, length us, event | category | flops | bytes accessed | tf_op | source)
XLA Modules:
  0.0 136.0 jit_solution(6840121167936815786)
XLA Ops:
  0.6 1.9 %multiply_reduce_fusion.7 = (f32[64]{0:T(128)S(1)}, f32[64]{0:T(128)S(1)}, f32[64]{0:T(128)S(1)}, f32[64]{0:T(128)S(1)}, bf16[64,2048]{1,0:T(8,128)(2,1)S(1)}, /...) fusion(f32[64,2048]{1,0:T(8,128)} %param.7, f32[64,2048]{1,0:T(8,128)} %param.6, ...), kind=kLoop, calls=%fused_computation.35 | loop fusion | flops 2096896 | bytes 3146752 | tf_op jit(solution)/shard_map/reduce_sum | solution.py:258
  2.7 4.0 %collective-permute-start.3 = (bf16[64,1024]{1,0:T(8,128)(2,1)S(1)}, bf16[64,1024]{1,0:T(8,128)(2,1)S(1)}, u32[]{:S(2)}, u32[]{:S(2)}) collective-permute-start(bf16[64,1024]{1,0:T(8,128)(2,1)S(1)} %slice_select_fusion.2), channel_id=1, source_target_pairs={{112,0},{65,1},{48,2},{113,3},{0,4},{33,5},{64,6},{17,7},{96,8},{9... | collective-permute-start | bytes 393224 | tf_op jit(solution)/shard_map/ppermute | solution.py:234
  6.8 0.7 collective-permute-start.1
  7.5 4.7 %shadow_rows.2 = f32[64,2048]{1,0:T(8,128)S(1)} custom-call(bf16[64,2048]{1,0:T(8,128)(2,1)S(1)} %get-tuple-element.36.left_ref, bf16[4096,2048]{1,0:T(8,128)(2,1)} %coupling_ref.11), custom_call_target="tpu_custom_call" | custom-call | flops 536870912 | bytes 8388608 | tf_op jit(solution)/shard_map/shadow_rows/pallas_call | solution.py:176
  12.2 4.5 %collective-permute-start.2 = (f32[4,64]{1,0:T(4,128)S(1)}, f32[4,64]{1,0:T(4,128)S(1)}, u32[]{:S(2)}, u32[]{:S(2)}) collective-permute-start(f32[4,64]{1,0:T(4,128)S(1)} %pad_maximum_fusion.7), channel_id=1, source_target_pairs={{2,0},{3,1},{0,2},{1,3},{6,4},{7,5},{4,6},{5,7},{10,8},{11,9},{8,1... | collective-permute-start | bytes 3080 | tf_op jit(solution)/shard_map/ppermute | solution.py:234
  16.7 4.7 %shadow_rows.3 = f32[64,2048]{1,0:T(8,128)S(1)} custom-call(bf16[64,2048]{1,0:T(8,128)(2,1)S(1)} %get-tuple-element.36.left_ref, bf16[4096,2048]{1,0:T(8,128)(2,1)} %coupling_ref.11), custom_call_target="tpu_custom_call" | custom-call | flops 536870912 | bytes 8388608 | tf_op jit(solution)/shard_map/shadow_rows/pallas_call | solution.py:176
  21.5 0.5 collective-permute-start.5
  22.0 4.2 %collective-permute-done.4 = f32[4,64]{1,0:T(4,128)S(1)} collective-permute-done((f32[4,64]{1,0:T(4,128)S(1)}, f32[4,64]{1,0:T(4,128)S(1)}, u32[]{:S(2)}, u32[]{:S(2)}) %collective-permute-start.4) | collective-permute-done | bytes 1056 | tf_op jit(solution)/shard_map/ppermute | solution.py:234
  26.3 0.3 collective-permute-done.5
  26.8 0.1 multiply_convert_fusion.2
  26.9 0.6 collective-permute-start.7
  27.4 0.8 collective-permute-done.6
  28.4 0.3 collective-permute-done.7
  28.6 0.2 add_convert_fusion.10
  28.8 0.4 collective-permute-start.8
  29.2 3.8 %primary_half.3 = f32[64,1024]{1,0:T(8,128)S(1)} custom-call(s32[1]{0:T(128)} %bitcast.9.offset_ref, bf16[64,4096]{1,0:T(8,128)(2,1)S(1)} %pad_maximum_fusion.left_ref, bf16[4096,2048]{1,0:T(8,128)(2,1)} %coupling_ref.11), custom_call_target="tpu_custom_call" | custom-call | flops 536870912 | bytes 8388608 | tf_op jit(solution)/shard_map/primary_half/pallas_call | solution.py:210
  33.1 3.1 %collective-permute-start.9 = (f16[64,1024]{1,0:T(8,128)(2,1)S(1)}, f16[64,1024]{1,0:T(8,128)(2,1)S(1)}, u32[]{:S(2)}, u32[]{:S(2)}) collective-permute-start(f16[64,1024]{1,0:T(8,128)(2,1)S(1)} %multiply_convert_fusion.4), channel_id=1, source_target_pairs={{32,0},{17,1},{34,2},{19,3},{36,4},{21,5},{38,6},{23,7},{40,8},{25... | collective-permute-start | bytes 393224 | tf_op jit(solution)/shard_map/ppermute | solution.py:234
  36.3 3.7 %primary_half.2 = f32[64,1024]{1,0:T(8,128)S(1)} custom-call(s32[1]{0:T(128)} %bitcast.6.offset_ref, bf16[64,4096]{1,0:T(8,128)(2,1)S(1)} %pad_maximum_fusion.left_ref, bf16[4096,2048]{1,0:T(8,128)(2,1)} %coupling_ref.11), custom_call_target="tpu_custom_call" | custom-call | flops 536870912 | bytes 8388608 | tf_op jit(solution)/shard_map/primary_half/pallas_call | solution.py:210
  40.1 1.3 collective-permute-start.10
  41.5 5.1 %collective-permute-done.10 = f16[64,2048]{1,0:T(8,128)(2,1)S(1)} collective-permute-done((f16[64,2048]{1,0:T(8,128)(2,1)S(1)}, f16[64,2048]{1,0:T(8,128)(2,1)S(1)}, u32[]{:S(2)}, u32[]{:S(2)}) %collective-permute-start.10) | collective-permute-done | bytes 262176 | tf_op jit(solution)/shard_map/ppermute | solution.py:234
  46.7 0.3 collective-permute-start.11
  47.0 2.3 %collective-permute-start.12 = (f16[64,2048]{1,0:T(8,128)(2,1)S(1)}, f16[64,2048]{1,0:T(8,128)(2,1)S(1)}, u32[]{:S(2)}, u32[]{:S(2)}) collective-permute-start(f16[64,2048]{1,0:T(8,128)(2,1)S(1)} %add_convert_fusion.8), channel_id=1, source_target_pairs={{6,0},{9,1},{4,2},{11,3},{2,4},{13,5},{0,6},{15,7},{14,8},{1,9},{1... | collective-permute-start | bytes 786440 | tf_op jit(solution)/shard_map/ppermute | solution.py:234
  49.3 3.6 %collective-permute-done.11 = f16[64,1024]{1,0:T(8,128)(2,1)S(1)} collective-permute-done((f16[64,1024]{1,0:T(8,128)(2,1)S(1)}, f16[64,1024]{1,0:T(8,128)(2,1)S(1)}, u32[]{:S(2)}, u32[]{:S(2)}) %collective-permute-start.11) | collective-permute-done | bytes 131104 | tf_op jit(solution)/shard_map/ppermute | solution.py:234
  53.0 1.6 %collective-permute-done.12 = f16[64,2048]{1,0:T(8,128)(2,1)S(1)} collective-permute-done((f16[64,2048]{1,0:T(8,128)(2,1)S(1)}, f16[64,2048]{1,0:T(8,128)(2,1)S(1)}, u32[]{:S(2)}, u32[]{:S(2)}) %collective-permute-start.12) | collective-permute-done | bytes 262176 | tf_op jit(solution)/shard_map/ppermute | solution.py:234
  54.6 2.2 %collective-permute-start.13 = (f16[64,1024]{1,0:T(8,128)(2,1)S(1)}, f16[64,1024]{1,0:T(8,128)(2,1)S(1)}, u32[]{:S(2)}, u32[]{:S(2)}) collective-permute-start(f16[64,1024]{1,0:T(8,128)(2,1)S(1)} %add_convert_fusion.12), channel_id=1, source_target_pairs={{16,0},{97,1},{18,2},{99,3},{20,4},{101,5},{22,6},{103,7},{24,8},{... | collective-permute-start | bytes 393224 | tf_op jit(solution)/shard_map/ppermute | solution.py:234
  56.8 2.5 %collective-permute-start.15 = (f16[64,2048]{1,0:T(8,128)(2,1)S(1)}, f16[64,2048]{1,0:T(8,128)(2,1)S(1)}, u32[]{:S(2)}, u32[]{:S(2)}) collective-permute-start(f16[64,2048]{1,0:T(8,128)(2,1)S(1)} %add_convert_fusion.7), channel_id=1, source_target_pairs={{4,0},{5,1},{30,2},{31,3},{34,4},{39,5},{60,6},{57,7},{72,8},{73,9... | collective-permute-start | bytes 786440 | tf_op jit(solution)/shard_map/ppermute | solution.py:234
  59.3 2.2 %collective-permute-done.13 = f16[64,1024]{1,0:T(8,128)(2,1)S(1)} collective-permute-done((f16[64,1024]{1,0:T(8,128)(2,1)S(1)}, f16[64,1024]{1,0:T(8,128)(2,1)S(1)}, u32[]{:S(2)}, u32[]{:S(2)}) %collective-permute-start.13) | collective-permute-done | bytes 131104 | tf_op jit(solution)/shard_map/ppermute | solution.py:234
  61.5 0.2 fusion.6
  61.6 0.8 collective-permute-start.14
  62.5 2.2 %collective-permute-done.15 = f16[64,2048]{1,0:T(8,128)(2,1)S(1)} collective-permute-done((f16[64,2048]{1,0:T(8,128)(2,1)S(1)}, f16[64,2048]{1,0:T(8,128)(2,1)S(1)}, u32[]{:S(2)}, u32[]{:S(2)}) %collective-permute-start.15) | collective-permute-done | bytes 262176 | tf_op jit(solution)/shard_map/ppermute | solution.py:234
  64.7 0.2 fusion.15
  64.9 7.7 %shadow.1 = f32[64,4096]{1,0:T(8,128)S(1)} custom-call(bf16[64,2048]{1,0:T(8,128)(2,1)S(1)} %get-tuple-element.82.left_ref, bf16[4096,2048]{1,0:T(8,128)(2,1)} %coupling_ref.11), custom_call_target="tpu_custom_call" | custom-call | flops 1073741824 | bytes 16777216 | tf_op jit(solution)/shard_map/shadow/pallas_call | solution.py:140
  72.7 0.5 collective-permute-done.14
  73.1 2.7 %collective-permute-start.16 = (bf16[64,1024]{1,0:T(8,128)(2,1)S(1)}, bf16[64,1024]{1,0:T(8,128)(2,1)S(1)}, u32[]{:S(2)}, u32[]{:S(2)}) collective-permute-start(bf16[64,1024]{1,0:T(8,128)(2,1)S(1)} %collective-permute-done.14), channel_id=1, source_target_pairs={{2,0},{3,1},{0,2},{1,3},{6,4},{7,5},{4,6},{5,7},{10,8},{11,9},{8,1... | collective-permute-start | bytes 393224 | tf_op jit(solution)/shard_map/ppermute | solution.py:234
  75.9 1.1 collective-permute-start.18
  76.9 0.1 multiply_convert_fusion.1
  77.1 1.7 %collective-permute-done.16 = bf16[64,1024]{1,0:T(8,128)(2,1)S(1)} collective-permute-done((bf16[64,1024]{1,0:T(8,128)(2,1)S(1)}, bf16[64,1024]{1,0:T(8,128)(2,1)S(1)}, u32[]{:S(2)}, u32[]{:S(2)}) %collective-permute-start.16) | collective-permute-done | bytes 131104 | tf_op jit(solution)/shard_map/ppermute | solution.py:234
  78.8 2.0 %collective-permute-done.18 = f16[64,1024]{1,0:T(8,128)(2,1)S(1)} collective-permute-done((f16[64,1024]{1,0:T(8,128)(2,1)S(1)}, f16[64,1024]{1,0:T(8,128)(2,1)S(1)}, u32[]{:S(2)}, u32[]{:S(2)}) %collective-permute-start.18) | collective-permute-done | bytes 131104 | tf_op jit(solution)/shard_map/ppermute | solution.py:234
  81.0 0.2 add_convert_fusion.6
  81.4 1.4 %collective-permute-done.19 = bf16[64,2048]{1,0:T(8,128)(2,1)S(1)} collective-permute-done((bf16[64,2048]{1,0:T(8,128)(2,1)S(1)}, bf16[64,2048]{1,0:T(8,128)(2,1)S(1)}, u32[]{:S(2)}, u32[]{:S(2)}) %collective-permute-start.19) | collective-permute-done | bytes 262176 | tf_op jit(solution)/shard_map/ppermute | solution.py:234
  82.9 6.2 %primary.1 = f32[64,2048]{1,0:T(8,128)S(1)} custom-call(bf16[64,4096]{1,0:T(8,128)(2,1)S(1)} %pad_maximum_fusion.1.left_ref, bf16[4096,2048]{1,0:T(8,128)(2,1)} %coupling_ref.11), custom_call_target="tpu_custom_call" | custom-call | flops 1073741824 | bytes 16777216 | tf_op jit(solution)/shard_map/primary/pallas_call | solution.py:140
  89.4 1.1 collective-permute-start.21
  90.5 0.9 collective-permute-start.22
  91.4 4.4 %collective-permute-done.21 = f16[64,2048]{1,0:T(8,128)(2,1)S(1)} collective-permute-done((f16[64,2048]{1,0:T(8,128)(2,1)S(1)}, f16[64,2048]{1,0:T(8,128)(2,1)S(1)}, u32[]{:S(2)}, u32[]{:S(2)}) %collective-permute-start.21) | collective-permute-done | bytes 262176 | tf_op jit(solution)/shard_map/ppermute | solution.py:234
  95.8 0.1 add_convert_fusion.4
  95.9 0.9 collective-permute-done.22
  97.0 1.4 %collective-permute-start.23 = (f16[64,2048]{1,0:T(8,128)(2,1)S(1)}, f16[64,2048]{1,0:T(8,128)(2,1)S(1)}, u32[]{:S(2)}, u32[]{:S(2)}) collective-permute-start(f16[64,2048]{1,0:T(8,128)(2,1)S(1)} %add_convert_fusion.4), channel_id=1, source_target_pairs={{96,0},{33,1},{98,2},{35,3},{100,4},{37,5},{102,6},{39,7},{104,8},... | collective-permute-start | bytes 786440 | tf_op jit(solution)/shard_map/ppermute | solution.py:234
  98.3 5.1 %collective-permute-start.24 = (f16[64,2048]{1,0:T(8,128)(2,1)S(1)}, f16[64,2048]{1,0:T(8,128)(2,1)S(1)}, u32[]{:S(2)}, u32[]{:S(2)}) collective-permute-start(f16[64,2048]{1,0:T(8,128)(2,1)S(1)} %add_convert_fusion.3), channel_id=1, source_target_pairs={{6,0},{9,1},{4,2},{11,3},{2,4},{13,5},{0,6},{15,7},{14,8},{1,9},{1... | collective-permute-start | bytes 786440 | tf_op jit(solution)/shard_map/ppermute | solution.py:234
  103.4 1.2 collective-permute-done.23
  104.7 3.0 %collective-permute-done.24 = f16[64,2048]{1,0:T(8,128)(2,1)S(1)} collective-permute-done((f16[64,2048]{1,0:T(8,128)(2,1)S(1)}, f16[64,2048]{1,0:T(8,128)(2,1)S(1)}, u32[]{:S(2)}, u32[]{:S(2)}) %collective-permute-start.24) | collective-permute-done | bytes 262176 | tf_op jit(solution)/shard_map/ppermute | solution.py:234
  107.8 0.8 add_convert_fusion.1
  108.5 3.5 %collective-permute-start.25 = (f16[64,2048]{1,0:T(8,128)(2,1)S(1)}, f16[64,2048]{1,0:T(8,128)(2,1)S(1)}, u32[]{:S(2)}, u32[]{:S(2)}) collective-permute-start(f16[64,2048]{1,0:T(8,128)(2,1)S(1)} %add_convert_fusion.2), channel_id=1, source_target_pairs={{16,0},{97,1},{18,2},{99,3},{20,4},{101,5},{22,6},{103,7},{24,8},{... | collective-permute-start | bytes 786440 | tf_op jit(solution)/shard_map/ppermute | solution.py:234
  112.0 1.4 %collective-permute-start.28 = (f16[64,2048]{1,0:T(8,128)(2,1)}, f16[64,2048]{1,0:T(8,128)(2,1)S(1)}, u32[]{:S(2)}, u32[]{:S(2)}) collective-permute-start(f16[64,2048]{1,0:T(8,128)(2,1)} %add_convert_fusion.1), channel_id=1, source_target_pairs={{4,0},{5,1},{30,2},{31,3},{34,4},{39,5},{60,6},{57,7},{72,8},{73,9... | collective-permute-start | bytes 786440 | tf_op jit(solution)/shard_map/ppermute | solution.py:234
  113.4 4.8 %collective-permute-done.25 = f16[64,2048]{1,0:T(8,128)(2,1)S(1)} collective-permute-done((f16[64,2048]{1,0:T(8,128)(2,1)S(1)}, f16[64,2048]{1,0:T(8,128)(2,1)S(1)}, u32[]{:S(2)}, u32[]{:S(2)}) %collective-permute-start.25) | collective-permute-done | bytes 262176 | tf_op jit(solution)/shard_map/ppermute | solution.py:234
  118.2 0.8 multiply_reduce_fusion
  119.0 0.2 collective-permute-start.26
  119.2 1.0 collective-permute-done.26
  120.2 2.9 %collective-permute-start.27 = (f32[6,64]{1,0:T(8,128)S(1)}, f32[6,64]{1,0:T(8,128)S(1)}, u32[]{:S(2)}, u32[]{:S(2)}) collective-permute-start(f32[6,64]{1,0:T(8,128)S(1)} %add.166), channel_id=1, source_target_pairs={{8,0},{9,1},{10,2},{11,3},{12,4},{13,5},{14,6},{15,7},{0,8},{1,9},... | collective-permute-start | bytes 4616 | tf_op jit(solution)/shard_map/ppermute | solution.py:234
  123.1 1.6 %collective-permute-done.27 = f32[6,64]{1,0:T(8,128)S(1)} collective-permute-done((f32[6,64]{1,0:T(8,128)S(1)}, f32[6,64]{1,0:T(8,128)S(1)}, u32[]{:S(2)}, u32[]{:S(2)}) %collective-permute-start.27) | collective-permute-done | bytes 1568 | tf_op jit(solution)/shard_map/ppermute | solution.py:234
  124.7 0.7 collective-permute-start.29
  125.4 2.9 %collective-permute-done.29 = f32[6,64]{1,0:T(8,128)S(1)} collective-permute-done((f32[6,64]{1,0:T(8,128)S(1)}, f32[6,64]{1,0:T(8,128)S(1)}, u32[]{:S(2)}, u32[]{:S(2)}) %collective-permute-start.29) | collective-permute-done | bytes 1568 | tf_op jit(solution)/shard_map/ppermute | solution.py:234
  128.3 0.7 collective-permute-start.30
  129.0 4.1 %collective-permute-done.30 = f32[6,64]{1,0:T(8,128)S(1)} collective-permute-done((f32[6,64]{1,0:T(8,128)S(1)}, f32[6,64]{1,0:T(8,128)S(1)}, u32[]{:S(2)}, u32[]{:S(2)}) %collective-permute-start.30) | collective-permute-done | bytes 1568 | tf_op jit(solution)/shard_map/ppermute | solution.py:234
  133.2 2.8 %multiply_subtract_fusion = (f32[64,2048]{1,0:T(8,128)}, f32[64,2048]{1,0:T(8,128)}, f32[64,2048]{1,0:T(8,128)}, f32[64,2048]{1,0:T(8,128)}) fusion(f16[64,2048]{1,0:T(8,128)(2,1)S(1)} %collective-permute-done.28, f32[64,2048]{1,0:T(8,128)S(1)} %get-tuple-element.83, f32[64,2048]{1,0:T(8,128)S(1)} %copy-done, f16[64,2048]{1,0:T(8,128)(2,1)S(1)} %collective-permute-done.15, ...), kind=kLoop, calls=%fused_computation.2 | loop fusion | flops 7077888 | bytes 5507328 | tf_op jit(solution)/shard_map/sub | solution.py:406
  (60 shorter events, 2.0 us)
Async XLA Ops:
  2.6 4.2 %collective-permute-start = (f32[4,64]{1,0:T(4,128)S(1)}, f32[4,64]{1,0:T(4,128)S(1)}, u32[]{:S(2)}, u32[]{:S(2)}) collective-permute-start(f32[4,64]{1,0:T(4,128)S(1)} %pad_maximum_fusion.5), channel_id=1, source_target_pairs={{1,0},{0,1},{3,2},{2,3},{5,4},{4,5},{7,6},{6,7},{9,8},{8,9},{11,10... | collective-permute-start | bytes 3080 | tf_op jit(solution)/shard_map/ppermute | solution.py:234
  2.7 18.6 %collective-permute-start.3 = (bf16[64,1024]{1,0:T(8,128)(2,1)S(1)}, bf16[64,1024]{1,0:T(8,128)(2,1)S(1)}, u32[]{:S(2)}, u32[]{:S(2)}) collective-permute-start(bf16[64,1024]{1,0:T(8,128)(2,1)S(1)} %slice_select_fusion.2), channel_id=1, source_target_pairs={{112,0},{65,1},{48,2},{113,3},{0,4},{33,5},{64,6},{17,7},{96,8},{9... | collective-permute-start | bytes 393224 | tf_op jit(solution)/shard_map/ppermute | solution.py:234
  6.8 5.4 %collective-permute-start.1 = (f32[4,64]{1,0:T(4,128)S(1)}, f32[4,64]{1,0:T(4,128)S(1)}, u32[]{:S(2)}, u32[]{:S(2)}) collective-permute-start(f32[4,64]{1,0:T(4,128)S(1)} %pad_maximum_fusion.6), channel_id=1, source_target_pairs={{8,0},{9,1},{10,2},{11,3},{12,4},{13,5},{14,6},{15,7},{0,8},{1,9},... | collective-permute-start | bytes 3080 | tf_op jit(solution)/shard_map/ppermute | solution.py:234
  12.2 9.1 %collective-permute-start.2 = (f32[4,64]{1,0:T(4,128)S(1)}, f32[4,64]{1,0:T(4,128)S(1)}, u32[]{:S(2)}, u32[]{:S(2)}) collective-permute-start(f32[4,64]{1,0:T(4,128)S(1)} %pad_maximum_fusion.7), channel_id=1, source_target_pairs={{2,0},{3,1},{0,2},{1,3},{6,4},{7,5},{4,6},{5,7},{10,8},{11,9},{8,1... | collective-permute-start | bytes 3080 | tf_op jit(solution)/shard_map/ppermute | solution.py:234
  21.4 4.9 %collective-permute-start.4 = (f32[4,64]{1,0:T(4,128)S(1)}, f32[4,64]{1,0:T(4,128)S(1)}, u32[]{:S(2)}, u32[]{:S(2)}) collective-permute-start(f32[4,64]{1,0:T(4,128)S(1)} %pad_maximum_fusion.8), channel_id=1, source_target_pairs={{6,0},{7,1},{4,2},{5,3},{2,4},{3,5},{0,6},{1,7},{14,8},{15,9},{12,... | collective-permute-start | bytes 3080 | tf_op jit(solution)/shard_map/ppermute | solution.py:234
  21.5 5.1 %collective-permute-start.5 = (bf16[64,1024]{1,0:T(8,128)(2,1)S(1)}, bf16[64,1024]{1,0:T(8,128)(2,1)S(1)}, u32[]{:S(2)}, u32[]{:S(2)}) collective-permute-start(bf16[64,1024]{1,0:T(8,128)(2,1)S(1)} %collective-permute-done.3), channel_id=1, source_target_pairs={{2,0},{3,1},{0,2},{1,3},{6,4},{7,5},{4,6},{5,7},{10,8},{11,9},{8,1... | collective-permute-start | bytes 393224 | tf_op jit(solution)/shard_map/ppermute | solution.py:234
  26.7 1.6 %collective-permute-start.6 = (bf16[64,2048]{1,0:T(8,128)(2,1)S(1)}, bf16[64,2048]{1,0:T(8,128)(2,1)S(1)}, u32[]{:S(2)}, u32[]{:S(2)}) collective-permute-start(bf16[64,2048]{1,0:T(8,128)(2,1)S(1)} %pad_maximum_fusion.2), channel_id=1, source_target_pairs={{1,0},{0,1},{3,2},{2,3},{5,4},{4,5},{7,6},{6,7},{9,8},{8,9},{11,10... | collective-permute-start | bytes 786440 | tf_op jit(solution)/shard_map/ppermute | solution.py:234
  26.9 1.8 %collective-permute-start.7 = (f16[64,2048]{1,0:T(8,128)(2,1)S(1)}, f16[64,2048]{1,0:T(8,128)(2,1)S(1)}, u32[]{:S(2)}, u32[]{:S(2)}) collective-permute-start(f16[64,2048]{1,0:T(8,128)(2,1)S(1)} %multiply_convert_fusion.2), channel_id=1, source_target_pairs={{1,0},{0,1},{3,2},{2,3},{5,4},{4,5},{7,6},{6,7},{9,8},{8,9},{11,10... | collective-permute-start | bytes 786440 | tf_op jit(solution)/shard_map/ppermute | solution.py:234
  28.8 11.2 %collective-permute-start.8 = (f16[64,2048]{1,0:T(8,128)(2,1)S(1)}, f16[64,2048]{1,0:T(8,128)(2,1)S(1)}, u32[]{:S(2)}, u32[]{:S(2)}) collective-permute-start(f16[64,2048]{1,0:T(8,128)(2,1)S(1)} %add_convert_fusion.10), channel_id=1, source_target_pairs={{8,0},{3,1},{10,2},{1,3},{12,4},{7,5},{14,6},{5,7},{0,8},{11,9},{2... | collective-permute-start | bytes 786440 | tf_op jit(solution)/shard_map/ppermute | solution.py:234
  29.2 32.3 %copy-start.1 = (f32[64,2048]{1,0:T(8,128)S(1)}, f32[64,2048]{1,0:T(8,128)}, u32[]{:S(2)}) copy-start(f32[64,2048]{1,0:T(8,128)} %param.6) | copy-start | bytes 1572868
  29.2 35.5 %copy-start = (f32[64,2048]{1,0:T(8,128)S(1)}, f32[64,2048]{1,0:T(8,128)}, u32[]{:S(2)}) copy-start(f32[64,2048]{1,0:T(8,128)} %param.7) | copy-start | bytes 1572868
  29.2 35.5 %copy-start.2 = (f32[64,2048]{1,0:T(8,128)S(1)}, f32[64,2048]{1,0:T(8,128)}, u32[]{:S(2)}) copy-start(f32[64,2048]{1,0:T(8,128)} %param.5) | copy-start | bytes 1572868
  33.1 8.2 %collective-permute-start.9 = (f16[64,1024]{1,0:T(8,128)(2,1)S(1)}, f16[64,1024]{1,0:T(8,128)(2,1)S(1)}, u32[]{:S(2)}, u32[]{:S(2)}) collective-permute-start(f16[64,1024]{1,0:T(8,128)(2,1)S(1)} %multiply_convert_fusion.4), channel_id=1, source_target_pairs={{32,0},{17,1},{34,2},{19,3},{36,4},{21,5},{38,6},{23,7},{40,8},{25... | collective-permute-start | bytes 393224 | tf_op jit(solution)/shard_map/ppermute | solution.py:234
  40.1 6.5 %collective-permute-start.10 = (f16[64,2048]{1,0:T(8,128)(2,1)S(1)}, f16[64,2048]{1,0:T(8,128)(2,1)S(1)}, u32[]{:S(2)}, u32[]{:S(2)}) collective-permute-start(f16[64,2048]{1,0:T(8,128)(2,1)S(1)} %add_convert_fusion.9), channel_id=1, source_target_pairs={{2,0},{7,1},{0,2},{5,3},{6,4},{3,5},{4,6},{1,7},{10,8},{15,9},{8,1... | collective-permute-start | bytes 786440 | tf_op jit(solution)/shard_map/ppermute | solution.py:234
  46.7 6.3 %collective-permute-start.11 = (f16[64,1024]{1,0:T(8,128)(2,1)S(1)}, f16[64,1024]{1,0:T(8,128)(2,1)S(1)}, u32[]{:S(2)}, u32[]{:S(2)}) collective-permute-start(f16[64,1024]{1,0:T(8,128)(2,1)S(1)} %add_convert_fusion.13), channel_id=1, source_target_pairs={{96,0},{33,1},{98,2},{35,3},{100,4},{37,5},{102,6},{39,7},{104,8},... | collective-permute-start | bytes 393224 | tf_op jit(solution)/shard_map/ppermute | solution.py:234
  47.0 7.6 %collective-permute-start.12 = (f16[64,2048]{1,0:T(8,128)(2,1)S(1)}, f16[64,2048]{1,0:T(8,128)(2,1)S(1)}, u32[]{:S(2)}, u32[]{:S(2)}) collective-permute-start(f16[64,2048]{1,0:T(8,128)(2,1)S(1)} %add_convert_fusion.8), channel_id=1, source_target_pairs={{6,0},{9,1},{4,2},{11,3},{2,4},{13,5},{0,6},{15,7},{14,8},{1,9},{1... | collective-permute-start | bytes 786440 | tf_op jit(solution)/shard_map/ppermute | solution.py:234
  54.6 6.8 %collective-permute-start.13 = (f16[64,1024]{1,0:T(8,128)(2,1)S(1)}, f16[64,1024]{1,0:T(8,128)(2,1)S(1)}, u32[]{:S(2)}, u32[]{:S(2)}) collective-permute-start(f16[64,1024]{1,0:T(8,128)(2,1)S(1)} %add_convert_fusion.12), channel_id=1, source_target_pairs={{16,0},{97,1},{18,2},{99,3},{20,4},{101,5},{22,6},{103,7},{24,8},{... | collective-permute-start | bytes 393224 | tf_op jit(solution)/shard_map/ppermute | solution.py:234
  56.8 7.9 %collective-permute-start.15 = (f16[64,2048]{1,0:T(8,128)(2,1)S(1)}, f16[64,2048]{1,0:T(8,128)(2,1)S(1)}, u32[]{:S(2)}, u32[]{:S(2)}) collective-permute-start(f16[64,2048]{1,0:T(8,128)(2,1)S(1)} %add_convert_fusion.7), channel_id=1, source_target_pairs={{4,0},{5,1},{30,2},{31,3},{34,4},{39,5},{60,6},{57,7},{72,8},{73,9... | collective-permute-start | bytes 786440 | tf_op jit(solution)/shard_map/ppermute | solution.py:234
  61.6 11.5 %collective-permute-start.14 = (bf16[64,1024]{1,0:T(8,128)(2,1)S(1)}, bf16[64,1024]{1,0:T(8,128)(2,1)S(1)}, u32[]{:S(2)}, u32[]{:S(2)}) collective-permute-start(bf16[64,1024]{1,0:T(8,128)(2,1)S(1)} %get-tuple-element.84), channel_id=1, source_target_pairs={{112,0},{65,1},{48,2},{113,3},{0,4},{33,5},{64,6},{17,7},{96,8},{9... | collective-permute-start | bytes 393224 | tf_op jit(solution)/shard_map/ppermute | solution.py:234
  73.1 5.7 %collective-permute-start.16 = (bf16[64,1024]{1,0:T(8,128)(2,1)S(1)}, bf16[64,1024]{1,0:T(8,128)(2,1)S(1)}, u32[]{:S(2)}, u32[]{:S(2)}) collective-permute-start(bf16[64,1024]{1,0:T(8,128)(2,1)S(1)} %collective-permute-done.14), channel_id=1, source_target_pairs={{2,0},{3,1},{0,2},{1,3},{6,4},{7,5},{4,6},{5,7},{10,8},{11,9},{8,1... | collective-permute-start | bytes 393224 | tf_op jit(solution)/shard_map/ppermute | solution.py:234
  75.9 5.0 %collective-permute-start.18 = (f16[64,1024]{1,0:T(8,128)(2,1)S(1)}, f16[64,1024]{1,0:T(8,128)(2,1)S(1)}, u32[]{:S(2)}, u32[]{:S(2)}) collective-permute-start(f16[64,1024]{1,0:T(8,128)(2,1)S(1)} %get-tuple-element.54), channel_id=1, source_target_pairs={{32,0},{17,1},{34,2},{19,3},{36,4},{21,5},{38,6},{23,7},{40,8},{25... | collective-permute-start | bytes 393224 | tf_op jit(solution)/shard_map/ppermute | solution.py:234
  77.0 4.0 %collective-permute-start.17 = (f16[64,2048]{1,0:T(8,128)(2,1)S(1)}, f16[64,2048]{1,0:T(8,128)(2,1)S(1)}, u32[]{:S(2)}, u32[]{:S(2)}) collective-permute-start(f16[64,2048]{1,0:T(8,128)(2,1)S(1)} %multiply_convert_fusion.1), channel_id=1, source_target_pairs={{1,0},{0,1},{3,2},{2,3},{5,4},{4,5},{7,6},{6,7},{9,8},{8,9},{11,10... | collective-permute-start | bytes 786440 | tf_op jit(solution)/shard_map/ppermute | solution.py:234
  81.2 1.6 %collective-permute-start.19 = (bf16[64,2048]{1,0:T(8,128)(2,1)S(1)}, bf16[64,2048]{1,0:T(8,128)(2,1)S(1)}, u32[]{:S(2)}, u32[]{:S(2)}) collective-permute-start(bf16[64,2048]{1,0:T(8,128)(2,1)S(1)} %pad_maximum_fusion.3), channel_id=1, source_target_pairs={{1,0},{0,1},{3,2},{2,3},{5,4},{4,5},{7,6},{6,7},{9,8},{8,9},{11,10... | collective-permute-start | bytes 786440 | tf_op jit(solution)/shard_map/ppermute | solution.py:234
  81.3 7.9 %collective-permute-start.20 = (f16[64,2048]{1,0:T(8,128)(2,1)S(1)}, f16[64,2048]{1,0:T(8,128)(2,1)S(1)}, u32[]{:S(2)}, u32[]{:S(2)}) collective-permute-start(f16[64,2048]{1,0:T(8,128)(2,1)S(1)} %add_convert_fusion.6), channel_id=1, source_target_pairs={{8,0},{3,1},{10,2},{1,3},{12,4},{7,5},{14,6},{5,7},{0,8},{11,9},{2... | collective-permute-start | bytes 786440 | tf_op jit(solution)/shard_map/ppermute | solution.py:234
  89.4 6.5 %collective-permute-start.21 = (f16[64,2048]{1,0:T(8,128)(2,1)S(1)}, f16[64,2048]{1,0:T(8,128)(2,1)S(1)}, u32[]{:S(2)}, u32[]{:S(2)}) collective-permute-start(f16[64,2048]{1,0:T(8,128)(2,1)S(1)} %multiply_convert_fusion), channel_id=1, source_target_pairs={{32,0},{17,1},{34,2},{19,3},{36,4},{21,5},{38,6},{23,7},{40,8},{25... | collective-permute-start | bytes 786440 | tf_op jit(solution)/shard_map/ppermute | solution.py:234
  90.5 6.4 %collective-permute-start.22 = (f16[64,2048]{1,0:T(8,128)(2,1)S(1)}, f16[64,2048]{1,0:T(8,128)(2,1)S(1)}, u32[]{:S(2)}, u32[]{:S(2)}) collective-permute-start(f16[64,2048]{1,0:T(8,128)(2,1)S(1)} %add_convert_fusion.5), channel_id=1, source_target_pairs={{2,0},{7,1},{0,2},{5,3},{6,4},{3,5},{4,6},{1,7},{10,8},{15,9},{8,1... | collective-permute-start | bytes 786440 | tf_op jit(solution)/shard_map/ppermute | solution.py:234
  97.0 7.7 %collective-permute-start.23 = (f16[64,2048]{1,0:T(8,128)(2,1)S(1)}, f16[64,2048]{1,0:T(8,128)(2,1)S(1)}, u32[]{:S(2)}, u32[]{:S(2)}) collective-permute-start(f16[64,2048]{1,0:T(8,128)(2,1)S(1)} %add_convert_fusion.4), channel_id=1, source_target_pairs={{96,0},{33,1},{98,2},{35,3},{100,4},{37,5},{102,6},{39,7},{104,8},... | collective-permute-start | bytes 786440 | tf_op jit(solution)/shard_map/ppermute | solution.py:234
  98.3 9.4 %collective-permute-start.24 = (f16[64,2048]{1,0:T(8,128)(2,1)S(1)}, f16[64,2048]{1,0:T(8,128)(2,1)S(1)}, u32[]{:S(2)}, u32[]{:S(2)}) collective-permute-start(f16[64,2048]{1,0:T(8,128)(2,1)S(1)} %add_convert_fusion.3), channel_id=1, source_target_pairs={{6,0},{9,1},{4,2},{11,3},{2,4},{13,5},{0,6},{15,7},{14,8},{1,9},{1... | collective-permute-start | bytes 786440 | tf_op jit(solution)/shard_map/ppermute | solution.py:234
  108.5 9.6 %collective-permute-start.25 = (f16[64,2048]{1,0:T(8,128)(2,1)S(1)}, f16[64,2048]{1,0:T(8,128)(2,1)S(1)}, u32[]{:S(2)}, u32[]{:S(2)}) collective-permute-start(f16[64,2048]{1,0:T(8,128)(2,1)S(1)} %add_convert_fusion.2), channel_id=1, source_target_pairs={{16,0},{97,1},{18,2},{99,3},{20,4},{101,5},{22,6},{103,7},{24,8},{... | collective-permute-start | bytes 786440 | tf_op jit(solution)/shard_map/ppermute | solution.py:234
  112.0 12.7 %collective-permute-start.28 = (f16[64,2048]{1,0:T(8,128)(2,1)}, f16[64,2048]{1,0:T(8,128)(2,1)S(1)}, u32[]{:S(2)}, u32[]{:S(2)}) collective-permute-start(f16[64,2048]{1,0:T(8,128)(2,1)} %add_convert_fusion.1), channel_id=1, source_target_pairs={{4,0},{5,1},{30,2},{31,3},{34,4},{39,5},{60,6},{57,7},{72,8},{73,9... | collective-permute-start | bytes 786440 | tf_op jit(solution)/shard_map/ppermute | solution.py:234
  119.0 1.2 collective-permute-start.26
  120.2 4.5 %collective-permute-start.27 = (f32[6,64]{1,0:T(8,128)S(1)}, f32[6,64]{1,0:T(8,128)S(1)}, u32[]{:S(2)}, u32[]{:S(2)}) collective-permute-start(f32[6,64]{1,0:T(8,128)S(1)} %add.166), channel_id=1, source_target_pairs={{8,0},{9,1},{10,2},{11,3},{12,4},{13,5},{14,6},{15,7},{0,8},{1,9},... | collective-permute-start | bytes 4616 | tf_op jit(solution)/shard_map/ppermute | solution.py:234
  124.7 3.6 %collective-permute-start.29 = (f32[6,64]{1,0:T(8,128)S(1)}, f32[6,64]{1,0:T(8,128)S(1)}, u32[]{:S(2)}, u32[]{:S(2)}) collective-permute-start(f32[6,64]{1,0:T(8,128)S(1)} %add.167), channel_id=1, source_target_pairs={{2,0},{3,1},{0,2},{1,3},{6,4},{7,5},{4,6},{5,7},{10,8},{11,9},{8,1... | collective-permute-start | bytes 4616 | tf_op jit(solution)/shard_map/ppermute | solution.py:234
  128.3 4.8 %collective-permute-start.30 = (f32[6,64]{1,0:T(8,128)S(1)}, f32[6,64]{1,0:T(8,128)S(1)}, u32[]{:S(2)}, u32[]{:S(2)}) collective-permute-start(f32[6,64]{1,0:T(8,128)S(1)} %add.168), channel_id=1, source_target_pairs={{6,0},{7,1},{4,2},{5,3},{2,4},{3,5},{0,6},{1,7},{14,8},{15,9},{12,... | collective-permute-start | bytes 4616 | tf_op jit(solution)/shard_map/ppermute | solution.py:234

commit v10 on v9

--- a/solution.py
+++ b/solution.py
@@ -343,22 +343,23 @@
 
     shadow_partial = shadow(us.astype(BF16), coupling)
     half, shadow_partial, held = tie(half, shadow_partial, held)
-    block = put(z_even, half, move(half, Z_PAIR))
     scale = SECOND_SCALE / shadow_top
     shadow_held = send_core(jnp.split(shadow_partial, 2, axis=1), scale)
+    half, shadow_held, held = tie(half, shadow_held, held)
+    block = put(z_even, half, move(half, Z_PAIR))
+    shadow_held = exchange(shadow_held, COL_STEPS[0])
     product = put(low_half, held, move(held, ROW_STEPS[0]))
     block, shadow_held, product = tie(block, shadow_held, product)
     left = put(first, block, move(block, CORE))
     partial = primary(left, coupling)
-    shadow_held = exchange(shadow_held, COL_STEPS[0])
+    shadow_held = exchange(shadow_held, COL_STEPS[1])
     partial, shadow_held = tie(partial, shadow_held)
     held = exchange((partial * (SECOND_SCALE / top)).astype(WIRE), ROW_STEPS[0])
-    shadow_held = exchange(shadow_held, COL_STEPS[1])
-    held, shadow_held = tie(held, shadow_held)
-    held = exchange(held, ROW_STEPS[1])
     shadow_held = exchange(shadow_held, COL_STEPS[2])
     held, shadow_held = tie(held, shadow_held)
     columns = move(shadow_held, TO_COLS)
+    held = exchange(held, ROW_STEPS[1])
+    held, columns = tie(held, columns)
     held = exchange(held, ROW_STEPS[2])
 
     p1, u = first_step(keep, g, product)
@@ -374,8 +375,6 @@
         ]
     )
     for pairs in SMALL_COL:
-        if pairs is SMALL_COL[2]:
-            dots, columns = tie(dots, columns)
         dots = dots + move(dots, pairs)
     curve, us_g, us_u, us_p1, q1_u, us_p2 = (dots[i] for i in range(6))
     q2 = keep * us - (COUPLE_GAIN / scale) * slope * columns.astype(F32)

time: 137 us -> 145 us (1.058)
  waiting for transfers between devices: 49.9 us -> 62.3 us
  starting transfers between devices: 45.4 us -> 42.4 us
    ppermute x31, waiting for transfers between devices: 49.9 us -> 62.3 us  [move(): return lax.ppermute(value, AXES, pairs)]
    ppermute x31, starting transfers between devices: 45.4 us -> 42.4 us  [move(): return lax.ppermute(value, AXES, pairs)]
  transfers between devices with their start and end apart: 31 -> 31, of which waited for: 22 -> 23; matrix products, arithmetic and copies ran while one was open for 2% -> 1% of each run, Pallas kernels for 23% -> 21%
where the time goes in v10:
time: 145 us
  waiting for transfers between devices  62.3 us (43%)
  starting transfers between devices  42.4 us (29%)
  Pallas kernels  30.8 us (21%)
  other arithmetic  8.09 us (6%)
    ppermute x31, waiting for transfers between devices, move(): return lax.ppermute(value, AXES, pairs)  62.3 us
    ppermute x31, starting transfers between devices, move(): return lax.ppermute(value, AXES, pairs)  42.4 us
    pallas_call x2, Pallas kernels, call(): pl.pallas_call(kernel, name=name, in_specs=[spec, pl.BlockSpec(memory_spa...  14 us
    pallas_call x2, Pallas kernels, shadow_rows(): pl.pallas_call(kernel, name='shadow_rows', in_specs=[spec, pl.BlockSpec(m...  9.31 us
    pallas_call x2, Pallas kernels, primary_half(): pl.pallas_call(half_kernel, name='primary_half', in_specs=[pl.BlockSpec(m...  7.56 us
  transfers between devices with their start and end apart: 31, of which 23 were waited for; matrix products, arithmetic and copies ran while one was open for 1% of the time, Pallas kernels for 21%

profile of v10, /device:TPU:0, one launch (start us, length us, event | category | flops | bytes accessed | tf_op | source)
XLA Modules:
  0.0 144.7 jit_solution(12075068551752517597)
XLA Ops:
  0.6 1.9 %multiply_reduce_fusion.7 = (f32[64]{0:T(128)S(1)}, f32[64]{0:T(128)S(1)}, f32[64]{0:T(128)S(1)}, f32[64]{0:T(128)S(1)}, bf16[64,2048]{1,0:T(8,128)(2,1)S(1)}, /...) fusion(f32[64,2048]{1,0:T(8,128)} %param.7, f32[64,2048]{1,0:T(8,128)} %param.6, ...), kind=kLoop, calls=%fused_computation.35 | loop fusion | flops 2096896 | bytes 3146752 | tf_op jit(solution)/shard_map/reduce_sum | solution.py:258
  2.7 4.0 %collective-permute-start.3 = (bf16[64,1024]{1,0:T(8,128)(2,1)S(1)}, bf16[64,1024]{1,0:T(8,128)(2,1)S(1)}, u32[]{:S(2)}, u32[]{:S(2)}) collective-permute-start(bf16[64,1024]{1,0:T(8,128)(2,1)S(1)} %slice_select_fusion.2), channel_id=1, source_target_pairs={{112,0},{65,1},{48,2},{113,3},{0,4},{33,5},{64,6},{17,7},{96,8},{9... | collective-permute-start | bytes 393224 | tf_op jit(solution)/shard_map/ppermute | solution.py:234
  6.8 0.7 collective-permute-start.1
  7.5 4.7 %shadow_rows.2 = f32[64,2048]{1,0:T(8,128)S(1)} custom-call(bf16[64,2048]{1,0:T(8,128)(2,1)S(1)} %get-tuple-element.37.left_ref, bf16[4096,2048]{1,0:T(8,128)(2,1)} %coupling_ref.11), custom_call_target="tpu_custom_call" | custom-call | flops 536870912 | bytes 8388608 | tf_op jit(solution)/shard_map/shadow_rows/pallas_call | solution.py:176
  12.2 4.5 %collective-permute-start.2 = (f32[4,64]{1,0:T(4,128)S(1)}, f32[4,64]{1,0:T(4,128)S(1)}, u32[]{:S(2)}, u32[]{:S(2)}) collective-permute-start(f32[4,64]{1,0:T(4,128)S(1)} %pad_maximum_fusion.7), channel_id=1, source_target_pairs={{2,0},{3,1},{0,2},{1,3},{6,4},{7,5},{4,6},{5,7},{10,8},{11,9},{8,1... | collective-permute-start | bytes 3080 | tf_op jit(solution)/shard_map/ppermute | solution.py:234
  16.7 4.7 %shadow_rows.3 = f32[64,2048]{1,0:T(8,128)S(1)} custom-call(bf16[64,2048]{1,0:T(8,128)(2,1)S(1)} %get-tuple-element.37.left_ref, bf16[4096,2048]{1,0:T(8,128)(2,1)} %coupling_ref.11), custom_call_target="tpu_custom_call" | custom-call | flops 536870912 | bytes 8388608 | tf_op jit(solution)/shard_map/shadow_rows/pallas_call | solution.py:176
  21.5 0.5 collective-permute-start.5
  22.0 4.2 %collective-permute-done.4 = f32[4,64]{1,0:T(4,128)S(1)} collective-permute-done((f32[4,64]{1,0:T(4,128)S(1)}, f32[4,64]{1,0:T(4,128)S(1)}, u32[]{:S(2)}, u32[]{:S(2)}) %collective-permute-start.4) | collective-permute-done | bytes 1056 | tf_op jit(solution)/shard_map/ppermute | solution.py:234
  26.3 0.3 collective-permute-done.5
  26.8 0.1 multiply_convert_fusion.2
  26.9 0.6 collective-permute-start.7
  27.4 0.8 collective-permute-done.6
  28.4 0.3 collective-permute-done.7
  28.6 0.2 add_convert_fusion.10
  28.8 0.4 collective-permute-start.8
  29.2 3.8 %primary_half.3 = f32[64,1024]{1,0:T(8,128)S(1)} custom-call(s32[1]{0:T(128)} %bitcast.9.offset_ref, bf16[64,4096]{1,0:T(8,128)(2,1)S(1)} %pad_maximum_fusion.left_ref, bf16[4096,2048]{1,0:T(8,128)(2,1)} %coupling_ref.11), custom_call_target="tpu_custom_call" | custom-call | flops 536870912 | bytes 8388608 | tf_op jit(solution)/shard_map/primary_half/pallas_call | solution.py:210
  33.1 3.1 %collective-permute-start.9 = (f16[64,1024]{1,0:T(8,128)(2,1)S(1)}, f16[64,1024]{1,0:T(8,128)(2,1)S(1)}, u32[]{:S(2)}, u32[]{:S(2)}) collective-permute-start(f16[64,1024]{1,0:T(8,128)(2,1)S(1)} %multiply_convert_fusion.4), channel_id=1, source_target_pairs={{32,0},{17,1},{34,2},{19,3},{36,4},{21,5},{38,6},{23,7},{40,8},{25... | collective-permute-start | bytes 393224 | tf_op jit(solution)/shard_map/ppermute | solution.py:234
  36.3 3.7 %primary_half.2 = f32[64,1024]{1,0:T(8,128)S(1)} custom-call(s32[1]{0:T(128)} %bitcast.6.offset_ref, bf16[64,4096]{1,0:T(8,128)(2,1)S(1)} %pad_maximum_fusion.left_ref, bf16[4096,2048]{1,0:T(8,128)(2,1)} %coupling_ref.11), custom_call_target="tpu_custom_call" | custom-call | flops 536870912 | bytes 8388608 | tf_op jit(solution)/shard_map/primary_half/pallas_call | solution.py:210
  40.1 1.3 collective-permute-start.10
  41.4 0.1 add_convert_fusion.13
  41.5 5.1 %collective-permute-done.10 = f16[64,2048]{1,0:T(8,128)(2,1)S(1)} collective-permute-done((f16[64,2048]{1,0:T(8,128)(2,1)S(1)}, f16[64,2048]{1,0:T(8,128)(2,1)S(1)}, u32[]{:S(2)}, u32[]{:S(2)}) %collective-permute-start.10) | collective-permute-done | bytes 262176 | tf_op jit(solution)/shard_map/ppermute | solution.py:234
  46.7 0.3 collective-permute-start.11
  47.0 2.3 %collective-permute-start.12 = (f16[64,2048]{1,0:T(8,128)(2,1)S(1)}, f16[64,2048]{1,0:T(8,128)(2,1)S(1)}, u32[]{:S(2)}, u32[]{:S(2)}) collective-permute-start(f16[64,2048]{1,0:T(8,128)(2,1)S(1)} %add_convert_fusion.8), channel_id=1, source_target_pairs={{6,0},{9,1},{4,2},{11,3},{2,4},{13,5},{0,6},{15,7},{14,8},{1,9},{1... | collective-permute-start | bytes 786440 | tf_op jit(solution)/shard_map/ppermute | solution.py:234
  49.3 3.6 %collective-permute-done.11 = f16[64,1024]{1,0:T(8,128)(2,1)S(1)} collective-permute-done((f16[64,1024]{1,0:T(8,128)(2,1)S(1)}, f16[64,1024]{1,0:T(8,128)(2,1)S(1)}, u32[]{:S(2)}, u32[]{:S(2)}) %collective-permute-start.11) | collective-permute-done | bytes 131104 | tf_op jit(solution)/shard_map/ppermute | solution.py:234
  53.0 1.6 %collective-permute-done.12 = f16[64,2048]{1,0:T(8,128)(2,1)S(1)} collective-permute-done((f16[64,2048]{1,0:T(8,128)(2,1)S(1)}, f16[64,2048]{1,0:T(8,128)(2,1)S(1)}, u32[]{:S(2)}, u32[]{:S(2)}) %collective-permute-start.12) | collective-permute-done | bytes 262176 | tf_op jit(solution)/shard_map/ppermute | solution.py:234
  54.6 2.2 %collective-permute-start.13 = (f16[64,1024]{1,0:T(8,128)(2,1)S(1)}, f16[64,1024]{1,0:T(8,128)(2,1)S(1)}, u32[]{:S(2)}, u32[]{:S(2)}) collective-permute-start(f16[64,1024]{1,0:T(8,128)(2,1)S(1)} %add_convert_fusion.12), channel_id=1, source_target_pairs={{16,0},{97,1},{18,2},{99,3},{20,4},{101,5},{22,6},{103,7},{24,8},{... | collective-permute-start | bytes 393224 | tf_op jit(solution)/shard_map/ppermute | solution.py:234
  56.8 2.5 %collective-permute-start.15 = (f16[64,2048]{1,0:T(8,128)(2,1)S(1)}, f16[64,2048]{1,0:T(8,128)(2,1)S(1)}, u32[]{:S(2)}, u32[]{:S(2)}) collective-permute-start(f16[64,2048]{1,0:T(8,128)(2,1)S(1)} %add_convert_fusion.7), channel_id=1, source_target_pairs={{4,0},{5,1},{30,2},{31,3},{34,4},{39,5},{60,6},{57,7},{72,8},{73,9... | collective-permute-start | bytes 786440 | tf_op jit(solution)/shard_map/ppermute | solution.py:234
  59.3 2.2 %collective-permute-done.13 = f16[64,1024]{1,0:T(8,128)(2,1)S(1)} collective-permute-done((f16[64,1024]{1,0:T(8,128)(2,1)S(1)}, f16[64,1024]{1,0:T(8,128)(2,1)S(1)}, u32[]{:S(2)}, u32[]{:S(2)}) %collective-permute-start.13) | collective-permute-done | bytes 131104 | tf_op jit(solution)/shard_map/ppermute | solution.py:234
  61.5 0.2 fusion.6
  61.6 0.8 collective-permute-start.14
  62.5 2.2 %collective-permute-done.15 = f16[64,2048]{1,0:T(8,128)(2,1)S(1)} collective-permute-done((f16[64,2048]{1,0:T(8,128)(2,1)S(1)}, f16[64,2048]{1,0:T(8,128)(2,1)S(1)}, u32[]{:S(2)}, u32[]{:S(2)}) %collective-permute-start.15) | collective-permute-done | bytes 262176 | tf_op jit(solution)/shard_map/ppermute | solution.py:234
  64.7 0.2 fusion.15
  64.9 7.7 %shadow.1 = f32[64,4096]{1,0:T(8,128)S(1)} custom-call(bf16[64,2048]{1,0:T(8,128)(2,1)S(1)} %get-tuple-element.84.left_ref, bf16[4096,2048]{1,0:T(8,128)(2,1)} %coupling_ref.11), custom_call_target="tpu_custom_call" | custom-call | flops 1073741824 | bytes 16777216 | tf_op jit(solution)/shard_map/shadow/pallas_call | solution.py:140
  72.7 0.5 collective-permute-done.14
  73.1 0.1 multiply_convert_fusion.1
  73.3 1.5 %collective-permute-done.16 = f16[64,2048]{1,0:T(8,128)(2,1)S(1)} collective-permute-done((f16[64,2048]{1,0:T(8,128)(2,1)S(1)}, f16[64,2048]{1,0:T(8,128)(2,1)S(1)}, u32[]{:S(2)}, u32[]{:S(2)}) %collective-permute-start.16) | collective-permute-done | bytes 262176 | tf_op jit(solution)/shard_map/ppermute | solution.py:234
  74.9 0.2 add_convert_fusion.6
  75.0 2.7 %collective-permute-start.17 = (bf16[64,1024]{1,0:T(8,128)(2,1)S(1)}, bf16[64,1024]{1,0:T(8,128)(2,1)S(1)}, u32[]{:S(2)}, u32[]{:S(2)}) collective-permute-start(bf16[64,1024]{1,0:T(8,128)(2,1)S(1)} %collective-permute-done.14), channel_id=1, source_target_pairs={{2,0},{3,1},{0,2},{1,3},{6,4},{7,5},{4,6},{5,7},{10,8},{11,9},{8,1... | collective-permute-start | bytes 393224 | tf_op jit(solution)/shard_map/ppermute | solution.py:234
  77.7 1.1 collective-permute-start.19
  78.8 2.7 %collective-permute-done.17 = bf16[64,1024]{1,0:T(8,128)(2,1)S(1)} collective-permute-done((bf16[64,1024]{1,0:T(8,128)(2,1)S(1)}, bf16[64,1024]{1,0:T(8,128)(2,1)S(1)}, u32[]{:S(2)}, u32[]{:S(2)}) %collective-permute-start.17) | collective-permute-done | bytes 131104 | tf_op jit(solution)/shard_map/ppermute | solution.py:234
  81.6 1.1 collective-permute-done.19
  82.9 3.1 %collective-permute-done.18 = f16[64,2048]{1,0:T(8,128)(2,1)S(1)} collective-permute-done((f16[64,2048]{1,0:T(8,128)(2,1)S(1)}, f16[64,2048]{1,0:T(8,128)(2,1)S(1)}, u32[]{:S(2)}, u32[]{:S(2)}) %collective-permute-start.18) | collective-permute-done | bytes 262176 | tf_op jit(solution)/shard_map/ppermute | solution.py:234
  86.1 0.4 collective-permute-start.20
  86.5 1.7 %collective-permute-start.21 = (f16[64,2048]{1,0:T(8,128)(2,1)S(1)}, f16[64,2048]{1,0:T(8,128)(2,1)S(1)}, u32[]{:S(2)}, u32[]{:S(2)}) collective-permute-start(f16[64,2048]{1,0:T(8,128)(2,1)S(1)} %add_convert_fusion.5), channel_id=1, source_target_pairs={{2,0},{7,1},{0,2},{5,3},{6,4},{3,5},{4,6},{1,7},{10,8},{15,9},{8,1... | collective-permute-start | bytes 786440 | tf_op jit(solution)/shard_map/ppermute | solution.py:234
  88.2 6.2 %primary.1 = f32[64,2048]{1,0:T(8,128)S(1)} custom-call(bf16[64,4096]{1,0:T(8,128)(2,1)S(1)} %pad_maximum_fusion.1.left_ref, bf16[4096,2048]{1,0:T(8,128)(2,1)} %coupling_ref.11), custom_call_target="tpu_custom_call" | custom-call | flops 1073741824 | bytes 16777216 | tf_op jit(solution)/shard_map/primary/pallas_call | solution.py:140
  94.6 0.1 multiply_convert_fusion
  94.7 0.2 collective-permute-start.22
  94.9 3.4 %collective-permute-start.23 = (f16[64,2048]{1,0:T(8,128)(2,1)S(1)}, f16[64,2048]{1,0:T(8,128)(2,1)S(1)}, u32[]{:S(2)}, u32[]{:S(2)}) collective-permute-start(f16[64,2048]{1,0:T(8,128)(2,1)S(1)} %add_convert_fusion.4), channel_id=1, source_target_pairs={{6,0},{9,1},{4,2},{11,3},{2,4},{13,5},{0,6},{15,7},{14,8},{1,9},{1... | collective-permute-start | bytes 786440 | tf_op jit(solution)/shard_map/ppermute | solution.py:234
  98.3 2.8 %collective-permute-done.22 = f16[64,2048]{1,0:T(8,128)(2,1)S(1)} collective-permute-done((f16[64,2048]{1,0:T(8,128)(2,1)S(1)}, f16[64,2048]{1,0:T(8,128)(2,1)S(1)}, u32[]{:S(2)}, u32[]{:S(2)}) %collective-permute-start.22) | collective-permute-done | bytes 262176 | tf_op jit(solution)/shard_map/ppermute | solution.py:234
  101.2 0.1 add_convert_fusion.3
  101.3 1.4 collective-permute-done.23
  102.8 3.9 %collective-permute-start.24 = (f16[64,2048]{1,0:T(8,128)(2,1)S(1)}, f16[64,2048]{1,0:T(8,128)(2,1)S(1)}, u32[]{:S(2)}, u32[]{:S(2)}) collective-permute-start(f16[64,2048]{1,0:T(8,128)(2,1)S(1)} %add_convert_fusion.3), channel_id=1, source_target_pairs={{96,0},{33,1},{98,2},{35,3},{100,4},{37,5},{102,6},{39,7},{104,8},... | collective-permute-start | bytes 786440 | tf_op jit(solution)/shard_map/ppermute | solution.py:234
  106.6 1.5 %collective-permute-start.25 = (f16[64,2048]{1,0:T(8,128)(2,1)S(1)}, f16[64,2048]{1,0:T(8,128)(2,1)S(1)}, u32[]{:S(2)}, u32[]{:S(2)}) collective-permute-start(f16[64,2048]{1,0:T(8,128)(2,1)S(1)} %add_convert_fusion.2), channel_id=1, source_target_pairs={{4,0},{5,1},{30,2},{31,3},{34,4},{39,5},{60,6},{57,7},{72,8},{73,9... | collective-permute-start | bytes 786440 | tf_op jit(solution)/shard_map/ppermute | solution.py:234
  108.1 2.9 %collective-permute-done.24 = f16[64,2048]{1,0:T(8,128)(2,1)S(1)} collective-permute-done((f16[64,2048]{1,0:T(8,128)(2,1)S(1)}, f16[64,2048]{1,0:T(8,128)(2,1)S(1)}, u32[]{:S(2)}, u32[]{:S(2)}) %collective-permute-start.24) | collective-permute-done | bytes 262176 | tf_op jit(solution)/shard_map/ppermute | solution.py:234
  111.1 8.7 %collective-permute-done.25 = f16[64,2048]{1,0:T(8,128)(2,1)S(1)} collective-permute-done((f16[64,2048]{1,0:T(8,128)(2,1)S(1)}, f16[64,2048]{1,0:T(8,128)(2,1)S(1)}, u32[]{:S(2)}, u32[]{:S(2)}) %collective-permute-start.25) | collective-permute-done | bytes 262176 | tf_op jit(solution)/shard_map/ppermute | solution.py:234
  119.8 2.2 %collective-permute-start.26 = (f16[64,2048]{1,0:T(8,128)(2,1)S(1)}, f16[64,2048]{1,0:T(8,128)(2,1)S(1)}, u32[]{:S(2)}, u32[]{:S(2)}) collective-permute-start(f16[64,2048]{1,0:T(8,128)(2,1)S(1)} %add_convert_fusion.1), channel_id=1, source_target_pairs={{16,0},{97,1},{18,2},{99,3},{20,4},{101,5},{22,6},{103,7},{24,8},{... | collective-permute-start | bytes 786440 | tf_op jit(solution)/shard_map/ppermute | solution.py:234
  122.0 5.7 %collective-permute-done.26 = f16[64,2048]{1,0:T(8,128)(2,1)S(1)} collective-permute-done((f16[64,2048]{1,0:T(8,128)(2,1)S(1)}, f16[64,2048]{1,0:T(8,128)(2,1)S(1)}, u32[]{:S(2)}, u32[]{:S(2)}) %collective-permute-start.26) | collective-permute-done | bytes 262176 | tf_op jit(solution)/shard_map/ppermute | solution.py:234
  127.7 0.8 multiply_reduce_fusion
  128.6 1.2 collective-permute-done.27
  129.8 3.6 %collective-permute-done.28 = f32[6,64]{1,0:T(8,128)S(1)} collective-permute-done((f32[6,64]{1,0:T(8,128)S(1)}, f32[6,64]{1,0:T(8,128)S(1)}, u32[]{:S(2)}, u32[]{:S(2)}) %collective-permute-start.28) | collective-permute-done | bytes 1568 | tf_op jit(solution)/shard_map/ppermute | solution.py:234
  133.4 1.8 %collective-permute-start.29 = (f32[6,64]{1,0:T(8,128)S(1)}, f32[6,64]{1,0:T(8,128)S(1)}, u32[]{:S(2)}, u32[]{:S(2)}) collective-permute-start(f32[6,64]{1,0:T(8,128)S(1)} %add.167), channel_id=1, source_target_pairs={{2,0},{3,1},{0,2},{1,3},{6,4},{7,5},{4,6},{5,7},{10,8},{11,9},{8,1... | collective-permute-start | bytes 4616 | tf_op jit(solution)/shard_map/ppermute | solution.py:234
  135.2 1.8 %collective-permute-done.29 = f32[6,64]{1,0:T(8,128)S(1)} collective-permute-done((f32[6,64]{1,0:T(8,128)S(1)}, f32[6,64]{1,0:T(8,128)S(1)}, u32[]{:S(2)}, u32[]{:S(2)}) %collective-permute-start.29) | collective-permute-done | bytes 1568 | tf_op jit(solution)/shard_map/ppermute | solution.py:234
  137.0 4.8 %collective-permute-done.30 = f32[6,64]{1,0:T(8,128)S(1)} collective-permute-done((f32[6,64]{1,0:T(8,128)S(1)}, f32[6,64]{1,0:T(8,128)S(1)}, u32[]{:S(2)}, u32[]{:S(2)}) %collective-permute-start.30) | collective-permute-done | bytes 1568 | tf_op jit(solution)/shard_map/ppermute | solution.py:234
  141.8 2.8 %multiply_subtract_fusion = (f32[64,2048]{1,0:T(8,128)}, f32[64,2048]{1,0:T(8,128)}, f32[64,2048]{1,0:T(8,128)}, f32[64,2048]{1,0:T(8,128)}) fusion(f16[64,2048]{1,0:T(8,128)(2,1)S(1)} %collective-permute-done.25, f32[64,2048]{1,0:T(8,128)S(1)} %get-tuple-element.85, f32[64,2048]{1,0:T(8,128)S(1)} %copy-done, f16[64,2048]{1,0:T(8,128)(2,1)S(1)} %collective-permute-done.15, ...), kind=kLoop, calls=%fused_computation.2 | loop fusion | flops 7077888 | bytes 5507328 | tf_op jit(solution)/shard_map/sub | solution.py:405
  (60 shorter events, 1.7 us)
Async XLA Ops:
  2.6 4.2 %collective-permute-start = (f32[4,64]{1,0:T(4,128)S(1)}, f32[4,64]{1,0:T(4,128)S(1)}, u32[]{:S(2)}, u32[]{:S(2)}) collective-permute-start(f32[4,64]{1,0:T(4,128)S(1)} %pad_maximum_fusion.5), channel_id=1, source_target_pairs={{1,0},{0,1},{3,2},{2,3},{5,4},{4,5},{7,6},{6,7},{9,8},{8,9},{11,10... | collective-permute-start | bytes 3080 | tf_op jit(solution)/shard_map/ppermute | solution.py:234
  2.7 18.6 %collective-permute-start.3 = (bf16[64,1024]{1,0:T(8,128)(2,1)S(1)}, bf16[64,1024]{1,0:T(8,128)(2,1)S(1)}, u32[]{:S(2)}, u32[]{:S(2)}) collective-permute-start(bf16[64,1024]{1,0:T(8,128)(2,1)S(1)} %slice_select_fusion.2), channel_id=1, source_target_pairs={{112,0},{65,1},{48,2},{113,3},{0,4},{33,5},{64,6},{17,7},{96,8},{9... | collective-permute-start | bytes 393224 | tf_op jit(solution)/shard_map/ppermute | solution.py:234
  6.8 5.4 %collective-permute-start.1 = (f32[4,64]{1,0:T(4,128)S(1)}, f32[4,64]{1,0:T(4,128)S(1)}, u32[]{:S(2)}, u32[]{:S(2)}) collective-permute-start(f32[4,64]{1,0:T(4,128)S(1)} %pad_maximum_fusion.6), channel_id=1, source_target_pairs={{8,0},{9,1},{10,2},{11,3},{12,4},{13,5},{14,6},{15,7},{0,8},{1,9},... | collective-permute-start | bytes 3080 | tf_op jit(solution)/shard_map/ppermute | solution.py:234
  12.2 9.1 %collective-permute-start.2 = (f32[4,64]{1,0:T(4,128)S(1)}, f32[4,64]{1,0:T(4,128)S(1)}, u32[]{:S(2)}, u32[]{:S(2)}) collective-permute-start(f32[4,64]{1,0:T(4,128)S(1)} %pad_maximum_fusion.7), channel_id=1, source_target_pairs={{2,0},{3,1},{0,2},{1,3},{6,4},{7,5},{4,6},{5,7},{10,8},{11,9},{8,1... | collective-permute-start | bytes 3080 | tf_op jit(solution)/shard_map/ppermute | solution.py:234
  21.4 4.9 %collective-permute-start.4 = (f32[4,64]{1,0:T(4,128)S(1)}, f32[4,64]{1,0:T(4,128)S(1)}, u32[]{:S(2)}, u32[]{:S(2)}) collective-permute-start(f32[4,64]{1,0:T(4,128)S(1)} %pad_maximum_fusion.8), channel_id=1, source_target_pairs={{6,0},{7,1},{4,2},{5,3},{2,4},{3,5},{0,6},{1,7},{14,8},{15,9},{12,... | collective-permute-start | bytes 3080 | tf_op jit(solution)/shard_map/ppermute | solution.py:234
  21.5 5.1 %collective-permute-start.5 = (bf16[64,1024]{1,0:T(8,128)(2,1)S(1)}, bf16[64,1024]{1,0:T(8,128)(2,1)S(1)}, u32[]{:S(2)}, u32[]{:S(2)}) collective-permute-start(bf16[64,1024]{1,0:T(8,128)(2,1)S(1)} %collective-permute-done.3), channel_id=1, source_target_pairs={{2,0},{3,1},{0,2},{1,3},{6,4},{7,5},{4,6},{5,7},{10,8},{11,9},{8,1... | collective-permute-start | bytes 393224 | tf_op jit(solution)/shard_map/ppermute | solution.py:234
  26.7 1.6 %collective-permute-start.6 = (bf16[64,2048]{1,0:T(8,128)(2,1)S(1)}, bf16[64,2048]{1,0:T(8,128)(2,1)S(1)}, u32[]{:S(2)}, u32[]{:S(2)}) collective-permute-start(bf16[64,2048]{1,0:T(8,128)(2,1)S(1)} %pad_maximum_fusion.2), channel_id=1, source_target_pairs={{1,0},{0,1},{3,2},{2,3},{5,4},{4,5},{7,6},{6,7},{9,8},{8,9},{11,10... | collective-permute-start | bytes 786440 | tf_op jit(solution)/shard_map/ppermute | solution.py:234
  26.9 1.8 %collective-permute-start.7 = (f16[64,2048]{1,0:T(8,128)(2,1)S(1)}, f16[64,2048]{1,0:T(8,128)(2,1)S(1)}, u32[]{:S(2)}, u32[]{:S(2)}) collective-permute-start(f16[64,2048]{1,0:T(8,128)(2,1)S(1)} %multiply_convert_fusion.2), channel_id=1, source_target_pairs={{1,0},{0,1},{3,2},{2,3},{5,4},{4,5},{7,6},{6,7},{9,8},{8,9},{11,10... | collective-permute-start | bytes 786440 | tf_op jit(solution)/shard_map/ppermute | solution.py:234
  28.8 11.2 %collective-permute-start.8 = (f16[64,2048]{1,0:T(8,128)(2,1)S(1)}, f16[64,2048]{1,0:T(8,128)(2,1)S(1)}, u32[]{:S(2)}, u32[]{:S(2)}) collective-permute-start(f16[64,2048]{1,0:T(8,128)(2,1)S(1)} %add_convert_fusion.10), channel_id=1, source_target_pairs={{8,0},{3,1},{10,2},{1,3},{12,4},{7,5},{14,6},{5,7},{0,8},{11,9},{2... | collective-permute-start | bytes 786440 | tf_op jit(solution)/shard_map/ppermute | solution.py:234
  29.2 32.3 %copy-start.1 = (f32[64,2048]{1,0:T(8,128)S(1)}, f32[64,2048]{1,0:T(8,128)}, u32[]{:S(2)}) copy-start(f32[64,2048]{1,0:T(8,128)} %param.6) | copy-start | bytes 1572868
  29.2 35.5 %copy-start = (f32[64,2048]{1,0:T(8,128)S(1)}, f32[64,2048]{1,0:T(8,128)}, u32[]{:S(2)}) copy-start(f32[64,2048]{1,0:T(8,128)} %param.7) | copy-start | bytes 1572868
  29.2 35.5 %copy-start.2 = (f32[64,2048]{1,0:T(8,128)S(1)}, f32[64,2048]{1,0:T(8,128)}, u32[]{:S(2)}) copy-start(f32[64,2048]{1,0:T(8,128)} %param.5) | copy-start | bytes 1572868
  33.1 8.2 %collective-permute-start.9 = (f16[64,1024]{1,0:T(8,128)(2,1)S(1)}, f16[64,1024]{1,0:T(8,128)(2,1)S(1)}, u32[]{:S(2)}, u32[]{:S(2)}) collective-permute-start(f16[64,1024]{1,0:T(8,128)(2,1)S(1)} %multiply_convert_fusion.4), channel_id=1, source_target_pairs={{32,0},{17,1},{34,2},{19,3},{36,4},{21,5},{38,6},{23,7},{40,8},{25... | collective-permute-start | bytes 393224 | tf_op jit(solution)/shard_map/ppermute | solution.py:234
  40.1 6.5 %collective-permute-start.10 = (f16[64,2048]{1,0:T(8,128)(2,1)S(1)}, f16[64,2048]{1,0:T(8,128)(2,1)S(1)}, u32[]{:S(2)}, u32[]{:S(2)}) collective-permute-start(f16[64,2048]{1,0:T(8,128)(2,1)S(1)} %add_convert_fusion.9), channel_id=1, source_target_pairs={{2,0},{7,1},{0,2},{5,3},{6,4},{3,5},{4,6},{1,7},{10,8},{15,9},{8,1... | collective-permute-start | bytes 786440 | tf_op jit(solution)/shard_map/ppermute | solution.py:234
  46.7 6.3 %collective-permute-start.11 = (f16[64,1024]{1,0:T(8,128)(2,1)S(1)}, f16[64,1024]{1,0:T(8,128)(2,1)S(1)}, u32[]{:S(2)}, u32[]{:S(2)}) collective-permute-start(f16[64,1024]{1,0:T(8,128)(2,1)S(1)} %add_convert_fusion.13), channel_id=1, source_target_pairs={{96,0},{33,1},{98,2},{35,3},{100,4},{37,5},{102,6},{39,7},{104,8},... | collective-permute-start | bytes 393224 | tf_op jit(solution)/shard_map/ppermute | solution.py:234
  47.0 7.6 %collective-permute-start.12 = (f16[64,2048]{1,0:T(8,128)(2,1)S(1)}, f16[64,2048]{1,0:T(8,128)(2,1)S(1)}, u32[]{:S(2)}, u32[]{:S(2)}) collective-permute-start(f16[64,2048]{1,0:T(8,128)(2,1)S(1)} %add_convert_fusion.8), channel_id=1, source_target_pairs={{6,0},{9,1},{4,2},{11,3},{2,4},{13,5},{0,6},{15,7},{14,8},{1,9},{1... | collective-permute-start | bytes 786440 | tf_op jit(solution)/shard_map/ppermute | solution.py:234
  54.6 6.8 %collective-permute-start.13 = (f16[64,1024]{1,0:T(8,128)(2,1)S(1)}, f16[64,1024]{1,0:T(8,128)(2,1)S(1)}, u32[]{:S(2)}, u32[]{:S(2)}) collective-permute-start(f16[64,1024]{1,0:T(8,128)(2,1)S(1)} %add_convert_fusion.12), channel_id=1, source_target_pairs={{16,0},{97,1},{18,2},{99,3},{20,4},{101,5},{22,6},{103,7},{24,8},{... | collective-permute-start | bytes 393224 | tf_op jit(solution)/shard_map/ppermute | solution.py:234
  56.8 7.9 %collective-permute-start.15 = (f16[64,2048]{1,0:T(8,128)(2,1)S(1)}, f16[64,2048]{1,0:T(8,128)(2,1)S(1)}, u32[]{:S(2)}, u32[]{:S(2)}) collective-permute-start(f16[64,2048]{1,0:T(8,128)(2,1)S(1)} %add_convert_fusion.7), channel_id=1, source_target_pairs={{4,0},{5,1},{30,2},{31,3},{34,4},{39,5},{60,6},{57,7},{72,8},{73,9... | collective-permute-start | bytes 786440 | tf_op jit(solution)/shard_map/ppermute | solution.py:234
  61.6 11.5 %collective-permute-start.14 = (bf16[64,1024]{1,0:T(8,128)(2,1)S(1)}, bf16[64,1024]{1,0:T(8,128)(2,1)S(1)}, u32[]{:S(2)}, u32[]{:S(2)}) collective-permute-start(bf16[64,1024]{1,0:T(8,128)(2,1)S(1)} %get-tuple-element.86), channel_id=1, source_target_pairs={{112,0},{65,1},{48,2},{113,3},{0,4},{33,5},{64,6},{17,7},{96,8},{9... | collective-permute-start | bytes 393224 | tf_op jit(solution)/shard_map/ppermute | solution.py:234
  73.2 1.6 %collective-permute-start.16 = (f16[64,2048]{1,0:T(8,128)(2,1)S(1)}, f16[64,2048]{1,0:T(8,128)(2,1)S(1)}, u32[]{:S(2)}, u32[]{:S(2)}) collective-permute-start(f16[64,2048]{1,0:T(8,128)(2,1)S(1)} %multiply_convert_fusion.1), channel_id=1, source_target_pairs={{1,0},{0,1},{3,2},{2,3},{5,4},{4,5},{7,6},{6,7},{9,8},{8,9},{11,10... | collective-permute-start | bytes 786440 | tf_op jit(solution)/shard_map/ppermute | solution.py:234
  75.0 6.5 %collective-permute-start.17 = (bf16[64,1024]{1,0:T(8,128)(2,1)S(1)}, bf16[64,1024]{1,0:T(8,128)(2,1)S(1)}, u32[]{:S(2)}, u32[]{:S(2)}) collective-permute-start(bf16[64,1024]{1,0:T(8,128)(2,1)S(1)} %collective-permute-done.14), channel_id=1, source_target_pairs={{2,0},{3,1},{0,2},{1,3},{6,4},{7,5},{4,6},{5,7},{10,8},{11,9},{8,1... | collective-permute-start | bytes 393224 | tf_op jit(solution)/shard_map/ppermute | solution.py:234
  77.7 5.0 %collective-permute-start.19 = (f16[64,1024]{1,0:T(8,128)(2,1)S(1)}, f16[64,1024]{1,0:T(8,128)(2,1)S(1)}, u32[]{:S(2)}, u32[]{:S(2)}) collective-permute-start(f16[64,1024]{1,0:T(8,128)(2,1)S(1)} %get-tuple-element.58), channel_id=1, source_target_pairs={{32,0},{17,1},{34,2},{19,3},{36,4},{21,5},{38,6},{23,7},{40,8},{25... | collective-permute-start | bytes 393224 | tf_op jit(solution)/shard_map/ppermute | solution.py:234
  78.8 7.2 %collective-permute-start.18 = (f16[64,2048]{1,0:T(8,128)(2,1)S(1)}, f16[64,2048]{1,0:T(8,128)(2,1)S(1)}, u32[]{:S(2)}, u32[]{:S(2)}) collective-permute-start(f16[64,2048]{1,0:T(8,128)(2,1)S(1)} %add_convert_fusion.6), channel_id=1, source_target_pairs={{8,0},{3,1},{10,2},{1,3},{12,4},{7,5},{14,6},{5,7},{0,8},{11,9},{2... | collective-permute-start | bytes 786440 | tf_op jit(solution)/shard_map/ppermute | solution.py:234
  86.1 2.1 %collective-permute-start.20 = (bf16[64,2048]{1,0:T(8,128)(2,1)S(1)}, bf16[64,2048]{1,0:T(8,128)(2,1)S(1)}, u32[]{:S(2)}, u32[]{:S(2)}) collective-permute-start(bf16[64,2048]{1,0:T(8,128)(2,1)S(1)} %pad_maximum_fusion.3), channel_id=1, source_target_pairs={{1,0},{0,1},{3,2},{2,3},{5,4},{4,5},{7,6},{6,7},{9,8},{8,9},{11,10... | collective-permute-start | bytes 786440 | tf_op jit(solution)/shard_map/ppermute | solution.py:234
  86.5 8.0 %collective-permute-start.21 = (f16[64,2048]{1,0:T(8,128)(2,1)S(1)}, f16[64,2048]{1,0:T(8,128)(2,1)S(1)}, u32[]{:S(2)}, u32[]{:S(2)}) collective-permute-start(f16[64,2048]{1,0:T(8,128)(2,1)S(1)} %add_convert_fusion.5), channel_id=1, source_target_pairs={{2,0},{7,1},{0,2},{5,3},{6,4},{3,5},{4,6},{1,7},{10,8},{15,9},{8,1... | collective-permute-start | bytes 786440 | tf_op jit(solution)/shard_map/ppermute | solution.py:234
  94.7 6.5 %collective-permute-start.22 = (f16[64,2048]{1,0:T(8,128)(2,1)S(1)}, f16[64,2048]{1,0:T(8,128)(2,1)S(1)}, u32[]{:S(2)}, u32[]{:S(2)}) collective-permute-start(f16[64,2048]{1,0:T(8,128)(2,1)S(1)} %multiply_convert_fusion), channel_id=1, source_target_pairs={{32,0},{17,1},{34,2},{19,3},{36,4},{21,5},{38,6},{23,7},{40,8},{25... | collective-permute-start | bytes 786440 | tf_op jit(solution)/shard_map/ppermute | solution.py:234
  94.9 7.8 %collective-permute-start.23 = (f16[64,2048]{1,0:T(8,128)(2,1)S(1)}, f16[64,2048]{1,0:T(8,128)(2,1)S(1)}, u32[]{:S(2)}, u32[]{:S(2)}) collective-permute-start(f16[64,2048]{1,0:T(8,128)(2,1)S(1)} %add_convert_fusion.4), channel_id=1, source_target_pairs={{6,0},{9,1},{4,2},{11,3},{2,4},{13,5},{0,6},{15,7},{14,8},{1,9},{1... | collective-permute-start | bytes 786440 | tf_op jit(solution)/shard_map/ppermute | solution.py:234
  102.8 8.2 %collective-permute-start.24 = (f16[64,2048]{1,0:T(8,128)(2,1)S(1)}, f16[64,2048]{1,0:T(8,128)(2,1)S(1)}, u32[]{:S(2)}, u32[]{:S(2)}) collective-permute-start(f16[64,2048]{1,0:T(8,128)(2,1)S(1)} %add_convert_fusion.3), channel_id=1, source_target_pairs={{96,0},{33,1},{98,2},{35,3},{100,4},{37,5},{102,6},{39,7},{104,8},... | collective-permute-start | bytes 786440 | tf_op jit(solution)/shard_map/ppermute | solution.py:234
  106.6 13.2 %collective-permute-start.25 = (f16[64,2048]{1,0:T(8,128)(2,1)S(1)}, f16[64,2048]{1,0:T(8,128)(2,1)S(1)}, u32[]{:S(2)}, u32[]{:S(2)}) collective-permute-start(f16[64,2048]{1,0:T(8,128)(2,1)S(1)} %add_convert_fusion.2), channel_id=1, source_target_pairs={{4,0},{5,1},{30,2},{31,3},{34,4},{39,5},{60,6},{57,7},{72,8},{73,9... | collective-permute-start | bytes 786440 | tf_op jit(solution)/shard_map/ppermute | solution.py:234
  119.8 7.9 %collective-permute-start.26 = (f16[64,2048]{1,0:T(8,128)(2,1)S(1)}, f16[64,2048]{1,0:T(8,128)(2,1)S(1)}, u32[]{:S(2)}, u32[]{:S(2)}) collective-permute-start(f16[64,2048]{1,0:T(8,128)(2,1)S(1)} %add_convert_fusion.1), channel_id=1, source_target_pairs={{16,0},{97,1},{18,2},{99,3},{20,4},{101,5},{22,6},{103,7},{24,8},{... | collective-permute-start | bytes 786440 | tf_op jit(solution)/shard_map/ppermute | solution.py:234
  128.5 1.2 collective-permute-start.27
  129.7 3.6 %collective-permute-start.28 = (f32[6,64]{1,0:T(8,128)S(1)}, f32[6,64]{1,0:T(8,128)S(1)}, u32[]{:S(2)}, u32[]{:S(2)}) collective-permute-start(f32[6,64]{1,0:T(8,128)S(1)} %add.166), channel_id=1, source_target_pairs={{8,0},{9,1},{10,2},{11,3},{12,4},{13,5},{14,6},{15,7},{0,8},{1,9},... | collective-permute-start | bytes 4616 | tf_op jit(solution)/shard_map/ppermute | solution.py:234
  133.4 3.6 %collective-permute-start.29 = (f32[6,64]{1,0:T(8,128)S(1)}, f32[6,64]{1,0:T(8,128)S(1)}, u32[]{:S(2)}, u32[]{:S(2)}) collective-permute-start(f32[6,64]{1,0:T(8,128)S(1)} %add.167), channel_id=1, source_target_pairs={{2,0},{3,1},{0,2},{1,3},{6,4},{7,5},{4,6},{5,7},{10,8},{11,9},{8,1... | collective-permute-start | bytes 4616 | tf_op jit(solution)/shard_map/ppermute | solution.py:234
  137.0 4.8 %collective-permute-start.30 = (f32[6,64]{1,0:T(8,128)S(1)}, f32[6,64]{1,0:T(8,128)S(1)}, u32[]{:S(2)}, u32[]{:S(2)}) collective-permute-start(f32[6,64]{1,0:T(8,128)S(1)} %add.168), channel_id=1, source_target_pairs={{6,0},{7,1},{4,2},{5,3},{2,4},{3,5},{0,6},{1,7},{14,8},{15,9},{12,... | collective-permute-start | bytes 4616 | tf_op jit(solution)/shard_map/ppermute | solution.py:234

commit v11 on v9

--- a/solution.py
+++ b/solution.py
@@ -346,12 +346,12 @@
     block = put(z_even, half, move(half, Z_PAIR))
     scale = SECOND_SCALE / shadow_top
     shadow_held = send_core(jnp.split(shadow_partial, 2, axis=1), scale)
-    product = put(low_half, held, move(held, ROW_STEPS[0]))
-    block, shadow_held, product = tie(block, shadow_held, product)
+    block, shadow_held, held = tie(block, shadow_held, held)
     left = put(first, block, move(block, CORE))
     partial = primary(left, coupling)
     shadow_held = exchange(shadow_held, COL_STEPS[0])
-    partial, shadow_held = tie(partial, shadow_held)
+    product = put(low_half, held, move(held, ROW_STEPS[0]))
+    partial, shadow_held, product = tie(partial, shadow_held, product)
     held = exchange((partial * (SECOND_SCALE / top)).astype(WIRE), ROW_STEPS[0])
     shadow_held = exchange(shadow_held, COL_STEPS[1])
     held, shadow_held = tie(held, shadow_held)

time: 137 us -> 138 us (level)
  transfers between devices with their start and end apart: 31 -> 31, of which waited for: 22 -> 21; matrix products, arithmetic and copies ran while one was open for 2% -> 2% of each run, Pallas kernels for 23% -> 22%
where the time goes in v11:
time: 138 us
  waiting for transfers between devices  50.5 us (37%)
  starting transfers between devices  46.7 us (34%)
  Pallas kernels  30.8 us (22%)
  other arithmetic  8.82 us (6%)
    ppermute x31, waiting for transfers between devices, move(): return lax.ppermute(value, AXES, pairs)  50.5 us
    ppermute x31, starting transfers between devices, move(): return lax.ppermute(value, AXES, pairs)  46.7 us
    pallas_call x2, Pallas kernels, call(): pl.pallas_call(kernel, name=name, in_specs=[spec, pl.BlockSpec(memory_spa...  14 us
    pallas_call x2, Pallas kernels, shadow_rows(): pl.pallas_call(kernel, name='shadow_rows', in_specs=[spec, pl.BlockSpec(m...  9.31 us
    pallas_call x2, Pallas kernels, primary_half(): pl.pallas_call(half_kernel, name='primary_half', in_specs=[pl.BlockSpec(m...  7.56 us
    sub x1, other arithmetic, on_device(): shadow_residual = gs - step * q1 - step_next * (lead * q1 + kappa * q2)  2.83 us
  transfers between devices with their start and end apart: 31, of which 21 were waited for; matrix products, arithmetic and copies ran while one was open for 2% of the time, Pallas kernels for 22%

profile of v11, /device:TPU:0, one launch (start us, length us, event | category | flops | bytes accessed | tf_op | source)
XLA Modules:
  0.0 137.9 jit_solution(3693421250688662600)
XLA Ops:
  0.6 1.9 %multiply_reduce_fusion.7 = (f32[64]{0:T(128)S(1)}, f32[64]{0:T(128)S(1)}, f32[64]{0:T(128)S(1)}, f32[64]{0:T(128)S(1)}, bf16[64,2048]{1,0:T(8,128)(2,1)S(1)}, /...) fusion(f32[64,2048]{1,0:T(8,128)} %param.7, f32[64,2048]{1,0:T(8,128)} %param.6, ...), kind=kLoop, calls=%fused_computation.35 | loop fusion | flops 2096896 | bytes 3146752 | tf_op jit(solution)/shard_map/reduce_sum | solution.py:258
  2.7 4.0 %collective-permute-start.3 = (bf16[64,1024]{1,0:T(8,128)(2,1)S(1)}, bf16[64,1024]{1,0:T(8,128)(2,1)S(1)}, u32[]{:S(2)}, u32[]{:S(2)}) collective-permute-start(bf16[64,1024]{1,0:T(8,128)(2,1)S(1)} %slice_select_fusion.2), channel_id=1, source_target_pairs={{112,0},{65,1},{48,2},{113,3},{0,4},{33,5},{64,6},{17,7},{96,8},{9... | collective-permute-start | bytes 393224 | tf_op jit(solution)/shard_map/ppermute | solution.py:234
  6.8 0.7 collective-permute-start.1
  7.5 4.7 %shadow_rows.2 = f32[64,2048]{1,0:T(8,128)S(1)} custom-call(bf16[64,2048]{1,0:T(8,128)(2,1)S(1)} %get-tuple-element.37.left_ref, bf16[4096,2048]{1,0:T(8,128)(2,1)} %coupling_ref.11), custom_call_target="tpu_custom_call" | custom-call | flops 536870912 | bytes 8388608 | tf_op jit(solution)/shard_map/shadow_rows/pallas_call | solution.py:176
  12.2 4.5 %collective-permute-start.2 = (f32[4,64]{1,0:T(4,128)S(1)}, f32[4,64]{1,0:T(4,128)S(1)}, u32[]{:S(2)}, u32[]{:S(2)}) collective-permute-start(f32[4,64]{1,0:T(4,128)S(1)} %pad_maximum_fusion.7), channel_id=1, source_target_pairs={{2,0},{3,1},{0,2},{1,3},{6,4},{7,5},{4,6},{5,7},{10,8},{11,9},{8,1... | collective-permute-start | bytes 3080 | tf_op jit(solution)/shard_map/ppermute | solution.py:234
  16.7 4.7 %shadow_rows.3 = f32[64,2048]{1,0:T(8,128)S(1)} custom-call(bf16[64,2048]{1,0:T(8,128)(2,1)S(1)} %get-tuple-element.37.left_ref, bf16[4096,2048]{1,0:T(8,128)(2,1)} %coupling_ref.11), custom_call_target="tpu_custom_call" | custom-call | flops 536870912 | bytes 8388608 | tf_op jit(solution)/shard_map/shadow_rows/pallas_call | solution.py:176
  21.5 0.5 collective-permute-start.5
  22.0 4.2 %collective-permute-done.4 = f32[4,64]{1,0:T(4,128)S(1)} collective-permute-done((f32[4,64]{1,0:T(4,128)S(1)}, f32[4,64]{1,0:T(4,128)S(1)}, u32[]{:S(2)}, u32[]{:S(2)}) %collective-permute-start.4) | collective-permute-done | bytes 1056 | tf_op jit(solution)/shard_map/ppermute | solution.py:234
  26.3 0.3 collective-permute-done.5
  26.8 0.1 multiply_convert_fusion.2
  26.9 0.6 collective-permute-start.7
  27.4 0.8 collective-permute-done.6
  28.4 0.3 collective-permute-done.7
  28.6 0.2 add_convert_fusion.10
  28.8 0.4 collective-permute-start.8
  29.2 3.8 %primary_half.3 = f32[64,1024]{1,0:T(8,128)S(1)} custom-call(s32[1]{0:T(128)} %bitcast.9.offset_ref, bf16[64,4096]{1,0:T(8,128)(2,1)S(1)} %pad_maximum_fusion.left_ref, bf16[4096,2048]{1,0:T(8,128)(2,1)} %coupling_ref.11), custom_call_target="tpu_custom_call" | custom-call | flops 536870912 | bytes 8388608 | tf_op jit(solution)/shard_map/primary_half/pallas_call | solution.py:210
  33.1 0.1 multiply_convert_fusion.4
  33.1 3.1 %collective-permute-start.9 = (f16[64,1024]{1,0:T(8,128)(2,1)S(1)}, f16[64,1024]{1,0:T(8,128)(2,1)S(1)}, u32[]{:S(2)}, u32[]{:S(2)}) collective-permute-start(f16[64,1024]{1,0:T(8,128)(2,1)S(1)} %multiply_convert_fusion.4), channel_id=1, source_target_pairs={{32,0},{17,1},{34,2},{19,3},{36,4},{21,5},{38,6},{23,7},{40,8},{25... | collective-permute-start | bytes 393224 | tf_op jit(solution)/shard_map/ppermute | solution.py:234
  36.3 3.7 %primary_half.2 = f32[64,1024]{1,0:T(8,128)S(1)} custom-call(s32[1]{0:T(128)} %bitcast.6.offset_ref, bf16[64,4096]{1,0:T(8,128)(2,1)S(1)} %pad_maximum_fusion.left_ref, bf16[4096,2048]{1,0:T(8,128)(2,1)} %coupling_ref.11), custom_call_target="tpu_custom_call" | custom-call | flops 536870912 | bytes 8388608 | tf_op jit(solution)/shard_map/primary_half/pallas_call | solution.py:210
  40.1 1.3 collective-permute-start.10
  41.4 0.1 add_convert_fusion.13
  41.5 5.1 %collective-permute-done.10 = f16[64,2048]{1,0:T(8,128)(2,1)S(1)} collective-permute-done((f16[64,2048]{1,0:T(8,128)(2,1)S(1)}, f16[64,2048]{1,0:T(8,128)(2,1)S(1)}, u32[]{:S(2)}, u32[]{:S(2)}) %collective-permute-start.10) | collective-permute-done | bytes 262176 | tf_op jit(solution)/shard_map/ppermute | solution.py:234
  46.7 0.3 collective-permute-start.11
  47.0 2.3 %collective-permute-start.12 = (f16[64,2048]{1,0:T(8,128)(2,1)S(1)}, f16[64,2048]{1,0:T(8,128)(2,1)S(1)}, u32[]{:S(2)}, u32[]{:S(2)}) collective-permute-start(f16[64,2048]{1,0:T(8,128)(2,1)S(1)} %add_convert_fusion.8), channel_id=1, source_target_pairs={{6,0},{9,1},{4,2},{11,3},{2,4},{13,5},{0,6},{15,7},{14,8},{1,9},{1... | collective-permute-start | bytes 786440 | tf_op jit(solution)/shard_map/ppermute | solution.py:234
  49.3 3.6 %collective-permute-done.11 = f16[64,1024]{1,0:T(8,128)(2,1)S(1)} collective-permute-done((f16[64,1024]{1,0:T(8,128)(2,1)S(1)}, f16[64,1024]{1,0:T(8,128)(2,1)S(1)}, u32[]{:S(2)}, u32[]{:S(2)}) %collective-permute-start.11) | collective-permute-done | bytes 131104 | tf_op jit(solution)/shard_map/ppermute | solution.py:234
  53.0 1.6 %collective-permute-done.12 = f16[64,2048]{1,0:T(8,128)(2,1)S(1)} collective-permute-done((f16[64,2048]{1,0:T(8,128)(2,1)S(1)}, f16[64,2048]{1,0:T(8,128)(2,1)S(1)}, u32[]{:S(2)}, u32[]{:S(2)}) %collective-permute-start.12) | collective-permute-done | bytes 262176 | tf_op jit(solution)/shard_map/ppermute | solution.py:234
  54.6 2.2 %collective-permute-start.13 = (f16[64,1024]{1,0:T(8,128)(2,1)S(1)}, f16[64,1024]{1,0:T(8,128)(2,1)S(1)}, u32[]{:S(2)}, u32[]{:S(2)}) collective-permute-start(f16[64,1024]{1,0:T(8,128)(2,1)S(1)} %add_convert_fusion.12), channel_id=1, source_target_pairs={{16,0},{97,1},{18,2},{99,3},{20,4},{101,5},{22,6},{103,7},{24,8},{... | collective-permute-start | bytes 393224 | tf_op jit(solution)/shard_map/ppermute | solution.py:234
  56.8 2.5 %collective-permute-start.15 = (f16[64,2048]{1,0:T(8,128)(2,1)S(1)}, f16[64,2048]{1,0:T(8,128)(2,1)S(1)}, u32[]{:S(2)}, u32[]{:S(2)}) collective-permute-start(f16[64,2048]{1,0:T(8,128)(2,1)S(1)} %add_convert_fusion.7), channel_id=1, source_target_pairs={{4,0},{5,1},{30,2},{31,3},{34,4},{39,5},{60,6},{57,7},{72,8},{73,9... | collective-permute-start | bytes 786440 | tf_op jit(solution)/shard_map/ppermute | solution.py:234
  59.3 2.2 %collective-permute-done.13 = f16[64,1024]{1,0:T(8,128)(2,1)S(1)} collective-permute-done((f16[64,1024]{1,0:T(8,128)(2,1)S(1)}, f16[64,1024]{1,0:T(8,128)(2,1)S(1)}, u32[]{:S(2)}, u32[]{:S(2)}) %collective-permute-start.13) | collective-permute-done | bytes 131104 | tf_op jit(solution)/shard_map/ppermute | solution.py:234
  61.5 0.2 fusion.6
  61.6 0.8 collective-permute-start.14
  62.5 2.2 %collective-permute-done.15 = f16[64,2048]{1,0:T(8,128)(2,1)S(1)} collective-permute-done((f16[64,2048]{1,0:T(8,128)(2,1)S(1)}, f16[64,2048]{1,0:T(8,128)(2,1)S(1)}, u32[]{:S(2)}, u32[]{:S(2)}) %collective-permute-start.15) | collective-permute-done | bytes 262176 | tf_op jit(solution)/shard_map/ppermute | solution.py:234
  64.7 0.2 fusion.15
  64.9 7.7 %shadow.1 = f32[64,4096]{1,0:T(8,128)S(1)} custom-call(bf16[64,2048]{1,0:T(8,128)(2,1)S(1)} %get-tuple-element.84.left_ref, bf16[4096,2048]{1,0:T(8,128)(2,1)} %coupling_ref.11), custom_call_target="tpu_custom_call" | custom-call | flops 1073741824 | bytes 16777216 | tf_op jit(solution)/shard_map/shadow/pallas_call | solution.py:140
  72.7 0.5 collective-permute-done.14
  73.1 2.7 %collective-permute-start.16 = (bf16[64,1024]{1,0:T(8,128)(2,1)S(1)}, bf16[64,1024]{1,0:T(8,128)(2,1)S(1)}, u32[]{:S(2)}, u32[]{:S(2)}) collective-permute-start(bf16[64,1024]{1,0:T(8,128)(2,1)S(1)} %collective-permute-done.14), channel_id=1, source_target_pairs={{2,0},{3,1},{0,2},{1,3},{6,4},{7,5},{4,6},{5,7},{10,8},{11,9},{8,1... | collective-permute-start | bytes 393224 | tf_op jit(solution)/shard_map/ppermute | solution.py:234
  75.9 0.1 multiply_convert_fusion.1
  76.1 2.7 %collective-permute-done.16 = bf16[64,1024]{1,0:T(8,128)(2,1)S(1)} collective-permute-done((bf16[64,1024]{1,0:T(8,128)(2,1)S(1)}, bf16[64,1024]{1,0:T(8,128)(2,1)S(1)}, u32[]{:S(2)}, u32[]{:S(2)}) %collective-permute-start.16) | collective-permute-done | bytes 131104 | tf_op jit(solution)/shard_map/ppermute | solution.py:234
  78.9 0.2 add_convert_fusion.6
  79.0 2.1 %collective-permute-start.20 = (f16[64,1024]{1,0:T(8,128)(2,1)S(1)}, f16[64,1024]{1,0:T(8,128)(2,1)S(1)}, u32[]{:S(2)}, u32[]{:S(2)}) collective-permute-start(f16[64,1024]{1,0:T(8,128)(2,1)S(1)} %get-tuple-element.58), channel_id=1, source_target_pairs={{32,0},{17,1},{34,2},{19,3},{36,4},{21,5},{38,6},{23,7},{40,8},{25... | collective-permute-start | bytes 393224 | tf_op jit(solution)/shard_map/ppermute | solution.py:234
  81.1 0.5 collective-permute-start.19
  81.6 2.4 %collective-permute-done.20 = f16[64,1024]{1,0:T(8,128)(2,1)S(1)} collective-permute-done((f16[64,1024]{1,0:T(8,128)(2,1)S(1)}, f16[64,1024]{1,0:T(8,128)(2,1)S(1)}, u32[]{:S(2)}, u32[]{:S(2)}) %collective-permute-start.20) | collective-permute-done | bytes 131104 | tf_op jit(solution)/shard_map/ppermute | solution.py:234
  84.3 6.2 %primary.1 = f32[64,2048]{1,0:T(8,128)S(1)} custom-call(bf16[64,4096]{1,0:T(8,128)(2,1)S(1)} %pad_maximum_fusion.1.left_ref, bf16[4096,2048]{1,0:T(8,128)(2,1)} %coupling_ref.11), custom_call_target="tpu_custom_call" | custom-call | flops 1073741824 | bytes 16777216 | tf_op jit(solution)/shard_map/primary/pallas_call | solution.py:140
  90.7 0.1 multiply_convert_fusion
  90.8 2.1 %collective-permute-start.21 = (f16[64,2048]{1,0:T(8,128)(2,1)S(1)}, f16[64,2048]{1,0:T(8,128)(2,1)S(1)}, u32[]{:S(2)}, u32[]{:S(2)}) collective-permute-start(f16[64,2048]{1,0:T(8,128)(2,1)S(1)} %multiply_convert_fusion), channel_id=1, source_target_pairs={{32,0},{17,1},{34,2},{19,3},{36,4},{21,5},{38,6},{23,7},{40,8},{25... | collective-permute-start | bytes 786440 | tf_op jit(solution)/shard_map/ppermute | solution.py:234
  92.9 1.1 collective-permute-start.22
  94.0 3.3 %collective-permute-done.21 = f16[64,2048]{1,0:T(8,128)(2,1)S(1)} collective-permute-done((f16[64,2048]{1,0:T(8,128)(2,1)S(1)}, f16[64,2048]{1,0:T(8,128)(2,1)S(1)}, u32[]{:S(2)}, u32[]{:S(2)}) %collective-permute-start.21) | collective-permute-done | bytes 262176 | tf_op jit(solution)/shard_map/ppermute | solution.py:234
  97.3 0.1 add_convert_fusion.4
  97.4 1.8 %collective-permute-done.22 = f16[64,2048]{1,0:T(8,128)(2,1)S(1)} collective-permute-done((f16[64,2048]{1,0:T(8,128)(2,1)S(1)}, f16[64,2048]{1,0:T(8,128)(2,1)S(1)}, u32[]{:S(2)}, u32[]{:S(2)}) %collective-permute-start.22) | collective-permute-done | bytes 262176 | tf_op jit(solution)/shard_map/ppermute | solution.py:234
  99.3 1.7 %collective-permute-start.23 = (f16[64,2048]{1,0:T(8,128)(2,1)S(1)}, f16[64,2048]{1,0:T(8,128)(2,1)S(1)}, u32[]{:S(2)}, u32[]{:S(2)}) collective-permute-start(f16[64,2048]{1,0:T(8,128)(2,1)S(1)} %add_convert_fusion.4), channel_id=1, source_target_pairs={{96,0},{33,1},{98,2},{35,3},{100,4},{37,5},{102,6},{39,7},{104,8},... | collective-permute-start | bytes 786440 | tf_op jit(solution)/shard_map/ppermute | solution.py:234
  101.0 5.8 %collective-permute-start.24 = (f16[64,2048]{1,0:T(8,128)(2,1)S(1)}, f16[64,2048]{1,0:T(8,128)(2,1)S(1)}, u32[]{:S(2)}, u32[]{:S(2)}) collective-permute-start(f16[64,2048]{1,0:T(8,128)(2,1)S(1)} %add_convert_fusion.3), channel_id=1, source_target_pairs={{6,0},{9,1},{4,2},{11,3},{2,4},{13,5},{0,6},{15,7},{14,8},{1,9},{1... | collective-permute-start | bytes 786440 | tf_op jit(solution)/shard_map/ppermute | solution.py:234
  106.8 0.2 collective-permute-done.23
  107.1 4.1 %collective-permute-done.24 = f16[64,2048]{1,0:T(8,128)(2,1)S(1)} collective-permute-done((f16[64,2048]{1,0:T(8,128)(2,1)S(1)}, f16[64,2048]{1,0:T(8,128)(2,1)S(1)}, u32[]{:S(2)}, u32[]{:S(2)}) %collective-permute-start.24) | collective-permute-done | bytes 262176 | tf_op jit(solution)/shard_map/ppermute | solution.py:234
  111.1 0.8 add_convert_fusion.1
  111.9 3.5 %collective-permute-start.25 = (f16[64,2048]{1,0:T(8,128)(2,1)S(1)}, f16[64,2048]{1,0:T(8,128)(2,1)S(1)}, u32[]{:S(2)}, u32[]{:S(2)}) collective-permute-start(f16[64,2048]{1,0:T(8,128)(2,1)S(1)} %add_convert_fusion.2), channel_id=1, source_target_pairs={{16,0},{97,1},{18,2},{99,3},{20,4},{101,5},{22,6},{103,7},{24,8},{... | collective-permute-start | bytes 786440 | tf_op jit(solution)/shard_map/ppermute | solution.py:234
  115.4 1.4 %collective-permute-start.28 = (f16[64,2048]{1,0:T(8,128)(2,1)}, f16[64,2048]{1,0:T(8,128)(2,1)S(1)}, u32[]{:S(2)}, u32[]{:S(2)}) collective-permute-start(f16[64,2048]{1,0:T(8,128)(2,1)} %add_convert_fusion.1), channel_id=1, source_target_pairs={{4,0},{5,1},{30,2},{31,3},{34,4},{39,5},{60,6},{57,7},{72,8},{73,9... | collective-permute-start | bytes 786440 | tf_op jit(solution)/shard_map/ppermute | solution.py:234
  116.8 4.1 %collective-permute-done.25 = f16[64,2048]{1,0:T(8,128)(2,1)S(1)} collective-permute-done((f16[64,2048]{1,0:T(8,128)(2,1)S(1)}, f16[64,2048]{1,0:T(8,128)(2,1)S(1)}, u32[]{:S(2)}, u32[]{:S(2)}) %collective-permute-start.25) | collective-permute-done | bytes 262176 | tf_op jit(solution)/shard_map/ppermute | solution.py:234
  120.9 0.8 multiply_reduce_fusion
  121.8 1.2 collective-permute-done.26
  123.0 3.6 %collective-permute-done.27 = f32[6,64]{1,0:T(8,128)S(1)} collective-permute-done((f32[6,64]{1,0:T(8,128)S(1)}, f32[6,64]{1,0:T(8,128)S(1)}, u32[]{:S(2)}, u32[]{:S(2)}) %collective-permute-start.27) | collective-permute-done | bytes 1568 | tf_op jit(solution)/shard_map/ppermute | solution.py:234
  126.6 3.6 %collective-permute-done.29 = f32[6,64]{1,0:T(8,128)S(1)} collective-permute-done((f32[6,64]{1,0:T(8,128)S(1)}, f32[6,64]{1,0:T(8,128)S(1)}, u32[]{:S(2)}, u32[]{:S(2)}) %collective-permute-start.29) | collective-permute-done | bytes 1568 | tf_op jit(solution)/shard_map/ppermute | solution.py:234
  130.2 2.2 %collective-permute-start.30 = (f32[6,64]{1,0:T(8,128)S(1)}, f32[6,64]{1,0:T(8,128)S(1)}, u32[]{:S(2)}, u32[]{:S(2)}) collective-permute-start(f32[6,64]{1,0:T(8,128)S(1)} %add.168), channel_id=1, source_target_pairs={{6,0},{7,1},{4,2},{5,3},{2,4},{3,5},{0,6},{1,7},{14,8},{15,9},{12,... | collective-permute-start | bytes 4616 | tf_op jit(solution)/shard_map/ppermute | solution.py:234
  132.4 2.6 %collective-permute-done.30 = f32[6,64]{1,0:T(8,128)S(1)} collective-permute-done((f32[6,64]{1,0:T(8,128)S(1)}, f32[6,64]{1,0:T(8,128)S(1)}, u32[]{:S(2)}, u32[]{:S(2)}) %collective-permute-start.30) | collective-permute-done | bytes 1568 | tf_op jit(solution)/shard_map/ppermute | solution.py:234
  135.1 2.8 %multiply_subtract_fusion = (f32[64,2048]{1,0:T(8,128)}, f32[64,2048]{1,0:T(8,128)}, f32[64,2048]{1,0:T(8,128)}, f32[64,2048]{1,0:T(8,128)}) fusion(f16[64,2048]{1,0:T(8,128)(2,1)S(1)} %collective-permute-done.28, f32[64,2048]{1,0:T(8,128)S(1)} %get-tuple-element.85, f32[64,2048]{1,0:T(8,128)S(1)} %copy-done, f16[64,2048]{1,0:T(8,128)(2,1)S(1)} %collective-permute-done.15, ...), kind=kLoop, calls=%fused_computation.2 | loop fusion | flops 7077888 | bytes 5507328 | tf_op jit(solution)/shard_map/sub | solution.py:406
  (60 shorter events, 1.6 us)
Async XLA Ops:
  2.6 4.2 %collective-permute-start = (f32[4,64]{1,0:T(4,128)S(1)}, f32[4,64]{1,0:T(4,128)S(1)}, u32[]{:S(2)}, u32[]{:S(2)}) collective-permute-start(f32[4,64]{1,0:T(4,128)S(1)} %pad_maximum_fusion.5), channel_id=1, source_target_pairs={{1,0},{0,1},{3,2},{2,3},{5,4},{4,5},{7,6},{6,7},{9,8},{8,9},{11,10... | collective-permute-start | bytes 3080 | tf_op jit(solution)/shard_map/ppermute | solution.py:234
  2.7 18.6 %collective-permute-start.3 = (bf16[64,1024]{1,0:T(8,128)(2,1)S(1)}, bf16[64,1024]{1,0:T(8,128)(2,1)S(1)}, u32[]{:S(2)}, u32[]{:S(2)}) collective-permute-start(bf16[64,1024]{1,0:T(8,128)(2,1)S(1)} %slice_select_fusion.2), channel_id=1, source_target_pairs={{112,0},{65,1},{48,2},{113,3},{0,4},{33,5},{64,6},{17,7},{96,8},{9... | collective-permute-start | bytes 393224 | tf_op jit(solution)/shard_map/ppermute | solution.py:234
  6.8 5.4 %collective-permute-start.1 = (f32[4,64]{1,0:T(4,128)S(1)}, f32[4,64]{1,0:T(4,128)S(1)}, u32[]{:S(2)}, u32[]{:S(2)}) collective-permute-start(f32[4,64]{1,0:T(4,128)S(1)} %pad_maximum_fusion.6), channel_id=1, source_target_pairs={{8,0},{9,1},{10,2},{11,3},{12,4},{13,5},{14,6},{15,7},{0,8},{1,9},... | collective-permute-start | bytes 3080 | tf_op jit(solution)/shard_map/ppermute | solution.py:234
  12.2 9.1 %collective-permute-start.2 = (f32[4,64]{1,0:T(4,128)S(1)}, f32[4,64]{1,0:T(4,128)S(1)}, u32[]{:S(2)}, u32[]{:S(2)}) collective-permute-start(f32[4,64]{1,0:T(4,128)S(1)} %pad_maximum_fusion.7), channel_id=1, source_target_pairs={{2,0},{3,1},{0,2},{1,3},{6,4},{7,5},{4,6},{5,7},{10,8},{11,9},{8,1... | collective-permute-start | bytes 3080 | tf_op jit(solution)/shard_map/ppermute | solution.py:234
  21.4 4.9 %collective-permute-start.4 = (f32[4,64]{1,0:T(4,128)S(1)}, f32[4,64]{1,0:T(4,128)S(1)}, u32[]{:S(2)}, u32[]{:S(2)}) collective-permute-start(f32[4,64]{1,0:T(4,128)S(1)} %pad_maximum_fusion.8), channel_id=1, source_target_pairs={{6,0},{7,1},{4,2},{5,3},{2,4},{3,5},{0,6},{1,7},{14,8},{15,9},{12,... | collective-permute-start | bytes 3080 | tf_op jit(solution)/shard_map/ppermute | solution.py:234
  21.5 5.1 %collective-permute-start.5 = (bf16[64,1024]{1,0:T(8,128)(2,1)S(1)}, bf16[64,1024]{1,0:T(8,128)(2,1)S(1)}, u32[]{:S(2)}, u32[]{:S(2)}) collective-permute-start(bf16[64,1024]{1,0:T(8,128)(2,1)S(1)} %collective-permute-done.3), channel_id=1, source_target_pairs={{2,0},{3,1},{0,2},{1,3},{6,4},{7,5},{4,6},{5,7},{10,8},{11,9},{8,1... | collective-permute-start | bytes 393224 | tf_op jit(solution)/shard_map/ppermute | solution.py:234
  26.7 1.6 %collective-permute-start.6 = (bf16[64,2048]{1,0:T(8,128)(2,1)S(1)}, bf16[64,2048]{1,0:T(8,128)(2,1)S(1)}, u32[]{:S(2)}, u32[]{:S(2)}) collective-permute-start(bf16[64,2048]{1,0:T(8,128)(2,1)S(1)} %pad_maximum_fusion.2), channel_id=1, source_target_pairs={{1,0},{0,1},{3,2},{2,3},{5,4},{4,5},{7,6},{6,7},{9,8},{8,9},{11,10... | collective-permute-start | bytes 786440 | tf_op jit(solution)/shard_map/ppermute | solution.py:234
  26.9 1.8 %collective-permute-start.7 = (f16[64,2048]{1,0:T(8,128)(2,1)S(1)}, f16[64,2048]{1,0:T(8,128)(2,1)S(1)}, u32[]{:S(2)}, u32[]{:S(2)}) collective-permute-start(f16[64,2048]{1,0:T(8,128)(2,1)S(1)} %multiply_convert_fusion.2), channel_id=1, source_target_pairs={{1,0},{0,1},{3,2},{2,3},{5,4},{4,5},{7,6},{6,7},{9,8},{8,9},{11,10... | collective-permute-start | bytes 786440 | tf_op jit(solution)/shard_map/ppermute | solution.py:234
  28.8 11.2 %collective-permute-start.8 = (f16[64,2048]{1,0:T(8,128)(2,1)S(1)}, f16[64,2048]{1,0:T(8,128)(2,1)S(1)}, u32[]{:S(2)}, u32[]{:S(2)}) collective-permute-start(f16[64,2048]{1,0:T(8,128)(2,1)S(1)} %add_convert_fusion.10), channel_id=1, source_target_pairs={{8,0},{3,1},{10,2},{1,3},{12,4},{7,5},{14,6},{5,7},{0,8},{11,9},{2... | collective-permute-start | bytes 786440 | tf_op jit(solution)/shard_map/ppermute | solution.py:234
  29.2 32.3 %copy-start.1 = (f32[64,2048]{1,0:T(8,128)S(1)}, f32[64,2048]{1,0:T(8,128)}, u32[]{:S(2)}) copy-start(f32[64,2048]{1,0:T(8,128)} %param.6) | copy-start | bytes 1572868
  29.2 35.5 %copy-start = (f32[64,2048]{1,0:T(8,128)S(1)}, f32[64,2048]{1,0:T(8,128)}, u32[]{:S(2)}) copy-start(f32[64,2048]{1,0:T(8,128)} %param.7) | copy-start | bytes 1572868
  29.2 35.5 %copy-start.2 = (f32[64,2048]{1,0:T(8,128)S(1)}, f32[64,2048]{1,0:T(8,128)}, u32[]{:S(2)}) copy-start(f32[64,2048]{1,0:T(8,128)} %param.5) | copy-start | bytes 1572868
  33.1 8.2 %collective-permute-start.9 = (f16[64,1024]{1,0:T(8,128)(2,1)S(1)}, f16[64,1024]{1,0:T(8,128)(2,1)S(1)}, u32[]{:S(2)}, u32[]{:S(2)}) collective-permute-start(f16[64,1024]{1,0:T(8,128)(2,1)S(1)} %multiply_convert_fusion.4), channel_id=1, source_target_pairs={{32,0},{17,1},{34,2},{19,3},{36,4},{21,5},{38,6},{23,7},{40,8},{25... | collective-permute-start | bytes 393224 | tf_op jit(solution)/shard_map/ppermute | solution.py:234
  40.1 6.5 %collective-permute-start.10 = (f16[64,2048]{1,0:T(8,128)(2,1)S(1)}, f16[64,2048]{1,0:T(8,128)(2,1)S(1)}, u32[]{:S(2)}, u32[]{:S(2)}) collective-permute-start(f16[64,2048]{1,0:T(8,128)(2,1)S(1)} %add_convert_fusion.9), channel_id=1, source_target_pairs={{2,0},{7,1},{0,2},{5,3},{6,4},{3,5},{4,6},{1,7},{10,8},{15,9},{8,1... | collective-permute-start | bytes 786440 | tf_op jit(solution)/shard_map/ppermute | solution.py:234
  46.7 6.3 %collective-permute-start.11 = (f16[64,1024]{1,0:T(8,128)(2,1)S(1)}, f16[64,1024]{1,0:T(8,128)(2,1)S(1)}, u32[]{:S(2)}, u32[]{:S(2)}) collective-permute-start(f16[64,1024]{1,0:T(8,128)(2,1)S(1)} %add_convert_fusion.13), channel_id=1, source_target_pairs={{96,0},{33,1},{98,2},{35,3},{100,4},{37,5},{102,6},{39,7},{104,8},... | collective-permute-start | bytes 393224 | tf_op jit(solution)/shard_map/ppermute | solution.py:234
  47.0 7.6 %collective-permute-start.12 = (f16[64,2048]{1,0:T(8,128)(2,1)S(1)}, f16[64,2048]{1,0:T(8,128)(2,1)S(1)}, u32[]{:S(2)}, u32[]{:S(2)}) collective-permute-start(f16[64,2048]{1,0:T(8,128)(2,1)S(1)} %add_convert_fusion.8), channel_id=1, source_target_pairs={{6,0},{9,1},{4,2},{11,3},{2,4},{13,5},{0,6},{15,7},{14,8},{1,9},{1... | collective-permute-start | bytes 786440 | tf_op jit(solution)/shard_map/ppermute | solution.py:234
  54.6 6.8 %collective-permute-start.13 = (f16[64,1024]{1,0:T(8,128)(2,1)S(1)}, f16[64,1024]{1,0:T(8,128)(2,1)S(1)}, u32[]{:S(2)}, u32[]{:S(2)}) collective-permute-start(f16[64,1024]{1,0:T(8,128)(2,1)S(1)} %add_convert_fusion.12), channel_id=1, source_target_pairs={{16,0},{97,1},{18,2},{99,3},{20,4},{101,5},{22,6},{103,7},{24,8},{... | collective-permute-start | bytes 393224 | tf_op jit(solution)/shard_map/ppermute | solution.py:234
  56.8 7.9 %collective-permute-start.15 = (f16[64,2048]{1,0:T(8,128)(2,1)S(1)}, f16[64,2048]{1,0:T(8,128)(2,1)S(1)}, u32[]{:S(2)}, u32[]{:S(2)}) collective-permute-start(f16[64,2048]{1,0:T(8,128)(2,1)S(1)} %add_convert_fusion.7), channel_id=1, source_target_pairs={{4,0},{5,1},{30,2},{31,3},{34,4},{39,5},{60,6},{57,7},{72,8},{73,9... | collective-permute-start | bytes 786440 | tf_op jit(solution)/shard_map/ppermute | solution.py:234
  61.6 11.5 %collective-permute-start.14 = (bf16[64,1024]{1,0:T(8,128)(2,1)S(1)}, bf16[64,1024]{1,0:T(8,128)(2,1)S(1)}, u32[]{:S(2)}, u32[]{:S(2)}) collective-permute-start(bf16[64,1024]{1,0:T(8,128)(2,1)S(1)} %get-tuple-element.86), channel_id=1, source_target_pairs={{112,0},{65,1},{48,2},{113,3},{0,4},{33,5},{64,6},{17,7},{96,8},{9... | collective-permute-start | bytes 393224 | tf_op jit(solution)/shard_map/ppermute | solution.py:234
  73.1 5.7 %collective-permute-start.16 = (bf16[64,1024]{1,0:T(8,128)(2,1)S(1)}, bf16[64,1024]{1,0:T(8,128)(2,1)S(1)}, u32[]{:S(2)}, u32[]{:S(2)}) collective-permute-start(bf16[64,1024]{1,0:T(8,128)(2,1)S(1)} %collective-permute-done.14), channel_id=1, source_target_pairs={{2,0},{3,1},{0,2},{1,3},{6,4},{7,5},{4,6},{5,7},{10,8},{11,9},{8,1... | collective-permute-start | bytes 393224 | tf_op jit(solution)/shard_map/ppermute | solution.py:234
  76.0 2.9 %collective-permute-start.17 = (f16[64,2048]{1,0:T(8,128)(2,1)S(1)}, f16[64,2048]{1,0:T(8,128)(2,1)S(1)}, u32[]{:S(2)}, u32[]{:S(2)}) collective-permute-start(f16[64,2048]{1,0:T(8,128)(2,1)S(1)} %multiply_convert_fusion.1), channel_id=1, source_target_pairs={{1,0},{0,1},{3,2},{2,3},{5,4},{4,5},{7,6},{6,7},{9,8},{8,9},{11,10... | collective-permute-start | bytes 786440 | tf_op jit(solution)/shard_map/ppermute | solution.py:234
  79.0 5.0 %collective-permute-start.20 = (f16[64,1024]{1,0:T(8,128)(2,1)S(1)}, f16[64,1024]{1,0:T(8,128)(2,1)S(1)}, u32[]{:S(2)}, u32[]{:S(2)}) collective-permute-start(f16[64,1024]{1,0:T(8,128)(2,1)S(1)} %get-tuple-element.58), channel_id=1, source_target_pairs={{32,0},{17,1},{34,2},{19,3},{36,4},{21,5},{38,6},{23,7},{40,8},{25... | collective-permute-start | bytes 393224 | tf_op jit(solution)/shard_map/ppermute | solution.py:234
  81.1 3.1 %collective-permute-start.18 = (bf16[64,2048]{1,0:T(8,128)(2,1)S(1)}, bf16[64,2048]{1,0:T(8,128)(2,1)S(1)}, u32[]{:S(2)}, u32[]{:S(2)}) collective-permute-start(bf16[64,2048]{1,0:T(8,128)(2,1)S(1)} %pad_maximum_fusion.3), channel_id=1, source_target_pairs={{1,0},{0,1},{3,2},{2,3},{5,4},{4,5},{7,6},{6,7},{9,8},{8,9},{11,10... | collective-permute-start | bytes 786440 | tf_op jit(solution)/shard_map/ppermute | solution.py:234
  81.1 9.5 %collective-permute-start.19 = (f16[64,2048]{1,0:T(8,128)(2,1)S(1)}, f16[64,2048]{1,0:T(8,128)(2,1)S(1)}, u32[]{:S(2)}, u32[]{:S(2)}) collective-permute-start(f16[64,2048]{1,0:T(8,128)(2,1)S(1)} %add_convert_fusion.6), channel_id=1, source_target_pairs={{8,0},{3,1},{10,2},{1,3},{12,4},{7,5},{14,6},{5,7},{0,8},{11,9},{2... | collective-permute-start | bytes 786440 | tf_op jit(solution)/shard_map/ppermute | solution.py:234
  90.8 6.5 %collective-permute-start.21 = (f16[64,2048]{1,0:T(8,128)(2,1)S(1)}, f16[64,2048]{1,0:T(8,128)(2,1)S(1)}, u32[]{:S(2)}, u32[]{:S(2)}) collective-permute-start(f16[64,2048]{1,0:T(8,128)(2,1)S(1)} %multiply_convert_fusion), channel_id=1, source_target_pairs={{32,0},{17,1},{34,2},{19,3},{36,4},{21,5},{38,6},{23,7},{40,8},{25... | collective-permute-start | bytes 786440 | tf_op jit(solution)/shard_map/ppermute | solution.py:234
  92.9 6.4 %collective-permute-start.22 = (f16[64,2048]{1,0:T(8,128)(2,1)S(1)}, f16[64,2048]{1,0:T(8,128)(2,1)S(1)}, u32[]{:S(2)}, u32[]{:S(2)}) collective-permute-start(f16[64,2048]{1,0:T(8,128)(2,1)S(1)} %add_convert_fusion.5), channel_id=1, source_target_pairs={{2,0},{7,1},{0,2},{5,3},{6,4},{3,5},{4,6},{1,7},{10,8},{15,9},{8,1... | collective-permute-start | bytes 786440 | tf_op jit(solution)/shard_map/ppermute | solution.py:234
  99.3 7.7 %collective-permute-start.23 = (f16[64,2048]{1,0:T(8,128)(2,1)S(1)}, f16[64,2048]{1,0:T(8,128)(2,1)S(1)}, u32[]{:S(2)}, u32[]{:S(2)}) collective-permute-start(f16[64,2048]{1,0:T(8,128)(2,1)S(1)} %add_convert_fusion.4), channel_id=1, source_target_pairs={{96,0},{33,1},{98,2},{35,3},{100,4},{37,5},{102,6},{39,7},{104,8},... | collective-permute-start | bytes 786440 | tf_op jit(solution)/shard_map/ppermute | solution.py:234
  101.0 10.1 %collective-permute-start.24 = (f16[64,2048]{1,0:T(8,128)(2,1)S(1)}, f16[64,2048]{1,0:T(8,128)(2,1)S(1)}, u32[]{:S(2)}, u32[]{:S(2)}) collective-permute-start(f16[64,2048]{1,0:T(8,128)(2,1)S(1)} %add_convert_fusion.3), channel_id=1, source_target_pairs={{6,0},{9,1},{4,2},{11,3},{2,4},{13,5},{0,6},{15,7},{14,8},{1,9},{1... | collective-permute-start | bytes 786440 | tf_op jit(solution)/shard_map/ppermute | solution.py:234
  111.9 9.0 %collective-permute-start.25 = (f16[64,2048]{1,0:T(8,128)(2,1)S(1)}, f16[64,2048]{1,0:T(8,128)(2,1)S(1)}, u32[]{:S(2)}, u32[]{:S(2)}) collective-permute-start(f16[64,2048]{1,0:T(8,128)(2,1)S(1)} %add_convert_fusion.2), channel_id=1, source_target_pairs={{16,0},{97,1},{18,2},{99,3},{20,4},{101,5},{22,6},{103,7},{24,8},{... | collective-permute-start | bytes 786440 | tf_op jit(solution)/shard_map/ppermute | solution.py:234
  115.4 11.2 %collective-permute-start.28 = (f16[64,2048]{1,0:T(8,128)(2,1)}, f16[64,2048]{1,0:T(8,128)(2,1)S(1)}, u32[]{:S(2)}, u32[]{:S(2)}) collective-permute-start(f16[64,2048]{1,0:T(8,128)(2,1)} %add_convert_fusion.1), channel_id=1, source_target_pairs={{4,0},{5,1},{30,2},{31,3},{34,4},{39,5},{60,6},{57,7},{72,8},{73,9... | collective-permute-start | bytes 786440 | tf_op jit(solution)/shard_map/ppermute | solution.py:234
  121.7 1.2 collective-permute-start.26
  123.0 3.6 %collective-permute-start.27 = (f32[6,64]{1,0:T(8,128)S(1)}, f32[6,64]{1,0:T(8,128)S(1)}, u32[]{:S(2)}, u32[]{:S(2)}) collective-permute-start(f32[6,64]{1,0:T(8,128)S(1)} %add.166), channel_id=1, source_target_pairs={{8,0},{9,1},{10,2},{11,3},{12,4},{13,5},{14,6},{15,7},{0,8},{1,9},... | collective-permute-start | bytes 4616 | tf_op jit(solution)/shard_map/ppermute | solution.py:234
  126.6 3.6 %collective-permute-start.29 = (f32[6,64]{1,0:T(8,128)S(1)}, f32[6,64]{1,0:T(8,128)S(1)}, u32[]{:S(2)}, u32[]{:S(2)}) collective-permute-start(f32[6,64]{1,0:T(8,128)S(1)} %add.167), channel_id=1, source_target_pairs={{2,0},{3,1},{0,2},{1,3},{6,4},{7,5},{4,6},{5,7},{10,8},{11,9},{8,1... | collective-permute-start | bytes 4616 | tf_op jit(solution)/shard_map/ppermute | solution.py:234
  130.2 4.8 %collective-permute-start.30 = (f32[6,64]{1,0:T(8,128)S(1)}, f32[6,64]{1,0:T(8,128)S(1)}, u32[]{:S(2)}, u32[]{:S(2)}) collective-permute-start(f32[6,64]{1,0:T(8,128)S(1)} %add.168), channel_id=1, source_target_pairs={{6,0},{7,1},{4,2},{5,3},{2,4},{3,5},{0,6},{1,7},{14,8},{15,9},{12,... | collective-permute-start | bytes 4616 | tf_op jit(solution)/shard_map/ppermute | solution.py:234

commit v12 on v9

--- a/solution.py
+++ b/solution.py
@@ -374,7 +374,7 @@
         ]
     )
     for pairs in SMALL_COL:
-        if pairs is SMALL_COL[2]:
+        if pairs is SMALL_COL[3]:
             dots, columns = tie(dots, columns)
         dots = dots + move(dots, pairs)
     curve, us_g, us_u, us_p1, q1_u, us_p2 = (dots[i] for i in range(6))

time: 137 us -> 137 us (level)
  no operation moved by 1% of the time
where the time goes in v12:
time: 137 us; the launch traced here: 136 us
  waiting for transfers between devices  49.9 us (36%)
  starting transfers between devices  45.4 us (33%)
  Pallas kernels  30.8 us (22%)
  other arithmetic  8.82 us (6%)
    ppermute x31, waiting for transfers between devices, move(): return lax.ppermute(value, AXES, pairs)  49.9 us
    ppermute x31, starting transfers between devices, move(): return lax.ppermute(value, AXES, pairs)  45.4 us
    pallas_call x2, Pallas kernels, call(): pl.pallas_call(kernel, name=name, in_specs=[spec, pl.BlockSpec(memory_spa...  14 us
    pallas_call x2, Pallas kernels, shadow_rows(): pl.pallas_call(kernel, name='shadow_rows', in_specs=[spec, pl.BlockSpec(m...  9.31 us
    pallas_call x2, Pallas kernels, primary_half(): pl.pallas_call(half_kernel, name='primary_half', in_specs=[pl.BlockSpec(m...  7.56 us
    sub x1, other arithmetic, on_device(): shadow_residual = gs - step * q1 - step_next * (lead * q1 + kappa * q2)  2.83 us
  transfers between devices with their start and end apart: 31, of which 22 were waited for; matrix products, arithmetic and copies ran while one was open for 2% of the time, Pallas kernels for 23%

profile of v12, /device:TPU:0, one launch (start us, length us, event | category | flops | bytes accessed | tf_op | source)
XLA Modules:
  0.0 136.0 jit_solution(3532848483342380949)
XLA Ops:
  0.6 1.9 %multiply_reduce_fusion.7 = (f32[64]{0:T(128)S(1)}, f32[64]{0:T(128)S(1)}, f32[64]{0:T(128)S(1)}, f32[64]{0:T(128)S(1)}, bf16[64,2048]{1,0:T(8,128)(2,1)S(1)}, /...) fusion(f32[64,2048]{1,0:T(8,128)} %param.7, f32[64,2048]{1,0:T(8,128)} %param.6, ...), kind=kLoop, calls=%fused_computation.35 | loop fusion | flops 2096896 | bytes 3146752 | tf_op jit(solution)/shard_map/reduce_sum | solution.py:258
  2.7 4.0 %collective-permute-start.3 = (bf16[64,1024]{1,0:T(8,128)(2,1)S(1)}, bf16[64,1024]{1,0:T(8,128)(2,1)S(1)}, u32[]{:S(2)}, u32[]{:S(2)}) collective-permute-start(bf16[64,1024]{1,0:T(8,128)(2,1)S(1)} %slice_select_fusion.2), channel_id=1, source_target_pairs={{112,0},{65,1},{48,2},{113,3},{0,4},{33,5},{64,6},{17,7},{96,8},{9... | collective-permute-start | bytes 393224 | tf_op jit(solution)/shard_map/ppermute | solution.py:234
  6.8 0.7 collective-permute-start.1
  7.5 4.7 %shadow_rows.2 = f32[64,2048]{1,0:T(8,128)S(1)} custom-call(bf16[64,2048]{1,0:T(8,128)(2,1)S(1)} %get-tuple-element.36.left_ref, bf16[4096,2048]{1,0:T(8,128)(2,1)} %coupling_ref.11), custom_call_target="tpu_custom_call" | custom-call | flops 536870912 | bytes 8388608 | tf_op jit(solution)/shard_map/shadow_rows/pallas_call | solution.py:176
  12.2 4.5 %collective-permute-start.2 = (f32[4,64]{1,0:T(4,128)S(1)}, f32[4,64]{1,0:T(4,128)S(1)}, u32[]{:S(2)}, u32[]{:S(2)}) collective-permute-start(f32[4,64]{1,0:T(4,128)S(1)} %pad_maximum_fusion.7), channel_id=1, source_target_pairs={{2,0},{3,1},{0,2},{1,3},{6,4},{7,5},{4,6},{5,7},{10,8},{11,9},{8,1... | collective-permute-start | bytes 3080 | tf_op jit(solution)/shard_map/ppermute | solution.py:234
  16.7 4.7 %shadow_rows.3 = f32[64,2048]{1,0:T(8,128)S(1)} custom-call(bf16[64,2048]{1,0:T(8,128)(2,1)S(1)} %get-tuple-element.36.left_ref, bf16[4096,2048]{1,0:T(8,128)(2,1)} %coupling_ref.11), custom_call_target="tpu_custom_call" | custom-call | flops 536870912 | bytes 8388608 | tf_op jit(solution)/shard_map/shadow_rows/pallas_call | solution.py:176
  21.5 0.5 collective-permute-start.5
  22.0 4.2 %collective-permute-done.4 = f32[4,64]{1,0:T(4,128)S(1)} collective-permute-done((f32[4,64]{1,0:T(4,128)S(1)}, f32[4,64]{1,0:T(4,128)S(1)}, u32[]{:S(2)}, u32[]{:S(2)}) %collective-permute-start.4) | collective-permute-done | bytes 1056 | tf_op jit(solution)/shard_map/ppermute | solution.py:234
  26.3 0.3 collective-permute-done.5
  26.8 0.1 multiply_convert_fusion.2
  26.9 0.6 collective-permute-start.7
  27.4 0.8 collective-permute-done.6
  28.4 0.3 collective-permute-done.7
  28.6 0.2 add_convert_fusion.10
  28.8 0.4 collective-permute-start.8
  29.2 3.8 %primary_half.3 = f32[64,1024]{1,0:T(8,128)S(1)} custom-call(s32[1]{0:T(128)} %bitcast.9.offset_ref, bf16[64,4096]{1,0:T(8,128)(2,1)S(1)} %pad_maximum_fusion.left_ref, bf16[4096,2048]{1,0:T(8,128)(2,1)} %coupling_ref.11), custom_call_target="tpu_custom_call" | custom-call | flops 536870912 | bytes 8388608 | tf_op jit(solution)/shard_map/primary_half/pallas_call | solution.py:210
  33.1 3.1 %collective-permute-start.9 = (f16[64,1024]{1,0:T(8,128)(2,1)S(1)}, f16[64,1024]{1,0:T(8,128)(2,1)S(1)}, u32[]{:S(2)}, u32[]{:S(2)}) collective-permute-start(f16[64,1024]{1,0:T(8,128)(2,1)S(1)} %multiply_convert_fusion.4), channel_id=1, source_target_pairs={{32,0},{17,1},{34,2},{19,3},{36,4},{21,5},{38,6},{23,7},{40,8},{25... | collective-permute-start | bytes 393224 | tf_op jit(solution)/shard_map/ppermute | solution.py:234
  36.3 3.7 %primary_half.2 = f32[64,1024]{1,0:T(8,128)S(1)} custom-call(s32[1]{0:T(128)} %bitcast.6.offset_ref, bf16[64,4096]{1,0:T(8,128)(2,1)S(1)} %pad_maximum_fusion.left_ref, bf16[4096,2048]{1,0:T(8,128)(2,1)} %coupling_ref.11), custom_call_target="tpu_custom_call" | custom-call | flops 536870912 | bytes 8388608 | tf_op jit(solution)/shard_map/primary_half/pallas_call | solution.py:210
  40.1 1.3 collective-permute-start.10
  41.5 5.1 %collective-permute-done.10 = f16[64,2048]{1,0:T(8,128)(2,1)S(1)} collective-permute-done((f16[64,2048]{1,0:T(8,128)(2,1)S(1)}, f16[64,2048]{1,0:T(8,128)(2,1)S(1)}, u32[]{:S(2)}, u32[]{:S(2)}) %collective-permute-start.10) | collective-permute-done | bytes 262176 | tf_op jit(solution)/shard_map/ppermute | solution.py:234
  46.7 0.3 collective-permute-start.11
  47.0 2.3 %collective-permute-start.12 = (f16[64,2048]{1,0:T(8,128)(2,1)S(1)}, f16[64,2048]{1,0:T(8,128)(2,1)S(1)}, u32[]{:S(2)}, u32[]{:S(2)}) collective-permute-start(f16[64,2048]{1,0:T(8,128)(2,1)S(1)} %add_convert_fusion.8), channel_id=1, source_target_pairs={{6,0},{9,1},{4,2},{11,3},{2,4},{13,5},{0,6},{15,7},{14,8},{1,9},{1... | collective-permute-start | bytes 786440 | tf_op jit(solution)/shard_map/ppermute | solution.py:234
  49.3 3.6 %collective-permute-done.11 = f16[64,1024]{1,0:T(8,128)(2,1)S(1)} collective-permute-done((f16[64,1024]{1,0:T(8,128)(2,1)S(1)}, f16[64,1024]{1,0:T(8,128)(2,1)S(1)}, u32[]{:S(2)}, u32[]{:S(2)}) %collective-permute-start.11) | collective-permute-done | bytes 131104 | tf_op jit(solution)/shard_map/ppermute | solution.py:234
  53.0 1.6 %collective-permute-done.12 = f16[64,2048]{1,0:T(8,128)(2,1)S(1)} collective-permute-done((f16[64,2048]{1,0:T(8,128)(2,1)S(1)}, f16[64,2048]{1,0:T(8,128)(2,1)S(1)}, u32[]{:S(2)}, u32[]{:S(2)}) %collective-permute-start.12) | collective-permute-done | bytes 262176 | tf_op jit(solution)/shard_map/ppermute | solution.py:234
  54.6 2.2 %collective-permute-start.13 = (f16[64,1024]{1,0:T(8,128)(2,1)S(1)}, f16[64,1024]{1,0:T(8,128)(2,1)S(1)}, u32[]{:S(2)}, u32[]{:S(2)}) collective-permute-start(f16[64,1024]{1,0:T(8,128)(2,1)S(1)} %add_convert_fusion.12), channel_id=1, source_target_pairs={{16,0},{97,1},{18,2},{99,3},{20,4},{101,5},{22,6},{103,7},{24,8},{... | collective-permute-start | bytes 393224 | tf_op jit(solution)/shard_map/ppermute | solution.py:234
  56.8 2.5 %collective-permute-start.15 = (f16[64,2048]{1,0:T(8,128)(2,1)S(1)}, f16[64,2048]{1,0:T(8,128)(2,1)S(1)}, u32[]{:S(2)}, u32[]{:S(2)}) collective-permute-start(f16[64,2048]{1,0:T(8,128)(2,1)S(1)} %add_convert_fusion.7), channel_id=1, source_target_pairs={{4,0},{5,1},{30,2},{31,3},{34,4},{39,5},{60,6},{57,7},{72,8},{73,9... | collective-permute-start | bytes 786440 | tf_op jit(solution)/shard_map/ppermute | solution.py:234
  59.3 2.2 %collective-permute-done.13 = f16[64,1024]{1,0:T(8,128)(2,1)S(1)} collective-permute-done((f16[64,1024]{1,0:T(8,128)(2,1)S(1)}, f16[64,1024]{1,0:T(8,128)(2,1)S(1)}, u32[]{:S(2)}, u32[]{:S(2)}) %collective-permute-start.13) | collective-permute-done | bytes 131104 | tf_op jit(solution)/shard_map/ppermute | solution.py:234
  61.5 0.2 fusion.6
  61.6 0.8 collective-permute-start.14
  62.5 2.2 %collective-permute-done.15 = f16[64,2048]{1,0:T(8,128)(2,1)S(1)} collective-permute-done((f16[64,2048]{1,0:T(8,128)(2,1)S(1)}, f16[64,2048]{1,0:T(8,128)(2,1)S(1)}, u32[]{:S(2)}, u32[]{:S(2)}) %collective-permute-start.15) | collective-permute-done | bytes 262176 | tf_op jit(solution)/shard_map/ppermute | solution.py:234
  64.7 0.2 fusion.15
  64.9 7.7 %shadow.1 = f32[64,4096]{1,0:T(8,128)S(1)} custom-call(bf16[64,2048]{1,0:T(8,128)(2,1)S(1)} %get-tuple-element.82.left_ref, bf16[4096,2048]{1,0:T(8,128)(2,1)} %coupling_ref.11), custom_call_target="tpu_custom_call" | custom-call | flops 1073741824 | bytes 16777216 | tf_op jit(solution)/shard_map/shadow/pallas_call | solution.py:140
  72.7 0.5 collective-permute-done.14
  73.1 2.7 %collective-permute-start.16 = (bf16[64,1024]{1,0:T(8,128)(2,1)S(1)}, bf16[64,1024]{1,0:T(8,128)(2,1)S(1)}, u32[]{:S(2)}, u32[]{:S(2)}) collective-permute-start(bf16[64,1024]{1,0:T(8,128)(2,1)S(1)} %collective-permute-done.14), channel_id=1, source_target_pairs={{2,0},{3,1},{0,2},{1,3},{6,4},{7,5},{4,6},{5,7},{10,8},{11,9},{8,1... | collective-permute-start | bytes 393224 | tf_op jit(solution)/shard_map/ppermute | solution.py:234
  75.9 1.1 collective-permute-start.18
  76.9 0.1 multiply_convert_fusion.1
  77.1 1.7 %collective-permute-done.16 = bf16[64,1024]{1,0:T(8,128)(2,1)S(1)} collective-permute-done((bf16[64,1024]{1,0:T(8,128)(2,1)S(1)}, bf16[64,1024]{1,0:T(8,128)(2,1)S(1)}, u32[]{:S(2)}, u32[]{:S(2)}) %collective-permute-start.16) | collective-permute-done | bytes 131104 | tf_op jit(solution)/shard_map/ppermute | solution.py:234
  78.8 2.0 %collective-permute-done.18 = f16[64,1024]{1,0:T(8,128)(2,1)S(1)} collective-permute-done((f16[64,1024]{1,0:T(8,128)(2,1)S(1)}, f16[64,1024]{1,0:T(8,128)(2,1)S(1)}, u32[]{:S(2)}, u32[]{:S(2)}) %collective-permute-start.18) | collective-permute-done | bytes 131104 | tf_op jit(solution)/shard_map/ppermute | solution.py:234
  81.0 0.2 add_convert_fusion.6
  81.4 1.4 %collective-permute-done.19 = bf16[64,2048]{1,0:T(8,128)(2,1)S(1)} collective-permute-done((bf16[64,2048]{1,0:T(8,128)(2,1)S(1)}, bf16[64,2048]{1,0:T(8,128)(2,1)S(1)}, u32[]{:S(2)}, u32[]{:S(2)}) %collective-permute-start.19) | collective-permute-done | bytes 262176 | tf_op jit(solution)/shard_map/ppermute | solution.py:234
  82.9 6.2 %primary.1 = f32[64,2048]{1,0:T(8,128)S(1)} custom-call(bf16[64,4096]{1,0:T(8,128)(2,1)S(1)} %pad_maximum_fusion.1.left_ref, bf16[4096,2048]{1,0:T(8,128)(2,1)} %coupling_ref.11), custom_call_target="tpu_custom_call" | custom-call | flops 1073741824 | bytes 16777216 | tf_op jit(solution)/shard_map/primary/pallas_call | solution.py:140
  89.4 1.1 collective-permute-start.21
  90.5 0.9 collective-permute-start.22
  91.4 4.4 %collective-permute-done.21 = f16[64,2048]{1,0:T(8,128)(2,1)S(1)} collective-permute-done((f16[64,2048]{1,0:T(8,128)(2,1)S(1)}, f16[64,2048]{1,0:T(8,128)(2,1)S(1)}, u32[]{:S(2)}, u32[]{:S(2)}) %collective-permute-start.21) | collective-permute-done | bytes 262176 | tf_op jit(solution)/shard_map/ppermute | solution.py:234
  95.8 0.1 add_convert_fusion.4
  95.9 0.9 collective-permute-done.22
  97.0 1.4 %collective-permute-start.23 = (f16[64,2048]{1,0:T(8,128)(2,1)S(1)}, f16[64,2048]{1,0:T(8,128)(2,1)S(1)}, u32[]{:S(2)}, u32[]{:S(2)}) collective-permute-start(f16[64,2048]{1,0:T(8,128)(2,1)S(1)} %add_convert_fusion.4), channel_id=1, source_target_pairs={{96,0},{33,1},{98,2},{35,3},{100,4},{37,5},{102,6},{39,7},{104,8},... | collective-permute-start | bytes 786440 | tf_op jit(solution)/shard_map/ppermute | solution.py:234
  98.3 5.1 %collective-permute-start.24 = (f16[64,2048]{1,0:T(8,128)(2,1)S(1)}, f16[64,2048]{1,0:T(8,128)(2,1)S(1)}, u32[]{:S(2)}, u32[]{:S(2)}) collective-permute-start(f16[64,2048]{1,0:T(8,128)(2,1)S(1)} %add_convert_fusion.3), channel_id=1, source_target_pairs={{6,0},{9,1},{4,2},{11,3},{2,4},{13,5},{0,6},{15,7},{14,8},{1,9},{1... | collective-permute-start | bytes 786440 | tf_op jit(solution)/shard_map/ppermute | solution.py:234
  103.4 1.2 collective-permute-done.23
  104.7 3.0 %collective-permute-done.24 = f16[64,2048]{1,0:T(8,128)(2,1)S(1)} collective-permute-done((f16[64,2048]{1,0:T(8,128)(2,1)S(1)}, f16[64,2048]{1,0:T(8,128)(2,1)S(1)}, u32[]{:S(2)}, u32[]{:S(2)}) %collective-permute-start.24) | collective-permute-done | bytes 262176 | tf_op jit(solution)/shard_map/ppermute | solution.py:234
  107.8 0.8 add_convert_fusion.1
  108.5 3.5 %collective-permute-start.25 = (f16[64,2048]{1,0:T(8,128)(2,1)S(1)}, f16[64,2048]{1,0:T(8,128)(2,1)S(1)}, u32[]{:S(2)}, u32[]{:S(2)}) collective-permute-start(f16[64,2048]{1,0:T(8,128)(2,1)S(1)} %add_convert_fusion.2), channel_id=1, source_target_pairs={{16,0},{97,1},{18,2},{99,3},{20,4},{101,5},{22,6},{103,7},{24,8},{... | collective-permute-start | bytes 786440 | tf_op jit(solution)/shard_map/ppermute | solution.py:234
  112.0 1.4 %collective-permute-start.29 = (f16[64,2048]{1,0:T(8,128)(2,1)}, f16[64,2048]{1,0:T(8,128)(2,1)S(1)}, u32[]{:S(2)}, u32[]{:S(2)}) collective-permute-start(f16[64,2048]{1,0:T(8,128)(2,1)} %add_convert_fusion.1), channel_id=1, source_target_pairs={{4,0},{5,1},{30,2},{31,3},{34,4},{39,5},{60,6},{57,7},{72,8},{73,9... | collective-permute-start | bytes 786440 | tf_op jit(solution)/shard_map/ppermute | solution.py:234
  113.4 4.8 %collective-permute-done.25 = f16[64,2048]{1,0:T(8,128)(2,1)S(1)} collective-permute-done((f16[64,2048]{1,0:T(8,128)(2,1)S(1)}, f16[64,2048]{1,0:T(8,128)(2,1)S(1)}, u32[]{:S(2)}, u32[]{:S(2)}) %collective-permute-start.25) | collective-permute-done | bytes 262176 | tf_op jit(solution)/shard_map/ppermute | solution.py:234
  118.2 0.8 multiply_reduce_fusion
  119.0 0.2 collective-permute-start.26
  119.2 1.0 collective-permute-done.26
  120.2 2.9 %collective-permute-start.27 = (f32[6,64]{1,0:T(8,128)S(1)}, f32[6,64]{1,0:T(8,128)S(1)}, u32[]{:S(2)}, u32[]{:S(2)}) collective-permute-start(f32[6,64]{1,0:T(8,128)S(1)} %add.166), channel_id=1, source_target_pairs={{8,0},{9,1},{10,2},{11,3},{12,4},{13,5},{14,6},{15,7},{0,8},{1,9},... | collective-permute-start | bytes 4616 | tf_op jit(solution)/shard_map/ppermute | solution.py:234
  123.1 1.6 %collective-permute-done.27 = f32[6,64]{1,0:T(8,128)S(1)} collective-permute-done((f32[6,64]{1,0:T(8,128)S(1)}, f32[6,64]{1,0:T(8,128)S(1)}, u32[]{:S(2)}, u32[]{:S(2)}) %collective-permute-start.27) | collective-permute-done | bytes 1568 | tf_op jit(solution)/shard_map/ppermute | solution.py:234
  124.7 0.7 collective-permute-start.28
  125.4 2.9 %collective-permute-done.28 = f32[6,64]{1,0:T(8,128)S(1)} collective-permute-done((f32[6,64]{1,0:T(8,128)S(1)}, f32[6,64]{1,0:T(8,128)S(1)}, u32[]{:S(2)}, u32[]{:S(2)}) %collective-permute-start.28) | collective-permute-done | bytes 1568 | tf_op jit(solution)/shard_map/ppermute | solution.py:234
  128.3 0.7 collective-permute-start.30
  129.0 4.1 %collective-permute-done.30 = f32[6,64]{1,0:T(8,128)S(1)} collective-permute-done((f32[6,64]{1,0:T(8,128)S(1)}, f32[6,64]{1,0:T(8,128)S(1)}, u32[]{:S(2)}, u32[]{:S(2)}) %collective-permute-start.30) | collective-permute-done | bytes 1568 | tf_op jit(solution)/shard_map/ppermute | solution.py:234
  133.2 2.8 %multiply_subtract_fusion = (f32[64,2048]{1,0:T(8,128)}, f32[64,2048]{1,0:T(8,128)}, f32[64,2048]{1,0:T(8,128)}, f32[64,2048]{1,0:T(8,128)}) fusion(f16[64,2048]{1,0:T(8,128)(2,1)S(1)} %collective-permute-done.29, f32[64,2048]{1,0:T(8,128)S(1)} %get-tuple-element.83, f32[64,2048]{1,0:T(8,128)S(1)} %copy-done, f16[64,2048]{1,0:T(8,128)(2,1)S(1)} %collective-permute-done.15, ...), kind=kLoop, calls=%fused_computation.2 | loop fusion | flops 7077888 | bytes 5507328 | tf_op jit(solution)/shard_map/sub | solution.py:406
  (60 shorter events, 2.0 us)
Async XLA Ops:
  2.6 4.2 %collective-permute-start = (f32[4,64]{1,0:T(4,128)S(1)}, f32[4,64]{1,0:T(4,128)S(1)}, u32[]{:S(2)}, u32[]{:S(2)}) collective-permute-start(f32[4,64]{1,0:T(4,128)S(1)} %pad_maximum_fusion.5), channel_id=1, source_target_pairs={{1,0},{0,1},{3,2},{2,3},{5,4},{4,5},{7,6},{6,7},{9,8},{8,9},{11,10... | collective-permute-start | bytes 3080 | tf_op jit(solution)/shard_map/ppermute | solution.py:234
  2.7 18.6 %collective-permute-start.3 = (bf16[64,1024]{1,0:T(8,128)(2,1)S(1)}, bf16[64,1024]{1,0:T(8,128)(2,1)S(1)}, u32[]{:S(2)}, u32[]{:S(2)}) collective-permute-start(bf16[64,1024]{1,0:T(8,128)(2,1)S(1)} %slice_select_fusion.2), channel_id=1, source_target_pairs={{112,0},{65,1},{48,2},{113,3},{0,4},{33,5},{64,6},{17,7},{96,8},{9... | collective-permute-start | bytes 393224 | tf_op jit(solution)/shard_map/ppermute | solution.py:234
  6.8 5.4 %collective-permute-start.1 = (f32[4,64]{1,0:T(4,128)S(1)}, f32[4,64]{1,0:T(4,128)S(1)}, u32[]{:S(2)}, u32[]{:S(2)}) collective-permute-start(f32[4,64]{1,0:T(4,128)S(1)} %pad_maximum_fusion.6), channel_id=1, source_target_pairs={{8,0},{9,1},{10,2},{11,3},{12,4},{13,5},{14,6},{15,7},{0,8},{1,9},... | collective-permute-start | bytes 3080 | tf_op jit(solution)/shard_map/ppermute | solution.py:234
  12.2 9.1 %collective-permute-start.2 = (f32[4,64]{1,0:T(4,128)S(1)}, f32[4,64]{1,0:T(4,128)S(1)}, u32[]{:S(2)}, u32[]{:S(2)}) collective-permute-start(f32[4,64]{1,0:T(4,128)S(1)} %pad_maximum_fusion.7), channel_id=1, source_target_pairs={{2,0},{3,1},{0,2},{1,3},{6,4},{7,5},{4,6},{5,7},{10,8},{11,9},{8,1... | collective-permute-start | bytes 3080 | tf_op jit(solution)/shard_map/ppermute | solution.py:234
  21.4 4.9 %collective-permute-start.4 = (f32[4,64]{1,0:T(4,128)S(1)}, f32[4,64]{1,0:T(4,128)S(1)}, u32[]{:S(2)}, u32[]{:S(2)}) collective-permute-start(f32[4,64]{1,0:T(4,128)S(1)} %pad_maximum_fusion.8), channel_id=1, source_target_pairs={{6,0},{7,1},{4,2},{5,3},{2,4},{3,5},{0,6},{1,7},{14,8},{15,9},{12,... | collective-permute-start | bytes 3080 | tf_op jit(solution)/shard_map/ppermute | solution.py:234
  21.5 5.1 %collective-permute-start.5 = (bf16[64,1024]{1,0:T(8,128)(2,1)S(1)}, bf16[64,1024]{1,0:T(8,128)(2,1)S(1)}, u32[]{:S(2)}, u32[]{:S(2)}) collective-permute-start(bf16[64,1024]{1,0:T(8,128)(2,1)S(1)} %collective-permute-done.3), channel_id=1, source_target_pairs={{2,0},{3,1},{0,2},{1,3},{6,4},{7,5},{4,6},{5,7},{10,8},{11,9},{8,1... | collective-permute-start | bytes 393224 | tf_op jit(solution)/shard_map/ppermute | solution.py:234
  26.7 1.6 %collective-permute-start.6 = (bf16[64,2048]{1,0:T(8,128)(2,1)S(1)}, bf16[64,2048]{1,0:T(8,128)(2,1)S(1)}, u32[]{:S(2)}, u32[]{:S(2)}) collective-permute-start(bf16[64,2048]{1,0:T(8,128)(2,1)S(1)} %pad_maximum_fusion.2), channel_id=1, source_target_pairs={{1,0},{0,1},{3,2},{2,3},{5,4},{4,5},{7,6},{6,7},{9,8},{8,9},{11,10... | collective-permute-start | bytes 786440 | tf_op jit(solution)/shard_map/ppermute | solution.py:234
  26.9 1.8 %collective-permute-start.7 = (f16[64,2048]{1,0:T(8,128)(2,1)S(1)}, f16[64,2048]{1,0:T(8,128)(2,1)S(1)}, u32[]{:S(2)}, u32[]{:S(2)}) collective-permute-start(f16[64,2048]{1,0:T(8,128)(2,1)S(1)} %multiply_convert_fusion.2), channel_id=1, source_target_pairs={{1,0},{0,1},{3,2},{2,3},{5,4},{4,5},{7,6},{6,7},{9,8},{8,9},{11,10... | collective-permute-start | bytes 786440 | tf_op jit(solution)/shard_map/ppermute | solution.py:234
  28.8 11.2 %collective-permute-start.8 = (f16[64,2048]{1,0:T(8,128)(2,1)S(1)}, f16[64,2048]{1,0:T(8,128)(2,1)S(1)}, u32[]{:S(2)}, u32[]{:S(2)}) collective-permute-start(f16[64,2048]{1,0:T(8,128)(2,1)S(1)} %add_convert_fusion.10), channel_id=1, source_target_pairs={{8,0},{3,1},{10,2},{1,3},{12,4},{7,5},{14,6},{5,7},{0,8},{11,9},{2... | collective-permute-start | bytes 786440 | tf_op jit(solution)/shard_map/ppermute | solution.py:234
  29.2 32.3 %copy-start.1 = (f32[64,2048]{1,0:T(8,128)S(1)}, f32[64,2048]{1,0:T(8,128)}, u32[]{:S(2)}) copy-start(f32[64,2048]{1,0:T(8,128)} %param.6) | copy-start | bytes 1572868
  29.2 35.5 %copy-start = (f32[64,2048]{1,0:T(8,128)S(1)}, f32[64,2048]{1,0:T(8,128)}, u32[]{:S(2)}) copy-start(f32[64,2048]{1,0:T(8,128)} %param.7) | copy-start | bytes 1572868
  29.2 35.5 %copy-start.2 = (f32[64,2048]{1,0:T(8,128)S(1)}, f32[64,2048]{1,0:T(8,128)}, u32[]{:S(2)}) copy-start(f32[64,2048]{1,0:T(8,128)} %param.5) | copy-start | bytes 1572868
  33.1 8.2 %collective-permute-start.9 = (f16[64,1024]{1,0:T(8,128)(2,1)S(1)}, f16[64,1024]{1,0:T(8,128)(2,1)S(1)}, u32[]{:S(2)}, u32[]{:S(2)}) collective-permute-start(f16[64,1024]{1,0:T(8,128)(2,1)S(1)} %multiply_convert_fusion.4), channel_id=1, source_target_pairs={{32,0},{17,1},{34,2},{19,3},{36,4},{21,5},{38,6},{23,7},{40,8},{25... | collective-permute-start | bytes 393224 | tf_op jit(solution)/shard_map/ppermute | solution.py:234
  40.1 6.5 %collective-permute-start.10 = (f16[64,2048]{1,0:T(8,128)(2,1)S(1)}, f16[64,2048]{1,0:T(8,128)(2,1)S(1)}, u32[]{:S(2)}, u32[]{:S(2)}) collective-permute-start(f16[64,2048]{1,0:T(8,128)(2,1)S(1)} %add_convert_fusion.9), channel_id=1, source_target_pairs={{2,0},{7,1},{0,2},{5,3},{6,4},{3,5},{4,6},{1,7},{10,8},{15,9},{8,1... | collective-permute-start | bytes 786440 | tf_op jit(solution)/shard_map/ppermute | solution.py:234
  46.7 6.3 %collective-permute-start.11 = (f16[64,1024]{1,0:T(8,128)(2,1)S(1)}, f16[64,1024]{1,0:T(8,128)(2,1)S(1)}, u32[]{:S(2)}, u32[]{:S(2)}) collective-permute-start(f16[64,1024]{1,0:T(8,128)(2,1)S(1)} %add_convert_fusion.13), channel_id=1, source_target_pairs={{96,0},{33,1},{98,2},{35,3},{100,4},{37,5},{102,6},{39,7},{104,8},... | collective-permute-start | bytes 393224 | tf_op jit(solution)/shard_map/ppermute | solution.py:234
  47.0 7.6 %collective-permute-start.12 = (f16[64,2048]{1,0:T(8,128)(2,1)S(1)}, f16[64,2048]{1,0:T(8,128)(2,1)S(1)}, u32[]{:S(2)}, u32[]{:S(2)}) collective-permute-start(f16[64,2048]{1,0:T(8,128)(2,1)S(1)} %add_convert_fusion.8), channel_id=1, source_target_pairs={{6,0},{9,1},{4,2},{11,3},{2,4},{13,5},{0,6},{15,7},{14,8},{1,9},{1... | collective-permute-start | bytes 786440 | tf_op jit(solution)/shard_map/ppermute | solution.py:234
  54.6 6.8 %collective-permute-start.13 = (f16[64,1024]{1,0:T(8,128)(2,1)S(1)}, f16[64,1024]{1,0:T(8,128)(2,1)S(1)}, u32[]{:S(2)}, u32[]{:S(2)}) collective-permute-start(f16[64,1024]{1,0:T(8,128)(2,1)S(1)} %add_convert_fusion.12), channel_id=1, source_target_pairs={{16,0},{97,1},{18,2},{99,3},{20,4},{101,5},{22,6},{103,7},{24,8},{... | collective-permute-start | bytes 393224 | tf_op jit(solution)/shard_map/ppermute | solution.py:234
  56.8 7.9 %collective-permute-start.15 = (f16[64,2048]{1,0:T(8,128)(2,1)S(1)}, f16[64,2048]{1,0:T(8,128)(2,1)S(1)}, u32[]{:S(2)}, u32[]{:S(2)}) collective-permute-start(f16[64,2048]{1,0:T(8,128)(2,1)S(1)} %add_convert_fusion.7), channel_id=1, source_target_pairs={{4,0},{5,1},{30,2},{31,3},{34,4},{39,5},{60,6},{57,7},{72,8},{73,9... | collective-permute-start | bytes 786440 | tf_op jit(solution)/shard_map/ppermute | solution.py:234
  61.6 11.5 %collective-permute-start.14 = (bf16[64,1024]{1,0:T(8,128)(2,1)S(1)}, bf16[64,1024]{1,0:T(8,128)(2,1)S(1)}, u32[]{:S(2)}, u32[]{:S(2)}) collective-permute-start(bf16[64,1024]{1,0:T(8,128)(2,1)S(1)} %get-tuple-element.84), channel_id=1, source_target_pairs={{112,0},{65,1},{48,2},{113,3},{0,4},{33,5},{64,6},{17,7},{96,8},{9... | collective-permute-start | bytes 393224 | tf_op jit(solution)/shard_map/ppermute | solution.py:234
  73.1 5.7 %collective-permute-start.16 = (bf16[64,1024]{1,0:T(8,128)(2,1)S(1)}, bf16[64,1024]{1,0:T(8,128)(2,1)S(1)}, u32[]{:S(2)}, u32[]{:S(2)}) collective-permute-start(bf16[64,1024]{1,0:T(8,128)(2,1)S(1)} %collective-permute-done.14), channel_id=1, source_target_pairs={{2,0},{3,1},{0,2},{1,3},{6,4},{7,5},{4,6},{5,7},{10,8},{11,9},{8,1... | collective-permute-start | bytes 393224 | tf_op jit(solution)/shard_map/ppermute | solution.py:234
  75.9 5.0 %collective-permute-start.18 = (f16[64,1024]{1,0:T(8,128)(2,1)S(1)}, f16[64,1024]{1,0:T(8,128)(2,1)S(1)}, u32[]{:S(2)}, u32[]{:S(2)}) collective-permute-start(f16[64,1024]{1,0:T(8,128)(2,1)S(1)} %get-tuple-element.54), channel_id=1, source_target_pairs={{32,0},{17,1},{34,2},{19,3},{36,4},{21,5},{38,6},{23,7},{40,8},{25... | collective-permute-start | bytes 393224 | tf_op jit(solution)/shard_map/ppermute | solution.py:234
  77.0 4.0 %collective-permute-start.17 = (f16[64,2048]{1,0:T(8,128)(2,1)S(1)}, f16[64,2048]{1,0:T(8,128)(2,1)S(1)}, u32[]{:S(2)}, u32[]{:S(2)}) collective-permute-start(f16[64,2048]{1,0:T(8,128)(2,1)S(1)} %multiply_convert_fusion.1), channel_id=1, source_target_pairs={{1,0},{0,1},{3,2},{2,3},{5,4},{4,5},{7,6},{6,7},{9,8},{8,9},{11,10... | collective-permute-start | bytes 786440 | tf_op jit(solution)/shard_map/ppermute | solution.py:234
  81.2 1.6 %collective-permute-start.19 = (bf16[64,2048]{1,0:T(8,128)(2,1)S(1)}, bf16[64,2048]{1,0:T(8,128)(2,1)S(1)}, u32[]{:S(2)}, u32[]{:S(2)}) collective-permute-start(bf16[64,2048]{1,0:T(8,128)(2,1)S(1)} %pad_maximum_fusion.3), channel_id=1, source_target_pairs={{1,0},{0,1},{3,2},{2,3},{5,4},{4,5},{7,6},{6,7},{9,8},{8,9},{11,10... | collective-permute-start | bytes 786440 | tf_op jit(solution)/shard_map/ppermute | solution.py:234
  81.3 7.9 %collective-permute-start.20 = (f16[64,2048]{1,0:T(8,128)(2,1)S(1)}, f16[64,2048]{1,0:T(8,128)(2,1)S(1)}, u32[]{:S(2)}, u32[]{:S(2)}) collective-permute-start(f16[64,2048]{1,0:T(8,128)(2,1)S(1)} %add_convert_fusion.6), channel_id=1, source_target_pairs={{8,0},{3,1},{10,2},{1,3},{12,4},{7,5},{14,6},{5,7},{0,8},{11,9},{2... | collective-permute-start | bytes 786440 | tf_op jit(solution)/shard_map/ppermute | solution.py:234
  89.4 6.5 %collective-permute-start.21 = (f16[64,2048]{1,0:T(8,128)(2,1)S(1)}, f16[64,2048]{1,0:T(8,128)(2,1)S(1)}, u32[]{:S(2)}, u32[]{:S(2)}) collective-permute-start(f16[64,2048]{1,0:T(8,128)(2,1)S(1)} %multiply_convert_fusion), channel_id=1, source_target_pairs={{32,0},{17,1},{34,2},{19,3},{36,4},{21,5},{38,6},{23,7},{40,8},{25... | collective-permute-start | bytes 786440 | tf_op jit(solution)/shard_map/ppermute | solution.py:234
  90.5 6.4 %collective-permute-start.22 = (f16[64,2048]{1,0:T(8,128)(2,1)S(1)}, f16[64,2048]{1,0:T(8,128)(2,1)S(1)}, u32[]{:S(2)}, u32[]{:S(2)}) collective-permute-start(f16[64,2048]{1,0:T(8,128)(2,1)S(1)} %add_convert_fusion.5), channel_id=1, source_target_pairs={{2,0},{7,1},{0,2},{5,3},{6,4},{3,5},{4,6},{1,7},{10,8},{15,9},{8,1... | collective-permute-start | bytes 786440 | tf_op jit(solution)/shard_map/ppermute | solution.py:234
  97.0 7.7 %collective-permute-start.23 = (f16[64,2048]{1,0:T(8,128)(2,1)S(1)}, f16[64,2048]{1,0:T(8,128)(2,1)S(1)}, u32[]{:S(2)}, u32[]{:S(2)}) collective-permute-start(f16[64,2048]{1,0:T(8,128)(2,1)S(1)} %add_convert_fusion.4), channel_id=1, source_target_pairs={{96,0},{33,1},{98,2},{35,3},{100,4},{37,5},{102,6},{39,7},{104,8},... | collective-permute-start | bytes 786440 | tf_op jit(solution)/shard_map/ppermute | solution.py:234
  98.3 9.4 %collective-permute-start.24 = (f16[64,2048]{1,0:T(8,128)(2,1)S(1)}, f16[64,2048]{1,0:T(8,128)(2,1)S(1)}, u32[]{:S(2)}, u32[]{:S(2)}) collective-permute-start(f16[64,2048]{1,0:T(8,128)(2,1)S(1)} %add_convert_fusion.3), channel_id=1, source_target_pairs={{6,0},{9,1},{4,2},{11,3},{2,4},{13,5},{0,6},{15,7},{14,8},{1,9},{1... | collective-permute-start | bytes 786440 | tf_op jit(solution)/shard_map/ppermute | solution.py:234
  108.5 9.6 %collective-permute-start.25 = (f16[64,2048]{1,0:T(8,128)(2,1)S(1)}, f16[64,2048]{1,0:T(8,128)(2,1)S(1)}, u32[]{:S(2)}, u32[]{:S(2)}) collective-permute-start(f16[64,2048]{1,0:T(8,128)(2,1)S(1)} %add_convert_fusion.2), channel_id=1, source_target_pairs={{16,0},{97,1},{18,2},{99,3},{20,4},{101,5},{22,6},{103,7},{24,8},{... | collective-permute-start | bytes 786440 | tf_op jit(solution)/shard_map/ppermute | solution.py:234
  112.0 16.3 %collective-permute-start.29 = (f16[64,2048]{1,0:T(8,128)(2,1)}, f16[64,2048]{1,0:T(8,128)(2,1)S(1)}, u32[]{:S(2)}, u32[]{:S(2)}) collective-permute-start(f16[64,2048]{1,0:T(8,128)(2,1)} %add_convert_fusion.1), channel_id=1, source_target_pairs={{4,0},{5,1},{30,2},{31,3},{34,4},{39,5},{60,6},{57,7},{72,8},{73,9... | collective-permute-start | bytes 786440 | tf_op jit(solution)/shard_map/ppermute | solution.py:234
  119.0 1.2 collective-permute-start.26
  120.2 4.5 %collective-permute-start.27 = (f32[6,64]{1,0:T(8,128)S(1)}, f32[6,64]{1,0:T(8,128)S(1)}, u32[]{:S(2)}, u32[]{:S(2)}) collective-permute-start(f32[6,64]{1,0:T(8,128)S(1)} %add.166), channel_id=1, source_target_pairs={{8,0},{9,1},{10,2},{11,3},{12,4},{13,5},{14,6},{15,7},{0,8},{1,9},... | collective-permute-start | bytes 4616 | tf_op jit(solution)/shard_map/ppermute | solution.py:234
  124.7 3.6 %collective-permute-start.28 = (f32[6,64]{1,0:T(8,128)S(1)}, f32[6,64]{1,0:T(8,128)S(1)}, u32[]{:S(2)}, u32[]{:S(2)}) collective-permute-start(f32[6,64]{1,0:T(8,128)S(1)} %add.167), channel_id=1, source_target_pairs={{2,0},{3,1},{0,2},{1,3},{6,4},{7,5},{4,6},{5,7},{10,8},{11,9},{8,1... | collective-permute-start | bytes 4616 | tf_op jit(solution)/shard_map/ppermute | solution.py:234
  128.3 4.8 %collective-permute-start.30 = (f32[6,64]{1,0:T(8,128)S(1)}, f32[6,64]{1,0:T(8,128)S(1)}, u32[]{:S(2)}, u32[]{:S(2)}) collective-permute-start(f32[6,64]{1,0:T(8,128)S(1)} %add.168), channel_id=1, source_target_pairs={{6,0},{7,1},{4,2},{5,3},{2,4},{3,5},{0,6},{1,7},{14,8},{15,9},{12,... | collective-permute-start | bytes 4616 | tf_op jit(solution)/shard_map/ppermute | solution.py:234
